TPU v7x, 32 devices: a whole 2x2x4 slice. The times are simulated.
32 devices in a mesh: grp: 4 (over z), tok: 8 (over y, x, core).
Axes of the slice: x: 2, y: 2, z: 4, core: 2. Of those that a mesh axis runs over, the one named last changes fastest.
Arguments:
- prompt_states: bfloat16 [8, 1024, 2048], P('grp', 'tok'), may hold values from -6 to 6
- answer_states: bfloat16 [32, 128, 2048], P(('grp', 'tok')), may hold values from -6 to 6
- answer_prompt: int32 [32], P('grp'), may hold values from 0 to 7, as said below
- prompt_teacher: bfloat16 [8, 1024, 2048], P('grp', 'tok'), may hold values from -6 to 6
- answer_teacher: bfloat16 [32, 128, 2048], P(('grp', 'tok')), may hold values from -6 to 6
- prompt_valid: int32 [8, 1024], P('grp', 'tok'), may hold values from 0 to 1
- answer_valid: int32 [32, 128], P(('grp', 'tok')), may hold values from 0 to 1, as said below
- first_gain: bfloat16 [2048], P(('grp', 'tok')), may hold values from 0.099609375 to 1.8984375
- first_shift: bfloat16 [2048], P(('grp', 'tok')), may hold values from -1.75 to 1.75
- query_weight: bfloat16 [2048, 2048], P('grp', 'tok'), may hold values from -0.125 to 0.125
- query_bias: bfloat16 [2048], P(('grp', 'tok')), may hold values from -1.75 to 1.75
- keyval_weight: bfloat16 [2048, 256], P(('grp', 'tok')), may hold values from -0.125 to 0.125
- value_bias: bfloat16 [128], replicated, may hold values from -3 to 3
- output_weight: bfloat16 [2048, 2048], P('grp', 'tok'), may hold values from -0.5 to 0.5
- output_bias: bfloat16 [2048], P(('grp', 'tok')), may hold values from -1.75 to 1.75
- second_gain: bfloat16 [2048], P(('grp', 'tok')), may hold values from 0.099609375 to 1.8984375
- second_shift: bfloat16 [2048], P(('grp', 'tok')), may hold values from -1.75 to 1.75
- up_weight: bfloat16 [2048, 8192], P('grp', 'tok'), may hold values from -0.125 to 0.125
- up_bias: bfloat16 [8192], P(('grp', 'tok')), may hold values from -3 to 3
- down_weight: bfloat16 [2048, 8192], P('grp', 'tok'), may hold values from -0.125 to 0.125
- down_bias: bfloat16 [2048], P(('grp', 'tok')), may hold values from -1.75 to 1.75
Outputs:
- prompt_out: bfloat16 [8, 1024, 2048], P('grp', 'tok')
- answer_out: bfloat16 [32, 128, 2048], P(('grp', 'tok'))
- prompt_grad: bfloat16 [8, 1024, 2048], P('grp', 'tok')
- answer_grad: bfloat16 [32, 128, 2048], P(('grp', 'tok'))
- grad_first_gain: float32 [2048], P(('grp', 'tok'))
- grad_first_shift: float32 [2048], P(('grp', 'tok'))
- grad_query_weight: float32 [2048, 2048], P('grp', 'tok')
- grad_query_bias: float32 [2048], P(('grp', 'tok'))
- grad_keyval_weight: float32 [2048, 256], P(('grp', 'tok'))
- grad_value_bias: float32 [128], replicated
- grad_output_weight: float32 [2048, 2048], P('grp', 'tok')
- grad_output_bias: float32 [2048], P(('grp', 'tok'))
- grad_second_gain: float32 [2048], P(('grp', 'tok'))
- grad_second_shift: float32 [2048], P(('grp', 'tok'))
- grad_up_weight: float32 [2048, 8192], P('grp', 'tok')
- grad_up_bias: float32 [8192], P(('grp', 'tok'))
- grad_down_weight: float32 [2048, 8192], P('grp', 'tok')
- grad_down_bias: float32 [2048], P(('grp', 'tok'))
- loss: float32 [], replicated
Inputs may be any that keep to these rules, and one draw needn't show every extreme that they name: `answer_prompt`: answer a continues one of the 2 prompts a // 8 * 2 + k, k = 0 .. 1, and each prompt is continued by exactly 4 answers. `answer_valid`: the first token of every answer is valid.
All inputs are finite; a program needn't handle non-finite values.
Results may differ from a plain program's by a relative error of at most 0.018.
Values may be sent and summed in bfloat16 or wider, within the bound.
A program may use at most 512 MiB of HBM per device.

v0:
```python
import jax
import jax.numpy as jnp
from jax import lax
from jax.sharding import PartitionSpec as P

HEAD_WIDTH = 128


epsilon = 1e-05
masked = -1e30


def for_sending(value):
    return jax.tree.map(lambda a: a.astype(jnp.bfloat16) if a.dtype == jnp.float32 else a, value)


def norm_forward(values, gain, shift):
    center = values - jnp.mean(values, axis=-1, keepdims=True)
    inverse = lax.rsqrt(jnp.mean(center * center, axis=-1, keepdims=True) + epsilon)
    scaled = center * inverse
    return (scaled * gain + shift, scaled, inverse)


def norm_backward(grad_out, gain, scaled, inverse):
    weighted = grad_out * gain
    grad_in = inverse * (
        weighted
        - jnp.mean(weighted, axis=-1, keepdims=True)
        - scaled * jnp.mean(weighted * scaled, axis=-1, keepdims=True)
    )
    return (grad_in, jnp.sum(grad_out * scaled, axis=0), jnp.sum(grad_out, axis=0))


def plain_product(left, right):
    return jnp.dot(left, right, preferred_element_type=jnp.float32)


def transposed_product(left, right):
    return lax.dot_general(
        left, right, (((1,), (1,)), ((), ())), preferred_element_type=jnp.float32
    )


def weight_product(left, right):
    return lax.dot_general(
        left, right, (((0,), (0,)), ((), ())), preferred_element_type=jnp.float32
    )


def score_block(query_matrix, key_slice, allowed, score_scale):
    unscaled_scores = (
        jnp.einsum("ngs,nhs->ngh", query_matrix, key_slice, preferred_element_type=jnp.float32)
        * score_scale
    )
    return jnp.where(allowed, unscaled_scores, masked)


def attend_forward(query_matrix, key_value_rows, allowed, head_width, score_scale):
    scores = score_block(query_matrix, key_value_rows[..., :head_width], allowed, score_scale)
    row_max = jnp.max(scores, axis=-1, keepdims=True)
    exponent = jnp.exp(scores - row_max)
    row_total = jnp.sum(exponent, axis=-1, keepdims=True)
    attention_weights = (exponent / row_total).astype(jnp.bfloat16)
    mixture = jnp.einsum(
        "mfl,mle->mfe",
        attention_weights,
        key_value_rows[..., head_width:],
        preferred_element_type=jnp.float32,
    )
    return (mixture, row_max + jnp.log(row_total))


def attend_backward(
    query_matrix, key_value_rows, allowed, log_total, mixture_gradient, head_width, score_scale
):
    key_slice = key_value_rows[..., :head_width]
    value_slice = key_value_rows[..., head_width:]
    scores = score_block(query_matrix, key_slice, allowed, score_scale)
    probabilities = jnp.exp(scores - log_total)
    attention_weights = probabilities.astype(jnp.bfloat16)
    grad_values = jnp.einsum(
        "yiv,yij->yvj", attention_weights, mixture_gradient, preferred_element_type=jnp.float32
    )
    grad_probs = jnp.einsum(
        "ngs,nhs->ngh", mixture_gradient, value_slice, preferred_element_type=jnp.float32
    )
    inner_sum = jnp.sum(probabilities * grad_probs, axis=-1, keepdims=True)
    score_gradient = (probabilities * (grad_probs - inner_sum)).astype(jnp.bfloat16)
    grad_queries = (
        jnp.einsum("mfl,mle->mfe", score_gradient, key_slice, preferred_element_type=jnp.float32)
        * score_scale
    )
    grad_keys = (
        jnp.einsum("yiv,yij->yvj", score_gradient, query_matrix, preferred_element_type=jnp.float32)
        * score_scale
    )
    return (grad_queries, jnp.concatenate([grad_keys, grad_values], axis=-1))


def column_sums(values):
    return jnp.sum(values.astype(jnp.float32), axis=0)


def fetch_weights(weight_pair):
    by_rows = (
        lax.all_gather(weight_pair[0], "grp", axis=0, tiled=True),
        lax.all_gather(weight_pair[1], "grp", axis=0, tiled=True),
    )
    return by_rows


def return_grads(grad_pair):
    return (
        lax.psum_scatter(
            grad_pair[0].astype(jnp.bfloat16), "grp", scatter_dimension=0, tiled=True
        ).astype(jnp.float32),
        lax.psum_scatter(
            grad_pair[1].astype(jnp.bfloat16), "grp", scatter_dimension=0, tiled=True
        ).astype(jnp.float32),
    )


def rows_gather(row_parts):
    return jax.tree.map(
        lambda part, own: part.astype(own.dtype),
        lax.all_gather(for_sending(row_parts), "tok", axis=0, tiled=True),
        row_parts,
    )


def rows_sum(row_parts):
    return jax.tree.map(
        lambda part: part.astype(jnp.float32),
        lax.psum_scatter(for_sending(row_parts), "tok", scatter_dimension=0, tiled=True),
    )


def prompt_heads(prompt_part, query_rows, prompt_count, heads_here, head_width):
    split_heads = prompt_part.reshape(query_rows, prompt_count, heads_here, head_width)
    return jnp.transpose(split_heads, (1, 0, 2, 3)).reshape(
        prompt_count, query_rows * heads_here, head_width
    )


def prompt_back(per_prompt, query_rows, prompt_count):
    row_width = per_prompt.shape[1] // query_rows * per_prompt.shape[2]
    return jnp.swapaxes(per_prompt.reshape(prompt_count, query_rows, row_width), 0, 1).reshape(
        -1, row_width
    )


def body(
    prompt_states,
    answer_states,
    answer_prompt,
    prompt_teacher,
    answer_teacher,
    prompt_valid,
    answer_valid,
    first_gain,
    first_shift,
    query_weight,
    query_bias,
    keyval_weight,
    value_bias,
    output_weight,
    output_bias,
    second_gain,
    second_shift,
    up_weight,
    up_bias,
    down_weight,
    down_bias,
):
    prompt_count, prompt_rows, model_width = prompt_states.shape
    answer_count, answer_len, _ = answer_states.shape
    token_devices = lax.axis_size("tok")
    token_index = lax.axis_index("tok")
    prompt_len = prompt_rows * token_devices
    head_width = HEAD_WIDTH
    score_scale = head_width ** (-0.5)
    own_prompt = prompt_rows * prompt_count
    hidden_units = up_bias.shape[0] * lax.axis_size("grp") * token_devices
    states = jnp.concatenate(
        [
            jnp.swapaxes(prompt_states, 0, 1).reshape(-1, model_width),
            answer_states.reshape(-1, model_width),
        ],
        axis=0,
    )
    inputs = states.astype(jnp.float32)
    teacher = jnp.concatenate(
        [
            jnp.swapaxes(prompt_teacher, 0, 1).reshape(-1, model_width),
            answer_teacher.reshape(-1, model_width),
        ],
        axis=0,
    ).astype(jnp.float32)
    valid_rows = jnp.concatenate(
        [jnp.swapaxes(prompt_valid, 0, 1).reshape(-1), answer_valid.reshape(-1)]
    ).astype(jnp.float32)
    heads_here = model_width // head_width // token_devices
    ff_here = hidden_units // token_devices
    answers_here = answer_count * token_devices
    first_place = 0
    column_width = heads_here * head_width
    column_start = token_index * column_width
    ff_start = token_index * ff_here
    group_prompt = prompt_len * prompt_count
    (
        gain_one,
        shift_one,
        query_offset,
        keyval_full,
        output_offset,
        gain_two,
        shift_two,
        up_offset,
        down_offset,
    ) = (
        lax.all_gather(first_gain, ("grp", "tok"), axis=0, tiled=True),
        lax.all_gather(first_shift, ("grp", "tok"), axis=0, tiled=True),
        lax.all_gather(query_bias, ("grp", "tok"), axis=0, tiled=True),
        lax.all_gather(keyval_weight, ("grp", "tok"), axis=0, tiled=True),
        lax.all_gather(output_bias, ("grp", "tok"), axis=0, tiled=True),
        lax.all_gather(second_gain, ("grp", "tok"), axis=0, tiled=True),
        lax.all_gather(second_shift, ("grp", "tok"), axis=0, tiled=True),
        lax.all_gather(up_bias, ("grp", "tok"), axis=0, tiled=True),
        lax.all_gather(down_bias, ("grp", "tok"), axis=0, tiled=True),
    )
    gain_one = gain_one.astype(jnp.float32)
    gain_two = gain_two.astype(jnp.float32)
    query_here = lax.dynamic_slice_in_dim(
        query_offset.astype(jnp.float32), column_start, column_width
    )
    up_here = lax.dynamic_slice_in_dim(up_offset.astype(jnp.float32), ff_start, ff_here)
    owning = answer_prompt - lax.axis_index("grp") * prompt_count
    normed_one, scaled_one, inverse_one = norm_forward(
        inputs, gain_one, shift_one.astype(jnp.float32)
    )
    normed_one = normed_one.astype(jnp.bfloat16)
    key_offset = jnp.concatenate(
        [jnp.zeros((head_width,), jnp.float32), value_bias.astype(jnp.float32)]
    )
    key_value_rows = (plain_product(normed_one, keyval_full) + key_offset).astype(jnp.bfloat16)
    query_cols, output_cols = fetch_weights((query_weight, output_weight))
    norm_prompt, norm_answer, kv_prompt, kv_answer = rows_gather(
        (
            normed_one[:own_prompt],
            normed_one[own_prompt:],
            key_value_rows[:own_prompt],
            key_value_rows[own_prompt:],
        )
    )
    group_norm = jnp.concatenate([norm_prompt, norm_answer], axis=0)
    query_matrix = (plain_product(group_norm, query_cols) + query_here).astype(jnp.bfloat16)
    prompt_queries = prompt_heads(
        query_matrix[:group_prompt], prompt_len, prompt_count, heads_here, head_width
    )
    answer_queries = query_matrix[group_prompt:].reshape(
        answers_here, answer_len * heads_here, head_width
    )
    prompt_keyvals = jnp.swapaxes(kv_prompt.reshape(prompt_len, prompt_count, 2 * head_width), 0, 1)
    chosen = jnp.take(prompt_keyvals, owning, axis=0)
    answer_keyvals = jnp.concatenate(
        [chosen, kv_answer.reshape(answers_here, answer_len, 2 * head_width)], axis=1
    )
    prompt_place = first_place + jnp.arange(prompt_len * heads_here) // heads_here
    prompt_allowed = (jnp.arange(prompt_len)[None, :] <= prompt_place[:, None])[None]
    answer_place = jnp.arange(answer_len * heads_here) // heads_here
    answer_key_place = jnp.arange(prompt_len + answer_len) - prompt_len
    answer_allowed = (answer_key_place[None, :] <= answer_place[:, None])[None]
    prompt_mixture, prompt_log = attend_forward(
        prompt_queries, prompt_keyvals, prompt_allowed, head_width, score_scale
    )
    answer_mixture, answer_log = attend_forward(
        answer_queries, answer_keyvals, answer_allowed, head_width, score_scale
    )
    mixture = jnp.concatenate(
        [
            prompt_back(prompt_mixture, prompt_len, prompt_count),
            answer_mixture.reshape(-1, column_width),
        ],
        axis=0,
    ).astype(jnp.bfloat16)
    attend_term = transposed_product(mixture, output_cols)
    attend_term = jnp.concatenate(
        rows_sum((attend_term[:group_prompt], attend_term[group_prompt:])), axis=0
    )
    hidden = inputs + attend_term + output_offset.astype(jnp.float32)
    normed_two, scaled_two, inverse_two = norm_forward(
        hidden, gain_two, shift_two.astype(jnp.float32)
    )
    normed_two = normed_two.astype(jnp.bfloat16)
    up_cols, down_cols = fetch_weights((up_weight, down_weight))
    group_two = jnp.concatenate(
        rows_gather((normed_two[:own_prompt], normed_two[own_prompt:])), axis=0
    )
    pre_active = plain_product(group_two, up_cols) + up_here
    activated = jax.nn.gelu(pre_active, approximate=True).astype(jnp.bfloat16)
    feed_term = transposed_product(activated, down_cols)
    feed_term = jnp.concatenate(
        rows_sum((feed_term[:group_prompt], feed_term[group_prompt:])), axis=0
    )
    result_rows = hidden + feed_term + down_offset.astype(jnp.float32)
    differ = result_rows - teacher
    valid_count, squared_sum = lax.psum(
        (jnp.sum(valid_rows), jnp.sum(valid_rows[:, None] * differ * differ)), ("grp", "tok")
    )
    loss_value = squared_sum / (valid_count * model_width)
    every_token = valid_rows.shape[0] * lax.axis_size("grp") * token_devices
    grad_result = every_token / valid_count * valid_rows[:, None] * differ
    up_back, down_back = fetch_weights((up_weight, down_weight))
    grad_branch_two = grad_result.astype(jnp.bfloat16)
    group_grad_two = jnp.concatenate(
        rows_gather((grad_branch_two[:own_prompt], grad_branch_two[own_prompt:])), axis=0
    )
    grad_down_cols = weight_product(group_grad_two, activated)
    grad_down_offset = column_sums(grad_branch_two)
    grad_activated = plain_product(group_grad_two, down_back)
    _, gelu_back = jax.vjp(lambda argument: jax.nn.gelu(argument, approximate=True), pre_active)
    grad_pre_active = gelu_back(grad_activated)[0].astype(jnp.bfloat16)
    grad_up_cols = weight_product(group_two, grad_pre_active)
    grad_up_offset = lax.dynamic_update_slice_in_dim(
        jnp.zeros((hidden_units,), jnp.float32), column_sums(grad_pre_active), ff_start, 0
    )
    grad_normed_two = transposed_product(grad_pre_active, up_back)
    grad_normed_two = jnp.concatenate(
        rows_sum((grad_normed_two[:group_prompt], grad_normed_two[group_prompt:])), axis=0
    )
    grad_norm_two, grad_gain_two, grad_shift_two = norm_backward(
        grad_normed_two, gain_two, scaled_two, inverse_two
    )
    grad_hidden = grad_result + grad_norm_two
    feed_grads = return_grads((grad_up_cols, grad_down_cols))
    query_back, output_back = fetch_weights((query_weight, output_weight))
    grad_branch_one = grad_hidden.astype(jnp.bfloat16)
    group_grad_one = jnp.concatenate(
        rows_gather((grad_branch_one[:own_prompt], grad_branch_one[own_prompt:])), axis=0
    )
    grad_output_cols = weight_product(group_grad_one, mixture)
    grad_output_offset = column_sums(grad_branch_one)
    mixture_gradient = plain_product(group_grad_one, output_back).astype(jnp.bfloat16)
    grad_prompt_mixture = prompt_heads(
        mixture_gradient[:group_prompt], prompt_len, prompt_count, heads_here, head_width
    )
    grad_answer_mixture = mixture_gradient[group_prompt:].reshape(
        answers_here, answer_len * heads_here, head_width
    )
    grad_prompt_queries, grad_prompt_kv = attend_backward(
        prompt_queries,
        prompt_keyvals,
        prompt_allowed,
        prompt_log,
        grad_prompt_mixture,
        head_width,
        score_scale,
    )
    grad_answer_queries, grad_answer_kv = attend_backward(
        answer_queries,
        answer_keyvals,
        answer_allowed,
        answer_log,
        grad_answer_mixture,
        head_width,
        score_scale,
    )
    chooser = (owning[:, None] == jnp.arange(prompt_count)[None, :]).astype(jnp.float32)
    prompt_terms = grad_prompt_kv + jnp.einsum(
        "ap,akd->pkd", chooser, grad_answer_kv[:, :prompt_len], precision=lax.Precision.HIGHEST
    )
    prompt_term_rows = jnp.swapaxes(prompt_terms, 0, 1).reshape(-1, 2 * head_width)
    answer_term_rows = grad_answer_kv[:, prompt_len:].reshape(-1, 2 * head_width)
    grad_queries = jnp.concatenate(
        [
            prompt_back(grad_prompt_queries, prompt_len, prompt_count),
            grad_answer_queries.reshape(-1, column_width),
        ],
        axis=0,
    ).astype(jnp.bfloat16)
    grad_query_cols = weight_product(group_norm, grad_queries)
    grad_query_offset = lax.dynamic_update_slice_in_dim(
        jnp.zeros((model_width,), jnp.float32), column_sums(grad_queries), column_start, 0
    )
    query_term = transposed_product(grad_queries, query_back)
    own_query_prompt, own_query_answer, own_kv_prompt, own_kv_answer = rows_sum(
        (query_term[:group_prompt], query_term[group_prompt:], prompt_term_rows, answer_term_rows)
    )
    query_term = jnp.concatenate([own_query_prompt, own_query_answer], axis=0)
    keyval_sums = jnp.concatenate([own_kv_prompt, own_kv_answer], axis=0)
    grad_keyvals = keyval_sums.astype(jnp.bfloat16)
    grad_keyval_full = weight_product(normed_one, grad_keyvals)
    grad_value_offset = column_sums(grad_keyvals[:, head_width:])
    grad_normed_one = query_term + transposed_product(grad_keyvals, keyval_full)
    grad_norm_one, grad_gain_one, grad_shift_one = norm_backward(
        grad_normed_one, gain_one, scaled_one, inverse_one
    )
    grad_inputs = grad_hidden + grad_norm_one
    attend_grads = return_grads((grad_query_cols, grad_output_cols))
    small_grads = (
        lax.psum_scatter(grad_gain_one, ("grp", "tok"), scatter_dimension=0, tiled=True),
        lax.psum_scatter(grad_shift_one, ("grp", "tok"), scatter_dimension=0, tiled=True),
        lax.psum_scatter(grad_query_offset, ("grp", "tok"), scatter_dimension=0, tiled=True),
        lax.psum_scatter(grad_keyval_full, ("grp", "tok"), scatter_dimension=0, tiled=True),
        lax.psum_scatter(grad_output_offset, ("grp", "tok"), scatter_dimension=0, tiled=True),
        lax.psum_scatter(grad_gain_two, ("grp", "tok"), scatter_dimension=0, tiled=True),
        lax.psum_scatter(grad_shift_two, ("grp", "tok"), scatter_dimension=0, tiled=True),
        lax.psum_scatter(grad_up_offset, ("grp", "tok"), scatter_dimension=0, tiled=True),
        lax.psum_scatter(grad_down_offset, ("grp", "tok"), scatter_dimension=0, tiled=True),
    )
    value_total = lax.psum(grad_value_offset, ("grp", "tok"))
    prompt_out = jnp.swapaxes(
        result_rows[:own_prompt].reshape(prompt_rows, prompt_count, model_width), 0, 1
    )
    answer_out = result_rows[own_prompt:].reshape(answer_count, answer_len, model_width)
    prompt_grad = jnp.swapaxes(
        grad_inputs[:own_prompt].reshape(prompt_rows, prompt_count, model_width), 0, 1
    )
    answer_grad = grad_inputs[own_prompt:].reshape(answer_count, answer_len, model_width)
    return (
        prompt_out.astype(jnp.bfloat16),
        answer_out.astype(jnp.bfloat16),
        prompt_grad.astype(jnp.bfloat16),
        answer_grad.astype(jnp.bfloat16),
        small_grads[0],
        small_grads[1],
        attend_grads[0],
        small_grads[2],
        small_grads[3],
        value_total,
        attend_grads[1],
        small_grads[4],
        small_grads[5],
        small_grads[6],
        feed_grads[0],
        small_grads[7],
        feed_grads[1],
        small_grads[8],
        loss_value,
    )


def solution(mesh):
    in_specs = (
        P("grp", "tok", None),
        P(("grp", "tok"), None, None),
        P("grp"),
        P("grp", "tok", None),
        P(("grp", "tok"), None, None),
        P("grp", "tok"),
        P(("grp", "tok"), None),
        P(("grp", "tok")),
        P(("grp", "tok")),
        P("grp", "tok"),
        P(("grp", "tok")),
        P(("grp", "tok"), None),
        P(),
        P("grp", "tok"),
        P(("grp", "tok")),
        P(("grp", "tok")),
        P(("grp", "tok")),
        P("grp", "tok"),
        P(("grp", "tok")),
        P("grp", "tok"),
        P(("grp", "tok")),
    )
    out_specs = (
        P("grp", "tok", None),
        P(("grp", "tok"), None, None),
        P("grp", "tok", None),
        P(("grp", "tok"), None, None),
        P(("grp", "tok")),
        P(("grp", "tok")),
        P("grp", "tok"),
        P(("grp", "tok")),
        P(("grp", "tok"), None),
        P(),
        P("grp", "tok"),
        P(("grp", "tok")),
        P(("grp", "tok")),
        P(("grp", "tok")),
        P("grp", "tok"),
        P(("grp", "tok")),
        P("grp", "tok"),
        P(("grp", "tok")),
        P(),
    )
    return jax.shard_map(body, mesh=mesh, in_specs=in_specs, out_specs=out_specs, check_vma=False)
```

profile of v0, /device:TPU:0, one launch (start us, length us, event | category | flops | bytes accessed | tf_op | source)
XLA Modules:
  0.0 1915.0 jit_solution(8922995352210948020)
XLA Ops:
  13.9 42.5 %all-reduce.17 = (bf16[2048]{0:T(1024)(128)(2,1)}, bf16[2048]{0:T(1024)(128)(2,1)S(1)}, bf16[2048]{0:T(1024)(128)(2,1)S(1)}, bf16[2048]{0:T(1024)(128)(2,1)S(1)}...) all-reduce(bf16[2048]{0:T(1024)(128)(2,1)S(1)} %dynamic-update-slic, ...), channel_id=1, replica_groups=mesh['grp'=4,'tok'=8] {'grp','tok'}, use_global_device_ids=true, to_apply=%add.7 | all-reduce | flops 14336 | bytes 57344
  104.7 45.6 %all-gather.16.cloned.1.call-done = bf16[2048,2048]{1,0:T(8,128)(2,1)} async-done(((bf16[256,2048]{1,0:T(8,128)(2,1)}), bf16[2048,2048]{1,0:T(8,128)(2,1)}) %all-gather.16.cloned.1.call-update) | async-done | bytes 8388624 | tf_op jit(solution)/shard_map/all_gather | solution.py:126
  158.7 30.7 %all-gather.18.cloned.1.call-done = bf16[1024,2048]{1,0:T(8,128)(2,1)} async-done(((bf16[128,2048]{1,0:T(8,128)(2,1)}), bf16[1024,2048]{1,0:T(8,128)(2,1)}) %all-gather.18.cloned.1.call-update) | async-done | bytes 4194320 | tf_op jit(solution)/shard_map/all_gather | solution.py:126
  194.2 24.6 %all-gather.20.cloned.1.call-done = bf16[2048,256]{1,0:T(8,128)(2,1)} async-done(((bf16[512,256]{1,0:T(8,128)(2,1)}), bf16[2048,256]{1,0:T(8,128)(2,1)}) %all-gather.20.cloned.1.call-update) | async-done | bytes 1048592 | tf_op jit(solution)/shard_map/all_gather | solution.py:106
  308.7 42.2 %reduce-scatter.18.cloned.1.call-done = bf16[128,2048]{1,0:T(8,128)(2,1)} async-done(((bf16[1024,2048]{1,0:T(8,128)(2,1)}), bf16[128,2048]{1,0:T(8,128)(2,1)}) %reduce-scatter.18.cloned.1.call-update) | async-done | bytes 524304 | tf_op jit(solution)/shard_map/reduce_scatter | solution.py:134
  350.9 75.2 %reduce-scatter.16.cloned.1.call-done = bf16[256,2048]{1,0:T(8,128)(2,1)} async-done(((bf16[2048,2048]{1,0:T(8,128)(2,1)}), bf16[256,2048]{1,0:T(8,128)(2,1)}) %reduce-scatter.16.cloned.1.call-update) | async-done | bytes 1048592 | tf_op jit(solution)/shard_map/reduce_scatter | solution.py:134
  437.0 40.6 %all-gather = bf16[32,1,256]{2,1,0:T(2,128)(2,1)S(1)} all-gather(bf16[1,1,256]{2,1,0:T(2,128)(2,1)S(1)} %reshape.343), channel_id=1, replica_groups=mesh['grp'=4,'tok'=8] {'grp','tok'}, dimensions={0}, use_global_device_ids=true | all-gather | bytes 16896 | tf_op jit(solution)/shard_map/all_gather | solution.py:228
  496.6 30.7 %all-gather.30.cloned.1.call-done = bf16[1024,2048]{1,0:T(8,128)(2,1)} async-done(((bf16[128,2048]{1,0:T(8,128)(2,1)}), bf16[1024,2048]{1,0:T(8,128)(2,1)}) %all-gather.30.cloned.1.call-update) | async-done | bytes 4194320 | tf_op jit(solution)/shard_map/all_gather | solution.py:126
  532.1 77.6 %all-gather.32.cloned.1.call-done = bf16[2048,1024]{1,0:T(8,128)(2,1)} async-done(((bf16[512,1024]{1,0:T(8,128)(2,1)}), bf16[2048,1024]{1,0:T(8,128)(2,1)}) %all-gather.32.cloned.1.call-update) | async-done | bytes 4194320 | tf_op jit(solution)/shard_map/all_gather | solution.py:106
  609.7 19.1 fusion.71
  628.8 61.6 %all-gather.34.cloned.1.call-done = bf16[2048,1024]{1,0:T(8,128)(2,1)} async-done(((bf16[512,1024]{1,0:T(8,128)(2,1)}), bf16[2048,1024]{1,0:T(8,128)(2,1)}) %all-gather.34.cloned.1.call-update) | async-done | bytes 4194320 | tf_op jit(solution)/shard_map/all_gather | solution.py:107
  690.5 25.2 %convolution_convert_fusion.1 = bf16[3072,2048]{1,0:T(8,128)(2,1)} fusion(bf16[2048,1024]{1,0:T(8,128)(2,1)} %all-gather.34.cloned.1.call-done, f32[3072,1024]{1,0:T(8,128)} %fusion.71, f32[1024]{0:T(1024)S(1)} %dynamic_slice.7), kind=kOutput, calls=%fused_computation.21 | convolution fusion | flops 12922650624 | bytes 29364224 | tf_op jit(solution)/shard_map/dot_general | solution.py:39
  731.1 38.9 %psum.21 = f32[]{:T(128)} all-reduce(f32[]{:T(128)} %fusion.64), channel_id=1, replica_groups=mesh['grp'=4,'tok'=8] {'grp','tok'}, use_global_device_ids=true, to_apply=%region_13.14 | all-reduce | flops 1 | bytes 8 | tf_op jit(solution)/shard_map/psum | solution.py:307
  776.2 69.8 %reduce-scatter.20.cloned.1.call-done = bf16[256,2048]{1,0:T(8,128)(2,1)} async-done(((bf16[2048,2048]{1,0:T(8,128)(2,1)}), bf16[256,2048]{1,0:T(8,128)(2,1)}) %reduce-scatter.20.cloned.1.call-update) | async-done | bytes 1048592 | tf_op jit(solution)/shard_map/reduce_scatter | solution.py:134
  853.5 52.5 %all-gather.36.cloned.1.call-done = bf16[2048,2048]{1,0:T(8,128)(2,1)} async-done(((bf16[256,2048]{1,0:T(8,128)(2,1)}), bf16[2048,2048]{1,0:T(8,128)(2,1)}) %all-gather.36.cloned.1.call-update) | async-done | bytes 8388624 | tf_op jit(solution)/shard_map/all_gather | solution.py:126
  914.4 30.7 %all-gather.38.cloned.1.call-done = bf16[1024,2048]{1,0:T(8,128)(2,1)} async-done(((bf16[128,2048]{1,0:T(8,128)(2,1)}), bf16[1024,2048]{1,0:T(8,128)(2,1)}) %all-gather.38.cloned.1.call-update) | async-done | bytes 4194320 | tf_op jit(solution)/shard_map/all_gather | solution.py:126
  949.8 29.7 %convert_reduce_fusion = (f32[1024]{0:T(1024)}, bf16[3072,1024]{1,0:T(8,128)(2,1)}) fusion(f32[3072,1024]{1,0:T(8,128)} %fusion.71, f32[1024]{0:T(1024)S(1)} %dynamic_slice.7, bf16[3072,2048]{1,0:T(8,128)(2,1)} %constant_dynamic-update-slice_fusion.6, bf16[2048,1024]{1,0:T(8,128)(2,1)} %all-gather.34.cloned.1.call-done), kind=kOutput, calls=%fused_computation.18 | convolution fusion | flops 12957252608 | bytes 35659776 | tf_op jit(solution)/shard_map/dot_general | solution.py:35
  979.5 18.9 convolution_convert_fusion
  1011.8 42.9 %reduce-scatter.26.cloned.1.call-done = bf16[128,2048]{1,0:T(8,128)(2,1)} async-done(((bf16[1024,2048]{1,0:T(8,128)(2,1)}), bf16[128,2048]{1,0:T(8,128)(2,1)}) %reduce-scatter.26.cloned.1.call-update) | async-done | bytes 524304 | tf_op jit(solution)/shard_map/reduce_scatter | solution.py:134
  1056.8 72.9 %reduce-scatter.24.cloned.1.call-done = bf16[256,2048]{1,0:T(8,128)(2,1)} async-done(((bf16[2048,2048]{1,0:T(8,128)(2,1)}), bf16[256,2048]{1,0:T(8,128)(2,1)}) %reduce-scatter.24.cloned.1.call-update) | async-done | bytes 1048592 | tf_op jit(solution)/shard_map/reduce_scatter | solution.py:134
  1144.9 52.3 %all-gather.40.cloned.1.call-done = bf16[2048,2048]{1,0:T(8,128)(2,1)} async-done(((bf16[256,2048]{1,0:T(8,128)(2,1)}), bf16[2048,2048]{1,0:T(8,128)(2,1)}) %all-gather.40.cloned.1.call-update) | async-done | bytes 8388624 | tf_op jit(solution)/shard_map/all_gather | solution.py:126
  1205.6 30.7 %all-gather.42.cloned.1.call-done = bf16[1024,2048]{1,0:T(8,128)(2,1)} async-done(((bf16[128,2048]{1,0:T(8,128)(2,1)}), bf16[1024,2048]{1,0:T(8,128)(2,1)}) %all-gather.42.cloned.1.call-update) | async-done | bytes 4194320 | tf_op jit(solution)/shard_map/all_gather | solution.py:126
  1350.6 23.2 %convolution_convert_fusion.5 = bf16[2048,1024]{1,0:T(8,128)(2,1)} fusion(bf16[3072,2048]{1,0:T(8,128)(2,1)} %constant_dynamic-update-slice_fusion.6, f32[3072,1024]{1,0:T(8,128)} %fusion.71, f32[1024]{0:T(1024)S(1)} %dynamic_slice.7), kind=kOutput, calls=%fused_computation.51 | convolution fusion | flops 12918456320 | bytes 29364224 | tf_op jit(solution)/shard_map/dot_general | solution.py:45
  1373.9 19.8 %convolution_convert_fusion.6 = bf16[2048,1024]{1,0:T(8,128)(2,1)} fusion(bf16[3072,2048]{1,0:T(8,128)(2,1)} %constant_dynamic-update-slice_fusion.4, bf16[3072,1024]{1,0:T(8,128)(2,1)} %get-tuple-element.46), kind=kOutput, calls=%fused_computation.52 | convolution fusion | flops 12886999040 | bytes 23068672 | tf_op jit(solution)/shard_map/dot_general | solution.py:45
  1466.2 35.1 %reduce-scatter.44.cloned.1.call-done = bf16[512,1024]{1,0:T(8,128)(2,1)} async-done(((bf16[2048,1024]{1,0:T(8,128)(2,1)}), bf16[512,1024]{1,0:T(8,128)(2,1)}) %reduce-scatter.44.cloned.1.call-update) | async-done | bytes 1048592 | tf_op jit(solution)/shard_map/reduce_scatter | solution.py:117
  1504.1 76.7 %reduce-scatter.42.cloned.1.call-done = bf16[512,1024]{1,0:T(8,128)(2,1)} async-done(((bf16[2048,1024]{1,0:T(8,128)(2,1)}), bf16[512,1024]{1,0:T(8,128)(2,1)}) %reduce-scatter.42.cloned.1.call-update) | async-done | bytes 1048592 | tf_op jit(solution)/shard_map/reduce_scatter | solution.py:114
  1584.6 26.2 %reduce-scatter.40.cloned.1.call-done = bf16[512,256]{1,0:T(8,128)(2,1)} async-done(((bf16[2048,256]{1,0:T(8,128)(2,1)}), bf16[512,256]{1,0:T(8,128)(2,1)}) %reduce-scatter.40.cloned.1.call-update) | async-done | bytes 262160 | tf_op jit(solution)/shard_map/reduce_scatter | solution.py:117
  1612.6 26.2 %reduce-scatter.36.cloned.1.call-done = bf16[512,256]{1,0:T(8,128)(2,1)} async-done(((bf16[2048,256]{1,0:T(8,128)(2,1)}), bf16[512,256]{1,0:T(8,128)(2,1)}) %reduce-scatter.36.cloned.1.call-update) | async-done | bytes 262160 | tf_op jit(solution)/shard_map/reduce_scatter | solution.py:114
  1640.6 51.8 %reduce-scatter.30.cloned.1.call-done = bf16[128,2048]{1,0:T(8,128)(2,1)} async-done(((bf16[1024,2048]{1,0:T(8,128)(2,1)}), bf16[128,2048]{1,0:T(8,128)(2,1)}) %reduce-scatter.30.cloned.1.call-update) | async-done | bytes 524304 | tf_op jit(solution)/shard_map/reduce_scatter | solution.py:134
  1692.4 74.7 %reduce-scatter.28.cloned.1.call-done = bf16[256,2048]{1,0:T(8,128)(2,1)} async-done(((bf16[2048,2048]{1,0:T(8,128)(2,1)}), bf16[256,2048]{1,0:T(8,128)(2,1)}) %reduce-scatter.28.cloned.1.call-update) | async-done | bytes 1048592 | tf_op jit(solution)/shard_map/reduce_scatter | solution.py:134
  1772.0 41.4 %all-reduce.19 = (f32[2048]{0:T(1024)S(1)}, f32[2048]{0:T(1024)S(1)}, f32[2048]{0:T(1024)S(1)}, f32[128]{0:T(128)}, f32[2048]{0:T(1024)S(1)}, /*index=5*/f32[204...) all-reduce(f32[2048]{0:T(1024)S(1)} %get-tuple-element.21, ...), channel_id=12, replica_groups=mesh['grp'=4,'tok'=8] {'grp','tok'}, use_global_device_ids=true, to_apply=%region_27.28.clone | all-reduce | flops 22657 | bytes 181256
  1827.5 79.4 %reduce-scatter.38.cloned.1.call-done = f32[64,256]{1,0:T(8,128)} async-done(((f32[2048,256]{1,0:T(8,128)}), f32[64,256]{1,0:T(8,128)}) %reduce-scatter.38.cloned.1.call-update) | async-done | bytes 65552 | tf_op jit(solution)/shard_map/reduce_scatter | solution.py:404
  (419 shorter events, 486.4 us)
Async XLA Ops:
  7.2 60.1 %all-gather.22.cloned.1.call-start = ((), (), s32[]{:S(2)}) async-start(), calls=%async_computation.18 | async-start | bytes 1081344 | tf_op jit(solution)/shard_map/all_gather | solution.py:224
  7.9 85.5 %all-gather.24.cloned.1.call-start = ((), (), s32[]{:S(2)}) async-start(), calls=%async_computation.19 | async-start | bytes 1179648 | tf_op jit(solution)/shard_map/all_gather | solution.py:126
  59.2 1074.6 %copy-start = (bf16[256,2048]{1,0:T(8,128)(2,1)}, bf16[256,2048]{1,0:T(8,128)(2,1)S(1)}, u32[]{:S(2)}) copy-start(bf16[256,2048]{1,0:T(8,128)(2,1)S(1)} %reshape.300) | copy-start | bytes 3145732
  70.5 79.9 %all-gather.16.cloned.1.call-start = ((), (), s32[]{:S(2)}) async-start(), calls=%async_computation.15 | async-start | bytes 9437184 | tf_op jit(solution)/shard_map/all_gather | solution.py:126
  71.6 117.8 %all-gather.18.cloned.1.call-start = ((), (), s32[]{:S(2)}) async-start(), calls=%async_computation.16 | async-start | bytes 4718592 | tf_op jit(solution)/shard_map/all_gather | solution.py:126
  72.5 146.3 %all-gather.20.cloned.1.call-start = ((), (), s32[]{:S(2)}) async-start(), calls=%async_computation.17 | async-start | bytes 1310720 | tf_op jit(solution)/shard_map/all_gather | solution.py:106
  73.1 213.9 %all-gather.26.cloned.1.call-start = ((), (), s32[]{:S(2)}) async-start(), calls=%async_computation.20 | async-start | bytes 1310720 | tf_op jit(solution)/shard_map/all_gather | solution.py:107
  73.7 277.2 %reduce-scatter.18.cloned.1.call-start = ((), (), s32[]{:S(2)}) async-start(), calls=%async_computation.22 | async-start | bytes 4718592 | tf_op jit(solution)/shard_map/reduce_scatter | solution.py:134
  299.9 126.1 %reduce-scatter.16.cloned.1.call-start = ((), (), s32[]{:S(2)}) async-start(), calls=%async_computation.21 | async-start | bytes 9437184 | tf_op jit(solution)/shard_map/reduce_scatter | solution.py:134
  308.6 179.7 %all-gather.28.cloned.1.call-start = ((), (), s32[]{:S(2)}) async-start(), calls=%async_computation.23 | async-start | bytes 9437184 | tf_op jit(solution)/shard_map/all_gather | solution.py:126
  308.6 825.2 %copy-start.42 = (f32[2048]{0:T(1024)}, f32[2048]{0:T(1024)S(1)}, u32[]{:S(2)}) copy-start(f32[2048]{0:T(1024)S(1)} %convert_element_type.195) | copy-start | bytes 24580
  433.6 93.7 %all-gather.30.cloned.1.call-start = ((), (), s32[]{:S(2)}) async-start(), calls=%async_computation.24 | async-start | bytes 4718592 | tf_op jit(solution)/shard_map/all_gather | solution.py:126
  435.6 174.1 %all-gather.32.cloned.1.call-start = ((), (), s32[]{:S(2)}) async-start(), calls=%async_computation.25 | async-start | bytes 5242880 | tf_op jit(solution)/shard_map/all_gather | solution.py:106
  436.3 254.1 %all-gather.34.cloned.1.call-start = ((), (), s32[]{:S(2)}) async-start(), calls=%async_computation.26 | async-start | bytes 5242880 | tf_op jit(solution)/shard_map/all_gather | solution.py:107
  436.9 339.3 %reduce-scatter.22.cloned.1.call-start = ((), (), s32[]{:S(2)}) async-start(), calls=%async_computation.28 | async-start | bytes 4718592 | tf_op jit(solution)/shard_map/reduce_scatter | solution.py:134
  720.4 125.6 %reduce-scatter.20.cloned.1.call-start = ((), (), s32[]{:S(2)}) async-start(), calls=%async_computation.27 | async-start | bytes 9437184 | tf_op jit(solution)/shard_map/reduce_scatter | solution.py:134
  729.6 176.5 %all-gather.36.cloned.1.call-start = ((), (), s32[]{:S(2)}) async-start(), calls=%async_computation.29 | async-start | bytes 9437184 | tf_op jit(solution)/shard_map/all_gather | solution.py:126
  770.0 363.8 %copy-start.45 = (f32[2048]{0:T(1024)}, f32[2048]{0:T(1024)S(1)}, u32[]{:S(2)}) copy-start(f32[2048]{0:T(1024)S(1)} %convert_element_type.201) | copy-start | bytes 24580
  851.5 93.6 %all-gather.38.cloned.1.call-start = ((), (), s32[]{:S(2)}) async-start(), calls=%async_computation.30 | async-start | bytes 4718592 | tf_op jit(solution)/shard_map/all_gather | solution.py:126
  853.4 201.3 %reduce-scatter.26.cloned.1.call-start = ((), (), s32[]{:S(2)}) async-start(), calls=%async_computation.32 | async-start | bytes 4718592 | tf_op jit(solution)/shard_map/reduce_scatter | solution.py:134
  1003.2 126.5 %reduce-scatter.24.cloned.1.call-start = ((), (), s32[]{:S(2)}) async-start(), calls=%async_computation.31 | async-start | bytes 9437184 | tf_op jit(solution)/shard_map/reduce_scatter | solution.py:134
  1011.8 185.4 %all-gather.40.cloned.1.call-start = ((), (), s32[]{:S(2)}) async-start(), calls=%async_computation.33 | async-start | bytes 9437184 | tf_op jit(solution)/shard_map/all_gather | solution.py:126
  1142.7 93.6 %all-gather.42.cloned.1.call-start = ((), (), s32[]{:S(2)}) async-start(), calls=%async_computation.34 | async-start | bytes 4718592 | tf_op jit(solution)/shard_map/all_gather | solution.py:126
  1144.6 304.4 %reduce-scatter.32.cloned.1.call-start = ((), (), s32[]{:S(2)}) async-start(), calls=%async_computation.37 | async-start | bytes 1179648 | tf_op jit(solution)/shard_map/reduce_scatter | solution.py:134
  1348.2 101.8 %reduce-scatter.34.cloned.1.call-start = ((), (), s32[]{:S(2)}) async-start(), calls=%async_computation.38 | async-start | bytes 589824 | tf_op jit(solution)/shard_map/reduce_scatter | solution.py:134
  1350.6 150.7 %reduce-scatter.44.cloned.1.call-start = ((), (), s32[]{:S(2)}) async-start(), calls=%async_computation.43 | async-start | bytes 5242880 | tf_op jit(solution)/shard_map/reduce_scatter | solution.py:117
  1373.9 206.9 %reduce-scatter.42.cloned.1.call-start = ((), (), s32[]{:S(2)}) async-start(), calls=%async_computation.42 | async-start | bytes 5242880 | tf_op jit(solution)/shard_map/reduce_scatter | solution.py:114
  1393.8 217.1 %reduce-scatter.40.cloned.1.call-start = ((), (), s32[]{:S(2)}) async-start(), calls=%async_computation.41 | async-start | bytes 1310720 | tf_op jit(solution)/shard_map/reduce_scatter | solution.py:117
  1409.8 229.0 %reduce-scatter.36.cloned.1.call-start = ((), (), s32[]{:S(2)}) async-start(), calls=%async_computation.39 | async-start | bytes 1310720 | tf_op jit(solution)/shard_map/reduce_scatter | solution.py:114
  1427.9 264.6 %reduce-scatter.30.cloned.1.call-start = ((), (), s32[]{:S(2)}) async-start(), calls=%async_computation.36 | async-start | bytes 4718592 | tf_op jit(solution)/shard_map/reduce_scatter | solution.py:134
  1440.3 326.8 %reduce-scatter.28.cloned.1.call-start = ((), (), s32[]{:S(2)}) async-start(), calls=%async_computation.35 | async-start | bytes 9437184 | tf_op jit(solution)/shard_map/reduce_scatter | solution.py:134
  1448.7 458.2 %reduce-scatter.38.cloned.1.call-start = ((), (), s32[]{:S(2)}) async-start(), calls=%async_computation.40 | async-start | bytes 2162688 | tf_op jit(solution)/shard_map/reduce_scatter | solution.py:404
  (83 other events, 2820.2 us)
Sparse Core Ops, SparseCore 0:
  10.9 56.3 all-gather.21
  70.6 22.8 all-gather.23
  95.9 54.3 all-gather.15
  152.7 36.7 all-gather.17
  190.8 27.9 all-gather.19
  220.2 27.4 all-gather.25
  300.1 50.7 reduce-scatter.17
  354.7 71.2 reduce-scatter.15
  433.8 54.5 all-gather.27
  490.6 36.6 all-gather.29
  528.9 80.7 all-gather.31
  611.1 79.2 all-gather.33
  720.5 50.5 reduce-scatter.21
  774.8 71.1 reduce-scatter.19
  851.6 54.3 all-gather.35
  908.4 36.7 all-gather.37
  1003.3 51.3 reduce-scatter.25
  1058.4 71.2 reduce-scatter.23
  1142.8 54.3 all-gather.39
  1199.5 36.7 all-gather.41
  1348.3 35.9 reduce-scatter.31
  1388.0 34.0 reduce-scatter.33
  1424.5 76.7 reduce-scatter.43
  1503.5 77.2 reduce-scatter.41
  1583.2 27.6 reduce-scatter.39
  1613.0 25.7 reduce-scatter.35
  1642.4 50.0 reduce-scatter.29
  1695.9 71.2 reduce-scatter.27
  1770.1 136.7 reduce-scatter.37
where the time goes:
time: 1920 us
  waiting for transfers between devices  1140 us (59%)
  matrix products  280 us (15%)
  local copies, waits for them, and re-layouts  221 us (12%)
  blocking collectives  173 us (9%)
  other arithmetic  83.5 us (4%)
    reduce_scatter x10, waiting for transfers between devices, rows_sum(): lax.psum_scatter(for_sending(row_parts), 'tok', scatter_dimension=0, tile...  430 us
    all_gather x9, waiting for transfers between devices, rows_gather(): lax.all_gather(for_sending(row_parts), 'tok', axis=0, tiled=True)  290 us
    reduce_scatter x2, waiting for transfers between devices, return_grads(): lax.psum_scatter(grad_pair[0].astype(jnp.bfloat16), 'grp', scatter_dimens...  103 us
    all_gather x2, waiting for transfers between devices, fetch_weights(): lax.all_gather(weight_pair[0], 'grp', axis=0, tiled=True)  102 us
    unnamed x2, blocking collectives  83.9 us
    reduce_scatter x1, waiting for transfers between devices, body(): lax.psum_scatter(grad_keyval_full, ('grp', 'tok'), scatter_dimension=0, t...  79.4 us
    unnamed x200, local copies, waits for them, and re-layouts  68.5 us
    dot_general x5, matrix products, plain_product(): return jnp.dot(left, right, preferred_element_type=jnp.float32)  66.9 us
  transfers between devices with their start and end apart: 29, of which 25 were waited for; matrix products, arithmetic and copies ran while one was open for 17% of the time, Pallas kernels for 0%

commit v1 on v0

v1 whole, which is shorter than its diff:
```python
import functools

import jax
import jax.numpy as jnp
from jax import lax
from jax.experimental import pallas as pl
from jax.experimental.pallas import tpu as pltpu
from jax.sharding import PartitionSpec as P

HEAD_WIDTH = 128
epsilon = 1e-05
masked = -1e30
MESH = pl.DeviceIdType.MESH
VMEM_BYTES = 56 * 1024 * 1024
SMALL_ROWS = 16


def for_sending(value):
    return value.astype(jnp.bfloat16)


def plain_product(left, right):
    return jnp.dot(left, right, preferred_element_type=jnp.float32)


def transposed_product(left, right):
    return lax.dot_general(
        left, right, (((1,), (1,)), ((), ())), preferred_element_type=jnp.float32
    )


def weight_product(left, right):
    return lax.dot_general(
        left, right, (((0,), (0,)), ((), ())), preferred_element_type=jnp.float32
    )


def norm_stats(values):
    center = values - jnp.mean(values, axis=-1, keepdims=True)
    inverse = lax.rsqrt(jnp.mean(center * center, axis=-1, keepdims=True) + epsilon)
    return center * inverse, inverse


def norm_backward(grad_out, gain, scaled, inverse):
    weighted = grad_out * gain
    grad_in = inverse * (
        weighted
        - jnp.mean(weighted, axis=-1, keepdims=True)
        - scaled * jnp.mean(weighted * scaled, axis=-1, keepdims=True)
    )
    return (grad_in, jnp.sum(grad_out * scaled, axis=0), jnp.sum(grad_out, axis=0))


def column_sums(values):
    return jnp.sum(values.astype(jnp.float32), axis=0)


def block_of_eight():
    here = lax.axis_index("tok")
    core, across, along = here % 2, (here // 2) % 2, here // 4
    on_x = here + 2 - 4 * across
    on_y = here + 4 - 8 * along
    on_chip = here + 1 - 2 * core
    corner = on_x + 4 - 8 * along
    return here, on_x, on_y, on_chip, corner


def greet(devices):
    barrier = pltpu.get_barrier_semaphore()
    for device in devices:
        pl.semaphore_signal(barrier, inc=1, device_id={"tok": device}, device_id_type=MESH)
    pl.semaphore_wait(barrier, len(devices))


def gather_kernel(own_ref, out_ref, send_sem, recv_sem, local_sem):
    half = own_ref.shape[0] // 2
    here, on_x, on_y, on_chip, corner = block_of_eight()
    first, second = pl.ds(0, half), pl.ds(half, half)

    def copy(index, source, target, device):
        return pltpu.make_async_remote_copy(
            src_ref=source,
            dst_ref=target,
            send_sem=send_sem.at[index],
            recv_sem=recv_sem.at[index],
            device_id={"tok": device},
            device_id_type=MESH,
        )

    greet((on_x, on_y, on_chip))
    own = pltpu.make_async_copy(own_ref, out_ref.at[here], local_sem)
    copies = [
        copy(0, own_ref, out_ref.at[here], on_x),
        copy(1, own_ref, out_ref.at[here], on_y),
        copy(2, own_ref, out_ref.at[here], on_chip),
        copy(3, out_ref.at[on_x, first], out_ref.at[on_x, first], on_y),
        copy(4, out_ref.at[on_x], out_ref.at[on_x], on_chip),
        copy(5, out_ref.at[on_y, second], out_ref.at[on_y, second], on_x),
        copy(6, out_ref.at[on_y], out_ref.at[on_y], on_chip),
        copy(7, out_ref.at[corner, first], out_ref.at[corner, first], on_chip),
        copy(8, out_ref.at[corner, second], out_ref.at[corner, second], on_chip),
    ]
    for index in range(3):
        copies[index].start()
    own.start()
    copies[0].wait_recv()
    copies[3].start()
    copies[4].start()
    copies[1].wait_recv()
    copies[5].start()
    copies[6].start()
    copies[3].wait_recv()
    copies[7].start()
    copies[5].wait_recv()
    copies[8].start()
    for index in (2, 4, 6, 7, 8):
        copies[index].wait_recv()
    for each in copies:
        each.wait_send()
    own.wait()


def tok_gather(own, call_number, kernels):
    if not kernels:
        return lax.all_gather(own, "tok", axis=0)
    return pl.pallas_call(
        gather_kernel,
        out_shape=jax.ShapeDtypeStruct((8,) + own.shape, own.dtype),
        in_specs=[pl.BlockSpec(memory_space=pl.ANY)],
        out_specs=pl.BlockSpec(memory_space=pl.ANY),
        scratch_shapes=[
            pltpu.SemaphoreType.DMA((9,)),
            pltpu.SemaphoreType.DMA((9,)),
            pltpu.SemaphoreType.DMA,
        ],
        compiler_params=pltpu.CompilerParams(collective_id=call_number, has_side_effects=True),
        cost_estimate=pl.CostEstimate(
            flops=0, bytes_accessed=own.size * 2 * 100, transcendentals=0
        ),
        name="tok_gather",
    )(own)


def reduce_kernel(part_ref, out_ref, mine, theirs, relayed, final, send_sem, recv_sem, load_sem):
    rows = part_ref.shape[1]
    half = rows // 2
    here, on_x, on_y, on_chip, corner = block_of_eight()
    shift = on_chip - here
    first, second = pl.ds(0, half), pl.ds(half, half)

    def copy(index, source, target, device):
        return pltpu.make_async_remote_copy(
            src_ref=source,
            dst_ref=target,
            send_sem=send_sem.at[index],
            recv_sem=recv_sem.at[index],
            device_id={"tok": device},
            device_id_type=MESH,
        )

    places = (corner, on_x, on_y, here)
    greet((on_x, on_y, on_chip))
    to_chip = [
        copy(index, part_ref.at[places[index] + shift], theirs.at[index], on_chip)
        for index in range(4)
    ]
    loads = [
        pltpu.make_async_copy(part_ref.at[places[index]], mine.at[index], load_sem.at[index])
        for index in range(4)
    ]
    for index in range(4):
        to_chip[index].start()
        loads[index].start()

    step = 16

    def add_into(target, other, start, count):
        @pl.loop(0, count // step)
        def _(turn):
            at = pl.ds(pl.multiple_of(start + turn * step, step), step)
            come = pl.ds(pl.multiple_of(turn * step, step), step)
            total = target[at, :].astype(jnp.float32) + other(at, come).astype(jnp.float32)
            target[at, :] = total.astype(target.dtype)

    def join(index):
        to_chip[index].wait_recv()
        loads[index].wait()
        if index < 3:
            add_into(mine.at[index], lambda at, come: theirs[index, at, :], 0, rows)

    join(0)
    corner_x = copy(4, mine.at[0, first], relayed.at[0], on_x)
    corner_y = copy(5, mine.at[0, second], relayed.at[1], on_y)
    corner_x.start()
    corner_y.start()
    join(1)
    x_first = copy(6, mine.at[1, first], final.at[0, first], on_x)
    x_first.start()
    join(2)
    y_second = copy(7, mine.at[2, second], final.at[1, second], on_y)
    y_second.start()
    corner_y.wait_recv()
    add_into(mine.at[1], lambda at, come: relayed[1, come, :], half, half)
    x_second = copy(8, mine.at[1, second], final.at[0, second], on_x)
    x_second.start()
    corner_x.wait_recv()
    add_into(mine.at[2], lambda at, come: relayed[0, come, :], 0, half)
    y_first = copy(9, mine.at[2, first], final.at[1, first], on_y)
    y_first.start()
    join(3)
    for each in (x_first, y_second, x_second, y_first):
        each.wait_recv()

    @pl.loop(0, rows // step)
    def _(turn):
        at = pl.ds(pl.multiple_of(turn * step, step), step)
        total = mine[3, at, :].astype(jnp.float32) + theirs[3, at, :].astype(jnp.float32)
        total = total + final[0, at, :].astype(jnp.float32) + final[1, at, :].astype(jnp.float32)
        out_ref[at, :] = total.astype(out_ref.dtype)

    for each in to_chip + [corner_x, corner_y, x_first, y_second, x_second, y_first]:
        each.wait_send()


def tok_reduce(parts, call_number, kernels, out_type=jnp.float32):
    if not kernels:
        return lax.psum_scatter(parts, "tok", scatter_dimension=0, tiled=False).astype(out_type)
    _, rows, columns = parts.shape
    kind = parts.dtype
    return pl.pallas_call(
        reduce_kernel,
        out_shape=jax.ShapeDtypeStruct((rows, columns), out_type),
        in_specs=[pl.BlockSpec(memory_space=pl.ANY)],
        out_specs=pl.BlockSpec(memory_space=pltpu.VMEM),
        scratch_shapes=[
            pltpu.VMEM((4, rows, columns), kind),
            pltpu.VMEM((4, rows, columns), kind),
            pltpu.VMEM((2, rows // 2, columns), kind),
            pltpu.VMEM((2, rows, columns), kind),
            pltpu.SemaphoreType.DMA((10,)),
            pltpu.SemaphoreType.DMA((10,)),
            pltpu.SemaphoreType.DMA((4,)),
        ],
        compiler_params=pltpu.CompilerParams(
            collective_id=call_number, has_side_effects=True, vmem_limit_bytes=VMEM_BYTES
        ),
        cost_estimate=pl.CostEstimate(
            flops=0, bytes_accessed=rows * columns * 2 * 100, transcendentals=0
        ),
        name="tok_reduce",
    )(parts)


def peers_of(count):
    here = lax.axis_index("tok")
    return here, [(here + step) % count for step in range(1, count)]


def small_gather_kernel(count, own_ref, out_ref, send_sem, recv_sem, local_sem):
    here, peers = peers_of(count)
    rows = own_ref.shape[1]
    place = pl.ds(pl.multiple_of(here * rows, rows), rows)
    greet(peers)
    own = pltpu.make_async_copy(own_ref, out_ref.at[:, place, :], local_sem)
    copies = [
        pltpu.make_async_remote_copy(
            src_ref=own_ref,
            dst_ref=out_ref.at[:, place, :],
            send_sem=send_sem.at[index],
            recv_sem=recv_sem.at[index],
            device_id={"tok": peers[index]},
            device_id_type=MESH,
        )
        for index in range(count - 1)
    ]
    for each in copies:
        each.start()
    own.start()
    for each in copies:
        each.wait_recv()
    for each in copies:
        each.wait_send()
    own.wait()


def tok_gather_small(own, call_number, kernels):
    if not kernels:
        return lax.all_gather(own, "tok", axis=1, tiled=True)
    count = 8
    prompts, rows, columns = own.shape
    return pl.pallas_call(
        functools.partial(small_gather_kernel, count),
        out_shape=jax.ShapeDtypeStruct((prompts, count * rows, columns), own.dtype),
        in_specs=[pl.BlockSpec(memory_space=pl.ANY)],
        out_specs=pl.BlockSpec(memory_space=pl.ANY),
        scratch_shapes=[
            pltpu.SemaphoreType.DMA((count - 1,)),
            pltpu.SemaphoreType.DMA((count - 1,)),
            pltpu.SemaphoreType.DMA,
        ],
        compiler_params=pltpu.CompilerParams(collective_id=call_number, has_side_effects=True),
        name="tok_gather_small",
    )(own)


def small_reduce_kernel(count, part_ref, out_ref, come, send_sem, recv_sem):
    here, peers = peers_of(count)
    rows = come.shape[2]

    def place(device):
        return pl.ds(pl.multiple_of(device * rows, rows), rows)

    greet(peers)
    copies = [
        pltpu.make_async_remote_copy(
            src_ref=part_ref.at[:, place(peers[index]), :],
            dst_ref=come.at[index],
            send_sem=send_sem.at[index],
            recv_sem=recv_sem.at[index],
            device_id={"tok": peers[index]},
            device_id_type=MESH,
        )
        for index in range(count - 1)
    ]
    for each in copies:
        each.start()
    total = part_ref[:, place(here), :].astype(jnp.float32)
    for index in range(count - 1):
        copies[index].wait_recv()
        total = total + come[index].astype(jnp.float32)
    out_ref[...] = total.astype(out_ref.dtype)
    for each in copies:
        each.wait_send()


def tok_reduce_small(parts, call_number, kernels):
    if not kernels:
        return lax.psum_scatter(parts, "tok", scatter_dimension=1, tiled=True).astype(jnp.float32)
    count = 8
    prompts, rows, columns = parts.shape
    rows = rows // count
    return pl.pallas_call(
        functools.partial(small_reduce_kernel, count),
        out_shape=jax.ShapeDtypeStruct((prompts, rows, columns), jnp.float32),
        in_specs=[pl.BlockSpec(memory_space=pltpu.VMEM)],
        out_specs=pl.BlockSpec(memory_space=pltpu.VMEM),
        scratch_shapes=[
            pltpu.VMEM((count - 1, prompts, rows, columns), parts.dtype),
            pltpu.SemaphoreType.DMA((count - 1,)),
            pltpu.SemaphoreType.DMA((count - 1,)),
        ],
        compiler_params=pltpu.CompilerParams(
            collective_id=call_number, has_side_effects=True, vmem_limit_bytes=VMEM_BYTES
        ),
        name="tok_reduce_small",
    )(parts)


def stack_heads(values, heads):
    return jnp.concatenate(
        [values[:, head * HEAD_WIDTH : (head + 1) * HEAD_WIDTH] for head in range(heads)], axis=0
    )


def unstack_heads(values, heads):
    rows = values.shape[0] // heads
    return jnp.concatenate(
        [values[head * rows : (head + 1) * rows, :] for head in range(heads)], axis=1
    )


def part_rows(part, prompts, answers, token_ref, answer_ref):
    answer_rows = answer_ref.shape[0] // answers
    prompt_rows = (token_ref.shape[0] - answer_ref.shape[0]) // prompts
    if part < prompts:
        return slice(part * prompt_rows, (part + 1) * prompt_rows), prompt_rows
    start = prompts * prompt_rows + (part - prompts) * answer_rows
    return slice(start, start + answer_rows), answer_rows


def as_row(column):
    wide = jnp.broadcast_to(column, (column.shape[0], HEAD_WIDTH))
    return jnp.transpose(wide)[0:1, :]


def attention_forward_kernel(
    prompts,
    answers,
    heads,
    scale,
    place_ref,
    owner_ref,
    normed_ref,
    query_ref,
    bias_ref,
    prompt_kv_ref,
    answer_kv_ref,
    output_ref,
    states_ref,
    offset_ref,
    gain_ref,
    shift_ref,
    queries_ref,
    mixture_ref,
    log_ref,
    hidden_ref,
    second_ref,
):
    step = pl.program_id(0)
    width = HEAD_WIDTH
    length = prompt_kv_ref.shape[1]
    query_block = query_ref[0].reshape(-1, query_ref.shape[-1])
    output_block = output_ref[0].reshape(-1, output_ref.shape[-1])
    queries = (plain_product(normed_ref[...], query_block) + bias_ref[0]).astype(jnp.bfloat16)
    queries_ref[...] = queries

    pieces = []
    for part in range(prompts + answers):
        here, rows = part_rows(part, prompts, answers, normed_ref, answer_kv_ref)
        token = lax.broadcasted_iota(jnp.int32, (heads * rows, 1), 0) % rows
        stacked = stack_heads(queries[here, :], heads)
        if part < prompts:
            keys = prompt_kv_ref[part, :, :width]
            values = prompt_kv_ref[part, :, width:]
            scores = transposed_product(stacked, keys)
            place = lax.broadcasted_iota(jnp.int32, (1, length), 1)
            scores = jnp.where(place <= place_ref[0] + token, scores, masked)
            top = jnp.max(scores, axis=-1, keepdims=True)
            exponent = jnp.exp((scores - top) * scale)
            total = jnp.sum(exponent, axis=-1, keepdims=True)
            mixed = plain_product(exponent.astype(jnp.bfloat16), values)
        else:
            answer = part - prompts
            owner = owner_ref[answer]
            own = slice(answer * rows, (answer + 1) * rows)
            keys = prompt_kv_ref[owner, :, :width]
            values = prompt_kv_ref[owner, :, width:]
            scores = transposed_product(stacked, keys)
            own_scores = transposed_product(stacked, answer_kv_ref[own, :width])
            place = lax.broadcasted_iota(jnp.int32, (1, rows), 1)
            own_scores = jnp.where(place <= token, own_scores, masked)
            top = jnp.maximum(
                jnp.max(scores, axis=-1, keepdims=True),
                jnp.max(own_scores, axis=-1, keepdims=True),
            )
            exponent = jnp.exp((scores - top) * scale)
            own_exponent = jnp.exp((own_scores - top) * scale)
            total = jnp.sum(exponent, axis=-1, keepdims=True) + jnp.sum(
                own_exponent, axis=-1, keepdims=True
            )
            mixed = plain_product(exponent.astype(jnp.bfloat16), values) + plain_product(
                own_exponent.astype(jnp.bfloat16), answer_kv_ref[own, width:]
            )
        pieces.append(unstack_heads((mixed / total).astype(jnp.bfloat16), heads))
        log_row = as_row(top * scale + jnp.log(total))
        for head in range(heads):
            log_ref[0, head : head + 1, here] = log_row[:, head * rows : (head + 1) * rows]
    mixture = jnp.concatenate(pieces, axis=0)
    mixture_ref[...] = mixture

    @pl.when(step == 0)
    def _():
        hidden_ref[...] = states_ref[...].astype(jnp.float32) + offset_ref[...]

    hidden_ref[...] += transposed_product(mixture, output_block)

    @pl.when(step == pl.num_programs(0) - 1)
    def _():
        scaled, _ = norm_stats(hidden_ref[...])
        second_ref[...] = (scaled * gain_ref[...] + shift_ref[...]).astype(jnp.bfloat16)


def attention_forward(
    place,
    owning,
    normed,
    packed,
    weight_rows,
    query_offset,
    prompt_kv,
    answer_kv,
    states,
    output_offset,
    gain,
    shift,
    prompts,
    answers,
):
    token_rows, model_width = normed.shape
    steps, groups, _, block = packed.shape
    heads = block // HEAD_WIDTH
    length = prompt_kv.shape[1]
    whole = lambda *shape: pl.BlockSpec(shape, lambda step, *_: (0,) * len(shape))
    scores = heads * token_rows * length
    return pl.pallas_call(
        functools.partial(
            attention_forward_kernel, prompts, answers, heads, HEAD_WIDTH ** (-0.5)
        ),
        out_shape=(
            jax.ShapeDtypeStruct((token_rows, model_width), jnp.bfloat16),
            jax.ShapeDtypeStruct((token_rows, model_width), jnp.bfloat16),
            jax.ShapeDtypeStruct((steps, heads, token_rows), jnp.float32),
            jax.ShapeDtypeStruct((token_rows, model_width), jnp.float32),
            jax.ShapeDtypeStruct((token_rows, model_width), jnp.bfloat16),
        ),
        grid_spec=pltpu.PrefetchScalarGridSpec(
            num_scalar_prefetch=2,
            grid=(steps,),
            in_specs=[
                whole(token_rows, model_width),
                pl.BlockSpec(
                    (1, groups, weight_rows, block), lambda step, *_: (step, 0, 0, 0)
                ),
                pl.BlockSpec((1, 1, block), lambda step, *_: (step, 0, 0)),
                whole(*prompt_kv.shape),
                whole(*answer_kv.shape),
                pl.BlockSpec(
                    (1, groups, weight_rows, block), lambda step, *_: (step, 0, 1, 0)
                ),
                whole(token_rows, model_width),
                whole(1, model_width),
                whole(1, model_width),
                whole(1, model_width),
            ],
            out_specs=(
                pl.BlockSpec((token_rows, block), lambda step, *_: (0, step)),
                pl.BlockSpec((token_rows, block), lambda step, *_: (0, step)),
                pl.BlockSpec((1, heads, token_rows), lambda step, *_: (step, 0, 0)),
                whole(token_rows, model_width),
                whole(token_rows, model_width),
            ),
        ),
        compiler_params=pltpu.CompilerParams(vmem_limit_bytes=VMEM_BYTES),
        cost_estimate=pl.CostEstimate(
            flops=steps * (4 * token_rows * model_width * block + 8 * scores * HEAD_WIDTH),
            bytes_accessed=8 * steps * model_width * block,
            transcendentals=steps * scores,
        ),
        name="attention_forward",
    )(
        place,
        owning,
        normed,
        packed,
        query_offset.reshape(steps, 1, block),
        prompt_kv,
        answer_kv,
        packed,
        states,
        output_offset.reshape(1, -1),
        gain.reshape(1, -1),
        shift.reshape(1, -1),
    )


def attention_backward_kernel(
    prompts,
    answers,
    heads,
    scale,
    place_ref,
    owner_ref,
    normed_ref,
    query_ref,
    prompt_kv_ref,
    answer_kv_ref,
    output_ref,
    branch_ref,
    queries_ref,
    mixture_ref,
    log_ref,
    grad_weights_ref,
    grad_normed_ref,
    grad_prompt_ref,
    grad_answer_ref,
    grad_bias_ref,
    normed_across,
    branch_across,
    key_sums,
    own_sums,
):
    step = pl.program_id(0)
    width = HEAD_WIDTH
    length = prompt_kv_ref.shape[1]
    block = queries_ref.shape[1]

    @pl.when(step == 0)
    def _():
        normed_across[...] = jnp.transpose(normed_ref[...])
        branch_across[...] = jnp.transpose(branch_ref[...])
        key_sums[...] = jnp.zeros_like(key_sums)
        own_sums[...] = jnp.zeros_like(own_sums)
        grad_normed_ref[...] = jnp.zeros_like(grad_normed_ref)

    query_block = query_ref[0].reshape(-1, block)
    output_block = output_ref[0].reshape(-1, block)
    weight_shape = query_ref.shape[1:]
    grad_weights_ref[0, :, 1] = (
        plain_product(branch_across[...], mixture_ref[...])
        .astype(jnp.bfloat16)
        .reshape(weight_shape)
    )
    grad_mixture = plain_product(branch_ref[...], output_block).astype(jnp.bfloat16)
    queries = queries_ref[...]
    mixture = mixture_ref[...]

    def backward(keys, values, stacked, grad_stacked, log_row, inner_row, allowed):
        scores = transposed_product(keys, stacked)
        probs = jnp.exp(scores * scale - log_row)
        if allowed is not None:
            probs = jnp.where(allowed, probs, 0.0)
        grad_values = plain_product(probs.astype(jnp.bfloat16), grad_stacked)
        grad_probs = transposed_product(values, grad_stacked)
        grad_scores = (probs * (grad_probs - inner_row)).astype(jnp.bfloat16)
        grad_keys = plain_product(grad_scores, stacked)
        grad_queries = weight_product(grad_scores, keys)
        return grad_queries, grad_keys, grad_values

    pieces = []
    for part in range(prompts + answers):
        here, rows = part_rows(part, prompts, answers, normed_ref, answer_kv_ref)
        token = lax.broadcasted_iota(jnp.int32, (1, heads * rows), 1) % rows
        stacked = stack_heads(queries[here, :], heads)
        grad_stacked = stack_heads(grad_mixture[here, :], heads)
        mixed = stack_heads(mixture[here, :], heads)
        product = grad_stacked.astype(jnp.float32) * mixed.astype(jnp.float32)
        inner_row = jnp.sum(jnp.transpose(product), axis=0, keepdims=True)
        log_row = jnp.concatenate(
            [log_ref[0, head : head + 1, here] for head in range(heads)], axis=1
        )
        if part < prompts:
            place = lax.broadcasted_iota(jnp.int32, (length, 1), 0)
            grad_queries, grad_keys, grad_values = backward(
                prompt_kv_ref[part, :, :width],
                prompt_kv_ref[part, :, width:],
                stacked,
                grad_stacked,
                log_row,
                inner_row,
                place <= place_ref[0] + token,
            )
            key_sums[part, :, :width] += grad_keys
            key_sums[part, :, width:] += grad_values
        else:
            answer = part - prompts
            owner = owner_ref[answer]
            own = slice(answer * rows, (answer + 1) * rows)
            grad_queries, grad_keys, grad_values = backward(
                prompt_kv_ref[owner, :, :width],
                prompt_kv_ref[owner, :, width:],
                stacked,
                grad_stacked,
                log_row,
                inner_row,
                None,
            )
            key_sums[owner, :, :width] += grad_keys
            key_sums[owner, :, width:] += grad_values
            place = lax.broadcasted_iota(jnp.int32, (rows, 1), 0)
            own_queries, own_keys, own_values = backward(
                answer_kv_ref[own, :width],
                answer_kv_ref[own, width:],
                stacked,
                grad_stacked,
                log_row,
                inner_row,
                place <= token,
            )
            grad_queries = grad_queries + own_queries
            own_sums[own, :width] += own_keys
            own_sums[own, width:] += own_values
        pieces.append(unstack_heads((grad_queries * scale).astype(jnp.bfloat16), heads))
    grad_queries = jnp.concatenate(pieces, axis=0)
    grad_weights_ref[0, :, 0] = (
        plain_product(normed_across[...], grad_queries).astype(jnp.bfloat16).reshape(weight_shape)
    )
    grad_normed_ref[...] += transposed_product(grad_queries, query_block)
    grad_bias_ref[0] = jnp.sum(grad_queries.astype(jnp.float32), axis=0, keepdims=True)

    @pl.when(step == pl.num_programs(0) - 1)
    def _():
        grad_prompt_ref[:, :, :width] = (key_sums[:, :, :width] * scale).astype(jnp.bfloat16)
        grad_prompt_ref[:, :, width:] = key_sums[:, :, width:].astype(jnp.bfloat16)
        grad_answer_ref[:, :width] = own_sums[:, :width] * scale
        grad_answer_ref[:, width:] = own_sums[:, width:]


def attention_backward(
    place,
    owning,
    normed,
    packed,
    weight_rows,
    prompt_kv,
    answer_kv,
    branch,
    queries,
    mixture,
    log_total,
    prompts,
    answers,
):
    token_rows, model_width = normed.shape
    steps, groups, _, block = packed.shape
    heads = block // HEAD_WIDTH
    length = prompt_kv.shape[1]
    whole = lambda *shape: pl.BlockSpec(shape, lambda step, *_: (0,) * len(shape))
    columns = lambda: pl.BlockSpec((token_rows, block), lambda step, *_: (0, step))
    scores = heads * token_rows * length
    return pl.pallas_call(
        functools.partial(
            attention_backward_kernel, prompts, answers, heads, HEAD_WIDTH ** (-0.5)
        ),
        out_shape=(
            jax.ShapeDtypeStruct((steps, groups, 2, weight_rows, block), jnp.bfloat16),
            jax.ShapeDtypeStruct((token_rows, model_width), jnp.float32),
            jax.ShapeDtypeStruct(prompt_kv.shape, jnp.bfloat16),
            jax.ShapeDtypeStruct(answer_kv.shape, jnp.float32),
            jax.ShapeDtypeStruct((steps, 1, block), jnp.float32),
        ),
        grid_spec=pltpu.PrefetchScalarGridSpec(
            num_scalar_prefetch=2,
            grid=(steps,),
            in_specs=[
                whole(token_rows, model_width),
                pl.BlockSpec(
                    (1, groups, weight_rows, block), lambda step, *_: (step, 0, 0, 0)
                ),
                whole(*prompt_kv.shape),
                whole(*answer_kv.shape),
                pl.BlockSpec(
                    (1, groups, weight_rows, block), lambda step, *_: (step, 0, 1, 0)
                ),
                whole(token_rows, model_width),
                columns(),
                columns(),
                pl.BlockSpec((1, heads, token_rows), lambda step, *_: (step, 0, 0)),
            ],
            out_specs=(
                pl.BlockSpec(
                    (1, groups, 2, weight_rows, block), lambda step, *_: (step, 0, 0, 0, 0)
                ),
                whole(token_rows, model_width),
                whole(*prompt_kv.shape),
                whole(*answer_kv.shape),
                pl.BlockSpec((1, 1, block), lambda step, *_: (step, 0, 0)),
            ),
            scratch_shapes=[
                pltpu.VMEM((model_width, token_rows), jnp.bfloat16),
                pltpu.VMEM((model_width, token_rows), jnp.bfloat16),
                pltpu.VMEM(prompt_kv.shape, jnp.float32),
                pltpu.VMEM(answer_kv.shape, jnp.float32),
            ],
        ),
        compiler_params=pltpu.CompilerParams(vmem_limit_bytes=VMEM_BYTES),
        cost_estimate=pl.CostEstimate(
            flops=steps * (8 * token_rows * model_width * block + 20 * scores * HEAD_WIDTH),
            bytes_accessed=16 * steps * model_width * block,
            transcendentals=steps * scores,
        ),
        name="attention_backward",
    )(
        place,
        owning,
        normed,
        packed,
        prompt_kv,
        answer_kv,
        packed,
        branch,
        queries,
        mixture,
        log_total,
    )


def by_group(values):
    return jnp.swapaxes(values, 0, 1).reshape(-1)


def body(
    kernels,
    prompt_states,
    answer_states,
    answer_prompt,
    prompt_teacher,
    answer_teacher,
    prompt_valid,
    answer_valid,
    first_gain,
    first_shift,
    query_weight,
    query_bias,
    keyval_weight,
    value_bias,
    output_weight,
    output_bias,
    second_gain,
    second_shift,
    up_weight,
    up_bias,
    down_weight,
    down_bias,
):
    prompt_count, prompt_rows, model_width = prompt_states.shape
    answer_count, answer_len, _ = answer_states.shape
    groups = lax.axis_size("grp")
    token_devices = lax.axis_size("tok")
    token_index = lax.axis_index("tok")
    group_index = lax.axis_index("grp")
    own_prompt = prompt_rows * prompt_count
    token_rows = own_prompt + answer_count * answer_len
    hidden_units = up_bias.shape[0] * groups * token_devices
    ff_here = hidden_units // token_devices
    ff_start = token_index * ff_here
    share = first_gain.shape[0]
    block = query_weight.shape[1]
    weight_rows = query_weight.shape[0]
    keyval_rows, keyval_width = keyval_weight.shape

    def own_rows(prompt_part, answer_part):
        return jnp.concatenate(
            [prompt_part.reshape(own_prompt, -1), answer_part.reshape(-1, prompt_part.shape[-1])],
            axis=0,
        )

    states = own_rows(prompt_states, answer_states)
    inputs = states.astype(jnp.float32)
    valid_rows = jnp.concatenate([prompt_valid.reshape(-1), answer_valid.reshape(-1)])
    own_count = jnp.sum(valid_rows)
    valid_rows = valid_rows.astype(jnp.float32)

    up_cols = lax.all_gather(up_weight, "grp", axis=0, tiled=True)
    down_cols = lax.all_gather(down_weight, "grp", axis=0, tiled=True)

    count_parts = jnp.stack([own_count // 128, own_count % 128]).astype(jnp.bfloat16)
    smalls = jnp.concatenate(
        [
            first_gain,
            first_shift,
            query_bias,
            output_bias,
            second_gain,
            second_shift,
            down_bias,
            up_bias,
            count_parts,
        ]
    )
    smalls = jnp.pad(smalls, (0, SMALL_ROWS * block - smalls.shape[0])).reshape(SMALL_ROWS, block)
    pack = jnp.concatenate(
        [query_weight, output_weight, keyval_weight.reshape(-1, block), smalls], axis=0
    )
    pack_rows = pack.shape[0]
    packed = lax.all_gather(pack, "grp", axis=0, tiled=True)
    packed = tok_gather(packed, 0, kernels).reshape(token_devices, groups, pack_rows, block)
    keyval_start = 2 * weight_rows
    keyval_end = pack_rows - SMALL_ROWS
    keyval_full = jnp.swapaxes(
        packed[:, :, keyval_start:keyval_end].reshape(
            token_devices, groups, keyval_rows, keyval_width
        ),
        0,
        1,
    ).reshape(model_width, keyval_width)
    small_full = packed[:, :, keyval_end:].reshape(token_devices, groups, SMALL_ROWS * block)
    small_full = jnp.swapaxes(small_full.astype(jnp.float32), 0, 1)

    def vector(start, size):
        return small_full[:, :, start : start + size].reshape(-1)

    gain_one, shift_one, query_offset, output_offset, gain_two, shift_two, down_offset = (
        vector(index * share, share) for index in range(7)
    )
    up_offset = vector(7 * share, up_bias.shape[0])
    count_at = 7 * share + up_bias.shape[0]
    counts = small_full[:, :, count_at : count_at + 2]
    valid_count = jnp.sum(counts[:, :, 0]) * 128.0 + jnp.sum(counts[:, :, 1])
    up_here = lax.dynamic_slice_in_dim(up_offset, ff_start, ff_here)

    scaled_one, inverse_one = norm_stats(inputs)
    normed_one = (scaled_one * gain_one + shift_one).astype(jnp.bfloat16)
    key_offset = jnp.concatenate(
        [jnp.zeros((HEAD_WIDTH,), jnp.float32), value_bias.astype(jnp.float32)]
    )
    key_value_rows = (plain_product(normed_one, keyval_full) + key_offset).astype(jnp.bfloat16)
    prompt_kv = tok_gather_small(
        key_value_rows[:own_prompt].reshape(prompt_count, prompt_rows, -1), 1, kernels
    )
    answer_kv = key_value_rows[own_prompt:]
    owning = answer_prompt - group_index * prompt_count
    owning = lax.dynamic_slice_in_dim(owning, token_index * answer_count, answer_count)
    place = jnp.reshape(token_index * prompt_rows, (1,)).astype(jnp.int32)
    queries, mixture, log_total, hidden, normed_two = attention_forward(
        place,
        owning,
        normed_one,
        packed,
        weight_rows,
        query_offset,
        prompt_kv,
        answer_kv,
        states,
        output_offset,
        gain_two,
        shift_two,
        prompt_count,
        answer_count,
    )

    group_two = tok_gather(normed_two, 2, kernels).reshape(-1, model_width)
    pre_active = plain_product(group_two, up_cols) + up_here
    activated = jax.nn.gelu(pre_active, approximate=True).astype(jnp.bfloat16)
    feed_term = for_sending(transposed_product(activated, down_cols))
    feed_term = tok_reduce(feed_term.reshape(token_devices, token_rows, model_width), 3, kernels)
    result_rows = hidden + feed_term + down_offset

    teacher = own_rows(prompt_teacher, answer_teacher).astype(jnp.float32)
    differ = result_rows - teacher
    own_squares = jnp.sum(valid_rows[:, None] * differ * differ)
    every_token = token_rows * groups * token_devices
    grad_result = every_token / valid_count * valid_rows[:, None] * differ
    grad_branch_two = grad_result.astype(jnp.bfloat16)

    group_grad_two = tok_gather(grad_branch_two, 4, kernels).reshape(-1, model_width)
    grad_activated = plain_product(group_grad_two, down_cols)
    _, gelu_back = jax.vjp(lambda argument: jax.nn.gelu(argument, approximate=True), pre_active)
    grad_pre_active = gelu_back(grad_activated)[0].astype(jnp.bfloat16)
    grad_normed_two = for_sending(transposed_product(grad_pre_active, up_cols))
    grad_normed_two = tok_reduce(
        grad_normed_two.reshape(token_devices, token_rows, model_width), 5, kernels
    )
    grad_down_cols = for_sending(weight_product(group_grad_two, activated))
    grad_down_weight = lax.psum_scatter(grad_down_cols, "grp", scatter_dimension=0, tiled=True)
    grad_up_cols = for_sending(weight_product(group_two, grad_pre_active))
    grad_up_weight = lax.psum_scatter(grad_up_cols, "grp", scatter_dimension=0, tiled=True)
    grad_down_offset = column_sums(grad_branch_two)
    grad_up_offset = column_sums(grad_pre_active)
    scaled_two, inverse_two = norm_stats(hidden)
    grad_norm_two, grad_gain_two, grad_shift_two = norm_backward(
        grad_normed_two, gain_two, scaled_two, inverse_two
    )
    grad_hidden = grad_result + grad_norm_two
    grad_branch_one = grad_hidden.astype(jnp.bfloat16)
    grad_output_offset = column_sums(grad_branch_one)

    grad_weights, grad_normed_one, grad_prompt_kv, grad_answer_kv, grad_query_offset = (
        attention_backward(
            place,
            owning,
            normed_one,
            packed,
            weight_rows,
            prompt_kv,
            answer_kv,
            grad_branch_one,
            queries,
            mixture,
            log_total,
            prompt_count,
            answer_count,
        )
    )
    grad_prompt_kv = tok_reduce_small(grad_prompt_kv, 6, kernels)
    grad_keyvals = jnp.concatenate(
        [grad_prompt_kv.reshape(own_prompt, -1), grad_answer_kv], axis=0
    ).astype(jnp.bfloat16)
    grad_keyval_full = weight_product(normed_one, grad_keyvals)
    grad_value_offset = column_sums(grad_keyvals[:, HEAD_WIDTH:])
    grad_normed_one = grad_normed_one + transposed_product(grad_keyvals, keyval_full)
    grad_norm_one, grad_gain_one, grad_shift_one = norm_backward(
        grad_normed_one, gain_one, scaled_one, inverse_one
    )
    grad_inputs = grad_hidden + grad_norm_one

    grad_weights = grad_weights.reshape(token_devices, -1, block)
    grad_weights = tok_reduce(grad_weights, 7, kernels, jnp.bfloat16)
    grad_weights = lax.psum_scatter(grad_weights, "grp", scatter_dimension=0, tiled=True)
    grad_weights = grad_weights.astype(jnp.float32).reshape(2, weight_rows, block)
    grad_keyval_own = lax.psum_scatter(
        grad_keyval_full, ("grp", "tok"), scatter_dimension=0, tiled=True
    )
    small_grads = jnp.concatenate(
        [
            vector_grad.reshape(groups * token_devices, -1)
            for vector_grad in (
                grad_gain_one,
                grad_shift_one,
                grad_query_offset.reshape(-1),
                grad_output_offset,
                grad_gain_two,
                grad_shift_two,
                grad_down_offset,
                lax.dynamic_update_slice_in_dim(
                    jnp.zeros((hidden_units,), jnp.float32), grad_up_offset, ff_start, 0
                ),
            )
        ],
        axis=1,
    ).reshape(-1)
    small_size = small_grads.shape[0]
    small_grads = lax.psum(
        jnp.concatenate([small_grads, grad_value_offset, own_squares.reshape(1)]), ("grp", "tok")
    )
    value_total = small_grads[small_size : small_size + HEAD_WIDTH]
    squared_sum = small_grads[small_size + HEAD_WIDTH]
    own_small = lax.dynamic_slice_in_dim(
        small_grads[:small_size].reshape(groups * token_devices, -1),
        group_index * token_devices + token_index,
        1,
    ).reshape(-1)
    loss_value = squared_sum / (valid_count * model_width)

    def split_rows(values):
        values = values.astype(jnp.bfloat16)
        return (
            values[:own_prompt].reshape(prompt_states.shape),
            values[own_prompt:].reshape(answer_states.shape),
        )

    prompt_out, answer_out = split_rows(result_rows)
    prompt_grad, answer_grad = split_rows(grad_inputs)
    pieces = [own_small[index * share : (index + 1) * share] for index in range(7)]
    return (
        prompt_out,
        answer_out,
        prompt_grad,
        answer_grad,
        pieces[0],
        pieces[1],
        grad_weights[0],
        pieces[2],
        grad_keyval_own,
        value_total,
        grad_weights[1],
        pieces[3],
        pieces[4],
        pieces[5],
        grad_up_weight.astype(jnp.float32),
        own_small[7 * share :],
        grad_down_weight.astype(jnp.float32),
        pieces[6],
        loss_value,
    )


def solution(mesh):
    rows = P(("grp", "tok"))
    table = P(("grp", "tok"), None)
    matrix = P("grp", "tok")
    prompt_part = P("grp", "tok", None)
    answer_part = P(("grp", "tok"), None, None)
    in_specs = (
        prompt_part,
        answer_part,
        P("grp"),
        prompt_part,
        answer_part,
        P("grp", "tok"),
        table,
        rows,
        rows,
        matrix,
        rows,
        table,
        P(),
        matrix,
        rows,
        rows,
        rows,
        matrix,
        rows,
        matrix,
        rows,
    )
    out_specs = (
        prompt_part,
        answer_part,
        prompt_part,
        answer_part,
        rows,
        rows,
        matrix,
        rows,
        table,
        P(),
        matrix,
        rows,
        rows,
        rows,
        matrix,
        rows,
        matrix,
        rows,
        P(),
    )
    kernels = mesh.shape["tok"] == 8
    return jax.shard_map(
        functools.partial(body, kernels),
        mesh=mesh,
        in_specs=in_specs,
        out_specs=out_specs,
        check_vma=False,
    )
```

time: 1920 us -> 1120 us (0.58)
  waiting for transfers between devices: 1140 us -> 364 us
  Pallas kernels: 0 us -> 516 us
  local copies, waits for them, and re-layouts: 221 us -> 30.3 us
  blocking collectives: 173 us -> 0 us
  matrix products: 280 us -> 143 us
  other arithmetic: 83.5 us -> 36.6 us
    pallas_call x0 -> x10, Pallas kernels: none -> 516 us  [the longest x3 202 us: tok_reduce(): pl.pallas_call(reduce_kernel, out_shape=jax.ShapeDtypeStruct((rows, colum...]
    reduce_scatter x14 -> x3, waiting for transfers between devices: 594 us -> 179 us  [the longest x1 76.8 us: body(): lax.psum_scatter(grad_up_cols, 'grp', scatter_dimension=0, tiled=True)]
    all_gather x14 -> x3, waiting for transfers between devices: 460 us -> 46.8 us  [the longest x1 46.8 us: body(): packed = lax.all_gather(pack, 'grp', axis=0, tiled=True)]
    dot_general x13 -> x0, matrix products: 88.6 us -> none  [the longest x2 18.8 us: attend_backward(): jnp.einsum('ngs,nhs->ngh', mixture_gradient, value_slice, preferred_eleme...]
    unnamed x2 -> x0, blocking collectives: 83.9 us -> none
    slice x27 -> x11, local copies, waits for them, and re-layouts: 76.9 us -> 11.3 us  [the longest x2 3.34 us: split_rows(): values[:own_prompt].reshape(prompt_states.shape)]
    unnamed x200 -> x54, local copies, waits for them, and re-layouts: 68.5 us -> 3.61 us
    reduce_scatter x1, waiting for transfers between devices: 79.4 us -> 137 us  [body(): lax.psum_scatter(grad_keyval_full, ('grp', 'tok'), scatter_dimension=0, t...]
  transfers between devices with their start and end apart: 29 -> 8, of which waited for: 25 -> 5; matrix products, arithmetic and copies ran while one was open for 17% -> 9% of each run, Pallas kernels for 0% -> 25%
where the time goes in v1:
time: 1120 us; the launch traced here: 1110 us
  Pallas kernels  516 us (46%)
  waiting for transfers between devices  364 us (32%)
  matrix products  143 us (13%)
  other arithmetic  36.6 us (3%)
  local copies, waits for them, and re-layouts  30.3 us (3%)
  between operations  19.7 us (2%)
    pallas_call x3, Pallas kernels, tok_reduce(): pl.pallas_call(reduce_kernel, out_shape=jax.ShapeDtypeStruct((rows, colum...  202 us
    pallas_call x3, Pallas kernels, tok_gather(): pl.pallas_call(gather_kernel, out_shape=jax.ShapeDtypeStruct((8,) + own.s...  202 us
    reduce_scatter x1, waiting for transfers between devices, body(): lax.psum_scatter(grad_keyval_full, ('grp', 'tok'), scatter_dimension=0, t...  137 us
    reduce_scatter x1, waiting for transfers between devices, body(): lax.psum_scatter(grad_up_cols, 'grp', scatter_dimension=0, tiled=True)  76.8 us
    reduce_scatter x1, waiting for transfers between devices, body(): lax.psum_scatter(grad_down_cols, 'grp', scatter_dimension=0, tiled=True)  76.3 us
    dot_general x3, matrix products, transposed_product(): lax.dot_general(left, right, (((1,), (1,)), ((), ())), preferred_element_...  50 us
    dot_general x3, matrix products, plain_product(): return jnp.dot(left, right, preferred_element_type=jnp.float32)  48.9 us
    all_gather x1, waiting for transfers between devices, body(): packed = lax.all_gather(pack, 'grp', axis=0, tiled=True)  46.8 us
  transfers between devices with their start and end apart: 8, of which 5 were waited for; matrix products, arithmetic and copies ran while one was open for 9% of the time, Pallas kernels for 25%

profile of v1, /device:TPU:0, one launch (start us, length us, event | category | flops | bytes accessed | tf_op | source)
XLA Modules:
  0.0 1110.9 jit_solution(13211682969430153882)
XLA Ops:
  11.3 5.4 concatenate.43
  23.6 46.8 %all-gather.4.cloned.1.call-done.own_ref = bf16[4416,256]{1,0:T(8,128)(2,1)} async-done(((bf16[1104,256]{1,0:T(8,128)(2,1)}), bf16[4416,256]{1,0:T(8,128)(2,1)}) %all-gather.4.cloned.1.call-update) | async-done | bytes 2261008 | tf_op jit(solution)/shard_map/all_gather | solution.py:855
  70.4 82.4 %tok_gather.3 = bf16[8,4416,256]{2,1,0:T(8,128)(2,1)} custom-call(bf16[4416,256]{1,0:T(8,128)(2,1)} %all-gather.4.cloned.1.call-done.own_ref), custom_call_target="tpu_custom_call" | custom-call | bytes 226099200 | tf_op jit(solution)/shard_map/tok_gather/pallas_call | solution.py:126
  163.8 12.9 %tok_gather_small.1.prompt_kv_ref = bf16[2,1024,256]{2,1,0:T(8,128)(2,1)} custom-call(bf16[2,128,256]{2,1,0:T(8,128)(2,1)} %bitcast.102), custom_call_target="tpu_custom_call" | custom-call | tf_op jit(solution)/shard_map/tok_gather_small/pallas_call | solution.py:291
  176.7 38.0 %attention_forward.1 = (bf16[384,2048]{1,0:T(8,128)(2,1)}, bf16[384,2048]{1,0:T(8,128)(2,1)}, f32[8,2,384]{2,1,0:T(2,128)}, f32[384,2048]{1,0:T(8,128)}, bf16[384,2048]{1,0:T(8,128)(2,1)}) custom-call(s32[1]{0:T(128)} %bitcast.place_ref, s32[1]{0:T(128)} %dynamic_slice.9.owner_ref, bf16[384,2048]{1,0:T(8,128)(2,1)} %copy-done.7, ...), custom_call_target="tpu_custom_call" | custom-call | flops 12884901888 | bytes 33554432 | tf_op jit(solution)/shard_map/attention_forward/pallas_call | solution.py:495
  214.7 61.0 %tok_gather.4 = bf16[8,384,2048]{2,1,0:T(8,128)(2,1)} custom-call(bf16[384,2048]{1,0:T(8,128)(2,1)} %get-tuple-element.30.own_ref), custom_call_target="tpu_custom_call" | custom-call | bytes 157286400 | tf_op jit(solution)/shard_map/tok_gather/pallas_call | solution.py:126
  278.9 18.9 %fusion.31 = f32[3072,1024]{1,0:T(8,128)} fusion(bf16[3072,2048]{1,0:T(8,128)(2,1)} %bitcast.84, bf16[2048,1024]{1,0:T(8,128)(2,1)} %all-gather.6.cloned.1.call-done), kind=kOutput, calls=%fused_computation.87 | convolution fusion | flops 12884901888 | bytes 29360128 | tf_op jit(solution)/shard_map/dot_general | solution.py:23
  297.8 25.4 %convolution_convert_fusion.1 = bf16[3072,2048]{1,0:T(8,128)(2,1)} fusion(bf16[2048,1024]{1,0:T(8,128)(2,1)} %all-gather.8.cloned.1.call-done, f32[3072,1024]{1,0:T(8,128)} %fusion.31, f32[1024]{0:T(1024)S(1)} %dynamic_slice.10), kind=kOutput, calls=%fused_computation.12 | convolution fusion | flops 12922650624 | bytes 29364224 | tf_op jit(solution)/shard_map/dot_general | solution.py:27
  323.2 60.3 %tok_reduce.3 = f32[384,2048]{1,0:T(8,128)} custom-call(bf16[8,384,2048]{2,1,0:T(8,128)(2,1)} %bitcast.89), custom_call_target="tpu_custom_call" | custom-call | bytes 157286400 | tf_op jit(solution)/shard_map/tok_reduce/pallas_call | solution.py:230
  383.6 4.7 convert_reduce_fusion.2
  388.4 58.1 %tok_gather.5 = bf16[8,384,2048]{2,1,0:T(8,128)(2,1)} custom-call(bf16[384,2048]{1,0:T(8,128)(2,1)} %get-tuple-element.52.own_ref), custom_call_target="tpu_custom_call" | custom-call | bytes 157286400 | tf_op jit(solution)/shard_map/tok_gather/pallas_call | solution.py:126
  446.5 29.4 %convert_reduce_fusion = (f32[1024]{0:T(1024)S(1)}, bf16[3072,1024]{1,0:T(8,128)(2,1)}) fusion(f32[3072,1024]{1,0:T(8,128)} %fusion.31, f32[1024]{0:T(1024)S(1)} %dynamic_slice.10, bf16[3072,2048]{1,0:T(8,128)(2,1)} %bitcast.86, bf16[2048,1024]{1,0:T(8,128)(2,1)} %all-gather.8.cloned.1.call-done), kind=kOutput, calls=%fused_computation.9 | convolution fusion | flops 12957252608 | bytes 35659776 | tf_op jit(solution)/shard_map/dot_general | solution.py:23
  476.1 19.6 %convolution_convert_fusion = bf16[3072,2048]{1,0:T(8,128)(2,1)} fusion(bf16[3072,1024]{1,0:T(8,128)(2,1)} %get-tuple-element.50, bf16[2048,1024]{1,0:T(8,128)(2,1)} %all-gather.6.cloned.1.call-done), kind=kOutput, calls=%fused_computation.11 | convolution fusion | flops 12891193344 | bytes 23068672 | tf_op jit(solution)/shard_map/dot_general | solution.py:27
  495.7 60.2 %tok_reduce.4 = f32[384,2048]{1,0:T(8,128)} custom-call(bf16[8,384,2048]{2,1,0:T(8,128)(2,1)} %bitcast.88), custom_call_target="tpu_custom_call" | custom-call | bytes 157286400 | tf_op jit(solution)/shard_map/tok_reduce/pallas_call | solution.py:230
  556.0 3.2 multiply_reduce_fusion
  559.8 4.4 convert_reduce_fusion.3
  564.2 46.8 %attention_backward.1 = (bf16[8,4,2,512,256]{4,3,2,1,0:T(8,128)(2,1)}, f32[384,2048]{1,0:T(8,128)}, bf16[2,1024,256]{2,1,0:T(8,128)(2,1)}, f32[128,256]{1,0:T(8,128)}, f32[8,1,256]{2,1,0:T(1,128)}) custom-call(s32[1]{0:T(128)} %bitcast.place_ref, s32[1]{0:T(128)} %dynamic_slice.9.owner_ref, bf16[384,2048]{1,0:T(8,128)(2,1)} %copy-done.7, ...), custom_call_target="tpu_custom_call" | custom-call | flops 28991029248 | bytes 67108864 | tf_op jit(solution)/shard_map/attention_backward/pallas_call | solution.py:710
  612.9 15.3 %tok_reduce_small.1 = f32[2,128,256]{2,1,0:T(8,128)} custom-call(bf16[2,1024,256]{2,1,0:T(8,128)(2,1)} %get-tuple-element.35.part_ref), custom_call_target="tpu_custom_call" | custom-call | tf_op jit(solution)/shard_map/tok_reduce_small/pallas_call | solution.py:342
  629.3 5.0 fusion.20
  635.9 81.4 %tok_reduce.5 = bf16[4096,256]{1,0:T(8,128)(2,1)} custom-call(bf16[8,4096,256]{2,1,0:T(8,128)(2,1)} %bitcast.77), custom_call_target="tpu_custom_call" | custom-call | bytes 209715200 | tf_op jit(solution)/shard_map/tok_reduce/pallas_call | solution.py:230
  717.4 22.6 %convolution_convert_fusion.2 = bf16[2048,1024]{1,0:T(8,128)(2,1)} fusion(bf16[3072,2048]{1,0:T(8,128)(2,1)} %bitcast.87, f32[3072,1024]{1,0:T(8,128)} %fusion.31, f32[1024]{0:T(1024)S(1)} %dynamic_slice.10), kind=kOutput, calls=%fused_computation.16 | convolution fusion | flops 12918456320 | bytes 29364224 | tf_op jit(solution)/shard_map/dot_general | solution.py:33
  740.1 19.8 %convolution_convert_fusion.3 = bf16[2048,1024]{1,0:T(8,128)(2,1)} fusion(bf16[3072,2048]{1,0:T(8,128)(2,1)} %bitcast.85, bf16[3072,1024]{1,0:T(8,128)(2,1)} %get-tuple-element.50), kind=kOutput, calls=%fused_computation.17 | convolution fusion | flops 12886999040 | bytes 23068672 | tf_op jit(solution)/shard_map/dot_general | solution.py:33
  761.3 2.0 fusion.25
  763.4 2.3 slice.177
  765.7 4.0 fusion.19
  778.8 25.6 %reduce-scatter.5.cloned.1.call-done = bf16[1024,256]{1,0:T(8,128)(2,1)} async-done(((bf16[4096,256]{1,0:T(8,128)(2,1)}), bf16[1024,256]{1,0:T(8,128)(2,1)}) %reduce-scatter.5.cloned.1.call-update) | async-done | bytes 524304 | tf_op jit(solution)/shard_map/reduce_scatter | solution.py:978
  804.4 2.1 fusion.29
  806.5 76.3 %reduce-scatter.11.cloned.1.call-done = bf16[512,1024]{1,0:T(8,128)(2,1)} async-done(((bf16[2048,1024]{1,0:T(8,128)(2,1)}), bf16[512,1024]{1,0:T(8,128)(2,1)}) %reduce-scatter.11.cloned.1.call-update) | async-done | bytes 1048592 | tf_op jit(solution)/shard_map/reduce_scatter | solution.py:934
  882.7 2.8 convert_element_type.104
  885.5 76.8 %reduce-scatter.9.cloned.1.call-done = bf16[512,1024]{1,0:T(8,128)(2,1)} async-done(((bf16[2048,1024]{1,0:T(8,128)(2,1)}), bf16[512,1024]{1,0:T(8,128)(2,1)}) %reduce-scatter.9.cloned.1.call-update) | async-done | bytes 1048592 | tf_op jit(solution)/shard_map/reduce_scatter | solution.py:936
  962.3 2.8 convert_element_type.102
  965.1 137.3 %reduce-scatter.7.cloned.1.call-done = f32[64,256]{1,0:T(8,128)} async-done(((f32[2048,256]{1,0:T(8,128)}), f32[64,256]{1,0:T(8,128)}) %reduce-scatter.7.cloned.1.call-update) | async-done | bytes 65552 | tf_op jit(solution)/shard_map/reduce_scatter | solution.py:980
  (140 shorter events, 37.6 us)
Async XLA Ops:
  7.2 13.0 %copy-start.4 = (bf16[1,128,2048]{2,1,0:T(8,128)(2,1)S(1)}, bf16[1,128,2048]{2,1,0:T(8,128)(2,1)}, u32[]{:S(2)}) copy-start(bf16[1,128,2048]{2,1,0:T(8,128)(2,1)} %param.22) | copy-start | bytes 1572868
  7.2 13.0 %copy-start.2 = (bf16[2,128,2048]{2,1,0:T(8,128)(2,1)S(1)}, bf16[2,128,2048]{2,1,0:T(8,128)(2,1)}, u32[]{:S(2)}) copy-start(bf16[2,128,2048]{2,1,0:T(8,128)(2,1)} %param.21) | copy-start | bytes 3145732
  7.2 63.2 %all-gather.4.cloned.1.call-start = ((), (), s32[]{:S(2)}) async-start(), calls=%async_computation.4 | async-start | bytes 2826240 | tf_op jit(solution)/shard_map/all_gather | solution.py:855
  18.7 260.2 %all-gather.6.cloned.1.call-start = ((), (), s32[]{:S(2)}) async-start(), calls=%async_computation.5 | async-start | bytes 5242880 | tf_op jit(solution)/shard_map/all_gather | solution.py:833
  19.4 2.4 copy-start.24
  19.4 278.4 %all-gather.8.cloned.1.call-start = ((), (), s32[]{:S(2)}) async-start(), calls=%async_computation.6 | async-start | bytes 5242880 | tf_op jit(solution)/shard_map/all_gather | solution.py:834
  20.2 753.3 %all-reduce.4.cloned.1.call-start = ((), (), s32[]{:S(2)}) async-start(), calls=%async_computation.7 | async-start | bytes 188416 | tf_op jit(solution)/shard_map/psum | solution.py:1002
  20.3 2.2 copy-start.25
  20.3 2.8 copy-start.21
  20.3 2.8 copy-start.23
  21.8 136.3 %copy-start.17 = (f32[384]{0:T(512)}, f32[384]{0:T(512)S(1)}, u32[]{:S(2)}) copy-start(f32[384]{0:T(512)S(1)} %broadcast_multiply_fusion.6) | copy-start | bytes 4612
  22.4 135.7 %copy-start.19 = (f32[384]{0:T(512)}, f32[384]{0:T(512)S(1)}, u32[]{:S(2)}) copy-start(f32[384]{0:T(512)S(1)} %add_rsqrt_fusion.1) | copy-start | bytes 4612
  156.7 2.1 copy-start.14
  158.8 17.8 %copy-start.7 = (bf16[384,2048]{1,0:T(8,128)(2,1)}, bf16[384,2048]{1,0:T(8,128)(2,1)S(1)}, u32[]{:S(2)}) copy-start(bf16[384,2048]{1,0:T(8,128)(2,1)S(1)} %fusion.14.normed_ref) | copy-start | bytes 4718596
  214.7 63.9 %copy-start = (f32[384,2048]{1,0:T(8,128)S(1)}, f32[384,2048]{1,0:T(8,128)}, u32[]{:S(2)}) copy-start(f32[384,2048]{1,0:T(8,128)} %get-tuple-element.29) | copy-start | bytes 9437188
  323.2 60.3 %copy-start.9 = (bf16[2,128,2048]{2,1,0:T(8,128)(2,1)S(1)}, bf16[2,128,2048]{2,1,0:T(8,128)(2,1)}, u32[]{:S(2)}) copy-start(bf16[2,128,2048]{2,1,0:T(8,128)(2,1)} %param.24) | copy-start | bytes 3145732
  323.2 60.3 %copy-start.13 = (bf16[1,128,2048]{2,1,0:T(8,128)(2,1)S(1)}, bf16[1,128,2048]{2,1,0:T(8,128)(2,1)}, u32[]{:S(2)}) copy-start(bf16[1,128,2048]{2,1,0:T(8,128)(2,1)} %param.25) | copy-start | bytes 1572868
  495.7 60.3 %copy-start.16 = (f32[2048]{0:T(1024)S(1)}, f32[2048]{0:T(1024)}, u32[]{:S(2)}) copy-start(f32[2048]{0:T(1024)} %mul.214) | copy-start | bytes 24580
  556.0 3.3 copy-start.1
  556.0 3.8 copy-start.6
  556.0 3.8 copy-start.22
  564.1 65.1 %copy-start.3 = (bf16[2,128,2048]{2,1,0:T(8,128)(2,1)S(1)}, bf16[2,128,2048]{2,1,0:T(8,128)(2,1)}, u32[]{:S(2)}) copy-start(bf16[2,128,2048]{2,1,0:T(8,128)(2,1)} %param.21) | copy-start | bytes 3145732
  564.1 65.1 %copy-start.5 = (bf16[1,128,2048]{2,1,0:T(8,128)(2,1)S(1)}, bf16[1,128,2048]{2,1,0:T(8,128)(2,1)}, u32[]{:S(2)}) copy-start(bf16[1,128,2048]{2,1,0:T(8,128)(2,1)} %param.22) | copy-start | bytes 1572868
  564.1 65.1 %copy-start.11 = (bf16[4,8,64,256]{3,2,1,0:T(8,128)(2,1)S(1)}, bf16[4,8,64,256]{3,2,1,0:T(8,128)(2,1)}, u32[]{:S(2)}) copy-start(bf16[4,8,64,256]{3,2,1,0:T(8,128)(2,1)} %copy-done.10) | copy-start | bytes 3145732
  564.1 65.1 %copy-start.15 = (f32[2048]{0:T(1024)S(1)}, f32[2048]{0:T(1024)}, u32[]{:S(2)}) copy-start(f32[2048]{0:T(1024)} %copy-done.14) | copy-start | bytes 24580
  564.1 65.1 %copy-start.18 = (f32[384]{0:T(512)S(1)}, f32[384]{0:T(512)}, u32[]{:S(2)}) copy-start(f32[384]{0:T(512)} %copy-done.17) | copy-start | bytes 4612
  564.2 65.1 %copy-start.20 = (f32[384]{0:T(512)S(1)}, f32[384]{0:T(512)}, u32[]{:S(2)}) copy-start(f32[384]{0:T(512)} %copy-done.19) | copy-start | bytes 4612
  635.9 168.5 %reduce-scatter.5.cloned.1.call-start = ((), (), s32[]{:S(2)}) async-start(), calls=%async_computation.8 | async-start | bytes 2621440 | tf_op jit(solution)/shard_map/reduce_scatter | solution.py:978
  717.4 165.4 %reduce-scatter.11.cloned.1.call-start = ((), (), s32[]{:S(2)}) async-start(), calls=%async_computation.11 | async-start | bytes 5242880 | tf_op jit(solution)/shard_map/reduce_scatter | solution.py:934
  740.0 222.3 %reduce-scatter.9.cloned.1.call-start = ((), (), s32[]{:S(2)}) async-start(), calls=%async_computation.10 | async-start | bytes 5242880 | tf_op jit(solution)/shard_map/reduce_scatter | solution.py:936
  759.9 1.4 copy-start.8
  759.9 342.5 %reduce-scatter.7.cloned.1.call-start = ((), (), s32[]{:S(2)}) async-start(), calls=%async_computation.9 | async-start | bytes 2162688 | tf_op jit(solution)/shard_map/reduce_scatter | solution.py:980
  (2 other events, 2.1 us)
Sparse Core Ops, SparseCore 0:
  18.8 51.5 all-gather.3
  72.0 79.5 all-gather.5
  153.2 79.2 all-gather.7
  636.0 121.4 all-reduce.3
  759.7 44.6 reduce-scatter.4
  806.6 76.0 reduce-scatter.10
  885.0 77.2 reduce-scatter.8
  965.3 137.1 reduce-scatter.6

commit v2 on v1

--- a/solution.py
+++ b/solution.py
@@ -13,6 +13,7 @@
 MESH = pl.DeviceIdType.MESH
 VMEM_BYTES = 56 * 1024 * 1024
 SMALL_ROWS = 16
+SMALL_SUMS = 1024
 
 
 def for_sending(value):
@@ -354,6 +355,277 @@
         ),
         name="tok_reduce_small",
     )(parts)
+
+
+def final_reduce_kernel(
+    groups,
+    part_ref,
+    small_ref,
+    out_ref,
+    small_out_ref,
+    mine,
+    theirs,
+    relayed,
+    final,
+    come,
+    small_come,
+    small_total,
+    small_across,
+    send_sem,
+    recv_sem,
+    load_sem,
+    across_send,
+    across_recv,
+    small_send,
+    small_recv,
+    small_across_send,
+    small_across_recv,
+):
+    rows = part_ref.shape[1] // groups
+    half = rows // 2
+    small_rows = small_ref.shape[1] // groups
+    here, on_x, on_y, on_chip, corner = block_of_eight()
+    group = lax.axis_index("grp")
+    shift = on_chip - here
+    _, peers = peers_of(8)
+    other_groups = [(group + turn) % groups for turn in range(1, groups)]
+    step = 16
+
+    barrier = pltpu.get_barrier_semaphore()
+    for peer in peers:
+        pl.semaphore_signal(barrier, inc=1, device_id={"tok": peer}, device_id_type=MESH)
+    for other in other_groups:
+        pl.semaphore_signal(barrier, inc=1, device_id={"grp": other}, device_id_type=MESH)
+    pl.semaphore_wait(barrier, len(peers) + len(other_groups))
+
+    def copy(chunk, index, source, target, device):
+        return pltpu.make_async_remote_copy(
+            src_ref=source,
+            dst_ref=target,
+            send_sem=send_sem.at[chunk, index],
+            recv_sem=recv_sem.at[chunk, index],
+            device_id={"tok": device},
+            device_id_type=MESH,
+        )
+
+    def add_into(target, other, start, count):
+        @pl.loop(0, count // step)
+        def _(turn):
+            at = pl.ds(pl.multiple_of(start + turn * step, step), step)
+            from_here = pl.ds(pl.multiple_of(turn * step, step), step)
+            total = target[at, :].astype(jnp.float32) + other[from_here, :].astype(jnp.float32)
+            target[at, :] = total.astype(target.dtype)
+
+    places = (corner, on_x, on_y, here)
+    first, second = pl.ds(0, half), pl.ds(half, half)
+    to_chip, loads, others = [], [], []
+    for chunk in range(groups):
+        owner = (group + 1 + chunk) % groups
+        span = pl.ds(pl.multiple_of(owner * rows, rows), rows)
+        to_chip.append(
+            [
+                copy(
+                    chunk,
+                    index,
+                    part_ref.at[places[index] + shift, span],
+                    theirs.at[chunk, index],
+                    on_chip,
+                )
+                for index in range(4)
+            ]
+        )
+        loads.append(
+            [
+                pltpu.make_async_copy(
+                    part_ref.at[places[index], span],
+                    mine.at[chunk, index],
+                    load_sem.at[chunk, index],
+                )
+                for index in range(4)
+            ]
+        )
+        own, two = mine.at[chunk], final.at[chunk]
+        others.append(
+            {
+                "corner_x": copy(chunk, 4, own.at[0, first], relayed.at[chunk, 0], on_x),
+                "corner_y": copy(chunk, 5, own.at[0, second], relayed.at[chunk, 1], on_y),
+                "x_first": copy(chunk, 6, own.at[1, first], two.at[0, first], on_x),
+                "y_second": copy(chunk, 7, own.at[2, second], two.at[1, second], on_y),
+                "x_second": copy(chunk, 8, own.at[1, second], two.at[0, second], on_x),
+                "y_first": copy(chunk, 9, own.at[2, first], two.at[1, first], on_y),
+            }
+        )
+    small_copies = [
+        pltpu.make_async_remote_copy(
+            src_ref=small_ref.at[peers[index]],
+            dst_ref=small_come.at[index],
+            send_sem=small_send.at[index],
+            recv_sem=small_recv.at[index],
+            device_id={"tok": peers[index]},
+            device_id_type=MESH,
+        )
+        for index in range(len(peers))
+    ]
+    across = [
+        pltpu.make_async_remote_copy(
+            src_ref=mine.at[chunk, 3],
+            dst_ref=come.at[chunk],
+            send_sem=across_send.at[chunk],
+            recv_sem=across_recv.at[chunk],
+            device_id={"grp": other_groups[chunk]},
+            device_id_type=MESH,
+        )
+        for chunk in range(groups - 1)
+    ]
+    small_over = [
+        pltpu.make_async_remote_copy(
+            src_ref=small_total.at[other_groups[chunk]],
+            dst_ref=small_across.at[chunk],
+            send_sem=small_across_send.at[chunk],
+            recv_sem=small_across_recv.at[chunk],
+            device_id={"grp": other_groups[chunk]},
+            device_id_type=MESH,
+        )
+        for chunk in range(groups - 1)
+    ]
+
+    for chunk in range(groups):
+        for index in range(4):
+            to_chip[chunk][index].start()
+            loads[chunk][index].start()
+        if chunk == 0:
+            for each in small_copies:
+                each.start()
+
+    def join(chunk, index):
+        to_chip[chunk][index].wait_recv()
+        loads[chunk][index].wait()
+        add_into(mine.at[chunk, index], theirs.at[chunk, index], 0, rows)
+
+    def open_chunk(chunk):
+        join(chunk, 0)
+        others[chunk]["corner_x"].start()
+        others[chunk]["corner_y"].start()
+        join(chunk, 1)
+        others[chunk]["x_first"].start()
+        join(chunk, 2)
+        others[chunk]["y_second"].start()
+
+    def relay_chunk(chunk):
+        others[chunk]["corner_y"].wait_recv()
+        add_into(mine.at[chunk, 1], relayed.at[chunk, 1], half, half)
+        others[chunk]["x_second"].start()
+        others[chunk]["corner_x"].wait_recv()
+        add_into(mine.at[chunk, 2], relayed.at[chunk, 0], 0, half)
+        others[chunk]["y_first"].start()
+
+    def close_chunk(chunk):
+        join(chunk, 3)
+        for name in ("x_first", "y_second", "x_second", "y_first"):
+            others[chunk][name].wait_recv()
+
+        @pl.loop(0, rows // step)
+        def _(turn):
+            at = pl.ds(pl.multiple_of(turn * step, step), step)
+            total = mine[chunk, 3, at, :].astype(jnp.float32)
+            total = total + final[chunk, 0, at, :].astype(jnp.float32)
+            total = total + final[chunk, 1, at, :].astype(jnp.float32)
+            mine[chunk, 3, at, :] = total.astype(mine.dtype)
+
+        if chunk < groups - 1:
+            across[chunk].start()
+
+    open_chunk(0)
+    for chunk in range(1, groups):
+        open_chunk(chunk)
+        relay_chunk(chunk - 1)
+        if chunk == 1:
+            sums = small_ref[here]
+            for index in range(len(peers)):
+                small_copies[index].wait_recv()
+                sums = sums + small_come[index]
+            small_total[...] = sums.reshape(small_total.shape)
+            for each in small_over:
+                each.start()
+        if chunk >= 2:
+            close_chunk(chunk - 2)
+    relay_chunk(groups - 1)
+    close_chunk(groups - 2)
+    close_chunk(groups - 1)
+    for each in across:
+        each.wait_recv()
+
+    @pl.loop(0, rows // step)
+    def _(turn):
+        at = pl.ds(pl.multiple_of(turn * step, step), step)
+        total = mine[groups - 1, 3, at, :].astype(jnp.float32)
+        for chunk in range(groups - 1):
+            total = total + come[chunk, at, :].astype(jnp.float32)
+        out_ref[at, :] = total
+
+    small_sum = small_total[group]
+    for chunk in range(groups - 1):
+        small_over[chunk].wait_recv()
+        small_sum = small_sum + small_across[chunk]
+    small_out_ref[...] = small_sum
+    for chunk in range(groups):
+        for each in to_chip[chunk] + list(others[chunk].values()):
+            each.wait_send()
+    for each in small_copies + across + small_over:
+        each.wait_send()
+
+
+def final_reduce(parts, small_parts, groups, call_number, kernels):
+    if not kernels:
+        sums = lax.psum_scatter(parts, "tok", scatter_dimension=0, tiled=False)
+        sums = lax.psum_scatter(sums, "grp", scatter_dimension=0, tiled=True)
+        small_sums = lax.psum_scatter(small_parts, "tok", scatter_dimension=0, tiled=False)
+        small_sums = lax.psum_scatter(small_sums, "grp", scatter_dimension=0, tiled=True)
+        return sums.astype(jnp.float32), small_sums
+    _, rows, columns = parts.shape
+    rows = rows // groups
+    small_rows, small_columns = small_parts.shape[1] // groups, small_parts.shape[2]
+    kind = parts.dtype
+    dma = pltpu.SemaphoreType.DMA
+    small = (small_rows, small_columns)
+    return pl.pallas_call(
+        functools.partial(final_reduce_kernel, groups),
+        out_shape=(
+            jax.ShapeDtypeStruct((rows, columns), jnp.float32),
+            jax.ShapeDtypeStruct(small, jnp.float32),
+        ),
+        in_specs=[
+            pl.BlockSpec(memory_space=pl.ANY),
+            pl.BlockSpec(memory_space=pltpu.VMEM),
+        ],
+        out_specs=(
+            pl.BlockSpec(memory_space=pltpu.VMEM),
+            pl.BlockSpec(memory_space=pltpu.VMEM),
+        ),
+        scratch_shapes=[
+            pltpu.VMEM((groups, 4, rows, columns), kind),
+            pltpu.VMEM((groups, 4, rows, columns), kind),
+            pltpu.VMEM((groups, 2, rows // 2, columns), kind),
+            pltpu.VMEM((groups, 2, rows, columns), kind),
+            pltpu.VMEM((groups - 1, rows, columns), kind),
+            pltpu.VMEM((7, groups * small_rows, small_columns), jnp.float32),
+            pltpu.VMEM((groups,) + small, jnp.float32),
+            pltpu.VMEM((groups - 1,) + small, jnp.float32),
+            dma((groups, 10)),
+            dma((groups, 10)),
+            dma((groups, 4)),
+            dma((groups - 1,)),
+            dma((groups - 1,)),
+            dma((7,)),
+            dma((7,)),
+            dma((groups - 1,)),
+            dma((groups - 1,)),
+        ],
+        compiler_params=pltpu.CompilerParams(
+            collective_id=call_number, has_side_effects=True, vmem_limit_bytes=VMEM_BYTES
+        ),
+        name="final_reduce",
+    )(parts, small_parts)
 
 
 def stack_heads(values, heads):
@@ -595,7 +867,8 @@
     query_block = query_ref[0].reshape(-1, block)
     output_block = output_ref[0].reshape(-1, block)
     weight_shape = query_ref.shape[1:]
-    grad_weights_ref[0, :, 1] = (
+    weight_rows = weight_shape[1]
+    grad_weights_ref[0, :, weight_rows : 2 * weight_rows] = (
         plain_product(branch_across[...], mixture_ref[...])
         .astype(jnp.bfloat16)
         .reshape(weight_shape)
@@ -671,7 +944,7 @@
             own_sums[own, width:] += own_values
         pieces.append(unstack_heads((grad_queries * scale).astype(jnp.bfloat16), heads))
     grad_queries = jnp.concatenate(pieces, axis=0)
-    grad_weights_ref[0, :, 0] = (
+    grad_weights_ref[0, :, :weight_rows] = (
         plain_product(normed_across[...], grad_queries).astype(jnp.bfloat16).reshape(weight_shape)
     )
     grad_normed_ref[...] += transposed_product(grad_queries, query_block)
@@ -691,6 +964,7 @@
     normed,
     packed,
     weight_rows,
+    grad_rows,
     prompt_kv,
     answer_kv,
     branch,
@@ -712,7 +986,7 @@
             attention_backward_kernel, prompts, answers, heads, HEAD_WIDTH ** (-0.5)
         ),
         out_shape=(
-            jax.ShapeDtypeStruct((steps, groups, 2, weight_rows, block), jnp.bfloat16),
+            jax.ShapeDtypeStruct((steps, groups, grad_rows, block), jnp.bfloat16),
             jax.ShapeDtypeStruct((token_rows, model_width), jnp.float32),
             jax.ShapeDtypeStruct(prompt_kv.shape, jnp.bfloat16),
             jax.ShapeDtypeStruct(answer_kv.shape, jnp.float32),
@@ -738,7 +1012,7 @@
             ],
             out_specs=(
                 pl.BlockSpec(
-                    (1, groups, 2, weight_rows, block), lambda step, *_: (step, 0, 0, 0, 0)
+                    (1, groups, grad_rows, block), lambda step, *_: (step, 0, 0, 0)
                 ),
                 whole(token_rows, model_width),
                 whole(*prompt_kv.shape),
@@ -927,13 +1201,16 @@
     _, gelu_back = jax.vjp(lambda argument: jax.nn.gelu(argument, approximate=True), pre_active)
     grad_pre_active = gelu_back(grad_activated)[0].astype(jnp.bfloat16)
     grad_normed_two = for_sending(transposed_product(grad_pre_active, up_cols))
+    grad_down_cols = for_sending(weight_product(group_grad_two, activated))
+    grad_up_cols = for_sending(weight_product(group_two, grad_pre_active))
+    grad_normed_two, grad_down_cols, grad_up_cols = lax.optimization_barrier(
+        (grad_normed_two, grad_down_cols, grad_up_cols)
+    )
+    grad_down_weight = lax.psum_scatter(grad_down_cols, "grp", scatter_dimension=0, tiled=True)
+    grad_up_weight = lax.psum_scatter(grad_up_cols, "grp", scatter_dimension=0, tiled=True)
     grad_normed_two = tok_reduce(
         grad_normed_two.reshape(token_devices, token_rows, model_width), 5, kernels
     )
-    grad_down_cols = for_sending(weight_product(group_grad_two, activated))
-    grad_down_weight = lax.psum_scatter(grad_down_cols, "grp", scatter_dimension=0, tiled=True)
-    grad_up_cols = for_sending(weight_product(group_two, grad_pre_active))
-    grad_up_weight = lax.psum_scatter(grad_up_cols, "grp", scatter_dimension=0, tiled=True)
     grad_down_offset = column_sums(grad_branch_two)
     grad_up_offset = column_sums(grad_pre_active)
     scaled_two, inverse_two = norm_stats(hidden)
@@ -944,6 +1221,7 @@
     grad_branch_one = grad_hidden.astype(jnp.bfloat16)
     grad_output_offset = column_sums(grad_branch_one)
 
+    grad_rows = keyval_end
     grad_weights, grad_normed_one, grad_prompt_kv, grad_answer_kv, grad_query_offset = (
         attention_backward(
             place,
@@ -951,6 +1229,7 @@
             normed_one,
             packed,
             weight_rows,
+            grad_rows,
             prompt_kv,
             answer_kv,
             grad_branch_one,
@@ -973,42 +1252,40 @@
     )
     grad_inputs = grad_hidden + grad_norm_one
 
-    grad_weights = grad_weights.reshape(token_devices, -1, block)
-    grad_weights = tok_reduce(grad_weights, 7, kernels, jnp.bfloat16)
-    grad_weights = lax.psum_scatter(grad_weights, "grp", scatter_dimension=0, tiled=True)
-    grad_weights = grad_weights.astype(jnp.float32).reshape(2, weight_rows, block)
-    grad_keyval_own = lax.psum_scatter(
-        grad_keyval_full, ("grp", "tok"), scatter_dimension=0, tiled=True
-    )
-    small_grads = jnp.concatenate(
-        [
-            vector_grad.reshape(groups * token_devices, -1)
-            for vector_grad in (
-                grad_gain_one,
-                grad_shift_one,
-                grad_query_offset.reshape(-1),
-                grad_output_offset,
-                grad_gain_two,
-                grad_shift_two,
-                grad_down_offset,
-                lax.dynamic_update_slice_in_dim(
-                    jnp.zeros((hidden_units,), jnp.float32), grad_up_offset, ff_start, 0
-                ),
-            )
-        ],
-        axis=1,
-    ).reshape(-1)
-    small_size = small_grads.shape[0]
-    small_grads = lax.psum(
-        jnp.concatenate([small_grads, grad_value_offset, own_squares.reshape(1)]), ("grp", "tok")
-    )
-    value_total = small_grads[small_size : small_size + HEAD_WIDTH]
-    squared_sum = small_grads[small_size + HEAD_WIDTH]
-    own_small = lax.dynamic_slice_in_dim(
-        small_grads[:small_size].reshape(groups * token_devices, -1),
-        group_index * token_devices + token_index,
-        1,
-    ).reshape(-1)
+    grad_keyval_blocks = jnp.swapaxes(
+        grad_keyval_full.astype(jnp.bfloat16).reshape(groups, token_devices, -1, block), 0, 1
+    )
+    grad_weights = lax.dynamic_update_slice(
+        grad_weights, grad_keyval_blocks, (0, 0, keyval_start, 0)
+    )
+    vectors = (
+        grad_gain_one,
+        grad_shift_one,
+        grad_query_offset.reshape(-1),
+        grad_output_offset,
+        grad_gain_two,
+        grad_shift_two,
+        grad_down_offset,
+        lax.dynamic_update_slice_in_dim(
+            jnp.zeros((hidden_units,), jnp.float32), grad_up_offset, ff_start, 0
+        ),
+    )
+    totals = jnp.concatenate([grad_value_offset, own_squares.reshape(1)])
+    blocks = jnp.concatenate(
+        [each.reshape(groups, token_devices, -1) for each in vectors]
+        + [jnp.broadcast_to(totals, (groups, token_devices, totals.shape[0]))],
+        axis=2,
+    )
+    blocks = jnp.pad(blocks, ((0, 0), (0, 0), (0, SMALL_SUMS - blocks.shape[2])))
+    blocks = jnp.swapaxes(blocks, 0, 1).reshape(token_devices, -1, HEAD_WIDTH)
+    grad_weights, small_sums = final_reduce(
+        grad_weights.reshape(token_devices, -1, block), blocks, groups, 7, kernels
+    )
+    small_sums = small_sums.reshape(-1)
+    up_share = up_bias.shape[0]
+    totals_at = 7 * share + up_share
+    value_total = small_sums[totals_at : totals_at + HEAD_WIDTH]
+    squared_sum = small_sums[totals_at + HEAD_WIDTH]
     loss_value = squared_sum / (valid_count * model_width)
 
     def split_rows(values):
@@ -1020,7 +1297,7 @@
 
     prompt_out, answer_out = split_rows(result_rows)
     prompt_grad, answer_grad = split_rows(grad_inputs)
-    pieces = [own_small[index * share : (index + 1) * share] for index in range(7)]
+    pieces = [small_sums[index * share : (index + 1) * share] for index in range(7)]
     return (
         prompt_out,
         answer_out,
@@ -1028,16 +1305,16 @@
         answer_grad,
         pieces[0],
         pieces[1],
-        grad_weights[0],
+        grad_weights[:weight_rows],
         pieces[2],
-        grad_keyval_own,
+        grad_weights[keyval_start:].reshape(keyval_rows, keyval_width),
         value_total,
-        grad_weights[1],
+        grad_weights[weight_rows:keyval_start],
         pieces[3],
         pieces[4],
         pieces[5],
         grad_up_weight.astype(jnp.float32),
-        own_small[7 * share :],
+        small_sums[7 * share : totals_at],
         grad_down_weight.astype(jnp.float32),
         pieces[6],
         loss_value,

time: 1120 us -> 823 us (0.73)
  waiting for transfers between devices: 364 us -> 49.3 us
  Pallas kernels: 516 us -> 533 us
    reduce_scatter x2 -> x0, waiting for transfers between devices: 163 us -> none  [the longest x1 137 us: body(): lax.psum_scatter(grad_keyval_full, ('grp', 'tok'), scatter_dimension=0, t...]
    pallas_call x0 -> x1, Pallas kernels: none -> 97.3 us  [final_reduce(): pl.pallas_call(functools.partial(final_reduce_kernel, groups), out_shape=...]
    pallas_call x3 -> x2, Pallas kernels: 202 us -> 121 us  [tok_reduce(): pl.pallas_call(reduce_kernel, out_shape=jax.ShapeDtypeStruct((rows, colum...]
    reduce_scatter x1, waiting for transfers between devices: 76.8 us -> 0.01 us  [body(): lax.psum_scatter(grad_up_cols, 'grp', scatter_dimension=0, tiled=True)]
    reduce_scatter x1, waiting for transfers between devices: 76.3 us -> 0.01 us  [body(): lax.psum_scatter(grad_down_cols, 'grp', scatter_dimension=0, tiled=True)]
  transfers between devices with their start and end apart: 8 -> 5, of which waited for: 5 -> 1; matrix products, arithmetic and copies ran while one was open for 9% -> 9% of each run, Pallas kernels for 25% -> 51%
where the time goes in v2:
time: 823 us; the launch traced here: 814 us
  Pallas kernels  533 us (65%)
  matrix products  139 us (17%)
  waiting for transfers between devices  49.3 us (6%)
  local copies, waits for them, and re-layouts  38.1 us (5%)
  other arithmetic  34.8 us (4%)
  between operations  19.1 us (2%)
    pallas_call x3, Pallas kernels, tok_gather(): pl.pallas_call(gather_kernel, out_shape=jax.ShapeDtypeStruct((8,) + own.s...  202 us
    pallas_call x2, Pallas kernels, tok_reduce(): pl.pallas_call(reduce_kernel, out_shape=jax.ShapeDtypeStruct((rows, colum...  121 us
    pallas_call x1, Pallas kernels, final_reduce(): pl.pallas_call(functools.partial(final_reduce_kernel, groups), out_shape=...  97.3 us
    dot_general x3, matrix products, transposed_product(): lax.dot_general(left, right, (((1,), (1,)), ((), ())), preferred_element_...  50.5 us
    all_gather x1, waiting for transfers between devices, body(): packed = lax.all_gather(pack, 'grp', axis=0, tiled=True)  47.4 us
    dot_general x3, matrix products, plain_product(): return jnp.dot(left, right, preferred_element_type=jnp.float32)  47.1 us
    pallas_call x1, Pallas kernels, attention_backward(): pl.pallas_call(functools.partial(attention_backward_kernel, prompts, answ...  46.7 us
    dot_general x3, matrix products, weight_product(): lax.dot_general(left, right, (((0,), (0,)), ((), ())), preferred_element_...  41.9 us
  transfers between devices with their start and end apart: 5, of which 1 were waited for; matrix products, arithmetic and copies ran while one was open for 9% of the time, Pallas kernels for 51%

profile of v2, /device:TPU:0, one launch (start us, length us, event | category | flops | bytes accessed | tf_op | source)
XLA Modules:
  0.0 813.7 jit_solution(1707318812824365517)
XLA Ops:
  11.3 5.4 concatenate.43
  16.8 1.9 pad_maximum_fusion.1
  23.1 47.4 %all-gather.4.cloned.1.call-done.own_ref = bf16[4416,256]{1,0:T(8,128)(2,1)} async-done(((bf16[1104,256]{1,0:T(8,128)(2,1)}), bf16[4416,256]{1,0:T(8,128)(2,1)}) %all-gather.4.cloned.1.call-update) | async-done | bytes 2261008 | tf_op jit(solution)/shard_map/all_gather | solution.py:1129
  70.4 82.4 %tok_gather.3 = bf16[8,4416,256]{2,1,0:T(8,128)(2,1)} custom-call(bf16[4416,256]{1,0:T(8,128)(2,1)} %all-gather.4.cloned.1.call-done.own_ref), custom_call_target="tpu_custom_call" | custom-call | bytes 226099200 | tf_op jit(solution)/shard_map/tok_gather/pallas_call | solution.py:127
  159.4 12.9 %tok_gather_small.1.prompt_kv_ref = bf16[2,1024,256]{2,1,0:T(8,128)(2,1)} custom-call(bf16[2,128,256]{2,1,0:T(8,128)(2,1)} %bitcast.94), custom_call_target="tpu_custom_call" | custom-call | tf_op jit(solution)/shard_map/tok_gather_small/pallas_call | solution.py:292
  175.0 38.0 %attention_forward.1 = (bf16[384,2048]{1,0:T(8,128)(2,1)}, bf16[384,2048]{1,0:T(8,128)(2,1)}, f32[8,2,384]{2,1,0:T(2,128)}, f32[384,2048]{1,0:T(8,128)}, bf16[384,2048]{1,0:T(8,128)(2,1)}) custom-call(s32[1]{0:T(128)} %bitcast.place_ref, s32[1]{0:T(128)} %dynamic_slice.6.owner_ref, bf16[384,2048]{1,0:T(8,128)(2,1)} %copy-done.10, ...), custom_call_target="tpu_custom_call" | custom-call | flops 12884901888 | bytes 33554432 | tf_op jit(solution)/shard_map/attention_forward/pallas_call | solution.py:767
  213.0 61.0 %tok_gather.4 = bf16[8,384,2048]{2,1,0:T(8,128)(2,1)} custom-call(bf16[384,2048]{1,0:T(8,128)(2,1)} %get-tuple-element.35.own_ref), custom_call_target="tpu_custom_call" | custom-call | bytes 157286400 | tf_op jit(solution)/shard_map/tok_gather/pallas_call | solution.py:127
  275.3 1.5 slice_reduce_fusion
  278.2 18.9 %fusion.31 = f32[3072,1024]{1,0:T(8,128)} fusion(bf16[3072,2048]{1,0:T(8,128)(2,1)} %bitcast.75, bf16[2048,1024]{1,0:T(8,128)(2,1)} %all-gather.6.cloned.1.call-done), kind=kOutput, calls=%fused_computation.83 | convolution fusion | flops 12884901888 | bytes 29360128 | tf_op jit(solution)/shard_map/dot_general | solution.py:24
  297.1 25.5 %convolution_convert_fusion.1 = bf16[3072,2048]{1,0:T(8,128)(2,1)} fusion(bf16[2048,1024]{1,0:T(8,128)(2,1)} %all-gather.8.cloned.1.call-done, f32[3072,1024]{1,0:T(8,128)} %fusion.31, f32[1024]{0:T(1024)S(1)} %dynamic_slice.7), kind=kOutput, calls=%fused_computation.12 | convolution fusion | flops 12922650624 | bytes 29364224 | tf_op jit(solution)/shard_map/dot_general | solution.py:28
  322.6 60.3 %tok_reduce.2 = f32[384,2048]{1,0:T(8,128)} custom-call(bf16[8,384,2048]{2,1,0:T(8,128)(2,1)} %bitcast.80), custom_call_target="tpu_custom_call" | custom-call | bytes 157286400 | tf_op jit(solution)/shard_map/tok_reduce/pallas_call | solution.py:231
  382.9 5.0 fusion.22
  387.9 1.7 copy-done.1
  389.6 2.1 convert_reduce_fusion.2
  391.7 58.1 %tok_gather.5 = bf16[8,384,2048]{2,1,0:T(8,128)(2,1)} custom-call(bf16[384,2048]{1,0:T(8,128)(2,1)} %get-tuple-element.64.own_ref), custom_call_target="tpu_custom_call" | custom-call | bytes 157286400 | tf_op jit(solution)/shard_map/tok_gather/pallas_call | solution.py:127
  449.8 22.9 %convolution_convert_fusion.3 = bf16[2048,1024]{1,0:T(8,128)(2,1)} fusion(bf16[3072,2048]{1,0:T(8,128)(2,1)} %bitcast.77, f32[3072,1024]{1,0:T(8,128)} %fusion.31, f32[1024]{0:T(1024)S(1)} %dynamic_slice.7), kind=kOutput, calls=%fused_computation.17 | convolution fusion | flops 12918456320 | bytes 29364224 | tf_op jit(solution)/shard_map/dot_general | solution.py:34
  472.7 27.5 %convert_reduce_fusion = (f32[1024]{0:T(1024)S(1)}, bf16[3072,1024]{1,0:T(8,128)(2,1)S(1)}) fusion(f32[3072,1024]{1,0:T(8,128)} %fusion.31, f32[1024]{0:T(1024)S(1)} %dynamic_slice.7, bf16[3072,2048]{1,0:T(8,128)(2,1)} %bitcast.78, bf16[2048,1024]{1,0:T(8,128)(2,1)} %all-gather.8.cloned.1.call-done), kind=kOutput, calls=%fused_computation.9 | convolution fusion | flops 12957252608 | bytes 35659776 | tf_op jit(solution)/shard_map/dot_general | solution.py:24
  500.2 2.6 copy-done.35
  502.8 18.2 %convolution_convert_fusion.2 = bf16[2048,1024]{1,0:T(8,128)(2,1)} fusion(bf16[3072,2048]{1,0:T(8,128)(2,1)} %bitcast.76, bf16[3072,1024]{1,0:T(8,128)(2,1)S(1)} %get-tuple-element.62), kind=kOutput, calls=%fused_computation.16 | convolution fusion | flops 12886999040 | bytes 23068672 | tf_op jit(solution)/shard_map/dot_general | solution.py:34
  521.1 19.4 %convolution_convert_fusion = bf16[3072,2048]{1,0:T(8,128)(2,1)} fusion(bf16[3072,1024]{1,0:T(8,128)(2,1)} %copy-done.35, bf16[2048,1024]{1,0:T(8,128)(2,1)} %all-gather.6.cloned.1.call-done), kind=kOutput, calls=%fused_computation.11 | convolution fusion | flops 12891193344 | bytes 23068672 | tf_op jit(solution)/shard_map/dot_general | solution.py:28
  541.3 60.6 %tok_reduce.3 = f32[384,2048]{1,0:T(8,128)} custom-call(bf16[8,384,2048]{2,1,0:T(8,128)(2,1)} %bitcast.79), custom_call_target="tpu_custom_call" | custom-call | bytes 157286400 | tf_op jit(solution)/shard_map/tok_reduce/pallas_call | solution.py:231
  602.0 3.2 multiply_reduce_fusion
  605.8 3.0 convert_reduce_fusion.3
  608.8 46.7 %attention_backward.1 = (bf16[8,4,1088,256]{3,2,1,0:T(8,128)(2,1)}, f32[384,2048]{1,0:T(8,128)}, bf16[2,1024,256]{2,1,0:T(8,128)(2,1)}, f32[128,256]{1,0:T(8,128)}, f32[8,1,256]{2,1,0:T(1,128)}) custom-call(s32[1]{0:T(128)} %bitcast.place_ref, s32[1]{0:T(128)} %dynamic_slice.6.owner_ref, bf16[384,2048]{1,0:T(8,128)(2,1)} %copy-done.10, ...), custom_call_target="tpu_custom_call" | custom-call | flops 28991029248 | bytes 67108864 | tf_op jit(solution)/shard_map/attention_backward/pallas_call | solution.py:984
  655.6 15.3 %tok_reduce_small.1 = f32[2,128,256]{2,1,0:T(8,128)} custom-call(bf16[2,1024,256]{2,1,0:T(8,128)(2,1)} %get-tuple-element.41.part_ref), custom_call_target="tpu_custom_call" | custom-call | tf_op jit(solution)/shard_map/tok_reduce_small/pallas_call | solution.py:343
  672.8 5.6 fusion.20
  687.2 97.3 %final_reduce.1 = (f32[1088,256]{1,0:T(8,128)}, f32[8,128]{1,0:T(8,128)}) custom-call(bf16[8,4352,256]{2,1,0:T(8,128)(2,1)} %bitcast.68, f32[8,32,128]{2,1,0:T(8,128)} %reshape.243.small_ref), custom_call_target="tpu_custom_call" | custom-call | tf_op jit(solution)/shard_map/final_reduce/pallas_call | solution.py:591
  788.3 1.5 slice.122
  789.8 3.2 fusion.19
  798.4 1.9 slice_bitcast_fusion.2
  800.2 2.8 convert_element_type.105
  803.0 2.8 convert_element_type.106
  (155 shorter events, 38.0 us)
Async XLA Ops:
  7.2 13.0 %copy-start.4 = (bf16[2,128,2048]{2,1,0:T(8,128)(2,1)S(1)}, bf16[2,128,2048]{2,1,0:T(8,128)(2,1)}, u32[]{:S(2)}) copy-start(bf16[2,128,2048]{2,1,0:T(8,128)(2,1)} %param.21) | copy-start | bytes 3145732
  7.2 13.0 %copy-start.6 = (bf16[1,128,2048]{2,1,0:T(8,128)(2,1)S(1)}, bf16[1,128,2048]{2,1,0:T(8,128)(2,1)}, u32[]{:S(2)}) copy-start(bf16[1,128,2048]{2,1,0:T(8,128)(2,1)} %param.22) | copy-start | bytes 1572868
  7.2 63.2 %all-gather.4.cloned.1.call-start = ((), (), s32[]{:S(2)}) async-start(), calls=%async_computation.2 | async-start | bytes 2826240 | tf_op jit(solution)/shard_map/all_gather | solution.py:1129
  18.7 259.5 %all-gather.6.cloned.1.call-start = ((), (), s32[]{:S(2)}) async-start(), calls=%async_computation.3 | async-start | bytes 5242880 | tf_op jit(solution)/shard_map/all_gather | solution.py:1107
  19.4 277.7 %all-gather.8.cloned.1.call-start = ((), (), s32[]{:S(2)}) async-start(), calls=%async_computation.4 | async-start | bytes 5242880 | tf_op jit(solution)/shard_map/all_gather | solution.py:1108
  20.2 780.1 %reduce-scatter.3.cloned.1.call-start = ((), (), s32[]{:S(2)}) async-start(), calls=%async_computation.5 | async-start | bytes 5242880 | tf_op jit(solution)/shard_map/reduce_scatter | solution.py:1210
  20.3 2.8 copy-start.27
  21.8 135.0 %copy-start.22 = (f32[384]{0:T(512)}, f32[384]{0:T(512)S(1)}, u32[]{:S(2)}) copy-start(f32[384]{0:T(512)S(1)} %broadcast_multiply_fusion.6) | copy-start | bytes 4612
  22.4 134.4 %copy-start.25 = (f32[384]{0:T(512)}, f32[384]{0:T(512)S(1)}, u32[]{:S(2)}) copy-start(f32[384]{0:T(512)S(1)} %add_rsqrt_fusion.1) | copy-start | bytes 4612
  155.3 17.0 %copy-start.18 = (f32[4,8,64]{2,1,0:T(8,128)}, f32[4,8,64]{2,1,0:T(8,128)S(1)}, u32[]{:S(2)}) copy-start(f32[4,8,64]{2,1,0:T(8,128)S(1)} %get-tuple-element.74) | copy-start | bytes 24580
  157.5 17.5 %copy-start.10 = (bf16[384,2048]{1,0:T(8,128)(2,1)}, bf16[384,2048]{1,0:T(8,128)(2,1)S(1)}, u32[]{:S(2)}) copy-start(bf16[384,2048]{1,0:T(8,128)(2,1)S(1)} %fusion.14.normed_ref) | copy-start | bytes 4718596
  213.0 62.0 %copy-start = (f32[384,2048]{1,0:T(8,128)S(1)}, f32[384,2048]{1,0:T(8,128)}, u32[]{:S(2)}) copy-start(f32[384,2048]{1,0:T(8,128)} %get-tuple-element.34) | copy-start | bytes 9437188
  322.6 60.3 %copy-start.13 = (bf16[2,128,2048]{2,1,0:T(8,128)(2,1)S(1)}, bf16[2,128,2048]{2,1,0:T(8,128)(2,1)}, u32[]{:S(2)}) copy-start(bf16[2,128,2048]{2,1,0:T(8,128)(2,1)} %param.24) | copy-start | bytes 3145732
  322.6 60.3 %copy-start.17 = (bf16[1,128,2048]{2,1,0:T(8,128)(2,1)S(1)}, bf16[1,128,2048]{2,1,0:T(8,128)(2,1)}, u32[]{:S(2)}) copy-start(bf16[1,128,2048]{2,1,0:T(8,128)(2,1)} %param.25) | copy-start | bytes 1572868
  540.5 262.5 %reduce-scatter.5.cloned.1.call-start = ((), (), s32[]{:S(2)}) async-start(), calls=%async_computation.6 | async-start | bytes 5242880 | tf_op jit(solution)/shard_map/reduce_scatter | solution.py:1209
  601.9 3.3 copy-start.2
  602.0 3.9 copy-start.3
  608.8 63.9 %copy-start.5 = (bf16[2,128,2048]{2,1,0:T(8,128)(2,1)S(1)}, bf16[2,128,2048]{2,1,0:T(8,128)(2,1)}, u32[]{:S(2)}) copy-start(bf16[2,128,2048]{2,1,0:T(8,128)(2,1)} %param.21) | copy-start | bytes 3145732
  608.8 63.9 %copy-start.7 = (bf16[1,128,2048]{2,1,0:T(8,128)(2,1)S(1)}, bf16[1,128,2048]{2,1,0:T(8,128)(2,1)}, u32[]{:S(2)}) copy-start(bf16[1,128,2048]{2,1,0:T(8,128)(2,1)} %param.22) | copy-start | bytes 1572868
  608.8 63.9 %copy-start.15 = (bf16[4,8,64,256]{3,2,1,0:T(8,128)(2,1)S(1)}, bf16[4,8,64,256]{3,2,1,0:T(8,128)(2,1)}, u32[]{:S(2)}) copy-start(bf16[4,8,64,256]{3,2,1,0:T(8,128)(2,1)} %copy-done.14) | copy-start | bytes 3145732
  608.8 63.9 %copy-start.21 = (f32[2048]{0:T(1024)S(1)}, f32[2048]{0:T(1024)}, u32[]{:S(2)}) copy-start(f32[2048]{0:T(1024)} %copy-done.20) | copy-start | bytes 24580
  608.8 63.9 %copy-start.23 = (f32[384]{0:T(512)S(1)}, f32[384]{0:T(512)}, u32[]{:S(2)}) copy-start(f32[384]{0:T(512)} %copy-done.22) | copy-start | bytes 4612
  608.8 63.9 %copy-start.26 = (f32[384]{0:T(512)S(1)}, f32[384]{0:T(512)}, u32[]{:S(2)}) copy-start(f32[384]{0:T(512)} %copy-done.25) | copy-start | bytes 4612
  672.8 6.4 copy-start.28
  672.8 9.5 %copy-start.24 = (f32[2048]{0:T(1024)S(1)}, f32[2048]{0:T(1024)}, u32[]{:S(2)}) copy-start(f32[2048]{0:T(1024)} %get-tuple-element.63) | copy-start | bytes 24580
  672.8 12.6 %copy-start.11 = (bf16[384,2048]{1,0:T(8,128)(2,1)S(1)}, bf16[384,2048]{1,0:T(8,128)(2,1)}, u32[]{:S(2)}) copy-start(bf16[384,2048]{1,0:T(8,128)(2,1)} %copy-done.10) | copy-start | bytes 4718596
  687.2 102.6 %copy-start.31 = (f32[384]{0:T(512)S(1)}, f32[384]{0:T(512)}, u32[]{:S(2)}) copy-start(f32[384]{0:T(512)} %get-tuple-element.52) | copy-start | bytes 4612
  687.2 102.6 %copy-start.30 = (f32[384]{0:T(512)S(1)}, f32[384]{0:T(512)}, u32[]{:S(2)}) copy-start(f32[384]{0:T(512)} %get-tuple-element.53) | copy-start | bytes 4612
  687.2 102.6 %copy-start.8 = (f32[384,2048]{1,0:T(8,128)S(1)}, f32[384,2048]{1,0:T(8,128)}, u32[]{:S(2)}) copy-start(f32[384,2048]{1,0:T(8,128)} %get-tuple-element.67) | copy-start | bytes 9437188
  789.8 4.3 copy-start.9
  793.1 2.8 copy-start.29
  793.1 3.4 copy-start.12
  (9 other events, 16.3 us)
Sparse Core Ops, SparseCore 0:
  18.8 51.5 all-gather.3
  72.0 79.5 all-gather.5
  153.2 79.2 all-gather.7
  540.6 75.2 reduce-scatter.2
  618.2 77.2 reduce-scatter.4

commit v3 on v2

--- a/solution.py
+++ b/solution.py
@@ -142,37 +142,353 @@
     )(own)
 
 
-def reduce_kernel(part_ref, out_ref, mine, theirs, relayed, final, send_sem, recv_sem, load_sem):
-    rows = part_ref.shape[1]
+def remote(index, source, target, device, send_sem, recv_sem):
+    return pltpu.make_async_remote_copy(
+        src_ref=source,
+        dst_ref=target,
+        send_sem=send_sem.at[index],
+        recv_sem=recv_sem.at[index],
+        device_id={"tok": device},
+        device_id_type=MESH,
+    )
+
+
+def chunk_of(index, size):
+    return pl.ds(pl.multiple_of(index * size, size), size)
+
+
+CHUNK = 256
+LINEAR = 0.7978845608
+CUBIC = 0.044715
+
+
+def gather_beside(own_ref, out_ref, send_sem, recv_sem, local_sem, use):
+    half = own_ref.shape[0] // 2
+    here, on_x, on_y, on_chip, corner = block_of_eight()
+    shift = on_chip - here
+    first, second = pl.ds(0, half), pl.ds(half, half)
+
+    def copy(index, source, target, device):
+        return remote(index, source, target, device, send_sem, recv_sem)
+
+    greet((on_x, on_y, on_chip))
+    own = pltpu.make_async_copy(own_ref, out_ref.at[here], local_sem)
+    copies = [
+        copy(0, own_ref, out_ref.at[here], on_x),
+        copy(1, own_ref, out_ref.at[here], on_y),
+        copy(2, own_ref, out_ref.at[here], on_chip),
+        copy(3, out_ref.at[on_x, first], out_ref.at[on_x, first], on_y),
+        copy(4, out_ref.at[on_x], out_ref.at[on_x], on_chip),
+        copy(5, out_ref.at[on_y, second], out_ref.at[on_y, second], on_x),
+        copy(6, out_ref.at[on_y], out_ref.at[on_y], on_chip),
+        copy(7, out_ref.at[corner, first], out_ref.at[corner, first], on_chip),
+        copy(8, out_ref.at[corner, second], out_ref.at[corner, second], on_chip),
+    ]
+    for index in range(3):
+        copies[index].start()
+    own.start()
+    use(0, here)
+    copies[2].wait_recv()
+    use(1, on_chip)
+    copies[0].wait_recv()
+    copies[3].start()
+    copies[4].start()
+    copies[1].wait_recv()
+    copies[5].start()
+    copies[6].start()
+    use(2, on_x)
+    use(3, on_y)
+    copies[4].wait_recv()
+    use(4, on_x + shift)
+    copies[6].wait_recv()
+    use(5, on_y + shift)
+    copies[3].wait_recv()
+    copies[7].start()
+    copies[5].wait_recv()
+    copies[8].start()
+    use(6, corner)
+    copies[7].wait_recv()
+    copies[8].wait_recv()
+    use(7, corner + shift)
+    own.wait()
+    for each in copies:
+        each.wait_send()
+
+
+def up_kernel(
+    own_ref,
+    up_hbm,
+    bias_ref,
+    rows_ref,
+    active_ref,
+    slope_ref,
+    up,
+    rows,
+    active,
+    slope,
+    send_sem,
+    recv_sem,
+    local_sem,
+    weight_sem,
+    row_sem,
+    store_sem,
+):
+    weights = pltpu.make_async_copy(up_hbm, up, weight_sem)
+    weights.start()
+    stores = {}
+
+    def use(place, block):
+        slot = place % 2
+        load = pltpu.make_async_copy(
+            rows_ref.at[block] if place else own_ref, rows, row_sem
+        )
+        load.start()
+        if place == 0:
+            weights.wait()
+        for each in stores.pop(slot, ()):
+            each.wait()
+        load.wait()
+
+        @pl.loop(0, up.shape[1] // CHUNK)
+        def _(turn):
+            at = chunk_of(turn, CHUNK)
+            value = plain_product(rows[...], up[:, at]) + bias_ref[:, at]
+            square = value * value
+            bent = jnp.tanh(value * (LINEAR + (LINEAR * CUBIC) * square))
+            level = 0.5 + 0.5 * bent
+            active[slot, :, at] = (value * level).astype(jnp.bfloat16)
+            slope[slot, :, at] = (
+                level
+                + (0.5 * value)
+                * (1.0 - bent * bent)
+                * (LINEAR + (3.0 * LINEAR * CUBIC) * square)
+            ).astype(jnp.bfloat16)
+
+        stores[slot] = (
+            pltpu.make_async_copy(active.at[slot], active_ref.at[block], store_sem.at[slot, 0]),
+            pltpu.make_async_copy(slope.at[slot], slope_ref.at[block], store_sem.at[slot, 1]),
+        )
+        for each in stores[slot]:
+            each.start()
+
+    gather_beside(own_ref, rows_ref, send_sem, recv_sem, local_sem, use)
+    for slot in (0, 1):
+        for each in stores[slot]:
+            each.wait()
+
+
+def gather_and_up(own, up_cols, bias, call_number):
+    token_rows, model_width = own.shape
+    width = up_cols.shape[1]
+    hidden = jax.ShapeDtypeStruct((8, token_rows, width), jnp.bfloat16)
+    anywhere = pl.BlockSpec(memory_space=pl.ANY)
+    dma = pltpu.SemaphoreType.DMA
+    return pl.pallas_call(
+        up_kernel,
+        out_shape=(
+            jax.ShapeDtypeStruct((8, token_rows, model_width), jnp.bfloat16),
+            hidden,
+            hidden,
+        ),
+        in_specs=[anywhere, anywhere, pl.BlockSpec(memory_space=pltpu.VMEM)],
+        out_specs=(anywhere, anywhere, anywhere),
+        scratch_shapes=[
+            pltpu.VMEM(up_cols.shape, jnp.bfloat16),
+            pltpu.VMEM((token_rows, model_width), jnp.bfloat16),
+            pltpu.VMEM((2, token_rows, width), jnp.bfloat16),
+            pltpu.VMEM((2, token_rows, width), jnp.bfloat16),
+            dma((9,)),
+            dma((9,)),
+            dma,
+            dma,
+            dma,
+            dma((2, 2)),
+        ],
+        compiler_params=pltpu.CompilerParams(
+            collective_id=call_number, has_side_effects=True, vmem_limit_bytes=VMEM_BYTES
+        ),
+        cost_estimate=pl.CostEstimate(
+            flops=16 * token_rows * model_width * width,
+            bytes_accessed=150 * 1000 * 1000,
+            transcendentals=0,
+        ),
+        name="gather_and_up",
+    )(own, up_cols, bias.reshape(1, -1))
+
+
+def grad_kernel(
+    own_ref,
+    down_hbm,
+    active_ref,
+    slope_ref,
+    rows_ref,
+    grad_ref,
+    weight_ref,
+    bias_ref,
+    down,
+    rows,
+    across,
+    active,
+    slope,
+    grads,
+    sums,
+    narrow,
+    send_sem,
+    recv_sem,
+    local_sem,
+    weight_sem,
+    row_sem,
+    load_sem,
+    store_sem,
+):
+    weights = pltpu.make_async_copy(down_hbm, down, weight_sem)
+    weights.start()
+    stores = {}
+
+    def use(place, block):
+        slot = place % 2
+        load = pltpu.make_async_copy(
+            rows_ref.at[block] if place else own_ref, rows, row_sem
+        )
+        load.start()
+        loads = (
+            pltpu.make_async_copy(active_ref.at[block], active, load_sem.at[0]),
+            pltpu.make_async_copy(slope_ref.at[block], slope, load_sem.at[1]),
+        )
+        for each in loads:
+            each.start()
+        if place == 0:
+            weights.wait()
+        if slot in stores:
+            stores.pop(slot).wait()
+        load.wait()
+        for each in loads:
+            each.wait()
+        across[...] = jnp.transpose(rows[...])
+
+        @pl.loop(0, down.shape[1] // CHUNK)
+        def _(turn):
+            at = chunk_of(turn, CHUNK)
+            value = plain_product(rows[...], down[:, at]) * slope[:, at].astype(jnp.float32)
+            value = value.astype(jnp.bfloat16)
+            grads[slot, :, at] = value
+            total = jnp.sum(value.astype(jnp.float32), axis=0, keepdims=True)
+            weight = plain_product(across[...], active[:, at])
+            if place == 0:
+                bias_ref[:, at] = total
+                sums[:, at] = weight
+            elif place < 7:
+                bias_ref[:, at] += total
+                sums[:, at] += weight
+            else:
+                bias_ref[:, at] += total
+                narrow[:, at] = (sums[:, at] + weight).astype(jnp.bfloat16)
+
+        stores[slot] = pltpu.make_async_copy(
+            grads.at[slot], grad_ref.at[block], store_sem.at[slot]
+        )
+        stores[slot].start()
+
+    gather_beside(own_ref, rows_ref, send_sem, recv_sem, local_sem, use)
+    last = pltpu.make_async_copy(narrow, weight_ref, weight_sem)
+    last.start()
+    for slot in (0, 1):
+        stores[slot].wait()
+    last.wait()
+
+
+def gather_and_grad(own, down_cols, active, slope, call_number):
+    token_rows, model_width = own.shape
+    width = down_cols.shape[1]
+    anywhere = pl.BlockSpec(memory_space=pl.ANY)
+    dma = pltpu.SemaphoreType.DMA
+    return pl.pallas_call(
+        grad_kernel,
+        out_shape=(
+            jax.ShapeDtypeStruct((8, token_rows, model_width), jnp.bfloat16),
+            jax.ShapeDtypeStruct((8, token_rows, width), jnp.bfloat16),
+            jax.ShapeDtypeStruct((model_width, width), jnp.bfloat16),
+            jax.ShapeDtypeStruct((1, width), jnp.float32),
+        ),
+        in_specs=[anywhere] * 4,
+        out_specs=(anywhere, anywhere, anywhere, pl.BlockSpec(memory_space=pltpu.VMEM)),
+        scratch_shapes=[
+            pltpu.VMEM(down_cols.shape, jnp.bfloat16),
+            pltpu.VMEM((token_rows, model_width), jnp.bfloat16),
+            pltpu.VMEM((model_width, token_rows), jnp.bfloat16),
+            pltpu.VMEM((token_rows, width), jnp.bfloat16),
+            pltpu.VMEM((token_rows, width), jnp.bfloat16),
+            pltpu.VMEM((2, token_rows, width), jnp.bfloat16),
+            pltpu.VMEM((model_width, width), jnp.float32),
+            pltpu.VMEM((model_width, width), jnp.bfloat16),
+            dma((9,)),
+            dma((9,)),
+            dma,
+            dma,
+            dma,
+            dma((2,)),
+            dma((2,)),
+        ],
+        compiler_params=pltpu.CompilerParams(
+            collective_id=call_number, has_side_effects=True, vmem_limit_bytes=VMEM_BYTES
+        ),
+        cost_estimate=pl.CostEstimate(
+            flops=32 * token_rows * model_width * width,
+            bytes_accessed=150 * 1000 * 1000,
+            transcendentals=0,
+        ),
+        name="gather_and_grad",
+    )(own, down_cols, active, slope)
+
+
+def product_reduce_kernel(
+    with_grad,
+    narrow_ref,
+    weight_hbm,
+    *refs,
+):
+    if with_grad:
+        wide_ref, out_ref, grad_ref, *refs = refs
+        *refs, wide, across, sums, wide_sem = refs
+    else:
+        out_ref, *refs = refs
+    (
+        weight,
+        narrow,
+        sent,
+        mine,
+        theirs,
+        relayed,
+        final,
+        send_sem,
+        recv_sem,
+        weight_sem,
+        narrow_sem,
+    ) = refs
+    rows = narrow.shape[1]
     half = rows // 2
     here, on_x, on_y, on_chip, corner = block_of_eight()
     shift = on_chip - here
     first, second = pl.ds(0, half), pl.ds(half, half)
+    load_weight = pltpu.make_async_copy(weight_hbm, weight, weight_sem)
+    load_weight.start()
 
     def copy(index, source, target, device):
-        return pltpu.make_async_remote_copy(
-            src_ref=source,
-            dst_ref=target,
-            send_sem=send_sem.at[index],
-            recv_sem=recv_sem.at[index],
-            device_id={"tok": device},
-            device_id_type=MESH,
-        )
+        return remote(index, source, target, device, send_sem, recv_sem)
 
     places = (corner, on_x, on_y, here)
+    order = []
+    for place in places:
+        order += [place + shift, place]
+
+    def fetch(turn):
+        return pltpu.make_async_copy(
+            narrow_ref.at[order[turn]], narrow.at[turn % 2], narrow_sem.at[turn % 2]
+        )
+
+    fetch(0).start()
     greet((on_x, on_y, on_chip))
-    to_chip = [
-        copy(index, part_ref.at[places[index] + shift], theirs.at[index], on_chip)
-        for index in range(4)
-    ]
-    loads = [
-        pltpu.make_async_copy(part_ref.at[places[index]], mine.at[index], load_sem.at[index])
-        for index in range(4)
-    ]
-    for index in range(4):
-        to_chip[index].start()
-        loads[index].start()
-
+    to_chip = [copy(index, sent.at[index], theirs.at[index], on_chip) for index in range(4)]
     step = 16
 
     def add_into(target, other, start, count):
@@ -180,76 +496,150 @@
         def _(turn):
             at = pl.ds(pl.multiple_of(start + turn * step, step), step)
             come = pl.ds(pl.multiple_of(turn * step, step), step)
-            total = target[at, :].astype(jnp.float32) + other(at, come).astype(jnp.float32)
+            total = target[at, :].astype(jnp.float32) + other[come, :].astype(jnp.float32)
             target[at, :] = total.astype(target.dtype)
 
     def join(index):
         to_chip[index].wait_recv()
-        loads[index].wait()
-        if index < 3:
-            add_into(mine.at[index], lambda at, come: theirs[index, at, :], 0, rows)
-
-    join(0)
+        add_into(mine.at[index], theirs.at[index], 0, rows)
+
     corner_x = copy(4, mine.at[0, first], relayed.at[0], on_x)
     corner_y = copy(5, mine.at[0, second], relayed.at[1], on_y)
-    corner_x.start()
-    corner_y.start()
-    join(1)
     x_first = copy(6, mine.at[1, first], final.at[0, first], on_x)
-    x_first.start()
-    join(2)
     y_second = copy(7, mine.at[2, second], final.at[1, second], on_y)
-    y_second.start()
+    x_second = copy(8, mine.at[1, second], final.at[0, second], on_x)
+    y_first = copy(9, mine.at[2, first], final.at[1, first], on_y)
+
+    for turn in range(8):
+        pair, own = turn // 2, turn % 2
+        if turn < 7:
+            fetch(turn + 1).start()
+        fetch(turn).wait()
+        if turn == 0:
+            load_weight.wait()
+        target = mine.at[pair] if own else sent.at[pair]
+
+        @pl.loop(0, weight.shape[0] // CHUNK)
+        def _(piece):
+            at = chunk_of(piece, CHUNK)
+            target[:, at] = transposed_product(narrow[turn % 2], weight[at, :]).astype(
+                jnp.bfloat16
+            )
+
+        if not own:
+            to_chip[pair].start()
+        if turn == 2:
+            join(0)
+            corner_x.start()
+            corner_y.start()
+        if turn == 4:
+            join(1)
+            x_first.start()
+        if turn == 6:
+            join(2)
+            y_second.start()
     corner_y.wait_recv()
-    add_into(mine.at[1], lambda at, come: relayed[1, come, :], half, half)
-    x_second = copy(8, mine.at[1, second], final.at[0, second], on_x)
+    add_into(mine.at[1], relayed.at[1], half, half)
     x_second.start()
     corner_x.wait_recv()
-    add_into(mine.at[2], lambda at, come: relayed[0, come, :], 0, half)
-    y_first = copy(9, mine.at[2, first], final.at[1, first], on_y)
+    add_into(mine.at[2], relayed.at[0], 0, half)
     y_first.start()
     join(3)
+
+    if with_grad:
+        def fetch_wide(turn):
+            return pltpu.make_async_copy(
+                wide_ref.at[order[turn]], wide.at[turn % 2], wide_sem.at[turn % 2]
+            )
+
+        fetch_wide(0).start()
+        fetch(0).start()
+        for turn in range(8):
+            if turn < 7:
+                fetch_wide(turn + 1).start()
+                fetch(turn + 1).start()
+            fetch_wide(turn).wait()
+            fetch(turn).wait()
+            across[...] = jnp.transpose(wide[turn % 2])
+
+            @pl.loop(0, sums.shape[1] // CHUNK)
+            def _(piece):
+                at = chunk_of(piece, CHUNK)
+                value = plain_product(across[...], narrow[turn % 2, :, at])
+                if turn == 0:
+                    sums[:, at] = value
+                elif turn < 7:
+                    sums[:, at] += value
+                else:
+                    weight[:, at] = (sums[:, at] + value).astype(jnp.bfloat16)
+
+        store = pltpu.make_async_copy(weight, grad_ref, weight_sem)
+        store.start()
+
     for each in (x_first, y_second, x_second, y_first):
         each.wait_recv()
 
     @pl.loop(0, rows // step)
     def _(turn):
         at = pl.ds(pl.multiple_of(turn * step, step), step)
-        total = mine[3, at, :].astype(jnp.float32) + theirs[3, at, :].astype(jnp.float32)
-        total = total + final[0, at, :].astype(jnp.float32) + final[1, at, :].astype(jnp.float32)
-        out_ref[at, :] = total.astype(out_ref.dtype)
-
+        total = mine[3, at, :].astype(jnp.float32) + final[0, at, :].astype(jnp.float32)
+        out_ref[at, :] = total + final[1, at, :].astype(jnp.float32)
+
+    if with_grad:
+        store.wait()
     for each in to_chip + [corner_x, corner_y, x_first, y_second, x_second, y_first]:
         each.wait_send()
 
 
-def tok_reduce(parts, call_number, kernels, out_type=jnp.float32):
-    if not kernels:
-        return lax.psum_scatter(parts, "tok", scatter_dimension=0, tiled=False).astype(out_type)
-    _, rows, columns = parts.shape
-    kind = parts.dtype
+def product_and_reduce(narrow, weight, wide, call_number):
+    _, token_rows, width = narrow.shape
+    model_width = weight.shape[0]
+    with_grad = wide is not None
+    anywhere = pl.BlockSpec(memory_space=pl.ANY)
+    inside = pl.BlockSpec(memory_space=pltpu.VMEM)
+    dma = pltpu.SemaphoreType.DMA
+    block = (token_rows, model_width)
+    kind = jnp.bfloat16
+    out_shape = [jax.ShapeDtypeStruct(block, jnp.float32)]
+    scratch = [
+        pltpu.VMEM(weight.shape, kind),
+        pltpu.VMEM((2, token_rows, width), kind),
+        pltpu.VMEM((4,) + block, kind),
+        pltpu.VMEM((4,) + block, kind),
+        pltpu.VMEM((4,) + block, kind),
+        pltpu.VMEM((2, token_rows // 2, model_width), kind),
+        pltpu.VMEM((2,) + block, kind),
+        dma((10,)),
+        dma((10,)),
+        dma,
+        dma((2,)),
+    ]
+    operands = [narrow, weight]
+    if with_grad:
+        out_shape.append(jax.ShapeDtypeStruct(weight.shape, kind))
+        scratch += [
+            pltpu.VMEM((2,) + block, kind),
+            pltpu.VMEM((model_width, token_rows), kind),
+            pltpu.VMEM(weight.shape, jnp.float32),
+            dma((2,)),
+        ]
+        operands.append(wide)
     return pl.pallas_call(
-        reduce_kernel,
-        out_shape=jax.ShapeDtypeStruct((rows, columns), out_type),
-        in_specs=[pl.BlockSpec(memory_space=pl.ANY)],
-        out_specs=pl.BlockSpec(memory_space=pltpu.VMEM),
-        scratch_shapes=[
-            pltpu.VMEM((4, rows, columns), kind),
-            pltpu.VMEM((4, rows, columns), kind),
-            pltpu.VMEM((2, rows // 2, columns), kind),
-            pltpu.VMEM((2, rows, columns), kind),
-            pltpu.SemaphoreType.DMA((10,)),
-            pltpu.SemaphoreType.DMA((10,)),
-            pltpu.SemaphoreType.DMA((4,)),
-        ],
+        functools.partial(product_reduce_kernel, with_grad),
+        out_shape=tuple(out_shape),
+        in_specs=[anywhere] * len(operands),
+        out_specs=(inside, anywhere)[: len(out_shape)],
+        scratch_shapes=scratch,
         compiler_params=pltpu.CompilerParams(
             collective_id=call_number, has_side_effects=True, vmem_limit_bytes=VMEM_BYTES
         ),
         cost_estimate=pl.CostEstimate(
-            flops=0, bytes_accessed=rows * columns * 2 * 100, transcendentals=0
-        ),
-        name="tok_reduce",
-    )(parts)
+            flops=(32 if with_grad else 16) * token_rows * model_width * width,
+            bytes_accessed=150 * 1000 * 1000,
+            transcendentals=0,
+        ),
+        name="product_and_reduce",
+    )(*operands)
 
 
 def peers_of(count):
@@ -1182,11 +1572,16 @@
         answer_count,
     )
 
-    group_two = tok_gather(normed_two, 2, kernels).reshape(-1, model_width)
-    pre_active = plain_product(group_two, up_cols) + up_here
-    activated = jax.nn.gelu(pre_active, approximate=True).astype(jnp.bfloat16)
-    feed_term = for_sending(transposed_product(activated, down_cols))
-    feed_term = tok_reduce(feed_term.reshape(token_devices, token_rows, model_width), 3, kernels)
+    if kernels:
+        group_two, activated, slope = gather_and_up(normed_two, up_cols, up_here, 2)
+        (feed_term,) = product_and_reduce(activated, down_cols, None, 3)
+    else:
+        group_two = lax.all_gather(normed_two, "tok", axis=0, tiled=True)
+        pre_active = plain_product(group_two, up_cols) + up_here
+        activated = jax.nn.gelu(pre_active, approximate=True).astype(jnp.bfloat16)
+        feed_term = for_sending(transposed_product(activated, down_cols))
+        feed_term = lax.psum_scatter(feed_term, "tok", scatter_dimension=0, tiled=True)
+        feed_term = feed_term.astype(jnp.float32)
     result_rows = hidden + feed_term + down_offset
 
     teacher = own_rows(prompt_teacher, answer_teacher).astype(jnp.float32)
@@ -1196,23 +1591,29 @@
     grad_result = every_token / valid_count * valid_rows[:, None] * differ
     grad_branch_two = grad_result.astype(jnp.bfloat16)
 
-    group_grad_two = tok_gather(grad_branch_two, 4, kernels).reshape(-1, model_width)
-    grad_activated = plain_product(group_grad_two, down_cols)
-    _, gelu_back = jax.vjp(lambda argument: jax.nn.gelu(argument, approximate=True), pre_active)
-    grad_pre_active = gelu_back(grad_activated)[0].astype(jnp.bfloat16)
-    grad_normed_two = for_sending(transposed_product(grad_pre_active, up_cols))
-    grad_down_cols = for_sending(weight_product(group_grad_two, activated))
-    grad_up_cols = for_sending(weight_product(group_two, grad_pre_active))
-    grad_normed_two, grad_down_cols, grad_up_cols = lax.optimization_barrier(
-        (grad_normed_two, grad_down_cols, grad_up_cols)
-    )
+    if kernels:
+        _, grad_pre_active, grad_down_cols, grad_up_offset = gather_and_grad(
+            grad_branch_two, down_cols, activated, slope, 4
+        )
+        grad_normed_two, grad_up_cols = product_and_reduce(grad_pre_active, up_cols, group_two, 5)
+        grad_up_offset = grad_up_offset.reshape(-1)
+    else:
+        group_grad_two = lax.all_gather(grad_branch_two, "tok", axis=0, tiled=True)
+        grad_activated = plain_product(group_grad_two, down_cols)
+        _, gelu_back = jax.vjp(
+            lambda argument: jax.nn.gelu(argument, approximate=True), pre_active
+        )
+        grad_pre_active = gelu_back(grad_activated)[0].astype(jnp.bfloat16)
+        grad_normed_two = for_sending(transposed_product(grad_pre_active, up_cols))
+        grad_normed_two = lax.psum_scatter(
+            grad_normed_two, "tok", scatter_dimension=0, tiled=True
+        ).astype(jnp.float32)
+        grad_down_cols = for_sending(weight_product(group_grad_two, activated))
+        grad_up_cols = for_sending(weight_product(group_two, grad_pre_active))
+        grad_up_offset = column_sums(grad_pre_active)
     grad_down_weight = lax.psum_scatter(grad_down_cols, "grp", scatter_dimension=0, tiled=True)
     grad_up_weight = lax.psum_scatter(grad_up_cols, "grp", scatter_dimension=0, tiled=True)
-    grad_normed_two = tok_reduce(
-        grad_normed_two.reshape(token_devices, token_rows, model_width), 5, kernels
-    )
     grad_down_offset = column_sums(grad_branch_two)
-    grad_up_offset = column_sums(grad_pre_active)
     scaled_two, inverse_two = norm_stats(hidden)
     grad_norm_two, grad_gain_two, grad_shift_two = norm_backward(
         grad_normed_two, gain_two, scaled_two, inverse_two

time: 823 us -> 751 us (0.913)
  matrix products: 139 us -> 6.96 us
  Pallas kernels: 533 us -> 589 us
    pallas_call x2 -> x4, Pallas kernels: 121 us -> 286 us  [the longest x2 134 us: product_and_reduce(): pl.pallas_call(functools.partial(product_reduce_kernel, with_grad), out_s...]
    pallas_call x3 -> x1, Pallas kernels: 202 us -> 82.4 us  [tok_gather(): pl.pallas_call(gather_kernel, out_shape=jax.ShapeDtypeStruct((8,) + own.s...]
    dot_general x3 -> x1, matrix products: 47.1 us -> 0.6 us  [plain_product(): return jnp.dot(left, right, preferred_element_type=jnp.float32)]
    dot_general x3 -> x1, matrix products: 50.5 us -> 5.62 us  [transposed_product(): lax.dot_general(left, right, (((1,), (1,)), ((), ())), preferred_element_...]
    dot_general x3 -> x1, matrix products: 41.9 us -> 0.75 us  [weight_product(): lax.dot_general(left, right, (((0,), (0,)), ((), ())), preferred_element_...]
    pallas_call x1, Pallas kernels: 97.3 us -> 108 us  [final_reduce(): pl.pallas_call(functools.partial(final_reduce_kernel, groups), out_shape=...]
  transfers between devices with their start and end apart: 5 -> 5, of which waited for: 1 -> 1; matrix products, arithmetic and copies ran while one was open for 9% -> 8% of each run, Pallas kernels for 51% -> 51%
where the time goes in v3:
time: 751 us; the launch traced here: 737 us
  Pallas kernels  589 us (78%)
  waiting for transfers between devices  49.4 us (7%)
  other arithmetic  36.3 us (5%)
  local copies, waits for them, and re-layouts  35.8 us (5%)
  between operations  19 us (3%)
    pallas_call x2, Pallas kernels, product_and_reduce(): pl.pallas_call(functools.partial(product_reduce_kernel, with_grad), out_s...  134 us
    pallas_call x1, Pallas kernels, final_reduce(): pl.pallas_call(functools.partial(final_reduce_kernel, groups), out_shape=...  108 us
    pallas_call x1, Pallas kernels, tok_gather(): pl.pallas_call(gather_kernel, out_shape=jax.ShapeDtypeStruct((8,) + own.s...  82.4 us
    pallas_call x1, Pallas kernels, gather_and_grad(): pl.pallas_call(grad_kernel, out_shape=(jax.ShapeDtypeStruct((8, token_row...  82 us
    pallas_call x1, Pallas kernels, gather_and_up(): pl.pallas_call(up_kernel, out_shape=(jax.ShapeDtypeStruct((8, token_rows,...  69.5 us
    all_gather x1, waiting for transfers between devices, body(): packed = lax.all_gather(pack, 'grp', axis=0, tiled=True)  47.4 us
    pallas_call x1, Pallas kernels, attention_backward(): pl.pallas_call(functools.partial(attention_backward_kernel, prompts, answ...  46.6 us
    pallas_call x1, Pallas kernels, attention_forward(): pl.pallas_call(functools.partial(attention_forward_kernel, prompts, answe...  38.2 us
  transfers between devices with their start and end apart: 5, of which 1 were waited for; matrix products, arithmetic and copies ran while one was open for 8% of the time, Pallas kernels for 51%

profile of v3, /device:TPU:0, one launch (start us, length us, event | category | flops | bytes accessed | tf_op | source)
XLA Modules:
  0.0 736.8 jit_solution(2663912035723102640)
XLA Ops:
  7.3 1.4 reduce_sum.181
  8.7 1.3 reduce_sum.182
  11.4 5.4 concatenate.43
  16.8 1.9 pad_maximum_fusion.1
  21.8 1.3 pad_maximum_fusion.states_ref
  23.0 47.4 %all-gather.4.cloned.1.call-done.own_ref = bf16[4416,256]{1,0:T(8,128)(2,1)} async-done(((bf16[1104,256]{1,0:T(8,128)(2,1)}), bf16[4416,256]{1,0:T(8,128)(2,1)}) %all-gather.4.cloned.1.call-update) | async-done | bytes 2261008 | tf_op jit(solution)/shard_map/all_gather | solution.py:1519
  70.4 82.4 %tok_gather.1 = bf16[8,4416,256]{2,1,0:T(8,128)(2,1)} custom-call(bf16[4416,256]{1,0:T(8,128)(2,1)} %all-gather.4.cloned.1.call-done.own_ref), custom_call_target="tpu_custom_call" | custom-call | bytes 226099200 | tf_op jit(solution)/shard_map/tok_gather/pallas_call | solution.py:127
  155.5 1.3 slice_bitcast_fusion
  159.4 12.9 %tok_gather_small.1.prompt_kv_ref = bf16[2,1024,256]{2,1,0:T(8,128)(2,1)} custom-call(bf16[2,128,256]{2,1,0:T(8,128)(2,1)} %bitcast.76), custom_call_target="tpu_custom_call" | custom-call | tf_op jit(solution)/shard_map/tok_gather_small/pallas_call | solution.py:682
  176.6 38.2 %attention_forward.1 = (bf16[384,2048]{1,0:T(8,128)(2,1)}, bf16[384,2048]{1,0:T(8,128)(2,1)}, f32[8,2,384]{2,1,0:T(2,128)}, f32[384,2048]{1,0:T(8,128)}, bf16[384,2048]{1,0:T(8,128)(2,1)}) custom-call(s32[1]{0:T(128)} %bitcast.place_ref, s32[1]{0:T(128)} %dynamic_slice.6.owner_ref, bf16[384,2048]{1,0:T(8,128)(2,1)} %copy-done.10, ...), custom_call_target="tpu_custom_call" | custom-call | flops 12884901888 | bytes 33554432 | tf_op jit(solution)/shard_map/attention_forward/pallas_call | solution.py:1157
  214.8 2.1 reduce_sum.186
  216.9 1.5 slice_reduce_fusion
  219.8 69.5 %gather_and_up.1 = (bf16[8,384,2048]{2,1,0:T(8,128)(2,1)}, bf16[8,384,1024]{2,1,0:T(8,128)(2,1)}, bf16[8,384,1024]{2,1,0:T(8,128)(2,1)}) custom-call(bf16[384,2048]{1,0:T(8,128)(2,1)} %get-tuple-element.40.own_ref, bf16[2048,1024]{1,0:T(8,128)(2,1)} %all-gather.6.cloned.1.call-done.up_hbm.weight_hbm, f32[1,1024]{1,0:T(1,128)} %bitcast.85), custom_call_target="tpu_custom_call" | custom-call | flops 12884901888 | bytes 150000000 | tf_op jit(solution)/shard_map/gather_and_up/pallas_call | solution.py:286
  289.4 68.0 %product_and_reduce.2 = f32[384,2048]{1,0:T(8,128)} custom-call(bf16[8,384,1024]{2,1,0:T(8,128)(2,1)} %get-tuple-element.41.narrow_ref.active_ref, bf16[2048,1024]{1,0:T(8,128)(2,1)} %all-gather.8.cloned.1.call-done.weight_hbm.down_hbm), custom_call_target="tpu_custom_call" | custom-call | flops 12884901888 | bytes 150000000 | tf_op jit(solution)/shard_map/product_and_reduce/pallas_call | solution.py:627
  357.4 5.0 fusion.15
  362.4 1.7 copy-done.1
  364.1 1.5 convert_reduce_fusion.1
  365.5 82.0 %gather_and_grad.1 = (bf16[8,384,2048]{2,1,0:T(8,128)(2,1)}, bf16[8,384,1024]{2,1,0:T(8,128)(2,1)}, bf16[2048,1024]{1,0:T(8,128)(2,1)}, f32[1,1024]{1,0:T(1,128)}) custom-call(bf16[384,2048]{1,0:T(8,128)(2,1)} %get-tuple-element.72.own_ref, bf16[2048,1024]{1,0:T(8,128)(2,1)} %all-gather.8.cloned.1.call-done.weight_hbm.down_hbm, ...), custom_call_target="tpu_custom_call" | custom-call | flops 25769803776 | bytes 150000000 | tf_op jit(solution)/shard_map/gather_and_grad/pallas_call | solution.py:405
  447.5 66.2 %product_and_reduce.3 = (f32[384,2048]{1,0:T(8,128)}, bf16[2048,1024]{1,0:T(8,128)(2,1)}) custom-call(bf16[8,384,1024]{2,1,0:T(8,128)(2,1)} %get-tuple-element.43.narrow_ref, bf16[2048,1024]{1,0:T(8,128)(2,1)} %all-gather.6.cloned.1.call-done.up_hbm.weight_hbm, bf16[8,384,2048]{2,1,0:T(8,128)(2,1)} %get-tuple-element.44.refs_0_), custom_call_target="tpu_custom_call" | custom-call | flops 25769803776 | bytes 150000000 | tf_op jit(solution)/shard_map/product_and_reduce/pallas_call | solution.py:627
  514.4 3.2 multiply_reduce_fusion
  518.2 3.1 convert_reduce_fusion.2
  521.3 46.6 %attention_backward.1 = (bf16[8,4,1088,256]{3,2,1,0:T(8,128)(2,1)}, f32[384,2048]{1,0:T(8,128)}, bf16[2,1024,256]{2,1,0:T(8,128)(2,1)}, f32[128,256]{1,0:T(8,128)}, f32[8,1,256]{2,1,0:T(1,128)}) custom-call(s32[1]{0:T(128)} %bitcast.place_ref, s32[1]{0:T(128)} %dynamic_slice.6.owner_ref, bf16[384,2048]{1,0:T(8,128)(2,1)} %copy-done.10, ...), custom_call_target="tpu_custom_call" | custom-call | flops 28991029248 | bytes 67108864 | tf_op jit(solution)/shard_map/attention_backward/pallas_call | solution.py:1374
  567.9 15.5 %tok_reduce_small.1 = f32[2,128,256]{2,1,0:T(8,128)} custom-call(bf16[2,1024,256]{2,1,0:T(8,128)(2,1)} %get-tuple-element.50.part_ref), custom_call_target="tpu_custom_call" | custom-call | tf_op jit(solution)/shard_map/tok_reduce_small/pallas_call | solution.py:733
  585.4 5.6 fusion.13
  599.7 107.9 %final_reduce.1 = (f32[1088,256]{1,0:T(8,128)}, f32[8,128]{1,0:T(8,128)}) custom-call(bf16[8,4352,256]{2,1,0:T(8,128)(2,1)} %bitcast.56, f32[8,32,128]{2,1,0:T(8,128)} %reshape.234.small_ref), custom_call_target="tpu_custom_call" | custom-call | tf_op jit(solution)/shard_map/final_reduce/pallas_call | solution.py:981
  707.6 1.3 slice.130
  708.9 1.3 slice.128
  711.4 1.5 slice.122
  712.9 3.2 fusion.12
  721.5 1.9 slice_bitcast_fusion.2
  723.3 2.8 convert_element_type.77
  726.1 2.8 convert_element_type.78
  (131 shorter events, 30.2 us)
Async XLA Ops:
  7.2 14.0 %copy-start.18 = (s32[2,128]{1,0:T(2,128)S(1)}, s32[2,128]{1,0:T(2,128)}, u32[]{:S(2)}) copy-start(s32[2,128]{1,0:T(2,128)} %param.26) | copy-start | bytes 3076
  7.2 14.0 %copy-start.24 = (s32[1,128]{1,0:T(1,128)S(1)}, s32[1,128]{1,0:T(1,128)}, u32[]{:S(2)}) copy-start(s32[1,128]{1,0:T(1,128)} %param.27) | copy-start | bytes 1540
  7.2 13.1 %copy-start.25 = (s32[8]{0:T(128)S(1)}, s32[8]{0:T(128)}, u32[]{:S(2)}) copy-start(s32[8]{0:T(128)} %param.23) | copy-start | bytes 100
  7.2 13.7 %copy-start.3 = (bf16[2,128,2048]{2,1,0:T(8,128)(2,1)S(1)}, bf16[2,128,2048]{2,1,0:T(8,128)(2,1)}, u32[]{:S(2)}) copy-start(bf16[2,128,2048]{2,1,0:T(8,128)(2,1)} %param.21) | copy-start | bytes 3145732
  7.2 13.6 %copy-start.5 = (bf16[1,128,2048]{2,1,0:T(8,128)(2,1)S(1)}, bf16[1,128,2048]{2,1,0:T(8,128)(2,1)}, u32[]{:S(2)}) copy-start(bf16[1,128,2048]{2,1,0:T(8,128)(2,1)} %param.22) | copy-start | bytes 1572868
  7.2 13.9 %copy-start.26 = (bf16[128]{0:T(256)(128)(2,1)S(1)}, bf16[128]{0:T(256)(128)(2,1)}, u32[]{:S(2)}) copy-start(bf16[128]{0:T(256)(128)(2,1)} %param.33) | copy-start | bytes 772
  7.3 63.2 %all-gather.4.cloned.1.call-start = ((), (), s32[]{:S(2)}) async-start(), calls=%async_computation.2 | async-start | bytes 2826240 | tf_op jit(solution)/shard_map/all_gather | solution.py:1519
  18.7 201.1 %all-gather.6.cloned.1.call-start = ((), (), s32[]{:S(2)}) async-start(), calls=%async_computation.3 | async-start | bytes 5242880 | tf_op jit(solution)/shard_map/all_gather | solution.py:1497
  19.5 269.8 %all-gather.8.cloned.1.call-start = ((), (), s32[]{:S(2)}) async-start(), calls=%async_computation.4 | async-start | bytes 5242880 | tf_op jit(solution)/shard_map/all_gather | solution.py:1498
  20.2 703.1 %reduce-scatter.3.cloned.1.call-start = ((), (), s32[]{:S(2)}) async-start(), calls=%async_computation.5 | async-start | bytes 5242880 | tf_op jit(solution)/shard_map/reduce_scatter | solution.py:1615
  154.4 0.8 copy-start.16
  156.8 1.3 copy-start.14
  157.5 19.1 %copy-start.10 = (bf16[384,2048]{1,0:T(8,128)(2,1)}, bf16[384,2048]{1,0:T(8,128)(2,1)S(1)}, u32[]{:S(2)}) copy-start(bf16[384,2048]{1,0:T(8,128)(2,1)S(1)} %fusion.7.normed_ref) | copy-start | bytes 4718596
  289.3 68.0 %copy-start = (f32[384,2048]{1,0:T(8,128)S(1)}, f32[384,2048]{1,0:T(8,128)}, u32[]{:S(2)}) copy-start(f32[384,2048]{1,0:T(8,128)} %get-tuple-element.39) | copy-start | bytes 9437188
  289.3 68.0 %copy-start.13 = (bf16[2,128,2048]{2,1,0:T(8,128)(2,1)S(1)}, bf16[2,128,2048]{2,1,0:T(8,128)(2,1)}, u32[]{:S(2)}) copy-start(bf16[2,128,2048]{2,1,0:T(8,128)(2,1)} %param.24) | copy-start | bytes 3145732
  289.4 68.0 %copy-start.17 = (bf16[1,128,2048]{2,1,0:T(8,128)(2,1)S(1)}, bf16[1,128,2048]{2,1,0:T(8,128)(2,1)}, u32[]{:S(2)}) copy-start(bf16[1,128,2048]{2,1,0:T(8,128)(2,1)} %param.25) | copy-start | bytes 1572868
  362.4 1.7 copy-start.1
  513.7 212.5 %reduce-scatter.5.cloned.1.call-start = ((), (), s32[]{:S(2)}) async-start(), calls=%async_computation.6 | async-start | bytes 5242880 | tf_op jit(solution)/shard_map/reduce_scatter | solution.py:1614
  514.4 3.3 copy-start.2
  514.4 3.8 copy-start.7
  521.3 64.0 %copy-start.4 = (bf16[2,128,2048]{2,1,0:T(8,128)(2,1)S(1)}, bf16[2,128,2048]{2,1,0:T(8,128)(2,1)}, u32[]{:S(2)}) copy-start(bf16[2,128,2048]{2,1,0:T(8,128)(2,1)} %param.21) | copy-start | bytes 3145732
  521.3 64.0 %copy-start.6 = (bf16[1,128,2048]{2,1,0:T(8,128)(2,1)S(1)}, bf16[1,128,2048]{2,1,0:T(8,128)(2,1)}, u32[]{:S(2)}) copy-start(bf16[1,128,2048]{2,1,0:T(8,128)(2,1)} %param.22) | copy-start | bytes 1572868
  521.3 64.0 %copy-start.15 = (bf16[4,8,64,256]{3,2,1,0:T(8,128)(2,1)S(1)}, bf16[4,8,64,256]{3,2,1,0:T(8,128)(2,1)}, u32[]{:S(2)}) copy-start(bf16[4,8,64,256]{3,2,1,0:T(8,128)(2,1)} %copy-done.14) | copy-start | bytes 3145732
  585.3 6.4 copy-start.19
  585.3 9.1 %copy-start.21 = (f32[1,1024]{1,0:T(1,128)S(1)}, f32[1,1024]{1,0:T(1,128)}, u32[]{:S(2)}) copy-start(f32[1,1024]{1,0:T(1,128)} %get-tuple-element.54) | copy-start | bytes 12292
  585.3 12.5 %copy-start.11 = (bf16[384,2048]{1,0:T(8,128)(2,1)S(1)}, bf16[384,2048]{1,0:T(8,128)(2,1)}, u32[]{:S(2)}) copy-start(bf16[384,2048]{1,0:T(8,128)(2,1)} %copy-done.10) | copy-start | bytes 4718596
  599.7 113.2 %copy-start.23 = (f32[384]{0:T(512)S(1)}, f32[384]{0:T(512)}, u32[]{:S(2)}) copy-start(f32[384]{0:T(512)} %get-tuple-element.62) | copy-start | bytes 4612
  599.7 113.2 %copy-start.22 = (f32[384]{0:T(512)S(1)}, f32[384]{0:T(512)}, u32[]{:S(2)}) copy-start(f32[384]{0:T(512)} %get-tuple-element.63) | copy-start | bytes 4612
  599.7 113.2 %copy-start.8 = (f32[384,2048]{1,0:T(8,128)S(1)}, f32[384,2048]{1,0:T(8,128)}, u32[]{:S(2)}) copy-start(f32[384,2048]{1,0:T(8,128)} %get-tuple-element.75) | copy-start | bytes 9437188
  712.9 4.3 copy-start.9
  716.2 2.8 copy-start.20
  716.2 3.4 copy-start.12
Sparse Core Ops, SparseCore 0:
  18.8 51.5 all-gather.3
  72.0 79.5 all-gather.5
  153.2 79.2 all-gather.7
  513.8 75.5 reduce-scatter.2
  591.7 102.1 reduce-scatter.4

commit v4 on v3

--- a/solution.py
+++ b/solution.py
@@ -66,6 +66,15 @@
     return here, on_x, on_y, on_chip, corner
 
 
+def greet_all(peers, other_groups):
+    barrier = pltpu.get_barrier_semaphore()
+    for peer in peers:
+        pl.semaphore_signal(barrier, inc=1, device_id={"tok": peer}, device_id_type=MESH)
+    for other in other_groups:
+        pl.semaphore_signal(barrier, inc=1, device_id={"grp": other}, device_id_type=MESH)
+    pl.semaphore_wait(barrier, len(peers) + len(other_groups))
+
+
 def greet(devices):
     barrier = pltpu.get_barrier_semaphore()
     for device in devices:
@@ -73,72 +82,59 @@
     pl.semaphore_wait(barrier, len(devices))
 
 
-def gather_kernel(own_ref, out_ref, send_sem, recv_sem, local_sem):
-    half = own_ref.shape[0] // 2
-    here, on_x, on_y, on_chip, corner = block_of_eight()
-    first, second = pl.ds(0, half), pl.ds(half, half)
-
-    def copy(index, source, target, device):
-        return pltpu.make_async_remote_copy(
-            src_ref=source,
-            dst_ref=target,
-            send_sem=send_sem.at[index],
-            recv_sem=recv_sem.at[index],
-            device_id={"tok": device},
+def spread_kernel(groups, own_ref, out_ref, held, send_sem, recv_sem, over_send, over_recv):
+    here, peers = peers_of(8)
+    group = lax.axis_index("grp")
+    other_groups = [(group + turn) % groups for turn in range(1, groups)]
+    greet_all(peers, other_groups)
+    over = [
+        pltpu.make_async_remote_copy(
+            src_ref=own_ref,
+            dst_ref=held.at[group],
+            send_sem=over_send.at[index],
+            recv_sem=over_recv.at[index],
+            device_id={"grp": other},
             device_id_type=MESH,
         )
-
-    greet((on_x, on_y, on_chip))
-    own = pltpu.make_async_copy(own_ref, out_ref.at[here], local_sem)
+        for index, other in enumerate(other_groups)
+    ]
+    for each in over:
+        each.start()
+    held[group] = own_ref[...]
+    for each in over:
+        each.wait_recv()
     copies = [
-        copy(0, own_ref, out_ref.at[here], on_x),
-        copy(1, own_ref, out_ref.at[here], on_y),
-        copy(2, own_ref, out_ref.at[here], on_chip),
-        copy(3, out_ref.at[on_x, first], out_ref.at[on_x, first], on_y),
-        copy(4, out_ref.at[on_x], out_ref.at[on_x], on_chip),
-        copy(5, out_ref.at[on_y, second], out_ref.at[on_y, second], on_x),
-        copy(6, out_ref.at[on_y], out_ref.at[on_y], on_chip),
-        copy(7, out_ref.at[corner, first], out_ref.at[corner, first], on_chip),
-        copy(8, out_ref.at[corner, second], out_ref.at[corner, second], on_chip),
+        remote(index, held, out_ref.at[here], peer, send_sem, recv_sem)
+        for index, peer in enumerate(peers)
     ]
-    for index in range(3):
-        copies[index].start()
-    own.start()
-    copies[0].wait_recv()
-    copies[3].start()
-    copies[4].start()
-    copies[1].wait_recv()
-    copies[5].start()
-    copies[6].start()
-    copies[3].wait_recv()
-    copies[7].start()
-    copies[5].wait_recv()
-    copies[8].start()
-    for index in (2, 4, 6, 7, 8):
-        copies[index].wait_recv()
     for each in copies:
+        each.start()
+    out_ref[here] = held[...]
+    for each in copies:
+        each.wait_recv()
+    for each in copies + over:
         each.wait_send()
-    own.wait()
-
-
-def tok_gather(own, call_number, kernels):
+
+
+def spread(own, groups, call_number, kernels):
     if not kernels:
-        return lax.all_gather(own, "tok", axis=0)
+        return lax.all_gather(lax.all_gather(own, "grp", axis=0), "tok", axis=0)
+    inside = pl.BlockSpec(memory_space=pltpu.VMEM)
+    dma = pltpu.SemaphoreType.DMA
     return pl.pallas_call(
-        gather_kernel,
-        out_shape=jax.ShapeDtypeStruct((8,) + own.shape, own.dtype),
-        in_specs=[pl.BlockSpec(memory_space=pl.ANY)],
-        out_specs=pl.BlockSpec(memory_space=pl.ANY),
+        functools.partial(spread_kernel, groups),
+        out_shape=jax.ShapeDtypeStruct((8, groups) + own.shape, own.dtype),
+        in_specs=[inside],
+        out_specs=inside,
         scratch_shapes=[
-            pltpu.SemaphoreType.DMA((9,)),
-            pltpu.SemaphoreType.DMA((9,)),
-            pltpu.SemaphoreType.DMA,
+            pltpu.VMEM((groups,) + own.shape, own.dtype),
+            dma((7,)),
+            dma((7,)),
+            dma((groups - 1,)),
+            dma((groups - 1,)),
         ],
         compiler_params=pltpu.CompilerParams(collective_id=call_number, has_side_effects=True),
-        cost_estimate=pl.CostEstimate(
-            flops=0, bytes_accessed=own.size * 2 * 100, transcendentals=0
-        ),
-        name="tok_gather",
+        name="spread",
     )(own)
 
 
@@ -781,12 +777,7 @@
     other_groups = [(group + turn) % groups for turn in range(1, groups)]
     step = 16
 
-    barrier = pltpu.get_barrier_semaphore()
-    for peer in peers:
-        pl.semaphore_signal(barrier, inc=1, device_id={"tok": peer}, device_id_type=MESH)
-    for other in other_groups:
-        pl.semaphore_signal(barrier, inc=1, device_id={"grp": other}, device_id_type=MESH)
-    pl.semaphore_wait(barrier, len(peers) + len(other_groups))
+    greet_all(peers, other_groups)
 
     def copy(chunk, index, source, target, device):
         return pltpu.make_async_remote_copy(
@@ -1045,38 +1036,23 @@
     return jnp.transpose(wide)[0:1, :]
 
 
-def attention_forward_kernel(
+def forward_block(
     prompts,
     answers,
     heads,
-    scale,
-    place_ref,
+    start,
     owner_ref,
     normed_ref,
-    query_ref,
-    bias_ref,
+    query_block,
+    bias,
     prompt_kv_ref,
     answer_kv_ref,
-    output_ref,
-    states_ref,
-    offset_ref,
-    gain_ref,
-    shift_ref,
-    queries_ref,
-    mixture_ref,
-    log_ref,
-    hidden_ref,
-    second_ref,
 ):
-    step = pl.program_id(0)
     width = HEAD_WIDTH
+    scale = HEAD_WIDTH ** (-0.5)
     length = prompt_kv_ref.shape[1]
-    query_block = query_ref[0].reshape(-1, query_ref.shape[-1])
-    output_block = output_ref[0].reshape(-1, output_ref.shape[-1])
-    queries = (plain_product(normed_ref[...], query_block) + bias_ref[0]).astype(jnp.bfloat16)
-    queries_ref[...] = queries
-
-    pieces = []
+    queries = (plain_product(normed_ref[...], query_block) + bias).astype(jnp.bfloat16)
+    pieces, logs = [], []
     for part in range(prompts + answers):
         here, rows = part_rows(part, prompts, answers, normed_ref, answer_kv_ref)
         token = lax.broadcasted_iota(jnp.int32, (heads * rows, 1), 0) % rows
@@ -1086,7 +1062,7 @@
             values = prompt_kv_ref[part, :, width:]
             scores = transposed_product(stacked, keys)
             place = lax.broadcasted_iota(jnp.int32, (1, length), 1)
-            scores = jnp.where(place <= place_ref[0] + token, scores, masked)
+            scores = jnp.where(place <= start + token, scores, masked)
             top = jnp.max(scores, axis=-1, keepdims=True)
             exponent = jnp.exp((scores - top) * scale)
             total = jnp.sum(exponent, axis=-1, keepdims=True)
@@ -1114,17 +1090,56 @@
                 own_exponent.astype(jnp.bfloat16), answer_kv_ref[own, width:]
             )
         pieces.append(unstack_heads((mixed / total).astype(jnp.bfloat16), heads))
-        log_row = as_row(top * scale + jnp.log(total))
+        logs.append((here, rows, as_row(top * scale + jnp.log(total))))
+    return queries, jnp.concatenate(pieces, axis=0), logs
+
+
+def attention_forward_kernel(
+    prompts,
+    answers,
+    heads,
+    place_ref,
+    owner_ref,
+    normed_ref,
+    query_ref,
+    bias_ref,
+    prompt_kv_ref,
+    answer_kv_ref,
+    output_ref,
+    states_ref,
+    offset_ref,
+    gain_ref,
+    shift_ref,
+    queries_ref,
+    mixture_ref,
+    log_ref,
+    hidden_ref,
+    second_ref,
+):
+    step = pl.program_id(0)
+    queries, mixture, logs = forward_block(
+        prompts,
+        answers,
+        heads,
+        place_ref[0],
+        owner_ref,
+        normed_ref,
+        query_ref[0],
+        bias_ref[0],
+        prompt_kv_ref,
+        answer_kv_ref,
+    )
+    queries_ref[0] = queries
+    mixture_ref[0] = mixture
+    for here, rows, log_row in logs:
         for head in range(heads):
             log_ref[0, head : head + 1, here] = log_row[:, head * rows : (head + 1) * rows]
-    mixture = jnp.concatenate(pieces, axis=0)
-    mixture_ref[...] = mixture
 
     @pl.when(step == 0)
     def _():
         hidden_ref[...] = states_ref[...].astype(jnp.float32) + offset_ref[...]
 
-    hidden_ref[...] += transposed_product(mixture, output_block)
+    hidden_ref[...] += transposed_product(mixture, output_ref[0])
 
     @pl.when(step == pl.num_programs(0) - 1)
     def _():
@@ -1136,8 +1151,8 @@
     place,
     owning,
     normed,
-    packed,
-    weight_rows,
+    query_blocks,
+    output_blocks,
     query_offset,
     prompt_kv,
     answer_kv,
@@ -1149,18 +1164,16 @@
     answers,
 ):
     token_rows, model_width = normed.shape
-    steps, groups, _, block = packed.shape
+    steps, _, block = query_blocks.shape
     heads = block // HEAD_WIDTH
-    length = prompt_kv.shape[1]
     whole = lambda *shape: pl.BlockSpec(shape, lambda step, *_: (0,) * len(shape))
-    scores = heads * token_rows * length
+    one = lambda *shape: pl.BlockSpec((1,) + shape, lambda step, *_: (step, 0, 0))
+    by_step = jax.ShapeDtypeStruct((steps, token_rows, block), jnp.bfloat16)
     return pl.pallas_call(
-        functools.partial(
-            attention_forward_kernel, prompts, answers, heads, HEAD_WIDTH ** (-0.5)
-        ),
+        functools.partial(attention_forward_kernel, prompts, answers, heads),
         out_shape=(
-            jax.ShapeDtypeStruct((token_rows, model_width), jnp.bfloat16),
-            jax.ShapeDtypeStruct((token_rows, model_width), jnp.bfloat16),
+            by_step,
+            by_step,
             jax.ShapeDtypeStruct((steps, heads, token_rows), jnp.float32),
             jax.ShapeDtypeStruct((token_rows, model_width), jnp.float32),
             jax.ShapeDtypeStruct((token_rows, model_width), jnp.bfloat16),
@@ -1170,44 +1183,254 @@
             grid=(steps,),
             in_specs=[
                 whole(token_rows, model_width),
-                pl.BlockSpec(
-                    (1, groups, weight_rows, block), lambda step, *_: (step, 0, 0, 0)
-                ),
-                pl.BlockSpec((1, 1, block), lambda step, *_: (step, 0, 0)),
+                one(model_width, block),
+                one(1, block),
                 whole(*prompt_kv.shape),
                 whole(*answer_kv.shape),
-                pl.BlockSpec(
-                    (1, groups, weight_rows, block), lambda step, *_: (step, 0, 1, 0)
-                ),
+                one(model_width, block),
                 whole(token_rows, model_width),
                 whole(1, model_width),
                 whole(1, model_width),
                 whole(1, model_width),
             ],
             out_specs=(
-                pl.BlockSpec((token_rows, block), lambda step, *_: (0, step)),
-                pl.BlockSpec((token_rows, block), lambda step, *_: (0, step)),
-                pl.BlockSpec((1, heads, token_rows), lambda step, *_: (step, 0, 0)),
+                one(token_rows, block),
+                one(token_rows, block),
+                one(heads, token_rows),
                 whole(token_rows, model_width),
                 whole(token_rows, model_width),
             ),
         ),
         compiler_params=pltpu.CompilerParams(vmem_limit_bytes=VMEM_BYTES),
-        cost_estimate=pl.CostEstimate(
-            flops=steps * (4 * token_rows * model_width * block + 8 * scores * HEAD_WIDTH),
-            bytes_accessed=8 * steps * model_width * block,
-            transcendentals=steps * scores,
-        ),
         name="attention_forward",
     )(
         place,
         owning,
         normed,
-        packed,
+        query_blocks,
         query_offset.reshape(steps, 1, block),
         prompt_kv,
         answer_kv,
-        packed,
+        output_blocks,
+        states,
+        output_offset.reshape(1, -1),
+        gain.reshape(1, -1),
+        shift.reshape(1, -1),
+    )
+
+
+def bits_away(index):
+    here = lax.axis_index("tok")
+    core = (here + index) % 2
+    across = (here // 2 + index // 2) % 2
+    along = (here // 4 + index // 4) % 2
+    return along * 4 + across * 2 + core
+
+
+def gather_attention_kernel(
+    prompts,
+    answers,
+    heads,
+    prompt_rows,
+    owner_ref,
+    query_own_ref,
+    output_own_ref,
+    normed_ref,
+    bias_ref,
+    prompt_kv_ref,
+    answer_kv_ref,
+    states_ref,
+    offset_ref,
+    gain_ref,
+    shift_ref,
+    weights_ref,
+    queries_ref,
+    mixture_ref,
+    log_ref,
+    hidden_ref,
+    second_ref,
+    held,
+    send_sem,
+    recv_sem,
+    local_sem,
+    load_sem,
+):
+    here, on_x, on_y, on_chip, corner = block_of_eight()
+
+    def copy(index, source, target, device):
+        return remote(index, source, target, device, send_sem, recv_sem)
+
+    own_refs = (query_own_ref, output_own_ref)
+    to_x = [copy(0 + kind, own_refs[kind], weights_ref.at[here, kind], on_x) for kind in (0, 1)]
+    to_y = [copy(2 + kind, own_refs[kind], weights_ref.at[here, kind], on_y) for kind in (0, 1)]
+    to_chip = [
+        copy(4 + kind, own_refs[kind], weights_ref.at[here, kind], on_chip) for kind in (0, 1)
+    ]
+    keep = [
+        pltpu.make_async_copy(own_refs[kind], weights_ref.at[here, kind], local_sem.at[kind])
+        for kind in (0, 1)
+    ]
+    x_to_y = copy(6, weights_ref.at[on_x, 0], weights_ref.at[on_x, 0], on_y)
+    y_to_x = copy(7, weights_ref.at[on_y, 1], weights_ref.at[on_y, 1], on_x)
+    x_to_chip = copy(8, weights_ref.at[on_x], weights_ref.at[on_x], on_chip)
+    y_to_chip = copy(9, weights_ref.at[on_y], weights_ref.at[on_y], on_chip)
+    corner_to_chip = [
+        copy(10 + kind, weights_ref.at[corner, kind], weights_ref.at[corner, kind], on_chip)
+        for kind in (0, 1)
+    ]
+
+    greet((on_x, on_y, on_chip))
+    for each in (to_x[0], to_y[1], to_x[1], to_y[0], *to_chip, *keep):
+        each.start()
+    hidden_ref[...] = states_ref[...].astype(jnp.float32) + offset_ref[...]
+
+    @pl.loop(0, 8)
+    def _(turn):
+        block = bits_away(turn)
+
+        @pl.when(turn == 0)
+        def _():
+            for kind in (0, 1):
+                load = pltpu.make_async_copy(own_refs[kind], held.at[kind], load_sem.at[kind])
+                load.start()
+                load.wait()
+
+        @pl.when(turn == 1)
+        def _():
+            for each in to_chip:
+                each.wait_recv()
+
+        @pl.when(turn == 2)
+        def _():
+            to_x[0].wait_recv()
+            x_to_y.start()
+            to_y[1].wait_recv()
+            y_to_x.start()
+            to_x[1].wait_recv()
+            x_to_chip.start()
+            to_y[0].wait_recv()
+            y_to_chip.start()
+
+        @pl.when(turn == 3)
+        def _():
+            x_to_chip.wait_recv()
+
+        @pl.when(turn == 5)
+        def _():
+            y_to_chip.wait_recv()
+
+        @pl.when(turn == 6)
+        def _():
+            x_to_y.wait_recv()
+            corner_to_chip[0].start()
+            y_to_x.wait_recv()
+            corner_to_chip[1].start()
+
+        @pl.when(turn == 7)
+        def _():
+            for each in corner_to_chip:
+                each.wait_recv()
+
+        @pl.when(turn > 0)
+        def _():
+            for kind in (0, 1):
+                pltpu.make_async_copy(
+                    weights_ref.at[block, kind], held.at[kind], load_sem.at[kind]
+                ).start()
+            for kind in (0, 1):
+                pltpu.make_async_copy(
+                    weights_ref.at[block, kind], held.at[kind], load_sem.at[kind]
+                ).wait()
+
+        queries, mixture, logs = forward_block(
+            prompts,
+            answers,
+            heads,
+            here * prompt_rows,
+            owner_ref,
+            normed_ref,
+            held[0],
+            bias_ref[block],
+            prompt_kv_ref,
+            answer_kv_ref,
+        )
+        queries_ref[block] = queries
+        mixture_ref[block] = mixture
+        for place, rows, log_row in logs:
+            for head in range(heads):
+                log_ref[block, head : head + 1, place] = log_row[
+                    :, head * rows : (head + 1) * rows
+                ]
+        hidden_ref[...] += transposed_product(mixture, held[1])
+
+    scaled, _ = norm_stats(hidden_ref[...])
+    second_ref[...] = (scaled * gain_ref[...] + shift_ref[...]).astype(jnp.bfloat16)
+    for each in (*to_x, *to_y, *to_chip, x_to_y, y_to_x, x_to_chip, y_to_chip, *corner_to_chip):
+        each.wait_send()
+    for each in keep:
+        each.wait()
+
+
+def gather_attention(
+    owning,
+    query_own,
+    output_own,
+    normed,
+    query_offset,
+    prompt_kv,
+    answer_kv,
+    states,
+    output_offset,
+    gain,
+    shift,
+    prompts,
+    answers,
+    prompt_rows,
+    call_number,
+):
+    token_rows, model_width = normed.shape
+    block = query_own.shape[1]
+    heads = block // HEAD_WIDTH
+    inside = pl.BlockSpec(memory_space=pltpu.VMEM)
+    anywhere = pl.BlockSpec(memory_space=pl.ANY)
+    dma = pltpu.SemaphoreType.DMA
+    by_step = jax.ShapeDtypeStruct((8, token_rows, block), jnp.bfloat16)
+    return pl.pallas_call(
+        functools.partial(gather_attention_kernel, prompts, answers, heads, prompt_rows),
+        out_shape=(
+            jax.ShapeDtypeStruct((8, 2, model_width, block), jnp.bfloat16),
+            by_step,
+            by_step,
+            jax.ShapeDtypeStruct((8, heads, token_rows), jnp.float32),
+            jax.ShapeDtypeStruct((token_rows, model_width), jnp.float32),
+            jax.ShapeDtypeStruct((token_rows, model_width), jnp.bfloat16),
+        ),
+        in_specs=[pl.BlockSpec(memory_space=pltpu.SMEM), anywhere, anywhere] + [inside] * 8,
+        out_specs=(anywhere,) + (inside,) * 5,
+        scratch_shapes=[
+            pltpu.VMEM((2, model_width, block), jnp.bfloat16),
+            dma((12,)),
+            dma((12,)),
+            dma((2,)),
+            dma((2,)),
+        ],
+        compiler_params=pltpu.CompilerParams(
+            collective_id=call_number, has_side_effects=True, vmem_limit_bytes=VMEM_BYTES
+        ),
+        cost_estimate=pl.CostEstimate(
+            flops=64 * token_rows * model_width * block,
+            bytes_accessed=250 * 1000 * 1000,
+            transcendentals=0,
+        ),
+        name="gather_attention",
+    )(
+        owning,
+        query_own,
+        output_own,
+        normed,
+        query_offset.reshape(8, 1, block),
+        prompt_kv,
+        answer_kv,
         states,
         output_offset.reshape(1, -1),
         gain.reshape(1, -1),
@@ -1244,7 +1467,7 @@
     step = pl.program_id(0)
     width = HEAD_WIDTH
     length = prompt_kv_ref.shape[1]
-    block = queries_ref.shape[1]
+    block = queries_ref.shape[2]
 
     @pl.when(step == 0)
     def _():
@@ -1254,18 +1477,17 @@
         own_sums[...] = jnp.zeros_like(own_sums)
         grad_normed_ref[...] = jnp.zeros_like(grad_normed_ref)
 
-    query_block = query_ref[0].reshape(-1, block)
-    output_block = output_ref[0].reshape(-1, block)
-    weight_shape = query_ref.shape[1:]
-    weight_rows = weight_shape[1]
+    query_block, output_block = query_ref[0, 0], output_ref[0, 0]
+    weight_shape = (grad_weights_ref.shape[1], -1, block)
+    weight_rows = query_block.shape[0] // grad_weights_ref.shape[1]
     grad_weights_ref[0, :, weight_rows : 2 * weight_rows] = (
-        plain_product(branch_across[...], mixture_ref[...])
+        plain_product(branch_across[...], mixture_ref[0])
         .astype(jnp.bfloat16)
         .reshape(weight_shape)
     )
     grad_mixture = plain_product(branch_ref[...], output_block).astype(jnp.bfloat16)
-    queries = queries_ref[...]
-    mixture = mixture_ref[...]
+    queries = queries_ref[0]
+    mixture = mixture_ref[0]
 
     def backward(keys, values, stacked, grad_stacked, log_row, inner_row, allowed):
         scores = transposed_product(keys, stacked)
@@ -1352,8 +1574,8 @@
     place,
     owning,
     normed,
-    packed,
-    weight_rows,
+    weights,
+    groups,
     grad_rows,
     prompt_kv,
     answer_kv,
@@ -1365,11 +1587,14 @@
     answers,
 ):
     token_rows, model_width = normed.shape
-    steps, groups, _, block = packed.shape
+    steps, _, _, block = weights.shape
     heads = block // HEAD_WIDTH
     length = prompt_kv.shape[1]
     whole = lambda *shape: pl.BlockSpec(shape, lambda step, *_: (0,) * len(shape))
-    columns = lambda: pl.BlockSpec((token_rows, block), lambda step, *_: (0, step))
+    columns = lambda: pl.BlockSpec((1, token_rows, block), lambda step, *_: (step, 0, 0))
+    kind = lambda which: pl.BlockSpec(
+        (1, 1, model_width, block), lambda step, *_: (step, which, 0, 0)
+    )
     scores = heads * token_rows * length
     return pl.pallas_call(
         functools.partial(
@@ -1387,14 +1612,10 @@
             grid=(steps,),
             in_specs=[
                 whole(token_rows, model_width),
-                pl.BlockSpec(
-                    (1, groups, weight_rows, block), lambda step, *_: (step, 0, 0, 0)
-                ),
+                kind(0),
                 whole(*prompt_kv.shape),
                 whole(*answer_kv.shape),
-                pl.BlockSpec(
-                    (1, groups, weight_rows, block), lambda step, *_: (step, 0, 1, 0)
-                ),
+                kind(1),
                 whole(token_rows, model_width),
                 columns(),
                 columns(),
@@ -1427,10 +1648,10 @@
         place,
         owning,
         normed,
-        packed,
+        weights,
         prompt_kv,
         answer_kv,
-        packed,
+        weights,
         branch,
         queries,
         mixture,
@@ -1497,6 +1718,8 @@
     up_cols = lax.all_gather(up_weight, "grp", axis=0, tiled=True)
     down_cols = lax.all_gather(down_weight, "grp", axis=0, tiled=True)
 
+    query_own = lax.all_gather(query_weight, "grp", axis=0, tiled=True)
+    output_own = lax.all_gather(output_weight, "grp", axis=0, tiled=True)
     count_parts = jnp.stack([own_count // 128, own_count % 128]).astype(jnp.bfloat16)
     smalls = jnp.concatenate(
         [
@@ -1512,22 +1735,16 @@
         ]
     )
     smalls = jnp.pad(smalls, (0, SMALL_ROWS * block - smalls.shape[0])).reshape(SMALL_ROWS, block)
-    pack = jnp.concatenate(
-        [query_weight, output_weight, keyval_weight.reshape(-1, block), smalls], axis=0
-    )
-    pack_rows = pack.shape[0]
-    packed = lax.all_gather(pack, "grp", axis=0, tiled=True)
-    packed = tok_gather(packed, 0, kernels).reshape(token_devices, groups, pack_rows, block)
+    pack = jnp.concatenate([keyval_weight.reshape(-1, block), smalls], axis=0)
+    packed = spread(pack, groups, 0, kernels)
+    keyval_pack = pack.shape[0] - SMALL_ROWS
     keyval_start = 2 * weight_rows
-    keyval_end = pack_rows - SMALL_ROWS
     keyval_full = jnp.swapaxes(
-        packed[:, :, keyval_start:keyval_end].reshape(
-            token_devices, groups, keyval_rows, keyval_width
-        ),
+        packed[:, :, :keyval_pack].reshape(token_devices, groups, keyval_rows, keyval_width),
         0,
         1,
     ).reshape(model_width, keyval_width)
-    small_full = packed[:, :, keyval_end:].reshape(token_devices, groups, SMALL_ROWS * block)
+    small_full = packed[:, :, keyval_pack:].reshape(token_devices, groups, SMALL_ROWS * block)
     small_full = jnp.swapaxes(small_full.astype(jnp.float32), 0, 1)
 
     def vector(start, size):
@@ -1555,22 +1772,42 @@
     owning = answer_prompt - group_index * prompt_count
     owning = lax.dynamic_slice_in_dim(owning, token_index * answer_count, answer_count)
     place = jnp.reshape(token_index * prompt_rows, (1,)).astype(jnp.int32)
-    queries, mixture, log_total, hidden, normed_two = attention_forward(
-        place,
-        owning,
-        normed_one,
-        packed,
-        weight_rows,
-        query_offset,
-        prompt_kv,
-        answer_kv,
-        states,
-        output_offset,
-        gain_two,
-        shift_two,
-        prompt_count,
-        answer_count,
-    )
+    if kernels:
+        weights, queries, mixture, log_total, hidden, normed_two = gather_attention(
+            owning,
+            query_own,
+            output_own,
+            normed_one,
+            query_offset,
+            prompt_kv,
+            answer_kv,
+            states,
+            output_offset,
+            gain_two,
+            shift_two,
+            prompt_count,
+            answer_count,
+            prompt_rows,
+            8,
+        )
+    else:
+        weights = lax.all_gather(jnp.stack([query_own, output_own]), "tok", axis=0)
+        queries, mixture, log_total, hidden, normed_two = attention_forward(
+            place,
+            owning,
+            normed_one,
+            weights[:, 0],
+            weights[:, 1],
+            query_offset,
+            prompt_kv,
+            answer_kv,
+            states,
+            output_offset,
+            gain_two,
+            shift_two,
+            prompt_count,
+            answer_count,
+        )
 
     if kernels:
         group_two, activated, slope = gather_and_up(normed_two, up_cols, up_here, 2)
@@ -1622,14 +1859,14 @@
     grad_branch_one = grad_hidden.astype(jnp.bfloat16)
     grad_output_offset = column_sums(grad_branch_one)
 
-    grad_rows = keyval_end
+    grad_rows = keyval_start + keyval_pack
     grad_weights, grad_normed_one, grad_prompt_kv, grad_answer_kv, grad_query_offset = (
         attention_backward(
             place,
             owning,
             normed_one,
-            packed,
-            weight_rows,
+            weights,
+            groups,
             grad_rows,
             prompt_kv,
             answer_kv,

time: 751 us -> 706 us (0.940)
  the two profiles are of different devices: /device:TPU:0 before, /device:TPU:15 now
where the time goes in v4:
time: 706 us; the launch traced here: 701 us
  Pallas kernels  599 us (85%)
  other arithmetic  36.6 us (5%)
  local copies, waits for them, and re-layouts  35.8 us (5%)
  between operations  19.4 us (3%)
    pallas_call x2, Pallas kernels, product_and_reduce(): pl.pallas_call(functools.partial(product_reduce_kernel, with_grad), out_s...  131 us
    pallas_call x1, Pallas kernels, final_reduce(): pl.pallas_call(functools.partial(final_reduce_kernel, groups), out_shape=...  119 us
    pallas_call x1, Pallas kernels, gather_attention(): pl.pallas_call(functools.partial(gather_attention_kernel, prompts, answer...  87.4 us
    pallas_call x1, Pallas kernels, gather_and_grad(): pl.pallas_call(grad_kernel, out_shape=(jax.ShapeDtypeStruct((8, token_row...  83.3 us
    pallas_call x1, Pallas kernels, gather_and_up(): pl.pallas_call(up_kernel, out_shape=(jax.ShapeDtypeStruct((8, token_rows,...  66.9 us
    pallas_call x1, Pallas kernels, attention_backward(): pl.pallas_call(functools.partial(attention_backward_kernel, prompts, answ...  47.7 us
    pallas_call x1, Pallas kernels, spread(): pl.pallas_call(functools.partial(spread_kernel, groups), out_shape=jax.Sh...  30 us
    pallas_call x1, Pallas kernels, tok_reduce_small(): pl.pallas_call(functools.partial(small_reduce_kernel, count), out_shape=j...  19.1 us
  transfers between devices with their start and end apart: 6, of which 0 were waited for; matrix products, arithmetic and copies ran while one was open for 10% of the time, Pallas kernels for 55%

profile of v4, /device:TPU:15, one launch (start us, length us, event | category | flops | bytes accessed | tf_op | source)
XLA Modules:
  0.0 700.7 jit_solution(5044068527533863184)
XLA Ops:
  10.0 1.3 reduce_sum.181
  11.3 1.3 reduce_sum.182
  14.0 5.4 concatenate.43
  19.4 1.4 pad_maximum_fusion.4.own_ref
  20.8 30.0 %spread.1 = bf16[8,4,80,256]{3,2,1,0:T(8,128)(2,1)} custom-call(bf16[80,256]{1,0:T(8,128)(2,1)} %pad_maximum_fusion.4.own_ref), custom_call_target="tpu_custom_call" | custom-call | tf_op jit(solution)/shard_map/spread/pallas_call | solution.py:124
  50.8 1.9 slice_convert_fusion
  52.8 1.4 reshape.232
  59.2 15.0 %tok_gather_small.1.prompt_kv_ref = bf16[2,1024,256]{2,1,0:T(8,128)(2,1)} custom-call(bf16[2,128,256]{2,1,0:T(8,128)(2,1)} %bitcast.69), custom_call_target="tpu_custom_call" | custom-call | tf_op jit(solution)/shard_map/tok_gather_small/pallas_call | solution.py:678
  79.2 1.5 slice_reduce_fusion
  83.3 87.4 %gather_attention.1 = (bf16[8,2,2048,256]{3,2,1,0:T(8,128)(2,1)}, bf16[8,384,256]{2,1,0:T(8,128)(2,1)}, bf16[8,384,256]{2,1,0:T(8,128)(2,1)}, f32[8,2,384]{2,1,0...) custom-call(s32[1]{0:T(128)} %dynamic_slice.6.owner_ref, ...), custom_call_target="tpu_custom_call" | custom-call | flops 12884901888 | bytes 250000000 | tf_op jit(solution)/shard_map/gather_attention/pallas_call | solution.py:1398
  170.7 2.1 reduce_sum.186
  172.9 66.9 %gather_and_up.1 = (bf16[8,384,2048]{2,1,0:T(8,128)(2,1)}, bf16[8,384,1024]{2,1,0:T(8,128)(2,1)}, bf16[8,384,1024]{2,1,0:T(8,128)(2,1)}) custom-call(bf16[384,2048]{1,0:T(8,128)(2,1)} %get-tuple-element.41.own_ref, bf16[2048,1024]{1,0:T(8,128)(2,1)} %all-gather.9.cloned.1.call-done.up_hbm.weight_hbm, f32[1,1024]{1,0:T(1,128)} %bitcast.78), custom_call_target="tpu_custom_call" | custom-call | flops 12884901888 | bytes 150000000 | tf_op jit(solution)/shard_map/gather_and_up/pallas_call | solution.py:282
  239.9 66.1 %product_and_reduce.2 = f32[384,2048]{1,0:T(8,128)} custom-call(bf16[8,384,1024]{2,1,0:T(8,128)(2,1)} %get-tuple-element.42.narrow_ref.active_ref, bf16[2048,1024]{1,0:T(8,128)(2,1)} %all-gather.11.cloned.1.call-done.weight_hbm.down_hbm), custom_call_target="tpu_custom_call" | custom-call | flops 12884901888 | bytes 150000000 | tf_op jit(solution)/shard_map/product_and_reduce/pallas_call | solution.py:623
  306.0 5.0 fusion.15
  311.0 1.6 copy-done.1
  312.6 1.5 convert_reduce_fusion.1
  314.1 83.3 %gather_and_grad.1 = (bf16[8,384,2048]{2,1,0:T(8,128)(2,1)}, bf16[8,384,1024]{2,1,0:T(8,128)(2,1)}, bf16[2048,1024]{1,0:T(8,128)(2,1)}, f32[1,1024]{1,0:T(1,128)}) custom-call(bf16[384,2048]{1,0:T(8,128)(2,1)} %get-tuple-element.74.own_ref, bf16[2048,1024]{1,0:T(8,128)(2,1)} %all-gather.11.cloned.1.call-done.weight_hbm.down_hbm, ...), custom_call_target="tpu_custom_call" | custom-call | flops 25769803776 | bytes 150000000 | tf_op jit(solution)/shard_map/gather_and_grad/pallas_call | solution.py:401
  397.4 64.4 %product_and_reduce.3 = (f32[384,2048]{1,0:T(8,128)}, bf16[2048,1024]{1,0:T(8,128)(2,1)}) custom-call(bf16[8,384,1024]{2,1,0:T(8,128)(2,1)} %get-tuple-element.44.narrow_ref, bf16[2048,1024]{1,0:T(8,128)(2,1)} %all-gather.9.cloned.1.call-done.up_hbm.weight_hbm, bf16[8,384,2048]{2,1,0:T(8,128)(2,1)} %get-tuple-element.45.refs_0_), custom_call_target="tpu_custom_call" | custom-call | flops 25769803776 | bytes 150000000 | tf_op jit(solution)/shard_map/product_and_reduce/pallas_call | solution.py:623
  462.5 3.2 multiply_reduce_fusion
  466.3 3.1 convert_reduce_fusion.2
  469.5 47.7 %attention_backward.1 = (bf16[8,4,1088,256]{3,2,1,0:T(8,128)(2,1)}, f32[384,2048]{1,0:T(8,128)}, bf16[2,1024,256]{2,1,0:T(8,128)(2,1)}, f32[128,256]{1,0:T(8,128)}, f32[8,1,256]{2,1,0:T(1,128)}) custom-call(s32[1]{0:T(128)} %bitcast.15.place_ref, s32[1]{0:T(128)} %dynamic_slice.6.owner_ref, bf16[384,2048]{1,0:T(8,128)(2,1)} %copy-done.11, ...), custom_call_target="tpu_custom_call" | custom-call | flops 28991029248 | bytes 67108864 | tf_op jit(solution)/shard_map/attention_backward/pallas_call | solution.py:1599
  517.1 19.1 %tok_reduce_small.1 = f32[2,128,256]{2,1,0:T(8,128)} custom-call(bf16[2,1024,256]{2,1,0:T(8,128)(2,1)} %get-tuple-element.52.part_ref), custom_call_target="tpu_custom_call" | custom-call | tf_op jit(solution)/shard_map/tok_reduce_small/pallas_call | solution.py:729
  538.2 5.7 fusion.13
  552.6 118.5 %final_reduce.1 = (f32[1088,256]{1,0:T(8,128)}, f32[8,128]{1,0:T(8,128)}) custom-call(bf16[8,4352,256]{2,1,0:T(8,128)(2,1)} %bitcast.49, f32[8,32,128]{2,1,0:T(8,128)} %reshape.230.small_ref), custom_call_target="tpu_custom_call" | custom-call | tf_op jit(solution)/shard_map/final_reduce/pallas_call | solution.py:972
  671.2 1.3 slice.130
  672.4 1.3 slice.128
  673.7 1.3 slice.123
  675.0 1.5 slice.122
  676.5 3.2 fusion.12
  685.0 1.9 slice_bitcast_fusion.2
  686.9 2.8 convert_element_type.77
  689.7 2.8 convert_element_type.78
  (136 shorter events, 30.3 us)
Async XLA Ops:
  7.2 76.1 %all-gather.5.cloned.1.call-start = ((), (), s32[]{:S(2)}) async-start(), calls=%async_computation.2 | async-start | bytes 1310720 | tf_op jit(solution)/shard_map/all_gather | solution.py:1721
  7.9 75.4 %all-gather.7.cloned.1.call-start = ((), (), s32[]{:S(2)}) async-start(), calls=%async_computation.3 | async-start | bytes 1310720 | tf_op jit(solution)/shard_map/all_gather | solution.py:1722
  8.7 164.2 %all-gather.9.cloned.1.call-start = ((), (), s32[]{:S(2)}) async-start(), calls=%async_computation.4 | async-start | bytes 5242880 | tf_op jit(solution)/shard_map/all_gather | solution.py:1718
  9.4 230.4 %all-gather.11.cloned.1.call-start = ((), (), s32[]{:S(2)}) async-start(), calls=%async_computation.5 | async-start | bytes 5242880 | tf_op jit(solution)/shard_map/all_gather | solution.py:1719
  10.0 676.9 %reduce-scatter.3.cloned.1.call-start = ((), (), s32[]{:S(2)}) async-start(), calls=%async_computation.6 | async-start | bytes 5242880 | tf_op jit(solution)/shard_map/reduce_scatter | solution.py:1852
  50.8 4.7 copy-start.10
  52.7 3.0 copy-start.3
  52.8 3.0 copy-start.5
  55.7 1.6 copy-start.15
  57.3 26.0 %copy-start.11 = (bf16[384,2048]{1,0:T(8,128)(2,1)}, bf16[384,2048]{1,0:T(8,128)(2,1)S(1)}, u32[]{:S(2)}) copy-start(bf16[384,2048]{1,0:T(8,128)(2,1)S(1)} %fusion.7.normed_ref) | copy-start | bytes 4718596
  57.3 20.7 %copy-start.27 = (s32[8]{0:T(128)S(1)}, s32[8]{0:T(128)}, u32[]{:S(2)}) copy-start(s32[8]{0:T(128)} %param.23) | copy-start | bytes 100
  57.3 24.7 %copy-start.19 = (s32[2,128]{1,0:T(2,128)S(1)}, s32[2,128]{1,0:T(2,128)}, u32[]{:S(2)}) copy-start(s32[2,128]{1,0:T(2,128)} %param.26) | copy-start | bytes 3076
  57.3 24.7 %copy-start.25 = (s32[1,128]{1,0:T(1,128)S(1)}, s32[1,128]{1,0:T(1,128)}, u32[]{:S(2)}) copy-start(s32[1,128]{1,0:T(1,128)} %param.27) | copy-start | bytes 1540
  239.8 66.1 %copy-start = (f32[384,2048]{1,0:T(8,128)S(1)}, f32[384,2048]{1,0:T(8,128)}, u32[]{:S(2)}) copy-start(f32[384,2048]{1,0:T(8,128)} %get-tuple-element.40) | copy-start | bytes 9437188
  239.8 66.1 %copy-start.14 = (bf16[2,128,2048]{2,1,0:T(8,128)(2,1)S(1)}, bf16[2,128,2048]{2,1,0:T(8,128)(2,1)}, u32[]{:S(2)}) copy-start(bf16[2,128,2048]{2,1,0:T(8,128)(2,1)} %param.24) | copy-start | bytes 3145732
  239.8 66.1 %copy-start.18 = (bf16[1,128,2048]{2,1,0:T(8,128)(2,1)S(1)}, bf16[1,128,2048]{2,1,0:T(8,128)(2,1)}, u32[]{:S(2)}) copy-start(bf16[1,128,2048]{2,1,0:T(8,128)(2,1)} %param.25) | copy-start | bytes 1572868
  311.0 1.7 copy-start.1
  461.9 227.8 %reduce-scatter.5.cloned.1.call-start = ((), (), s32[]{:S(2)}) async-start(), calls=%async_computation.7 | async-start | bytes 5242880 | tf_op jit(solution)/shard_map/reduce_scatter | solution.py:1851
  462.5 3.3 copy-start.2
  462.5 3.8 copy-start.7
  469.5 68.7 %copy-start.4 = (bf16[2,128,2048]{2,1,0:T(8,128)(2,1)S(1)}, bf16[2,128,2048]{2,1,0:T(8,128)(2,1)}, u32[]{:S(2)}) copy-start(bf16[2,128,2048]{2,1,0:T(8,128)(2,1)} %param.21) | copy-start | bytes 3145732
  469.5 68.7 %copy-start.6 = (bf16[1,128,2048]{2,1,0:T(8,128)(2,1)S(1)}, bf16[1,128,2048]{2,1,0:T(8,128)(2,1)}, u32[]{:S(2)}) copy-start(bf16[1,128,2048]{2,1,0:T(8,128)(2,1)} %param.22) | copy-start | bytes 1572868
  469.5 68.7 %copy-start.16 = (bf16[4,8,64,256]{3,2,1,0:T(8,128)(2,1)S(1)}, bf16[4,8,64,256]{3,2,1,0:T(8,128)(2,1)}, u32[]{:S(2)}) copy-start(bf16[4,8,64,256]{3,2,1,0:T(8,128)(2,1)} %copy-done.15) | copy-start | bytes 3145732
  538.2 6.5 copy-start.20
  538.2 9.2 %copy-start.22 = (f32[1,1024]{1,0:T(1,128)S(1)}, f32[1,1024]{1,0:T(1,128)}, u32[]{:S(2)}) copy-start(f32[1,1024]{1,0:T(1,128)} %get-tuple-element.56) | copy-start | bytes 12292
  538.2 12.6 %copy-start.12 = (bf16[384,2048]{1,0:T(8,128)(2,1)S(1)}, bf16[384,2048]{1,0:T(8,128)(2,1)}, u32[]{:S(2)}) copy-start(bf16[384,2048]{1,0:T(8,128)(2,1)} %copy-done.11) | copy-start | bytes 4718596
  552.6 123.9 %copy-start.24 = (f32[384]{0:T(512)S(1)}, f32[384]{0:T(512)}, u32[]{:S(2)}) copy-start(f32[384]{0:T(512)} %get-tuple-element.64) | copy-start | bytes 4612
  552.6 123.9 %copy-start.23 = (f32[384]{0:T(512)S(1)}, f32[384]{0:T(512)}, u32[]{:S(2)}) copy-start(f32[384]{0:T(512)} %get-tuple-element.65) | copy-start | bytes 4612
  552.6 123.9 %copy-start.8 = (f32[384,2048]{1,0:T(8,128)S(1)}, f32[384,2048]{1,0:T(8,128)}, u32[]{:S(2)}) copy-start(f32[384,2048]{1,0:T(8,128)} %get-tuple-element.77) | copy-start | bytes 9437188
  676.5 4.3 copy-start.9
  679.8 2.8 copy-start.21
  679.8 3.4 copy-start.13
  (2 other events, 2.3 us)
Sparse Core Ops, SparseCore 0:
  9.6 31.3 all-gather.4
  42.6 28.2 all-gather.6
  72.4 78.1 all-gather.8
  152.1 79.2 all-gather.10
  462.0 79.9 reduce-scatter.2
  544.2 111.1 reduce-scatter.4

commit v5 on v4

--- a/solution.py
+++ b/solution.py
@@ -153,62 +153,96 @@
     return pl.ds(pl.multiple_of(index * size, size), size)
 
 
-CHUNK = 256
+CHUNK = 512
 LINEAR = 0.7978845608
 CUBIC = 0.044715
 
 
 def gather_beside(own_ref, out_ref, send_sem, recv_sem, local_sem, use):
-    half = own_ref.shape[0] // 2
+    rows = own_ref.shape[0]
+    half, quarter = rows // 2, rows // 4
     here, on_x, on_y, on_chip, corner = block_of_eight()
     shift = on_chip - here
-    first, second = pl.ds(0, half), pl.ds(half, half)
-
-    def copy(index, source, target, device):
-        return remote(index, source, target, device, send_sem, recv_sem)
+    counter = iter(range(GATHER_COPIES))
+
+    def copy(source, block, start, count, device):
+        place = pl.ds(start, count)
+        return remote(
+            next(counter),
+            source.at[place] if source is own_ref else source.at[block, place],
+            out_ref.at[block, place],
+            device,
+            send_sem,
+            recv_sem,
+        )
 
     greet((on_x, on_y, on_chip))
     own = pltpu.make_async_copy(own_ref, out_ref.at[here], local_sem)
-    copies = [
-        copy(0, own_ref, out_ref.at[here], on_x),
-        copy(1, own_ref, out_ref.at[here], on_y),
-        copy(2, own_ref, out_ref.at[here], on_chip),
-        copy(3, out_ref.at[on_x, first], out_ref.at[on_x, first], on_y),
-        copy(4, out_ref.at[on_x], out_ref.at[on_x], on_chip),
-        copy(5, out_ref.at[on_y, second], out_ref.at[on_y, second], on_x),
-        copy(6, out_ref.at[on_y], out_ref.at[on_y], on_chip),
-        copy(7, out_ref.at[corner, first], out_ref.at[corner, first], on_chip),
-        copy(8, out_ref.at[corner, second], out_ref.at[corner, second], on_chip),
-    ]
-    for index in range(3):
-        copies[index].start()
-    own.start()
-    use(0, here)
-    copies[2].wait_recv()
-    use(1, on_chip)
-    copies[0].wait_recv()
-    copies[3].start()
-    copies[4].start()
-    copies[1].wait_recv()
-    copies[5].start()
-    copies[6].start()
-    use(2, on_x)
-    use(3, on_y)
-    copies[4].wait_recv()
-    use(4, on_x + shift)
-    copies[6].wait_recv()
-    use(5, on_y + shift)
-    copies[3].wait_recv()
-    copies[7].start()
-    copies[5].wait_recv()
-    copies[8].start()
-    use(6, corner)
-    copies[7].wait_recv()
-    copies[8].wait_recv()
-    use(7, corner + shift)
+    x_low = copy(own_ref, here, 0, half, on_x)
+    y_high = copy(own_ref, here, half, half, on_y)
+    x_high = copy(own_ref, here, half, half, on_x)
+    y_low = copy(own_ref, here, 0, half, on_y)
+    to_chip = copy(own_ref, here, 0, rows, on_chip)
+    to_y = [copy(out_ref, on_x, turn * quarter, quarter, on_y) for turn in (0, 1)]
+    to_x = [copy(out_ref, on_y, half + turn * quarter, quarter, on_x) for turn in (0, 1)]
+    chip_x = [copy(out_ref, on_x, turn * half, half, on_chip) for turn in (0, 1)]
+    chip_y = [copy(out_ref, on_y, turn * half, half, on_chip) for turn in (0, 1)]
+    chip_corner = [copy(out_ref, corner, turn * quarter, quarter, on_chip) for turn in range(4)]
+    for each in (x_low, y_high, x_high, y_low, to_chip, own):
+        each.start()
+    use(0, [(here, 0, rows)])
+    to_chip.wait_recv()
+    use(1, [(on_chip, 0, rows)])
+    x_low.wait_recv()
+    for each in (*to_y, chip_x[0]):
+        each.start()
+    y_high.wait_recv()
+    for each in (*to_x, chip_y[1]):
+        each.start()
+    use(2, [(on_x, 0, half), (on_y, half, half)])
+    chip_x[0].wait_recv()
+    chip_y[1].wait_recv()
+    use(3, [(on_x + shift, 0, half), (on_y + shift, half, half)])
+    x_high.wait_recv()
+    chip_x[1].start()
+    y_low.wait_recv()
+    chip_y[0].start()
+    use(4, [(on_x, half, half), (on_y, 0, half)])
+    chip_x[1].wait_recv()
+    chip_y[0].wait_recv()
+    use(5, [(on_x + shift, half, half), (on_y + shift, 0, half)])
+    for turn in (0, 1):
+        to_y[turn].wait_recv()
+        chip_corner[turn].start()
+        to_x[turn].wait_recv()
+        chip_corner[2 + turn].start()
+        chip_corner[turn].wait_recv()
+        chip_corner[2 + turn].wait_recv()
+        use(
+            6 + turn,
+            [
+                (block, start + turn * quarter, quarter)
+                for block in (corner, corner + shift)
+                for start in (0, half)
+            ],
+        )
     own.wait()
-    for each in copies:
+    for each in (x_low, y_high, x_high, y_low, to_chip, *to_y, *to_x, *chip_x, *chip_y, *chip_corner):
         each.wait_send()
+
+
+GATHER_COPIES = 17
+
+
+def moves(outside, inside, pieces, semaphores, outward):
+    done, copies = 0, []
+    for index, (block, start, count) in enumerate(pieces):
+        away = outside.at[block, pl.ds(start, count)]
+        near = inside.at[pl.ds(done, count)]
+        pair = (near, away) if outward else (away, near)
+        copies.append(pltpu.make_async_copy(*pair, semaphores.at[index]))
+        done += count
+    return copies
 
 
 def up_kernel(
@@ -233,17 +267,20 @@
     weights.start()
     stores = {}
 
-    def use(place, block):
+    def use(place, pieces):
         slot = place % 2
-        load = pltpu.make_async_copy(
-            rows_ref.at[block] if place else own_ref, rows, row_sem
-        )
-        load.start()
+        if place:
+            loads = moves(rows_ref, rows, pieces, row_sem, False)
+        else:
+            loads = [pltpu.make_async_copy(own_ref, rows, row_sem.at[0])]
+        for each in loads:
+            each.start()
         if place == 0:
             weights.wait()
         for each in stores.pop(slot, ()):
             each.wait()
-        load.wait()
+        for each in loads:
+            each.wait()
 
         @pl.loop(0, up.shape[1] // CHUNK)
         def _(turn):
@@ -260,10 +297,9 @@
                 * (LINEAR + (3.0 * LINEAR * CUBIC) * square)
             ).astype(jnp.bfloat16)
 
-        stores[slot] = (
-            pltpu.make_async_copy(active.at[slot], active_ref.at[block], store_sem.at[slot, 0]),
-            pltpu.make_async_copy(slope.at[slot], slope_ref.at[block], store_sem.at[slot, 1]),
-        )
+        stores[slot] = moves(
+            active_ref, active.at[slot], pieces, store_sem.at[slot, 0], True
+        ) + moves(slope_ref, slope.at[slot], pieces, store_sem.at[slot, 1], True)
         for each in stores[slot]:
             each.start()
 
@@ -293,12 +329,12 @@
             pltpu.VMEM((token_rows, model_width), jnp.bfloat16),
             pltpu.VMEM((2, token_rows, width), jnp.bfloat16),
             pltpu.VMEM((2, token_rows, width), jnp.bfloat16),
-            dma((9,)),
-            dma((9,)),
+            dma((GATHER_COPIES,)),
+            dma((GATHER_COPIES,)),
             dma,
             dma,
-            dma,
-            dma((2, 2)),
+            dma((4,)),
+            dma((2, 2, 4)),
         ],
         compiler_params=pltpu.CompilerParams(
             collective_id=call_number, has_side_effects=True, vmem_limit_bytes=VMEM_BYTES
@@ -323,7 +359,6 @@
     bias_ref,
     down,
     rows,
-    across,
     active,
     slope,
     grads,
@@ -341,26 +376,22 @@
     weights.start()
     stores = {}
 
-    def use(place, block):
+    def use(place, pieces):
         slot = place % 2
-        load = pltpu.make_async_copy(
-            rows_ref.at[block] if place else own_ref, rows, row_sem
-        )
-        load.start()
-        loads = (
-            pltpu.make_async_copy(active_ref.at[block], active, load_sem.at[0]),
-            pltpu.make_async_copy(slope_ref.at[block], slope, load_sem.at[1]),
-        )
+        if place:
+            loads = moves(rows_ref, rows, pieces, row_sem, False)
+        else:
+            loads = [pltpu.make_async_copy(own_ref, rows, row_sem.at[0])]
+        loads += moves(active_ref, active, pieces, load_sem.at[0], False)
+        loads += moves(slope_ref, slope, pieces, load_sem.at[1], False)
         for each in loads:
             each.start()
         if place == 0:
             weights.wait()
-        if slot in stores:
-            stores.pop(slot).wait()
-        load.wait()
+        for each in stores.pop(slot, ()):
+            each.wait()
         for each in loads:
             each.wait()
-        across[...] = jnp.transpose(rows[...])
 
         @pl.loop(0, down.shape[1] // CHUNK)
         def _(turn):
@@ -369,7 +400,7 @@
             value = value.astype(jnp.bfloat16)
             grads[slot, :, at] = value
             total = jnp.sum(value.astype(jnp.float32), axis=0, keepdims=True)
-            weight = plain_product(across[...], active[:, at])
+            weight = weight_product(rows[...], active[:, at])
             if place == 0:
                 bias_ref[:, at] = total
                 sums[:, at] = weight
@@ -380,16 +411,16 @@
                 bias_ref[:, at] += total
                 narrow[:, at] = (sums[:, at] + weight).astype(jnp.bfloat16)
 
-        stores[slot] = pltpu.make_async_copy(
-            grads.at[slot], grad_ref.at[block], store_sem.at[slot]
-        )
-        stores[slot].start()
+        stores[slot] = moves(grad_ref, grads.at[slot], pieces, store_sem.at[slot], True)
+        for each in stores[slot]:
+            each.start()
 
     gather_beside(own_ref, rows_ref, send_sem, recv_sem, local_sem, use)
     last = pltpu.make_async_copy(narrow, weight_ref, weight_sem)
     last.start()
     for slot in (0, 1):
-        stores[slot].wait()
+        for each in stores[slot]:
+            each.wait()
     last.wait()
 
 
@@ -411,19 +442,18 @@
         scratch_shapes=[
             pltpu.VMEM(down_cols.shape, jnp.bfloat16),
             pltpu.VMEM((token_rows, model_width), jnp.bfloat16),
-            pltpu.VMEM((model_width, token_rows), jnp.bfloat16),
             pltpu.VMEM((token_rows, width), jnp.bfloat16),
             pltpu.VMEM((token_rows, width), jnp.bfloat16),
             pltpu.VMEM((2, token_rows, width), jnp.bfloat16),
             pltpu.VMEM((model_width, width), jnp.float32),
             pltpu.VMEM((model_width, width), jnp.bfloat16),
-            dma((9,)),
-            dma((9,)),
+            dma((GATHER_COPIES,)),
+            dma((GATHER_COPIES,)),
             dma,
             dma,
-            dma,
-            dma((2,)),
-            dma((2,)),
+            dma((4,)),
+            dma((2, 4)),
+            dma((2, 4)),
         ],
         compiler_params=pltpu.CompilerParams(
             collective_id=call_number, has_side_effects=True, vmem_limit_bytes=VMEM_BYTES
@@ -688,325 +718,6 @@
         compiler_params=pltpu.CompilerParams(collective_id=call_number, has_side_effects=True),
         name="tok_gather_small",
     )(own)
-
-
-def small_reduce_kernel(count, part_ref, out_ref, come, send_sem, recv_sem):
-    here, peers = peers_of(count)
-    rows = come.shape[2]
-
-    def place(device):
-        return pl.ds(pl.multiple_of(device * rows, rows), rows)
-
-    greet(peers)
-    copies = [
-        pltpu.make_async_remote_copy(
-            src_ref=part_ref.at[:, place(peers[index]), :],
-            dst_ref=come.at[index],
-            send_sem=send_sem.at[index],
-            recv_sem=recv_sem.at[index],
-            device_id={"tok": peers[index]},
-            device_id_type=MESH,
-        )
-        for index in range(count - 1)
-    ]
-    for each in copies:
-        each.start()
-    total = part_ref[:, place(here), :].astype(jnp.float32)
-    for index in range(count - 1):
-        copies[index].wait_recv()
-        total = total + come[index].astype(jnp.float32)
-    out_ref[...] = total.astype(out_ref.dtype)
-    for each in copies:
-        each.wait_send()
-
-
-def tok_reduce_small(parts, call_number, kernels):
-    if not kernels:
-        return lax.psum_scatter(parts, "tok", scatter_dimension=1, tiled=True).astype(jnp.float32)
-    count = 8
-    prompts, rows, columns = parts.shape
-    rows = rows // count
-    return pl.pallas_call(
-        functools.partial(small_reduce_kernel, count),
-        out_shape=jax.ShapeDtypeStruct((prompts, rows, columns), jnp.float32),
-        in_specs=[pl.BlockSpec(memory_space=pltpu.VMEM)],
-        out_specs=pl.BlockSpec(memory_space=pltpu.VMEM),
-        scratch_shapes=[
-            pltpu.VMEM((count - 1, prompts, rows, columns), parts.dtype),
-            pltpu.SemaphoreType.DMA((count - 1,)),
-            pltpu.SemaphoreType.DMA((count - 1,)),
-        ],
-        compiler_params=pltpu.CompilerParams(
-            collective_id=call_number, has_side_effects=True, vmem_limit_bytes=VMEM_BYTES
-        ),
-        name="tok_reduce_small",
-    )(parts)
-
-
-def final_reduce_kernel(
-    groups,
-    part_ref,
-    small_ref,
-    out_ref,
-    small_out_ref,
-    mine,
-    theirs,
-    relayed,
-    final,
-    come,
-    small_come,
-    small_total,
-    small_across,
-    send_sem,
-    recv_sem,
-    load_sem,
-    across_send,
-    across_recv,
-    small_send,
-    small_recv,
-    small_across_send,
-    small_across_recv,
-):
-    rows = part_ref.shape[1] // groups
-    half = rows // 2
-    small_rows = small_ref.shape[1] // groups
-    here, on_x, on_y, on_chip, corner = block_of_eight()
-    group = lax.axis_index("grp")
-    shift = on_chip - here
-    _, peers = peers_of(8)
-    other_groups = [(group + turn) % groups for turn in range(1, groups)]
-    step = 16
-
-    greet_all(peers, other_groups)
-
-    def copy(chunk, index, source, target, device):
-        return pltpu.make_async_remote_copy(
-            src_ref=source,
-            dst_ref=target,
-            send_sem=send_sem.at[chunk, index],
-            recv_sem=recv_sem.at[chunk, index],
-            device_id={"tok": device},
-            device_id_type=MESH,
-        )
-
-    def add_into(target, other, start, count):
-        @pl.loop(0, count // step)
-        def _(turn):
-            at = pl.ds(pl.multiple_of(start + turn * step, step), step)
-            from_here = pl.ds(pl.multiple_of(turn * step, step), step)
-            total = target[at, :].astype(jnp.float32) + other[from_here, :].astype(jnp.float32)
-            target[at, :] = total.astype(target.dtype)
-
-    places = (corner, on_x, on_y, here)
-    first, second = pl.ds(0, half), pl.ds(half, half)
-    to_chip, loads, others = [], [], []
-    for chunk in range(groups):
-        owner = (group + 1 + chunk) % groups
-        span = pl.ds(pl.multiple_of(owner * rows, rows), rows)
-        to_chip.append(
-            [
-                copy(
-                    chunk,
-                    index,
-                    part_ref.at[places[index] + shift, span],
-                    theirs.at[chunk, index],
-                    on_chip,
-                )
-                for index in range(4)
-            ]
-        )
-        loads.append(
-            [
-                pltpu.make_async_copy(
-                    part_ref.at[places[index], span],
-                    mine.at[chunk, index],
-                    load_sem.at[chunk, index],
-                )
-                for index in range(4)
-            ]
-        )
-        own, two = mine.at[chunk], final.at[chunk]
-        others.append(
-            {
-                "corner_x": copy(chunk, 4, own.at[0, first], relayed.at[chunk, 0], on_x),
-                "corner_y": copy(chunk, 5, own.at[0, second], relayed.at[chunk, 1], on_y),
-                "x_first": copy(chunk, 6, own.at[1, first], two.at[0, first], on_x),
-                "y_second": copy(chunk, 7, own.at[2, second], two.at[1, second], on_y),
-                "x_second": copy(chunk, 8, own.at[1, second], two.at[0, second], on_x),
-                "y_first": copy(chunk, 9, own.at[2, first], two.at[1, first], on_y),
-            }
-        )
-    small_copies = [
-        pltpu.make_async_remote_copy(
-            src_ref=small_ref.at[peers[index]],
-            dst_ref=small_come.at[index],
-            send_sem=small_send.at[index],
-            recv_sem=small_recv.at[index],
-            device_id={"tok": peers[index]},
-            device_id_type=MESH,
-        )
-        for index in range(len(peers))
-    ]
-    across = [
-        pltpu.make_async_remote_copy(
-            src_ref=mine.at[chunk, 3],
-            dst_ref=come.at[chunk],
-            send_sem=across_send.at[chunk],
-            recv_sem=across_recv.at[chunk],
-            device_id={"grp": other_groups[chunk]},
-            device_id_type=MESH,
-        )
-        for chunk in range(groups - 1)
-    ]
-    small_over = [
-        pltpu.make_async_remote_copy(
-            src_ref=small_total.at[other_groups[chunk]],
-            dst_ref=small_across.at[chunk],
-            send_sem=small_across_send.at[chunk],
-            recv_sem=small_across_recv.at[chunk],
-            device_id={"grp": other_groups[chunk]},
-            device_id_type=MESH,
-        )
-        for chunk in range(groups - 1)
-    ]
-
-    for chunk in range(groups):
-        for index in range(4):
-            to_chip[chunk][index].start()
-            loads[chunk][index].start()
-        if chunk == 0:
-            for each in small_copies:
-                each.start()
-
-    def join(chunk, index):
-        to_chip[chunk][index].wait_recv()
-        loads[chunk][index].wait()
-        add_into(mine.at[chunk, index], theirs.at[chunk, index], 0, rows)
-
-    def open_chunk(chunk):
-        join(chunk, 0)
-        others[chunk]["corner_x"].start()
-        others[chunk]["corner_y"].start()
-        join(chunk, 1)
-        others[chunk]["x_first"].start()
-        join(chunk, 2)
-        others[chunk]["y_second"].start()
-
-    def relay_chunk(chunk):
-        others[chunk]["corner_y"].wait_recv()
-        add_into(mine.at[chunk, 1], relayed.at[chunk, 1], half, half)
-        others[chunk]["x_second"].start()
-        others[chunk]["corner_x"].wait_recv()
-        add_into(mine.at[chunk, 2], relayed.at[chunk, 0], 0, half)
-        others[chunk]["y_first"].start()
-
-    def close_chunk(chunk):
-        join(chunk, 3)
-        for name in ("x_first", "y_second", "x_second", "y_first"):
-            others[chunk][name].wait_recv()
-
-        @pl.loop(0, rows // step)
-        def _(turn):
-            at = pl.ds(pl.multiple_of(turn * step, step), step)
-            total = mine[chunk, 3, at, :].astype(jnp.float32)
-            total = total + final[chunk, 0, at, :].astype(jnp.float32)
-            total = total + final[chunk, 1, at, :].astype(jnp.float32)
-            mine[chunk, 3, at, :] = total.astype(mine.dtype)
-
-        if chunk < groups - 1:
-            across[chunk].start()
-
-    open_chunk(0)
-    for chunk in range(1, groups):
-        open_chunk(chunk)
-        relay_chunk(chunk - 1)
-        if chunk == 1:
-            sums = small_ref[here]
-            for index in range(len(peers)):
-                small_copies[index].wait_recv()
-                sums = sums + small_come[index]
-            small_total[...] = sums.reshape(small_total.shape)
-            for each in small_over:
-                each.start()
-        if chunk >= 2:
-            close_chunk(chunk - 2)
-    relay_chunk(groups - 1)
-    close_chunk(groups - 2)
-    close_chunk(groups - 1)
-    for each in across:
-        each.wait_recv()
-
-    @pl.loop(0, rows // step)
-    def _(turn):
-        at = pl.ds(pl.multiple_of(turn * step, step), step)
-        total = mine[groups - 1, 3, at, :].astype(jnp.float32)
-        for chunk in range(groups - 1):
-            total = total + come[chunk, at, :].astype(jnp.float32)
-        out_ref[at, :] = total
-
-    small_sum = small_total[group]
-    for chunk in range(groups - 1):
-        small_over[chunk].wait_recv()
-        small_sum = small_sum + small_across[chunk]
-    small_out_ref[...] = small_sum
-    for chunk in range(groups):
-        for each in to_chip[chunk] + list(others[chunk].values()):
-            each.wait_send()
-    for each in small_copies + across + small_over:
-        each.wait_send()
-
-
-def final_reduce(parts, small_parts, groups, call_number, kernels):
-    if not kernels:
-        sums = lax.psum_scatter(parts, "tok", scatter_dimension=0, tiled=False)
-        sums = lax.psum_scatter(sums, "grp", scatter_dimension=0, tiled=True)
-        small_sums = lax.psum_scatter(small_parts, "tok", scatter_dimension=0, tiled=False)
-        small_sums = lax.psum_scatter(small_sums, "grp", scatter_dimension=0, tiled=True)
-        return sums.astype(jnp.float32), small_sums
-    _, rows, columns = parts.shape
-    rows = rows // groups
-    small_rows, small_columns = small_parts.shape[1] // groups, small_parts.shape[2]
-    kind = parts.dtype
-    dma = pltpu.SemaphoreType.DMA
-    small = (small_rows, small_columns)
-    return pl.pallas_call(
-        functools.partial(final_reduce_kernel, groups),
-        out_shape=(
-            jax.ShapeDtypeStruct((rows, columns), jnp.float32),
-            jax.ShapeDtypeStruct(small, jnp.float32),
-        ),
-        in_specs=[
-            pl.BlockSpec(memory_space=pl.ANY),
-            pl.BlockSpec(memory_space=pltpu.VMEM),
-        ],
-        out_specs=(
-            pl.BlockSpec(memory_space=pltpu.VMEM),
-            pl.BlockSpec(memory_space=pltpu.VMEM),
-        ),
-        scratch_shapes=[
-            pltpu.VMEM((groups, 4, rows, columns), kind),
-            pltpu.VMEM((groups, 4, rows, columns), kind),
-            pltpu.VMEM((groups, 2, rows // 2, columns), kind),
-            pltpu.VMEM((groups, 2, rows, columns), kind),
-            pltpu.VMEM((groups - 1, rows, columns), kind),
-            pltpu.VMEM((7, groups * small_rows, small_columns), jnp.float32),
-            pltpu.VMEM((groups,) + small, jnp.float32),
-            pltpu.VMEM((groups - 1,) + small, jnp.float32),
-            dma((groups, 10)),
-            dma((groups, 10)),
-            dma((groups, 4)),
-            dma((groups - 1,)),
-            dma((groups - 1,)),
-            dma((7,)),
-            dma((7,)),
-            dma((groups - 1,)),
-            dma((groups - 1,)),
-        ],
-        compiler_params=pltpu.CompilerParams(
-            collective_id=call_number, has_side_effects=True, vmem_limit_bytes=VMEM_BYTES
-        ),
-        name="final_reduce",
-    )(parts, small_parts)
 
 
 def stack_heads(values, heads):
@@ -1438,13 +1149,114 @@
     )
 
 
+def backward_block(
+    prompts,
+    answers,
+    heads,
+    start,
+    owner_ref,
+    share_ref,
+    normed_ref,
+    branch_ref,
+    query_block,
+    output_block,
+    queries,
+    mixture,
+    log_ref,
+    prompt_kv_ref,
+    answer_kv_ref,
+    normed_across,
+    branch_across,
+    key_sums,
+    own_sums,
+    grad_normed_ref,
+):
+    width = HEAD_WIDTH
+    scale = HEAD_WIDTH ** (-0.5)
+    length = prompt_kv_ref.shape[1]
+    grad_output_block = plain_product(branch_across[...], mixture).astype(jnp.bfloat16)
+    grad_mixture = plain_product(branch_ref[...], output_block).astype(jnp.bfloat16)
+
+    def backward(keys, values, stacked, grad_stacked, log_row, inner_row, allowed):
+        scores = transposed_product(keys, stacked)
+        probs = jnp.exp(scores * scale - log_row)
+        if allowed is not None:
+            probs = jnp.where(allowed, probs, 0.0)
+        grad_values = plain_product(probs.astype(jnp.bfloat16), grad_stacked)
+        grad_probs = transposed_product(values, grad_stacked)
+        grad_scores = (probs * (grad_probs - inner_row)).astype(jnp.bfloat16)
+        grad_keys = plain_product(grad_scores, stacked)
+        grad_queries = weight_product(grad_scores, keys)
+        return grad_queries, grad_keys, grad_values
+
+    pieces = []
+    for part in range(prompts + answers):
+        here, rows = part_rows(part, prompts, answers, normed_ref, answer_kv_ref)
+        token = lax.broadcasted_iota(jnp.int32, (1, heads * rows), 1) % rows
+        stacked = stack_heads(queries[here, :], heads)
+        grad_stacked = stack_heads(grad_mixture[here, :], heads)
+        mixed = stack_heads(mixture[here, :], heads)
+        product = grad_stacked.astype(jnp.float32) * mixed.astype(jnp.float32)
+        inner_row = jnp.sum(jnp.transpose(product), axis=0, keepdims=True)
+        log_row = jnp.concatenate([log_ref[head : head + 1, here] for head in range(heads)], axis=1)
+        if part < prompts:
+            place = lax.broadcasted_iota(jnp.int32, (length, 1), 0)
+            grad_queries, grad_keys, grad_values = backward(
+                prompt_kv_ref[part, :, :width],
+                prompt_kv_ref[part, :, width:],
+                stacked,
+                grad_stacked,
+                log_row,
+                inner_row,
+                place <= start + token,
+            )
+            key_sums[part, :, :width] += grad_keys
+            key_sums[part, :, width:] += grad_values
+        else:
+            answer = part - prompts
+            owner = owner_ref[answer]
+            own = slice(answer * rows, (answer + 1) * rows)
+            grad_queries, grad_keys, grad_values = backward(
+                prompt_kv_ref[owner, :, :width],
+                prompt_kv_ref[owner, :, width:],
+                stacked,
+                grad_stacked,
+                log_row,
+                inner_row,
+                None,
+            )
+            for prompt in range(prompts):
+                share = share_ref[answer * prompts + prompt]
+                key_sums[prompt, :, :width] += share * grad_keys
+                key_sums[prompt, :, width:] += share * grad_values
+            place = lax.broadcasted_iota(jnp.int32, (rows, 1), 0)
+            own_queries, own_keys, own_values = backward(
+                answer_kv_ref[own, :width],
+                answer_kv_ref[own, width:],
+                stacked,
+                grad_stacked,
+                log_row,
+                inner_row,
+                place <= token,
+            )
+            grad_queries = grad_queries + own_queries
+            own_sums[own, :width] += own_keys
+            own_sums[own, width:] += own_values
+        pieces.append(unstack_heads((grad_queries * scale).astype(jnp.bfloat16), heads))
+    grad_queries = jnp.concatenate(pieces, axis=0)
+    grad_query_block = plain_product(normed_across[...], grad_queries).astype(jnp.bfloat16)
+    grad_normed_ref[...] += transposed_product(grad_queries, query_block)
+    grad_bias = jnp.sum(grad_queries.astype(jnp.float32), axis=0, keepdims=True)
+    return grad_query_block, grad_output_block, grad_bias
+
+
 def attention_backward_kernel(
     prompts,
     answers,
     heads,
-    scale,
     place_ref,
     owner_ref,
+    share_ref,
     normed_ref,
     query_ref,
     prompt_kv_ref,
@@ -1466,7 +1278,7 @@
 ):
     step = pl.program_id(0)
     width = HEAD_WIDTH
-    length = prompt_kv_ref.shape[1]
+    scale = HEAD_WIDTH ** (-0.5)
     block = queries_ref.shape[2]
 
     @pl.when(step == 0)
@@ -1478,89 +1290,35 @@
         grad_normed_ref[...] = jnp.zeros_like(grad_normed_ref)
 
     query_block, output_block = query_ref[0, 0], output_ref[0, 0]
-    weight_shape = (grad_weights_ref.shape[1], -1, block)
-    weight_rows = query_block.shape[0] // grad_weights_ref.shape[1]
-    grad_weights_ref[0, :, weight_rows : 2 * weight_rows] = (
-        plain_product(branch_across[...], mixture_ref[0])
-        .astype(jnp.bfloat16)
-        .reshape(weight_shape)
-    )
-    grad_mixture = plain_product(branch_ref[...], output_block).astype(jnp.bfloat16)
-    queries = queries_ref[0]
-    mixture = mixture_ref[0]
-
-    def backward(keys, values, stacked, grad_stacked, log_row, inner_row, allowed):
-        scores = transposed_product(keys, stacked)
-        probs = jnp.exp(scores * scale - log_row)
-        if allowed is not None:
-            probs = jnp.where(allowed, probs, 0.0)
-        grad_values = plain_product(probs.astype(jnp.bfloat16), grad_stacked)
-        grad_probs = transposed_product(values, grad_stacked)
-        grad_scores = (probs * (grad_probs - inner_row)).astype(jnp.bfloat16)
-        grad_keys = plain_product(grad_scores, stacked)
-        grad_queries = weight_product(grad_scores, keys)
-        return grad_queries, grad_keys, grad_values
-
-    pieces = []
-    for part in range(prompts + answers):
-        here, rows = part_rows(part, prompts, answers, normed_ref, answer_kv_ref)
-        token = lax.broadcasted_iota(jnp.int32, (1, heads * rows), 1) % rows
-        stacked = stack_heads(queries[here, :], heads)
-        grad_stacked = stack_heads(grad_mixture[here, :], heads)
-        mixed = stack_heads(mixture[here, :], heads)
-        product = grad_stacked.astype(jnp.float32) * mixed.astype(jnp.float32)
-        inner_row = jnp.sum(jnp.transpose(product), axis=0, keepdims=True)
-        log_row = jnp.concatenate(
-            [log_ref[0, head : head + 1, here] for head in range(heads)], axis=1
-        )
-        if part < prompts:
-            place = lax.broadcasted_iota(jnp.int32, (length, 1), 0)
-            grad_queries, grad_keys, grad_values = backward(
-                prompt_kv_ref[part, :, :width],
-                prompt_kv_ref[part, :, width:],
-                stacked,
-                grad_stacked,
-                log_row,
-                inner_row,
-                place <= place_ref[0] + token,
-            )
-            key_sums[part, :, :width] += grad_keys
-            key_sums[part, :, width:] += grad_values
-        else:
-            answer = part - prompts
-            owner = owner_ref[answer]
-            own = slice(answer * rows, (answer + 1) * rows)
-            grad_queries, grad_keys, grad_values = backward(
-                prompt_kv_ref[owner, :, :width],
-                prompt_kv_ref[owner, :, width:],
-                stacked,
-                grad_stacked,
-                log_row,
-                inner_row,
-                None,
-            )
-            key_sums[owner, :, :width] += grad_keys
-            key_sums[owner, :, width:] += grad_values
-            place = lax.broadcasted_iota(jnp.int32, (rows, 1), 0)
-            own_queries, own_keys, own_values = backward(
-                answer_kv_ref[own, :width],
-                answer_kv_ref[own, width:],
-                stacked,
-                grad_stacked,
-                log_row,
-                inner_row,
-                place <= token,
-            )
-            grad_queries = grad_queries + own_queries
-            own_sums[own, :width] += own_keys
-            own_sums[own, width:] += own_values
-        pieces.append(unstack_heads((grad_queries * scale).astype(jnp.bfloat16), heads))
-    grad_queries = jnp.concatenate(pieces, axis=0)
-    grad_weights_ref[0, :, :weight_rows] = (
-        plain_product(normed_across[...], grad_queries).astype(jnp.bfloat16).reshape(weight_shape)
-    )
-    grad_normed_ref[...] += transposed_product(grad_queries, query_block)
-    grad_bias_ref[0] = jnp.sum(grad_queries.astype(jnp.float32), axis=0, keepdims=True)
+    groups = grad_weights_ref.shape[1]
+    weight_rows = query_block.shape[0] // groups
+    grad_query_block, grad_output_block, grad_bias = backward_block(
+        prompts,
+        answers,
+        heads,
+        place_ref[0],
+        owner_ref,
+        share_ref,
+        normed_ref,
+        branch_ref,
+        query_block,
+        output_block,
+        queries_ref[0],
+        mixture_ref[0],
+        log_ref.at[0],
+        prompt_kv_ref,
+        answer_kv_ref,
+        normed_across,
+        branch_across,
+        key_sums,
+        own_sums,
+        grad_normed_ref,
+    )
+    grad_weights_ref[0, :, :weight_rows] = grad_query_block.reshape(groups, weight_rows, block)
+    grad_weights_ref[0, :, weight_rows : 2 * weight_rows] = grad_output_block.reshape(
+        groups, weight_rows, block
+    )
+    grad_bias_ref[0] = grad_bias
 
     @pl.when(step == pl.num_programs(0) - 1)
     def _():
@@ -1573,6 +1331,7 @@
 def attention_backward(
     place,
     owning,
+    share,
     normed,
     weights,
     groups,
@@ -1598,7 +1357,7 @@
     scores = heads * token_rows * length
     return pl.pallas_call(
         functools.partial(
-            attention_backward_kernel, prompts, answers, heads, HEAD_WIDTH ** (-0.5)
+            attention_backward_kernel, prompts, answers, heads
         ),
         out_shape=(
             jax.ShapeDtypeStruct((steps, groups, grad_rows, block), jnp.bfloat16),
@@ -1608,7 +1367,7 @@
             jax.ShapeDtypeStruct((steps, 1, block), jnp.float32),
         ),
         grid_spec=pltpu.PrefetchScalarGridSpec(
-            num_scalar_prefetch=2,
+            num_scalar_prefetch=3,
             grid=(steps,),
             in_specs=[
                 whole(token_rows, model_width),
@@ -1647,6 +1406,7 @@
     )(
         place,
         owning,
+        share,
         normed,
         weights,
         prompt_kv,
@@ -1656,6 +1416,480 @@
         queries,
         mixture,
         log_total,
+    )
+
+
+VECTOR_ROWS = 16
+KNOWN_ROWS = 8
+
+
+def backward_reduce_kernel(
+    prompts,
+    answers,
+    heads,
+    groups,
+    prompt_rows,
+    owner_ref,
+    share_ref,
+    weights_ref,
+    queries_ref,
+    mixture_ref,
+    hidden_hbm,
+    normed_ref,
+    branch_ref,
+    log_ref,
+    prompt_kv_ref,
+    answer_kv_ref,
+    states_ref,
+    gain_ref,
+    keyval_ref,
+    known_ref,
+    grad_query_ref,
+    grad_output_ref,
+    grad_keyval_ref,
+    vectors_ref,
+    grad_input_ref,
+    normed_across,
+    branch_across,
+    key_sums,
+    own_sums,
+    grad_normed,
+    grad_hidden,
+    held,
+    pair,
+    kept,
+    theirs,
+    relayed,
+    final,
+    come,
+    kv_part,
+    kv_come,
+    kv_rows,
+    keyval_part,
+    keyval_come,
+    keyval_sum,
+    keyval_over,
+    vectors,
+    vector_come,
+    vector_sum,
+    vector_over,
+    send_sem,
+    recv_sem,
+    over_send,
+    over_recv,
+    peer_send,
+    peer_recv,
+    load_sem,
+    hidden_sem,
+):
+    width = HEAD_WIDTH
+    scale = HEAD_WIDTH ** (-0.5)
+    here, on_x, on_y, on_chip, corner = block_of_eight()
+    _, peers = peers_of(8)
+    group = lax.axis_index("grp")
+    other_groups = [(group + turn) % groups for turn in range(1, groups)]
+    model_width, block = held.shape[1:]
+    chunk_rows = model_width // groups
+    step = 64
+    counter = iter(range(4 + 6 * groups))
+
+    def copy(source, target, device):
+        return remote(next(counter), source, target, device, send_sem, recv_sem)
+
+    def over(index, source, target, turn):
+        return pltpu.make_async_remote_copy(
+            src_ref=source,
+            dst_ref=target,
+            send_sem=over_send.at[index],
+            recv_sem=over_recv.at[index],
+            device_id={"grp": other_groups[turn]},
+            device_id_type=MESH,
+        )
+
+    def to_peers(row, source, target):
+        return [
+            pltpu.make_async_remote_copy(
+                src_ref=source(peers[index]),
+                dst_ref=target(index),
+                send_sem=peer_send.at[row, index],
+                recv_sem=peer_recv.at[row, index],
+                device_id={"tok": peers[index]},
+                device_id_type=MESH,
+            )
+            for index in range(len(peers))
+        ]
+
+    spans = [
+        pl.ds(pl.multiple_of(((group + 1 + chunk) % groups) * chunk_rows, chunk_rows), chunk_rows)
+        for chunk in range(groups)
+    ]
+    chunks = range(groups)
+    to_chip = [copy(kept.at[turn % 2], theirs.at[turn], on_chip) for turn in range(4)]
+    corner_x = [copy(kept.at[2, 0, span], relayed.at[0, span], on_x) for span in spans]
+    corner_y = [copy(kept.at[2, 1, span], relayed.at[1, span], on_y) for span in spans]
+    x_first = [copy(kept.at[4, 0, span], final.at[0, 0, span], on_x) for span in spans]
+    y_second = [copy(kept.at[3, 1, span], final.at[1, 1, span], on_y) for span in spans]
+    x_second = [copy(kept.at[4, 1, span], final.at[0, 1, span], on_x) for span in spans]
+    y_first = [copy(kept.at[3, 0, span], final.at[1, 0, span], on_y) for span in spans]
+    across = [
+        [over(2 * turn + kind, kept.at[5, kind, spans[turn]], come.at[turn, kind], turn) for kind in (0, 1)]
+        for turn in range(groups - 1)
+    ]
+
+    def lanes(device):
+        return pl.ds(pl.multiple_of(device * block, block), block)
+
+    def prompt_place(device):
+        return pl.ds(pl.multiple_of(device * prompt_rows, prompt_rows), prompt_rows)
+
+    kv_copies = to_peers(
+        0, lambda peer: kv_part.at[:, prompt_place(peer), :], lambda index: kv_come.at[index]
+    )
+    keyval_copies = to_peers(
+        1, lambda peer: keyval_part.at[:, peer], lambda index: keyval_come.at[index]
+    )
+    vector_copies = to_peers(
+        2, lambda peer: vectors.at[:, lanes(peer)], lambda index: vector_come.at[index]
+    )
+    vector_out = to_peers(
+        3, lambda peer: vector_sum, lambda index: vectors_ref.at[:, lanes(here)]
+    )
+    first_over = 2 * (groups - 1)
+    keyval_across = [
+        over(first_over + turn, keyval_sum.at[other_groups[turn]], keyval_over.at[turn], turn)
+        for turn in range(groups - 1)
+    ]
+    vector_across = [
+        over(first_over + groups - 1 + turn, vectors.at[:, lanes(here)], vector_over.at[turn], turn)
+        for turn in range(groups - 1)
+    ]
+
+    load_hidden = pltpu.make_async_copy(hidden_hbm, grad_hidden, hidden_sem)
+    load_hidden.start()
+    greet_all(peers, other_groups)
+    normed_across[...] = jnp.transpose(normed_ref[...])
+    branch_across[...] = jnp.transpose(branch_ref[...])
+    key_sums[...] = jnp.zeros_like(key_sums)
+    own_sums[...] = jnp.zeros_like(own_sums)
+    grad_normed[...] = jnp.zeros_like(grad_normed)
+    vectors[:KNOWN_ROWS, :] = known_ref[:KNOWN_ROWS, :]
+    vectors[KNOWN_ROWS:, :] = known_ref[KNOWN_ROWS:, :]
+
+    def add_into(target, other, rows):
+        @pl.loop(0, rows // step)
+        def _(turn):
+            at = chunk_of(turn, step)
+            total = target[at, :].astype(jnp.float32) + other[at, :].astype(jnp.float32)
+            target[at, :] = total.astype(target.dtype)
+
+    def join(turn):
+        to_chip[turn].wait_recv()
+        for kind in (0, 1):
+            add_into(kept.at[2 + turn, kind], theirs.at[turn, kind], model_width)
+
+    @pl.loop(0, 8)
+    def _(turn):
+        source = bits_away(7 - turn)
+        slot = (turn % 2) * (2 + turn // 2) + (1 - turn % 2) * ((turn // 2) % 2)
+        loads = (
+            pltpu.make_async_copy(weights_ref.at[source], held, load_sem.at[0]),
+            pltpu.make_async_copy(queries_ref.at[source], pair.at[0], load_sem.at[1]),
+            pltpu.make_async_copy(mixture_ref.at[source], pair.at[1], load_sem.at[2]),
+        )
+        for each in loads:
+            each.start()
+        for index in (2, 3):
+
+            @pl.when(turn == 2 * index)
+            def _():
+                to_chip[index - 2].wait_send()
+
+        for each in loads:
+            each.wait()
+        grad_query_block, grad_output_block, grad_bias = backward_block(
+            prompts,
+            answers,
+            heads,
+            here * prompt_rows,
+            owner_ref,
+            share_ref,
+            normed_ref,
+            branch_ref,
+            held[0],
+            held[1],
+            pair[0],
+            pair[1],
+            log_ref.at[source],
+            prompt_kv_ref,
+            answer_kv_ref,
+            normed_across,
+            branch_across,
+            key_sums,
+            own_sums,
+            grad_normed,
+        )
+        kept[slot, 0] = grad_query_block
+        kept[slot, 1] = grad_output_block
+        vectors[10:11, lanes(source)] = grad_bias
+        for index in range(4):
+
+            @pl.when(turn == 2 * index)
+            def _():
+                to_chip[index].start()
+
+        @pl.when(turn == 2)
+        def _():
+            join(0)
+            for chunk in chunks:
+                corner_x[chunk].start()
+                corner_y[chunk].start()
+
+        @pl.when(turn == 4)
+        def _():
+            join(1)
+            for chunk in chunks[:2]:
+                y_second[chunk].start()
+
+        @pl.when(turn == 6)
+        def _():
+            join(2)
+            for chunk in chunks[:2]:
+                x_first[chunk].start()
+
+    kv_part[:, :, :width] = (key_sums[:, :, :width] * scale).astype(jnp.bfloat16)
+    kv_part[:, :, width:] = key_sums[:, :, width:].astype(jnp.bfloat16)
+    for each in kv_copies:
+        each.start()
+    for chunk in chunks:
+        span = spans[chunk]
+        corner_y[chunk].wait_recv()
+        add_into(kept.at[4, 1, span], relayed.at[1, span], chunk_rows)
+        x_second[chunk].start()
+        corner_x[chunk].wait_recv()
+        add_into(kept.at[3, 0, span], relayed.at[0, span], chunk_rows)
+        y_first[chunk].start()
+        if chunk + 2 < groups:
+            x_first[chunk + 2].start()
+            y_second[chunk + 2].start()
+    join(3)
+
+    def close(chunk):
+        span = spans[chunk]
+        for kind, parts in ((0, (x_first, y_first)), (1, (x_second, y_second))):
+            for part in parts:
+                part[chunk].wait_recv()
+            for turn in (0, 1):
+                add_into(kept.at[5, kind, span], final.at[turn, kind, span], chunk_rows)
+            if chunk < groups - 1:
+                across[chunk][kind].start()
+
+    for each in kv_copies:
+        each.wait_recv()
+    own_prompt = prompts * prompt_rows
+    for prompt in range(prompts):
+        total = kv_part[prompt, prompt_place(here), :].astype(jnp.float32)
+        for index in range(len(peers)):
+            total = total + kv_come[index, prompt].astype(jnp.float32)
+        kv_rows[prompt * prompt_rows : (prompt + 1) * prompt_rows, :] = total.astype(jnp.bfloat16)
+    kv_rows[own_prompt:, :width] = (own_sums[:, :width] * scale).astype(jnp.bfloat16)
+    kv_rows[own_prompt:, width:] = own_sums[:, width:].astype(jnp.bfloat16)
+    keyval_part[...] = (
+        plain_product(normed_across[...], kv_rows[...])
+        .astype(jnp.bfloat16)
+        .reshape(keyval_part.shape)
+    )
+    for each in keyval_copies:
+        each.start()
+    close(0)
+    load_hidden.wait()
+    vectors[11:12, :width] = jnp.sum(
+        kv_rows[:, width:].astype(jnp.float32), axis=0, keepdims=True
+    )
+    piece = 64
+    vectors[8:10, :] = jnp.zeros((2, model_width), jnp.float32)
+
+    @pl.loop(0, states_ref.shape[0] // piece)
+    def _(turn):
+        at = chunk_of(turn, piece)
+        scaled, inverse = norm_stats(states_ref[at, :].astype(jnp.float32))
+        grad_out = grad_normed[at, :] + transposed_product(kv_rows[at, :], keyval_ref[...])
+        weighted = grad_out * gain_ref[...]
+        grad_in = inverse * (
+            weighted
+            - jnp.mean(weighted, axis=-1, keepdims=True)
+            - scaled * jnp.mean(weighted * scaled, axis=-1, keepdims=True)
+        )
+        grad_input_ref[at, :] = (grad_hidden[at, :] + grad_in).astype(jnp.bfloat16)
+        vectors[8:9, :] += jnp.sum(grad_out * scaled, axis=0, keepdims=True)
+        vectors[9:10, :] += jnp.sum(grad_out, axis=0, keepdims=True)
+
+    for each in vector_copies:
+        each.start()
+    close(1)
+    for each in keyval_copies:
+        each.wait_recv()
+    for other in range(groups):
+        total = keyval_part[other, here].astype(jnp.float32)
+        for index in range(len(peers)):
+            total = total + keyval_come[index, other].astype(jnp.float32)
+        keyval_sum[other] = total.astype(jnp.bfloat16)
+    for each in keyval_across:
+        each.start()
+    for each in vector_copies:
+        each.wait_recv()
+    total = vectors[:, lanes(here)]
+    for index in range(len(peers)):
+        total = total + vector_come[index]
+    vectors[:, lanes(here)] = total
+    for each in vector_across:
+        each.start()
+    close(2)
+    for each in vector_across:
+        each.wait_recv()
+    total = vectors[:, lanes(here)]
+    for turn in range(groups - 1):
+        total = total + vector_over[turn]
+    vector_sum[...] = total
+    for each in vector_out:
+        each.start()
+    vectors_ref[:, lanes(here)] = vector_sum[...]
+    for chunk in chunks[3:]:
+        close(chunk)
+    for each in keyval_across:
+        each.wait_recv()
+    total = keyval_sum[group].astype(jnp.float32)
+    for turn in range(groups - 1):
+        total = total + keyval_over[turn].astype(jnp.float32)
+    grad_keyval_ref[...] = total
+    for kind, out_ref in ((0, grad_query_ref), (1, grad_output_ref)):
+        for turn in range(groups - 1):
+            across[turn][kind].wait_recv()
+        own = pl.multiple_of(group * chunk_rows, chunk_rows)
+
+        @pl.loop(0, chunk_rows // step)
+        def _(turn):
+            at = chunk_of(turn, step)
+            total = kept[5, kind, pl.ds(own + turn * step, step), :].astype(jnp.float32)
+            for other in range(groups - 1):
+                total = total + come[other, kind, at, :].astype(jnp.float32)
+            out_ref[at, :] = total
+
+    for each in vector_out:
+        each.wait_recv()
+    for each in to_chip[2:] + corner_x + corner_y + x_first + y_second + x_second + y_first:
+        each.wait_send()
+    for each in kv_copies + keyval_copies + vector_copies + vector_out:
+        each.wait_send()
+    for each in sum(across, []) + keyval_across + vector_across:
+        each.wait_send()
+
+
+def backward_reduce(
+    owning,
+    share,
+    weights,
+    queries,
+    mixture,
+    grad_hidden,
+    normed,
+    branch,
+    log_total,
+    prompt_kv,
+    answer_kv,
+    states,
+    gain,
+    keyval_full,
+    known,
+    groups,
+    prompts,
+    answers,
+    prompt_rows,
+    call_number,
+):
+    token_rows, model_width = normed.shape
+    block = weights.shape[3]
+    heads = block // HEAD_WIDTH
+    keyval_width = keyval_full.shape[1]
+    weight_rows = model_width // groups
+    keyval_rows = model_width // groups // 8
+    kind, wide = jnp.bfloat16, jnp.float32
+    inside = pl.BlockSpec(memory_space=pltpu.VMEM)
+    anywhere = pl.BlockSpec(memory_space=pl.ANY)
+    scalars = pl.BlockSpec(memory_space=pltpu.SMEM)
+    dma = pltpu.SemaphoreType.DMA
+    others = groups - 1
+    return pl.pallas_call(
+        functools.partial(backward_reduce_kernel, prompts, answers, heads, groups, prompt_rows),
+        out_shape=(
+            jax.ShapeDtypeStruct((weight_rows, block), wide),
+            jax.ShapeDtypeStruct((weight_rows, block), wide),
+            jax.ShapeDtypeStruct((keyval_rows, keyval_width), wide),
+            jax.ShapeDtypeStruct((VECTOR_ROWS, model_width), wide),
+            jax.ShapeDtypeStruct((token_rows, model_width), kind),
+        ),
+        in_specs=[scalars] * 2 + [anywhere] * 4 + [inside] * 9,
+        out_specs=(inside,) * 5,
+        scratch_shapes=[
+            pltpu.VMEM((model_width, token_rows), kind),
+            pltpu.VMEM((model_width, token_rows), kind),
+            pltpu.VMEM(prompt_kv.shape, wide),
+            pltpu.VMEM(answer_kv.shape, wide),
+            pltpu.VMEM((token_rows, model_width), wide),
+            pltpu.VMEM((token_rows, model_width), wide),
+            pltpu.VMEM((2, model_width, block), kind),
+            pltpu.VMEM((2, token_rows, block), kind),
+            pltpu.VMEM((6, 2, model_width, block), kind),
+            pltpu.VMEM((4, 2, model_width, block), kind),
+            pltpu.VMEM((2, model_width, block), kind),
+            pltpu.VMEM((2, 2, model_width, block), kind),
+            pltpu.VMEM((others, 2, weight_rows, block), kind),
+            pltpu.VMEM(prompt_kv.shape, kind),
+            pltpu.VMEM((7, prompts, prompt_rows, keyval_width), kind),
+            pltpu.VMEM((token_rows, keyval_width), kind),
+            pltpu.VMEM((groups, 8, keyval_rows, keyval_width), kind),
+            pltpu.VMEM((7, groups, keyval_rows, keyval_width), kind),
+            pltpu.VMEM((groups, keyval_rows, keyval_width), kind),
+            pltpu.VMEM((others, keyval_rows, keyval_width), kind),
+            pltpu.VMEM((VECTOR_ROWS, model_width), wide),
+            pltpu.VMEM((7, VECTOR_ROWS, block), wide),
+            pltpu.VMEM((VECTOR_ROWS, block), wide),
+            pltpu.VMEM((others, VECTOR_ROWS, block), wide),
+            dma((4 + 6 * groups,)),
+            dma((4 + 6 * groups,)),
+            dma((4 * others,)),
+            dma((4 * others,)),
+            dma((4, 7)),
+            dma((4, 7)),
+            dma((3,)),
+            dma,
+        ],
+        compiler_params=pltpu.CompilerParams(
+            collective_id=call_number,
+            has_side_effects=True,
+            vmem_limit_bytes=63 * 1024 * 1024,
+        ),
+        cost_estimate=pl.CostEstimate(
+            flops=100 * token_rows * model_width * block,
+            bytes_accessed=250 * 1000 * 1000,
+            transcendentals=0,
+        ),
+        name="backward_reduce",
+    )(
+        owning,
+        share,
+        weights,
+        queries,
+        mixture,
+        grad_hidden,
+        normed,
+        branch,
+        log_total,
+        prompt_kv,
+        answer_kv,
+        states,
+        gain.reshape(1, -1),
+        keyval_full,
+        known,
     )
 
 
@@ -1698,7 +1932,7 @@
     hidden_units = up_bias.shape[0] * groups * token_devices
     ff_here = hidden_units // token_devices
     ff_start = token_index * ff_here
-    share = first_gain.shape[0]
+    share_size = first_gain.shape[0]
     block = query_weight.shape[1]
     weight_rows = query_weight.shape[0]
     keyval_rows, keyval_width = keyval_weight.shape
@@ -1751,10 +1985,10 @@
         return small_full[:, :, start : start + size].reshape(-1)
 
     gain_one, shift_one, query_offset, output_offset, gain_two, shift_two, down_offset = (
-        vector(index * share, share) for index in range(7)
-    )
-    up_offset = vector(7 * share, up_bias.shape[0])
-    count_at = 7 * share + up_bias.shape[0]
+        vector(index * share_size, share_size) for index in range(7)
+    )
+    up_offset = vector(7 * share_size, up_bias.shape[0])
+    count_at = 7 * share_size + up_bias.shape[0]
     counts = small_full[:, :, count_at : count_at + 2]
     valid_count = jnp.sum(counts[:, :, 0]) * 128.0 + jnp.sum(counts[:, :, 1])
     up_here = lax.dynamic_slice_in_dim(up_offset, ff_start, ff_here)
@@ -1849,7 +2083,6 @@
         grad_up_cols = for_sending(weight_product(group_two, grad_pre_active))
         grad_up_offset = column_sums(grad_pre_active)
     grad_down_weight = lax.psum_scatter(grad_down_cols, "grp", scatter_dimension=0, tiled=True)
-    grad_up_weight = lax.psum_scatter(grad_up_cols, "grp", scatter_dimension=0, tiled=True)
     grad_down_offset = column_sums(grad_branch_two)
     scaled_two, inverse_two = norm_stats(hidden)
     grad_norm_two, grad_gain_two, grad_shift_two = norm_backward(
@@ -1857,73 +2090,142 @@
     )
     grad_hidden = grad_result + grad_norm_two
     grad_branch_one = grad_hidden.astype(jnp.bfloat16)
+    grad_down_weight, grad_up_cols, grad_branch_one = lax.optimization_barrier(
+        (grad_down_weight, grad_up_cols, grad_branch_one)
+    )
+    grad_up_weight = lax.psum_scatter(grad_up_cols, "grp", scatter_dimension=0, tiled=True)
     grad_output_offset = column_sums(grad_branch_one)
 
-    grad_rows = keyval_start + keyval_pack
-    grad_weights, grad_normed_one, grad_prompt_kv, grad_answer_kv, grad_query_offset = (
-        attention_backward(
-            place,
+    share = (owning[:, None] == jnp.arange(prompt_count)[None, :]).astype(jnp.float32).reshape(-1)
+    grad_up_place = lax.dynamic_update_slice_in_dim(
+        jnp.zeros((hidden_units,), jnp.float32), grad_up_offset, ff_start, 0
+    )
+    if kernels:
+        known = jnp.concatenate(
+            [
+                grad_up_place,
+                grad_output_offset,
+                grad_gain_two,
+                grad_shift_two,
+                grad_down_offset,
+                jnp.zeros((3 * model_width + HEAD_WIDTH,), jnp.float32),
+                own_squares.reshape(1),
+            ]
+        )
+        known = jnp.pad(known, (0, VECTOR_ROWS * model_width - known.shape[0]))
+        grad_query_own, grad_output_own, grad_keyval_own, vectors, grad_inputs = backward_reduce(
             owning,
+            share,
+            weights,
+            queries,
+            mixture,
+            grad_hidden,
             normed_one,
-            weights,
-            groups,
-            grad_rows,
+            grad_branch_one,
+            log_total,
             prompt_kv,
             answer_kv,
-            grad_branch_one,
-            queries,
-            mixture,
-            log_total,
+            states,
+            gain_one,
+            keyval_full,
+            known.reshape(VECTOR_ROWS, model_width),
+            groups,
             prompt_count,
             answer_count,
-        )
-    )
-    grad_prompt_kv = tok_reduce_small(grad_prompt_kv, 6, kernels)
-    grad_keyvals = jnp.concatenate(
-        [grad_prompt_kv.reshape(own_prompt, -1), grad_answer_kv], axis=0
-    ).astype(jnp.bfloat16)
-    grad_keyval_full = weight_product(normed_one, grad_keyvals)
-    grad_value_offset = column_sums(grad_keyvals[:, HEAD_WIDTH:])
-    grad_normed_one = grad_normed_one + transposed_product(grad_keyvals, keyval_full)
-    grad_norm_one, grad_gain_one, grad_shift_one = norm_backward(
-        grad_normed_one, gain_one, scaled_one, inverse_one
-    )
-    grad_inputs = grad_hidden + grad_norm_one
-
-    grad_keyval_blocks = jnp.swapaxes(
-        grad_keyval_full.astype(jnp.bfloat16).reshape(groups, token_devices, -1, block), 0, 1
-    )
-    grad_weights = lax.dynamic_update_slice(
-        grad_weights, grad_keyval_blocks, (0, 0, keyval_start, 0)
-    )
-    vectors = (
-        grad_gain_one,
-        grad_shift_one,
-        grad_query_offset.reshape(-1),
-        grad_output_offset,
-        grad_gain_two,
-        grad_shift_two,
-        grad_down_offset,
-        lax.dynamic_update_slice_in_dim(
-            jnp.zeros((hidden_units,), jnp.float32), grad_up_offset, ff_start, 0
-        ),
-    )
-    totals = jnp.concatenate([grad_value_offset, own_squares.reshape(1)])
-    blocks = jnp.concatenate(
-        [each.reshape(groups, token_devices, -1) for each in vectors]
-        + [jnp.broadcast_to(totals, (groups, token_devices, totals.shape[0]))],
-        axis=2,
-    )
-    blocks = jnp.pad(blocks, ((0, 0), (0, 0), (0, SMALL_SUMS - blocks.shape[2])))
-    blocks = jnp.swapaxes(blocks, 0, 1).reshape(token_devices, -1, HEAD_WIDTH)
-    grad_weights, small_sums = final_reduce(
-        grad_weights.reshape(token_devices, -1, block), blocks, groups, 7, kernels
-    )
-    small_sums = small_sums.reshape(-1)
-    up_share = up_bias.shape[0]
-    totals_at = 7 * share + up_share
-    value_total = small_sums[totals_at : totals_at + HEAD_WIDTH]
-    squared_sum = small_sums[totals_at + HEAD_WIDTH]
+            prompt_rows,
+            6,
+        )
+        value_total = vectors[11, :HEAD_WIDTH]
+        squared_sum = vectors[11, HEAD_WIDTH]
+        device = group_index * token_devices + token_index
+        mine = lax.dynamic_slice_in_dim(
+            vectors.reshape(VECTOR_ROWS, -1, share_size), device, 1, axis=1
+        )[:, 0]
+        own_vectors = [mine[row] for row in (8, 9, 10, 4, 5, 6, 7)]
+        grad_up_own = lax.dynamic_slice_in_dim(
+            vectors[: hidden_units // model_width].reshape(-1),
+            device * up_bias.shape[0],
+            up_bias.shape[0],
+        )
+    else:
+        grad_rows = keyval_start + keyval_pack
+        grad_weights, grad_normed_one, grad_prompt_kv, grad_answer_kv, grad_query_offset = (
+            attention_backward(
+                place,
+                owning,
+                share,
+                normed_one,
+                weights,
+                groups,
+                grad_rows,
+                prompt_kv,
+                answer_kv,
+                grad_branch_one,
+                queries,
+                mixture,
+                log_total,
+                prompt_count,
+                answer_count,
+            )
+        )
+        grad_prompt_kv = lax.psum_scatter(
+            grad_prompt_kv, "tok", scatter_dimension=1, tiled=True
+        ).astype(jnp.float32)
+        grad_keyvals = jnp.concatenate(
+            [grad_prompt_kv.reshape(own_prompt, -1), grad_answer_kv], axis=0
+        ).astype(jnp.bfloat16)
+        grad_keyval_full = weight_product(normed_one, grad_keyvals)
+        grad_value_offset = column_sums(grad_keyvals[:, HEAD_WIDTH:])
+        grad_normed_one = grad_normed_one + transposed_product(grad_keyvals, keyval_full)
+        grad_norm_one, grad_gain_one, grad_shift_one = norm_backward(
+            grad_normed_one, gain_one, scaled_one, inverse_one
+        )
+        grad_inputs = grad_hidden + grad_norm_one
+
+        grad_keyval_blocks = jnp.swapaxes(
+            grad_keyval_full.astype(jnp.bfloat16).reshape(groups, token_devices, -1, block), 0, 1
+        )
+        grad_weights = lax.dynamic_update_slice(
+            grad_weights, grad_keyval_blocks, (0, 0, keyval_start, 0)
+        )
+        vectors = (
+            grad_gain_one,
+            grad_shift_one,
+            grad_query_offset.reshape(-1),
+            grad_output_offset,
+            grad_gain_two,
+            grad_shift_two,
+            grad_down_offset,
+            grad_up_place,
+        )
+        totals = jnp.concatenate([grad_value_offset, own_squares.reshape(1)])
+        blocks = jnp.concatenate(
+            [each.reshape(groups, token_devices, -1) for each in vectors]
+            + [jnp.broadcast_to(totals, (groups, token_devices, totals.shape[0]))],
+            axis=2,
+        )
+        blocks = jnp.pad(blocks, ((0, 0), (0, 0), (0, SMALL_SUMS - blocks.shape[2])))
+        blocks = jnp.swapaxes(blocks, 0, 1).reshape(token_devices, -1, HEAD_WIDTH)
+        grad_weights = lax.psum_scatter(
+            grad_weights.reshape(token_devices, -1, block), "tok", scatter_dimension=0, tiled=False
+        )
+        grad_weights = lax.psum_scatter(grad_weights, "grp", scatter_dimension=0, tiled=True)
+        grad_weights = grad_weights.astype(jnp.float32)
+        small_sums = lax.psum_scatter(blocks, "tok", scatter_dimension=0, tiled=False)
+        small_sums = lax.psum_scatter(small_sums, "grp", scatter_dimension=0, tiled=True)
+        small_sums = small_sums.reshape(-1)
+        up_share = up_bias.shape[0]
+        totals_at = 7 * share_size + up_share
+        value_total = small_sums[totals_at : totals_at + HEAD_WIDTH]
+        squared_sum = small_sums[totals_at + HEAD_WIDTH]
+        own_vectors = [
+            small_sums[index * share_size : (index + 1) * share_size] for index in range(7)
+        ]
+        grad_up_own = small_sums[7 * share_size : totals_at]
+        grad_query_own = grad_weights[:weight_rows]
+        grad_output_own = grad_weights[weight_rows:keyval_start]
+        grad_keyval_own = grad_weights[keyval_start:].reshape(keyval_rows, keyval_width)
+        grad_inputs = grad_inputs.astype(jnp.bfloat16)
     loss_value = squared_sum / (valid_count * model_width)
 
     def split_rows(values):
@@ -1935,7 +2237,7 @@
 
     prompt_out, answer_out = split_rows(result_rows)
     prompt_grad, answer_grad = split_rows(grad_inputs)
-    pieces = [small_sums[index * share : (index + 1) * share] for index in range(7)]
+    pieces = own_vectors
     return (
         prompt_out,
         answer_out,
@@ -1943,16 +2245,16 @@
         answer_grad,
         pieces[0],
         pieces[1],
-        grad_weights[:weight_rows],
+        grad_query_own,
         pieces[2],
-        grad_weights[keyval_start:].reshape(keyval_rows, keyval_width),
+        grad_keyval_own,
         value_total,
-        grad_weights[weight_rows:keyval_start],
+        grad_output_own,
         pieces[3],
         pieces[4],
         pieces[5],
         grad_up_weight.astype(jnp.float32),
-        small_sums[7 * share : totals_at],
+        grad_up_own,
         grad_down_weight.astype(jnp.float32),
         pieces[6],
         loss_value,

time: 706 us -> 640 us (0.907)
  the two profiles are of different devices: /device:TPU:15 before, /device:TPU:0 now
where the time goes in v5:
time: 640 us; the launch traced here: 633 us
  Pallas kernels  539 us (84%)
  local copies, waits for them, and re-layouts  33 us (5%)
  other arithmetic  30.8 us (5%)
  between operations  19.4 us (3%)
  waiting for transfers between devices  9.43 us (1%)
    pallas_call x1, Pallas kernels, backward_reduce(): pl.pallas_call(functools.partial(backward_reduce_kernel, prompts, answers...  144 us
    pallas_call x2, Pallas kernels, product_and_reduce(): pl.pallas_call(functools.partial(product_reduce_kernel, with_grad), out_s...  130 us
    pallas_call x1, Pallas kernels, gather_attention(): pl.pallas_call(functools.partial(gather_attention_kernel, prompts, answer...  89.1 us
    pallas_call x1, Pallas kernels, gather_and_grad(): pl.pallas_call(grad_kernel, out_shape=(jax.ShapeDtypeStruct((8, token_row...  69.8 us
    pallas_call x1, Pallas kernels, gather_and_up(): pl.pallas_call(up_kernel, out_shape=(jax.ShapeDtypeStruct((8, token_rows,...  61.8 us
    pallas_call x1, Pallas kernels, spread(): pl.pallas_call(functools.partial(spread_kernel, groups), out_shape=jax.Sh...  29 us
    pallas_call x1, Pallas kernels, tok_gather_small(): pl.pallas_call(functools.partial(small_gather_kernel, count), out_shape=j...  15.1 us
  transfers between devices with their start and end apart: 6, of which 1 were waited for; matrix products, arithmetic and copies ran while one was open for 8% of the time, Pallas kernels for 64%

profile of v5, /device:TPU:0, one launch (start us, length us, event | category | flops | bytes accessed | tf_op | source)
XLA Modules:
  0.0 632.9 jit_solution(12277181971836159482)
XLA Ops:
  10.0 1.3 reduce_sum.136
  11.3 1.3 reduce_sum.137
  14.0 5.4 concatenate.36
  19.4 1.4 pad_maximum_fusion.1.own_ref
  20.8 29.0 %spread.1 = bf16[8,4,80,256]{3,2,1,0:T(8,128)(2,1)} custom-call(bf16[80,256]{1,0:T(8,128)(2,1)} %pad_maximum_fusion.1.own_ref), custom_call_target="tpu_custom_call" | custom-call | tf_op jit(solution)/shard_map/spread/pallas_call | solution.py:124
  49.8 1.9 slice_convert_fusion
  51.7 1.4 reshape.205
  58.2 15.1 %tok_gather_small.1.prompt_kv_ref = bf16[2,1024,256]{2,1,0:T(8,128)(2,1)} custom-call(bf16[2,128,256]{2,1,0:T(8,128)(2,1)} %bitcast.69), custom_call_target="tpu_custom_call" | custom-call | tf_op jit(solution)/shard_map/tok_gather_small/pallas_call | solution.py:708
  78.1 1.5 slice_reduce_fusion
  81.0 1.2 pad_maximum_fusion.states_ref
  82.3 89.1 %gather_attention.1 = (bf16[8,2,2048,256]{3,2,1,0:T(8,128)(2,1)}, bf16[8,384,256]{2,1,0:T(8,128)(2,1)}, bf16[8,384,256]{2,1,0:T(8,128)(2,1)}, f32[8,2,384]{2,1,0...) custom-call(s32[1]{0:T(128)} %dynamic_slice.12.owner_ref, ...), custom_call_target="tpu_custom_call" | custom-call | flops 12884901888 | bytes 250000000 | tf_op jit(solution)/shard_map/gather_attention/pallas_call | solution.py:1109
  171.4 2.1 reduce_sum.141
  173.5 61.8 %gather_and_up.1 = (bf16[8,384,2048]{2,1,0:T(8,128)(2,1)}, bf16[8,384,1024]{2,1,0:T(8,128)(2,1)}, bf16[8,384,1024]{2,1,0:T(8,128)(2,1)}) custom-call(bf16[384,2048]{1,0:T(8,128)(2,1)} %get-tuple-element.42.own_ref, bf16[2048,1024]{1,0:T(8,128)(2,1)} %all-gather.9.cloned.1.call-done.up_hbm.weight_hbm, f32[1,1024]{1,0:T(1,128)} %bitcast.75), custom_call_target="tpu_custom_call" | custom-call | flops 12884901888 | bytes 150000000 | tf_op jit(solution)/shard_map/gather_and_up/pallas_call | solution.py:318
  235.4 66.3 %product_and_reduce.2 = f32[384,2048]{1,0:T(8,128)} custom-call(bf16[8,384,1024]{2,1,0:T(8,128)(2,1)} %get-tuple-element.43.narrow_ref.active_ref, bf16[2048,1024]{1,0:T(8,128)(2,1)} %all-gather.11.cloned.1.call-done.weight_hbm.down_hbm), custom_call_target="tpu_custom_call" | custom-call | flops 12884901888 | bytes 150000000 | tf_op jit(solution)/shard_map/product_and_reduce/pallas_call | solution.py:653
  301.8 5.1 fusion.6
  306.9 1.7 copy-done.1
  308.6 1.5 convert_reduce_fusion.1
  310.0 69.8 %gather_and_grad.1 = (bf16[8,384,2048]{2,1,0:T(8,128)(2,1)}, bf16[8,384,1024]{2,1,0:T(8,128)(2,1)}, bf16[2048,1024]{1,0:T(8,128)(2,1)}, f32[1,1024]{1,0:T(1,128)}) custom-call(bf16[384,2048]{1,0:T(8,128)(2,1)} %get-tuple-element.72.own_ref, bf16[2048,1024]{1,0:T(8,128)(2,1)} %all-gather.11.cloned.1.call-done.weight_hbm.down_hbm, ...), custom_call_target="tpu_custom_call" | custom-call | flops 25769803776 | bytes 150000000 | tf_op jit(solution)/shard_map/gather_and_grad/pallas_call | solution.py:432
  380.0 63.9 %product_and_reduce.3 = (f32[384,2048]{1,0:T(8,128)}, bf16[2048,1024]{1,0:T(8,128)(2,1)}) custom-call(bf16[8,384,1024]{2,1,0:T(8,128)(2,1)} %get-tuple-element.48.narrow_ref, bf16[2048,1024]{1,0:T(8,128)(2,1)} %all-gather.9.cloned.1.call-done.up_hbm.weight_hbm, bf16[8,384,2048]{2,1,0:T(8,128)(2,1)} %get-tuple-element.49.refs_0_), custom_call_target="tpu_custom_call" | custom-call | flops 25769803776 | bytes 150000000 | tf_op jit(solution)/shard_map/product_and_reduce/pallas_call | solution.py:653
  443.9 3.2 multiply_reduce_fusion
  447.7 2.9 fusion.16
  450.7 6.8 %reduce-scatter.3.cloned.1.call-done = bf16[512,1024]{1,0:T(8,128)(2,1)} async-done(((bf16[2048,1024]{1,0:T(8,128)(2,1)}), bf16[512,1024]{1,0:T(8,128)(2,1)}) %reduce-scatter.3.cloned.1.call-update) | async-done | bytes 1048592 | tf_op jit(solution)/shard_map/reduce_scatter | solution.py:2085
  458.2 1.2 compare_convert_fusion.share_ref
  459.3 1.0 slice.132
  463.1 144.5 %backward_reduce.1 = (f32[512,256]{1,0:T(8,128)}, f32[512,256]{1,0:T(8,128)}, f32[64,256]{1,0:T(8,128)}, f32[16,2048]{1,0:T(8,128)}, bf16[384,2048]{1,0:T(8,128)(2,1)}) custom-call(s32[1]{0:T(128)} %dynamic_slice.12.owner_ref, f32[2]{0:T(128)} %compare_convert_fusion.share_ref, bf16[8,2,2048,256]{3,2,1,0:T(8,128)(2,1)} %get-tuple-element.44.weights_ref, ...), custom_call_target="tpu_custom_call" | custom-call | flops 20132659200 | bytes 250000000 | tf_op jit(solution)/shard_map/backward_reduce/pallas_call | solution.py:1821
  607.6 1.3 slice.121
  608.9 1.0 reshape.203
  609.9 2.3 slice.110
  613.1 1.6 convert_element_type.72
  616.5 1.2 slice_bitcast_fusion.5
  617.7 1.9 slice_bitcast_fusion.2
  619.6 2.8 convert_element_type.71
  (116 shorter events, 21.1 us)
Async XLA Ops:
  7.2 75.1 %all-gather.5.cloned.1.call-start = ((), (), s32[]{:S(2)}) async-start(), calls=%async_computation.2 | async-start | bytes 1310720 | tf_op jit(solution)/shard_map/all_gather | solution.py:1955
  7.9 74.3 %all-gather.7.cloned.1.call-start = ((), (), s32[]{:S(2)}) async-start(), calls=%async_computation.3 | async-start | bytes 1310720 | tf_op jit(solution)/shard_map/all_gather | solution.py:1956
  8.7 164.9 %all-gather.9.cloned.1.call-start = ((), (), s32[]{:S(2)}) async-start(), calls=%async_computation.4 | async-start | bytes 5242880 | tf_op jit(solution)/shard_map/all_gather | solution.py:1952
  9.4 226.0 %all-gather.11.cloned.1.call-start = ((), (), s32[]{:S(2)}) async-start(), calls=%async_computation.5 | async-start | bytes 5242880 | tf_op jit(solution)/shard_map/all_gather | solution.py:1953
  10.0 447.5 %reduce-scatter.3.cloned.1.call-start = ((), (), s32[]{:S(2)}) async-start(), calls=%async_computation.6 | async-start | bytes 5242880 | tf_op jit(solution)/shard_map/reduce_scatter | solution.py:2085
  49.8 4.7 copy-start.8
  51.7 3.0 copy-start.3
  51.7 3.0 copy-start.5
  53.4 0.8 copy-start.13
  53.5 1.5 copy-start.21
  54.7 1.6 copy-start.12
  56.2 26.0 %copy-start.9 = (bf16[384,2048]{1,0:T(8,128)(2,1)}, bf16[384,2048]{1,0:T(8,128)(2,1)S(1)}, u32[]{:S(2)}) copy-start(bf16[384,2048]{1,0:T(8,128)(2,1)S(1)} %fusion.5.normed_ref) | copy-start | bytes 4718596
  56.2 20.7 %copy-start.22 = (s32[8]{0:T(128)S(1)}, s32[8]{0:T(128)}, u32[]{:S(2)}) copy-start(s32[8]{0:T(128)} %param.23) | copy-start | bytes 100
  56.3 24.7 %copy-start.18 = (s32[2,128]{1,0:T(2,128)S(1)}, s32[2,128]{1,0:T(2,128)}, u32[]{:S(2)}) copy-start(s32[2,128]{1,0:T(2,128)} %param.26) | copy-start | bytes 3076
  56.3 24.7 %copy-start.20 = (s32[1,128]{1,0:T(1,128)S(1)}, s32[1,128]{1,0:T(1,128)}, u32[]{:S(2)}) copy-start(s32[1,128]{1,0:T(1,128)} %param.27) | copy-start | bytes 1540
  235.4 66.4 %copy-start = (f32[384,2048]{1,0:T(8,128)S(1)}, f32[384,2048]{1,0:T(8,128)}, u32[]{:S(2)}) copy-start(f32[384,2048]{1,0:T(8,128)} %get-tuple-element.41) | copy-start | bytes 9437188
  235.4 66.4 %copy-start.10 = (bf16[2,128,2048]{2,1,0:T(8,128)(2,1)S(1)}, bf16[2,128,2048]{2,1,0:T(8,128)(2,1)}, u32[]{:S(2)}) copy-start(bf16[2,128,2048]{2,1,0:T(8,128)(2,1)} %param.24) | copy-start | bytes 3145732
  235.4 66.4 %copy-start.14 = (bf16[1,128,2048]{2,1,0:T(8,128)(2,1)S(1)}, bf16[1,128,2048]{2,1,0:T(8,128)(2,1)}, u32[]{:S(2)}) copy-start(bf16[1,128,2048]{2,1,0:T(8,128)(2,1)} %param.25) | copy-start | bytes 1572868
  306.9 1.7 copy-start.1
  379.9 239.8 %reduce-scatter.5.cloned.1.call-start = ((), (), s32[]{:S(2)}) async-start(), calls=%async_computation.7 | async-start | bytes 5242880 | tf_op jit(solution)/shard_map/reduce_scatter | solution.py:2096
  443.9 3.3 copy-start.2
  443.9 3.9 copy-start.4
  450.7 8.6 %copy-start.7 = (bf16[384,2048]{1,0:T(8,128)(2,1)S(1)}, bf16[384,2048]{1,0:T(8,128)(2,1)}, u32[]{:S(2)}) copy-start(bf16[384,2048]{1,0:T(8,128)(2,1)} %get-tuple-element.75) | copy-start | bytes 4718596
  457.4 2.9 copy-start.19
  457.4 4.0 copy-start.6
  607.6 5.5 copy-start.11
  613.0 9.3 %copy-start.16 = (f32[512,256]{1,0:T(8,128)S(1)}, f32[512,256]{1,0:T(8,128)}, u32[]{:S(2)}) copy-start(f32[512,256]{1,0:T(8,128)} %get-tuple-element.118) | copy-start | bytes 1572868
  614.6 8.6 %copy-start.17 = (f32[64,256]{1,0:T(8,128)S(1)}, f32[64,256]{1,0:T(8,128)}, u32[]{:S(2)}) copy-start(f32[64,256]{1,0:T(8,128)} %get-tuple-element.120) | copy-start | bytes 196612
  614.6 9.2 %copy-start.15 = (f32[512,256]{1,0:T(8,128)S(1)}, f32[512,256]{1,0:T(8,128)}, u32[]{:S(2)}) copy-start(f32[512,256]{1,0:T(8,128)} %get-tuple-element.122) | copy-start | bytes 1572868
Sparse Core Ops, SparseCore 0:
  9.6 34.6 all-gather.4
  45.9 26.7 all-gather.6
  74.3 80.2 all-gather.8
  156.1 79.2 all-gather.10
  380.0 77.4 reduce-scatter.2
  459.7 77.2 reduce-scatter.4

commit v6 on v5

--- a/solution.py
+++ b/solution.py
@@ -82,11 +82,32 @@
     pl.semaphore_wait(barrier, len(devices))
 
 
+def paired_gather(source, place, send_sem, recv_sem):
+    here, on_x, on_y, on_chip, corner = block_of_eight()
+    over = [
+        remote(index, source, place(here), device, send_sem, recv_sem)
+        for index, device in enumerate((on_x, on_y, corner, on_chip))
+    ]
+    handed = [
+        remote(4 + index, place(device), place(device), on_chip, send_sem, recv_sem)
+        for index, device in enumerate((on_x, on_y, corner))
+    ]
+    for each in over:
+        each.start()
+    for each, then in zip(over, handed):
+        each.wait_recv()
+        then.start()
+    for each in [over[3]] + handed:
+        each.wait_recv()
+    for each in over + handed:
+        each.wait_send()
+
+
 def spread_kernel(groups, own_ref, out_ref, held, send_sem, recv_sem, over_send, over_recv):
-    here, peers = peers_of(8)
+    here, on_x, on_y, on_chip, corner = block_of_eight()
     group = lax.axis_index("grp")
     other_groups = [(group + turn) % groups for turn in range(1, groups)]
-    greet_all(peers, other_groups)
+    greet_all((on_x, on_y, on_chip, corner), other_groups)
     over = [
         pltpu.make_async_remote_copy(
             src_ref=own_ref,
@@ -103,16 +124,9 @@
     held[group] = own_ref[...]
     for each in over:
         each.wait_recv()
-    copies = [
-        remote(index, held, out_ref.at[here], peer, send_sem, recv_sem)
-        for index, peer in enumerate(peers)
-    ]
-    for each in copies:
-        each.start()
     out_ref[here] = held[...]
-    for each in copies:
-        each.wait_recv()
-    for each in copies + over:
+    paired_gather(held, lambda device: out_ref.at[device], send_sem, recv_sem)
+    for each in over:
         each.wait_send()
 
 
@@ -438,7 +452,7 @@
             jax.ShapeDtypeStruct((1, width), jnp.float32),
         ),
         in_specs=[anywhere] * 4,
-        out_specs=(anywhere, anywhere, anywhere, pl.BlockSpec(memory_space=pltpu.VMEM)),
+        out_specs=(anywhere,) * 3 + (pl.BlockSpec(memory_space=pltpu.VMEM),),
         scratch_shapes=[
             pltpu.VMEM(down_cols.shape, jnp.bfloat16),
             pltpu.VMEM((token_rows, model_width), jnp.bfloat16),
@@ -474,10 +488,12 @@
     *refs,
 ):
     if with_grad:
-        wide_ref, out_ref, grad_ref, *refs = refs
+        wide_ref, hidden_hbm, result_hbm, gain_ref, *refs = refs
+        grad_hidden_ref, grad_ref, branch_ref, sums_ref, *refs = refs
         *refs, wide, across, sums, wide_sem = refs
     else:
-        out_ref, *refs = refs
+        hidden_hbm, teacher_hbm, offset_ref, valid_ref, factor_ref, *refs = refs
+        out_ref, branch_ref, grad_result_ref, squares_ref, columns_ref, *refs = refs
     (
         weight,
         narrow,
@@ -486,11 +502,18 @@
         theirs,
         relayed,
         final,
+        hidden_rows,
+        other_rows,
         send_sem,
         recv_sem,
         weight_sem,
         narrow_sem,
+        row_sem,
     ) = refs
+    row_loads = (
+        pltpu.make_async_copy(hidden_hbm, hidden_rows, row_sem.at[0]),
+        pltpu.make_async_copy(result_hbm if with_grad else teacher_hbm, other_rows, row_sem.at[1]),
+    )
     rows = narrow.shape[1]
     half = rows // 2
     here, on_x, on_y, on_chip, corner = block_of_eight()
@@ -522,8 +545,7 @@
         def _(turn):
             at = pl.ds(pl.multiple_of(start + turn * step, step), step)
             come = pl.ds(pl.multiple_of(turn * step, step), step)
-            total = target[at, :].astype(jnp.float32) + other[come, :].astype(jnp.float32)
-            target[at, :] = total.astype(target.dtype)
+            target[at, :] = target[at, :] + other[come, :]
 
     def join(index):
         to_chip[index].wait_recv()
@@ -536,6 +558,8 @@
     x_second = copy(8, mine.at[1, second], final.at[0, second], on_x)
     y_first = copy(9, mine.at[2, first], final.at[1, first], on_y)
 
+    for each in row_loads:
+        each.start()
     for turn in range(8):
         pair, own = turn // 2, turn % 2
         if turn < 7:
@@ -605,11 +629,51 @@
     for each in (x_first, y_second, x_second, y_first):
         each.wait_recv()
 
-    @pl.loop(0, rows // step)
-    def _(turn):
-        at = pl.ds(pl.multiple_of(turn * step, step), step)
+    for each in row_loads:
+        each.wait()
+
+    def total_of(at):
         total = mine[3, at, :].astype(jnp.float32) + final[0, at, :].astype(jnp.float32)
-        out_ref[at, :] = total + final[1, at, :].astype(jnp.float32)
+        return total + final[1, at, :].astype(jnp.float32)
+
+    if with_grad:
+        sums_ref[...] = jnp.zeros_like(sums_ref)
+
+        @pl.loop(0, rows // step)
+        def _(turn):
+            at = chunk_of(turn, step)
+            grad_out = total_of(at)
+            scaled, inverse = norm_stats(hidden_rows[at, :])
+            weighted = grad_out * gain_ref[...]
+            grad_in = inverse * (
+                weighted
+                - jnp.mean(weighted, axis=-1, keepdims=True)
+                - scaled * jnp.mean(weighted * scaled, axis=-1, keepdims=True)
+            )
+            grad_hidden = other_rows[at, :] + grad_in
+            branch = grad_hidden.astype(jnp.bfloat16)
+            grad_hidden_ref[at, :] = grad_hidden
+            branch_ref[at, :] = branch
+            sums_ref[0:1, :] += jnp.sum(branch.astype(jnp.float32), axis=0, keepdims=True)
+            sums_ref[1:2, :] += jnp.sum(grad_out * scaled, axis=0, keepdims=True)
+            sums_ref[2:3, :] += jnp.sum(grad_out, axis=0, keepdims=True)
+
+    else:
+        squares_ref[...] = jnp.zeros_like(squares_ref)
+        columns_ref[...] = jnp.zeros_like(columns_ref)
+
+        @pl.loop(0, rows // step)
+        def _(turn):
+            at = chunk_of(turn, step)
+            result = hidden_rows[at, :] + total_of(at) + offset_ref[...]
+            differ = result - other_rows[at, :].astype(jnp.float32)
+            grad_result = factor_ref[at, :] * differ
+            branch = grad_result.astype(jnp.bfloat16)
+            out_ref[at, :] = result.astype(jnp.bfloat16)
+            grad_result_ref[at, :] = grad_result
+            branch_ref[at, :] = branch
+            squares_ref[...] += jnp.sum(valid_ref[at, :] * differ * differ, axis=0, keepdims=True)
+            columns_ref[...] += jnp.sum(branch.astype(jnp.float32), axis=0, keepdims=True)
 
     if with_grad:
         store.wait()
@@ -617,7 +681,7 @@
         each.wait_send()
 
 
-def product_and_reduce(narrow, weight, wide, call_number):
+def product_and_reduce(narrow, weight, wide, rows, second, call_number, *small):
     _, token_rows, width = narrow.shape
     model_width = weight.shape[0]
     with_grad = wide is not None
@@ -625,8 +689,9 @@
     inside = pl.BlockSpec(memory_space=pltpu.VMEM)
     dma = pltpu.SemaphoreType.DMA
     block = (token_rows, model_width)
-    kind = jnp.bfloat16
-    out_shape = [jax.ShapeDtypeStruct(block, jnp.float32)]
+    kind, long = jnp.bfloat16, jnp.float32
+    line = jax.ShapeDtypeStruct((1, model_width), long)
+    narrow_rows, long_rows = jax.ShapeDtypeStruct(block, kind), jax.ShapeDtypeStruct(block, long)
     scratch = [
         pltpu.VMEM(weight.shape, kind),
         pltpu.VMEM((2, token_rows, width), kind),
@@ -635,29 +700,44 @@
         pltpu.VMEM((4,) + block, kind),
         pltpu.VMEM((2, token_rows // 2, model_width), kind),
         pltpu.VMEM((2,) + block, kind),
+        pltpu.VMEM(block, long),
+        pltpu.VMEM(block, second.dtype),
         dma((10,)),
         dma((10,)),
         dma,
         dma((2,)),
+        dma((2,)),
     ]
     operands = [narrow, weight]
     if with_grad:
-        out_shape.append(jax.ShapeDtypeStruct(weight.shape, kind))
+        out_shape = (
+            long_rows,
+            jax.ShapeDtypeStruct(weight.shape, kind),
+            narrow_rows,
+            jax.ShapeDtypeStruct((8, model_width), long),
+        )
+        out_specs = (inside, anywhere, inside, inside)
         scratch += [
             pltpu.VMEM((2,) + block, kind),
             pltpu.VMEM((model_width, token_rows), kind),
-            pltpu.VMEM(weight.shape, jnp.float32),
+            pltpu.VMEM(weight.shape, long),
             dma((2,)),
         ]
         operands.append(wide)
+    else:
+        out_shape = (narrow_rows, narrow_rows, long_rows, line, line)
+        out_specs = (inside,) * 5
+    operands += [rows, second]
     return pl.pallas_call(
         functools.partial(product_reduce_kernel, with_grad),
-        out_shape=tuple(out_shape),
-        in_specs=[anywhere] * len(operands),
-        out_specs=(inside, anywhere)[: len(out_shape)],
+        out_shape=out_shape,
+        in_specs=[anywhere] * len(operands) + [inside] * len(small),
+        out_specs=out_specs,
         scratch_shapes=scratch,
         compiler_params=pltpu.CompilerParams(
-            collective_id=call_number, has_side_effects=True, vmem_limit_bytes=VMEM_BYTES
+            collective_id=call_number,
+            has_side_effects=True,
+            vmem_limit_bytes=62 * 1024 * 1024,
         ),
         cost_estimate=pl.CostEstimate(
             flops=(32 if with_grad else 16) * token_rows * model_width * width,
@@ -665,7 +745,7 @@
             transcendentals=0,
         ),
         name="product_and_reduce",
-    )(*operands)
+    )(*operands, *small)
 
 
 def peers_of(count):
@@ -673,48 +753,28 @@
     return here, [(here + step) % count for step in range(1, count)]
 
 
-def small_gather_kernel(count, own_ref, out_ref, send_sem, recv_sem, local_sem):
-    here, peers = peers_of(count)
+def small_gather_kernel(own_ref, out_ref, send_sem, recv_sem):
+    here, on_x, on_y, on_chip, corner = block_of_eight()
     rows = own_ref.shape[1]
-    place = pl.ds(pl.multiple_of(here * rows, rows), rows)
-    greet(peers)
-    own = pltpu.make_async_copy(own_ref, out_ref.at[:, place, :], local_sem)
-    copies = [
-        pltpu.make_async_remote_copy(
-            src_ref=own_ref,
-            dst_ref=out_ref.at[:, place, :],
-            send_sem=send_sem.at[index],
-            recv_sem=recv_sem.at[index],
-            device_id={"tok": peers[index]},
-            device_id_type=MESH,
-        )
-        for index in range(count - 1)
-    ]
-    for each in copies:
-        each.start()
-    own.start()
-    for each in copies:
-        each.wait_recv()
-    for each in copies:
-        each.wait_send()
-    own.wait()
+
+    def place(device):
+        return pl.ds(pl.multiple_of(device * rows, rows), rows)
+
+    greet((on_x, on_y, on_chip, corner))
+    out_ref[:, place(here), :] = own_ref[...]
+    paired_gather(own_ref, lambda device: out_ref.at[:, place(device), :], send_sem, recv_sem)
 
 
 def tok_gather_small(own, call_number, kernels):
     if not kernels:
         return lax.all_gather(own, "tok", axis=1, tiled=True)
-    count = 8
     prompts, rows, columns = own.shape
     return pl.pallas_call(
-        functools.partial(small_gather_kernel, count),
-        out_shape=jax.ShapeDtypeStruct((prompts, count * rows, columns), own.dtype),
-        in_specs=[pl.BlockSpec(memory_space=pl.ANY)],
-        out_specs=pl.BlockSpec(memory_space=pl.ANY),
-        scratch_shapes=[
-            pltpu.SemaphoreType.DMA((count - 1,)),
-            pltpu.SemaphoreType.DMA((count - 1,)),
-            pltpu.SemaphoreType.DMA,
-        ],
+        small_gather_kernel,
+        out_shape=jax.ShapeDtypeStruct((prompts, 8 * rows, columns), own.dtype),
+        in_specs=[pl.BlockSpec(memory_space=pltpu.VMEM)],
+        out_specs=pl.BlockSpec(memory_space=pltpu.VMEM),
+        scratch_shapes=[pltpu.SemaphoreType.DMA((7,)), pltpu.SemaphoreType.DMA((7,))],
         compiler_params=pltpu.CompilerParams(collective_id=call_number, has_side_effects=True),
         name="tok_gather_small",
     )(own)
@@ -944,8 +1004,7 @@
     heads,
     prompt_rows,
     owner_ref,
-    query_own_ref,
-    output_own_ref,
+    own_ref,
     normed_ref,
     bias_ref,
     prompt_kv_ref,
@@ -971,23 +1030,19 @@
     def copy(index, source, target, device):
         return remote(index, source, target, device, send_sem, recv_sem)
 
-    own_refs = (query_own_ref, output_own_ref)
-    to_x = [copy(0 + kind, own_refs[kind], weights_ref.at[here, kind], on_x) for kind in (0, 1)]
-    to_y = [copy(2 + kind, own_refs[kind], weights_ref.at[here, kind], on_y) for kind in (0, 1)]
-    to_chip = [
-        copy(4 + kind, own_refs[kind], weights_ref.at[here, kind], on_chip) for kind in (0, 1)
-    ]
-    keep = [
-        pltpu.make_async_copy(own_refs[kind], weights_ref.at[here, kind], local_sem.at[kind])
-        for kind in (0, 1)
-    ]
-    x_to_y = copy(6, weights_ref.at[on_x, 0], weights_ref.at[on_x, 0], on_y)
-    y_to_x = copy(7, weights_ref.at[on_y, 1], weights_ref.at[on_y, 1], on_x)
-    x_to_chip = copy(8, weights_ref.at[on_x], weights_ref.at[on_x], on_chip)
-    y_to_chip = copy(9, weights_ref.at[on_y], weights_ref.at[on_y], on_chip)
+    def kind_of(device, kind):
+        return weights_ref.at[device, :, kind]
+
+    to_x = [copy(0 + kind, own_ref.at[:, kind], kind_of(here, kind), on_x) for kind in (0, 1)]
+    to_y = [copy(2 + kind, own_ref.at[:, kind], kind_of(here, kind), on_y) for kind in (0, 1)]
+    to_chip = [copy(4, own_ref, weights_ref.at[here], on_chip)]
+    keep = [pltpu.make_async_copy(own_ref, weights_ref.at[here], local_sem)]
+    x_to_y = copy(5, kind_of(on_x, 0), kind_of(on_x, 0), on_y)
+    y_to_x = copy(6, kind_of(on_y, 1), kind_of(on_y, 1), on_x)
+    x_to_chip = copy(7, weights_ref.at[on_x], weights_ref.at[on_x], on_chip)
+    y_to_chip = copy(8, weights_ref.at[on_y], weights_ref.at[on_y], on_chip)
     corner_to_chip = [
-        copy(10 + kind, weights_ref.at[corner, kind], weights_ref.at[corner, kind], on_chip)
-        for kind in (0, 1)
+        copy(9 + kind, kind_of(corner, kind), kind_of(corner, kind), on_chip) for kind in (0, 1)
     ]
 
     greet((on_x, on_y, on_chip))
@@ -1001,10 +1056,9 @@
 
         @pl.when(turn == 0)
         def _():
-            for kind in (0, 1):
-                load = pltpu.make_async_copy(own_refs[kind], held.at[kind], load_sem.at[kind])
-                load.start()
-                load.wait()
+            load = pltpu.make_async_copy(own_ref, held, load_sem)
+            load.start()
+            load.wait()
 
         @pl.when(turn == 1)
         def _():
@@ -1044,14 +1098,9 @@
 
         @pl.when(turn > 0)
         def _():
-            for kind in (0, 1):
-                pltpu.make_async_copy(
-                    weights_ref.at[block, kind], held.at[kind], load_sem.at[kind]
-                ).start()
-            for kind in (0, 1):
-                pltpu.make_async_copy(
-                    weights_ref.at[block, kind], held.at[kind], load_sem.at[kind]
-                ).wait()
+            load = pltpu.make_async_copy(weights_ref.at[block], held, load_sem)
+            load.start()
+            load.wait()
 
         queries, mixture, logs = forward_block(
             prompts,
@@ -1060,7 +1109,7 @@
             here * prompt_rows,
             owner_ref,
             normed_ref,
-            held[0],
+            held[:, 0].reshape(-1, held.shape[-1]),
             bias_ref[block],
             prompt_kv_ref,
             answer_kv_ref,
@@ -1072,7 +1121,7 @@
                 log_ref[block, head : head + 1, place] = log_row[
                     :, head * rows : (head + 1) * rows
                 ]
-        hidden_ref[...] += transposed_product(mixture, held[1])
+        hidden_ref[...] += transposed_product(mixture, held[:, 1].reshape(-1, held.shape[-1]))
 
     scaled, _ = norm_stats(hidden_ref[...])
     second_ref[...] = (scaled * gain_ref[...] + shift_ref[...]).astype(jnp.bfloat16)
@@ -1084,8 +1133,7 @@
 
 def gather_attention(
     owning,
-    query_own,
-    output_own,
+    projections,
     normed,
     query_offset,
     prompt_kv,
@@ -1100,7 +1148,7 @@
     call_number,
 ):
     token_rows, model_width = normed.shape
-    block = query_own.shape[1]
+    block = projections.shape[3]
     heads = block // HEAD_WIDTH
     inside = pl.BlockSpec(memory_space=pltpu.VMEM)
     anywhere = pl.BlockSpec(memory_space=pl.ANY)
@@ -1109,21 +1157,21 @@
     return pl.pallas_call(
         functools.partial(gather_attention_kernel, prompts, answers, heads, prompt_rows),
         out_shape=(
-            jax.ShapeDtypeStruct((8, 2, model_width, block), jnp.bfloat16),
+            jax.ShapeDtypeStruct((8,) + projections.shape, jnp.bfloat16),
             by_step,
             by_step,
             jax.ShapeDtypeStruct((8, heads, token_rows), jnp.float32),
             jax.ShapeDtypeStruct((token_rows, model_width), jnp.float32),
             jax.ShapeDtypeStruct((token_rows, model_width), jnp.bfloat16),
         ),
-        in_specs=[pl.BlockSpec(memory_space=pltpu.SMEM), anywhere, anywhere] + [inside] * 8,
+        in_specs=[pl.BlockSpec(memory_space=pltpu.SMEM), anywhere] + [inside] * 8,
         out_specs=(anywhere,) + (inside,) * 5,
         scratch_shapes=[
-            pltpu.VMEM((2, model_width, block), jnp.bfloat16),
-            dma((12,)),
-            dma((12,)),
-            dma((2,)),
-            dma((2,)),
+            pltpu.VMEM(projections.shape, jnp.bfloat16),
+            dma((11,)),
+            dma((11,)),
+            dma,
+            dma,
         ],
         compiler_params=pltpu.CompilerParams(
             collective_id=call_number, has_side_effects=True, vmem_limit_bytes=VMEM_BYTES
@@ -1136,8 +1184,7 @@
         name="gather_attention",
     )(
         owning,
-        query_own,
-        output_own,
+        projections,
         normed,
         query_offset.reshape(8, 1, block),
         prompt_kv,
@@ -1166,7 +1213,6 @@
     prompt_kv_ref,
     answer_kv_ref,
     normed_across,
-    branch_across,
     key_sums,
     own_sums,
     grad_normed_ref,
@@ -1174,7 +1220,6 @@
     width = HEAD_WIDTH
     scale = HEAD_WIDTH ** (-0.5)
     length = prompt_kv_ref.shape[1]
-    grad_output_block = plain_product(branch_across[...], mixture).astype(jnp.bfloat16)
     grad_mixture = plain_product(branch_ref[...], output_block).astype(jnp.bfloat16)
 
     def backward(keys, values, stacked, grad_stacked, log_row, inner_row, allowed):
@@ -1247,7 +1292,7 @@
     grad_query_block = plain_product(normed_across[...], grad_queries).astype(jnp.bfloat16)
     grad_normed_ref[...] += transposed_product(grad_queries, query_block)
     grad_bias = jnp.sum(grad_queries.astype(jnp.float32), axis=0, keepdims=True)
-    return grad_query_block, grad_output_block, grad_bias
+    return grad_query_block, grad_bias
 
 
 def attention_backward_kernel(
@@ -1292,7 +1337,8 @@
     query_block, output_block = query_ref[0, 0], output_ref[0, 0]
     groups = grad_weights_ref.shape[1]
     weight_rows = query_block.shape[0] // groups
-    grad_query_block, grad_output_block, grad_bias = backward_block(
+    grad_output_block = plain_product(branch_across[...], mixture_ref[0]).astype(jnp.bfloat16)
+    grad_query_block, grad_bias = backward_block(
         prompts,
         answers,
         heads,
@@ -1309,7 +1355,6 @@
         prompt_kv_ref,
         answer_kv_ref,
         normed_across,
-        branch_across,
         key_sums,
         own_sums,
         grad_normed_ref,
@@ -1419,8 +1464,49 @@
     )
 
 
+class PairedSum:
+    def __init__(self, part, pair, sent, come, send_sem, recv_sem):
+        here, on_x, on_y, on_chip, corner = block_of_eight()
+        shift = on_chip - here
+        self.places = (here, on_x, on_y, corner)
+        self.part, self.pair, self.sent, self.come = part, pair, sent, come
+        self.to_chip = [
+            remote(index, part(place + shift), pair.at[index], on_chip, send_sem, recv_sem)
+            for index, place in enumerate(self.places)
+        ]
+        self.over = [
+            remote(3 + index, sent.at[index], come.at[index - 1], place, send_sem, recv_sem)
+            for index, place in enumerate(self.places)
+            if index
+        ]
+
+    def start(self):
+        for each in self.to_chip:
+            each.start()
+
+    def pass_on(self):
+        for each in self.to_chip:
+            each.wait_recv()
+        for index, place in enumerate(self.places):
+            total = self.part(place)[...].astype(jnp.float32)
+            total = total + self.pair[index].astype(jnp.float32)
+            self.sent[index] = total.astype(self.sent.dtype)
+        for each in self.over:
+            each.start()
+
+    def total(self):
+        total = self.sent[0].astype(jnp.float32)
+        for index, each in enumerate(self.over):
+            each.wait_recv()
+            total = total + self.come[index].astype(jnp.float32)
+        return total
+
+    def finish(self):
+        for each in self.to_chip + self.over:
+            each.wait_send()
+
+
 VECTOR_ROWS = 16
-KNOWN_ROWS = 8
 
 
 def backward_reduce_kernel(
@@ -1443,11 +1529,16 @@
     states_ref,
     gain_ref,
     keyval_ref,
-    known_ref,
+    known_up_ref,
+    known_sums_ref,
+    known_columns_ref,
+    known_squares_ref,
     grad_query_ref,
     grad_output_ref,
     grad_keyval_ref,
     vectors_ref,
+    own_vectors_ref,
+    own_up_ref,
     grad_input_ref,
     normed_across,
     branch_across,
@@ -1463,9 +1554,13 @@
     final,
     come,
     kv_part,
+    kv_pair,
+    kv_sent,
     kv_come,
     kv_rows,
     keyval_part,
+    keyval_pair,
+    keyval_sent,
     keyval_come,
     keyval_sum,
     keyval_over,
@@ -1488,10 +1583,10 @@
     _, peers = peers_of(8)
     group = lax.axis_index("grp")
     other_groups = [(group + turn) % groups for turn in range(1, groups)]
-    model_width, block = held.shape[1:]
+    model_width, block = kept.shape[1:]
     chunk_rows = model_width // groups
     step = 64
-    counter = iter(range(4 + 6 * groups))
+    counter = iter(range(8 + 6 * groups))
 
     def copy(source, target, device):
         return remote(next(counter), source, target, device, send_sem, recv_sem)
@@ -1524,15 +1619,37 @@
         for chunk in range(groups)
     ]
     chunks = range(groups)
-    to_chip = [copy(kept.at[turn % 2], theirs.at[turn], on_chip) for turn in range(4)]
-    corner_x = [copy(kept.at[2, 0, span], relayed.at[0, span], on_x) for span in spans]
-    corner_y = [copy(kept.at[2, 1, span], relayed.at[1, span], on_y) for span in spans]
-    x_first = [copy(kept.at[4, 0, span], final.at[0, 0, span], on_x) for span in spans]
-    y_second = [copy(kept.at[3, 1, span], final.at[1, 1, span], on_y) for span in spans]
-    x_second = [copy(kept.at[4, 1, span], final.at[0, 1, span], on_x) for span in spans]
-    y_first = [copy(kept.at[3, 0, span], final.at[1, 0, span], on_y) for span in spans]
+    by_x, by_y = chunks[: groups // 2], chunks[groups // 2 :]
+    kinds = (0, 1)
+
+    def mine(place, kind):
+        return kept.at[4 + 2 * place + kind]
+
+    def pieces_to(place, target, device):
+        return [
+            [copy(mine(place, kind).at[span], target(kind).at[span], device) for span in spans]
+            for kind in kinds
+        ]
+
+    to_chip = [
+        [copy(kept.at[place], theirs.at[place, kind], on_chip) for place in range(4)]
+        for kind in kinds
+    ]
+    corners = [
+        [
+            copy(
+                mine(0, kind).at[spans[chunk]],
+                relayed.at[kind, spans[chunk]],
+                on_x if chunk in by_x else on_y,
+            )
+            for chunk in chunks
+        ]
+        for kind in kinds
+    ]
+    to_x = pieces_to(2, lambda kind: final.at[0, kind], on_x)
+    to_y = pieces_to(1, lambda kind: final.at[1, kind], on_y)
     across = [
-        [over(2 * turn + kind, kept.at[5, kind, spans[turn]], come.at[turn, kind], turn) for kind in (0, 1)]
+        [over(2 * turn + kind, mine(3, kind).at[spans[turn]], come.at[turn, kind], turn) for kind in kinds]
         for turn in range(groups - 1)
     ]
 
@@ -1542,11 +1659,21 @@
     def prompt_place(device):
         return pl.ds(pl.multiple_of(device * prompt_rows, prompt_rows), prompt_rows)
 
-    kv_copies = to_peers(
-        0, lambda peer: kv_part.at[:, prompt_place(peer), :], lambda index: kv_come.at[index]
-    )
-    keyval_copies = to_peers(
-        1, lambda peer: keyval_part.at[:, peer], lambda index: keyval_come.at[index]
+    kv_sums = PairedSum(
+        lambda device: kv_part.at[:, prompt_place(device), :],
+        kv_pair,
+        kv_sent,
+        kv_come,
+        peer_send.at[0],
+        peer_recv.at[0],
+    )
+    keyval_sums = PairedSum(
+        lambda device: keyval_part.at[:, device],
+        keyval_pair,
+        keyval_sent,
+        keyval_come,
+        peer_send.at[1],
+        peer_recv.at[1],
     )
     vector_copies = to_peers(
         2, lambda peer: vectors.at[:, lanes(peer)], lambda index: vector_come.at[index]
@@ -1572,25 +1699,80 @@
     key_sums[...] = jnp.zeros_like(key_sums)
     own_sums[...] = jnp.zeros_like(own_sums)
     grad_normed[...] = jnp.zeros_like(grad_normed)
-    vectors[:KNOWN_ROWS, :] = known_ref[:KNOWN_ROWS, :]
-    vectors[KNOWN_ROWS:, :] = known_ref[KNOWN_ROWS:, :]
+    vectors[...] = jnp.zeros_like(vectors)
+    vectors[: known_up_ref.shape[0], :] = known_up_ref[...]
+    vectors[4:7, :] = known_sums_ref[0:3, :]
+    vectors[7:8, :] = known_columns_ref[...]
+    squares = jnp.sum(known_squares_ref[...], axis=1, keepdims=True)
+    vectors[12:13, :] = jnp.broadcast_to(squares, (1, model_width))
 
     def add_into(target, other, rows):
         @pl.loop(0, rows // step)
         def _(turn):
             at = chunk_of(turn, step)
-            total = target[at, :].astype(jnp.float32) + other[at, :].astype(jnp.float32)
-            target[at, :] = total.astype(target.dtype)
-
-    def join(turn):
-        to_chip[turn].wait_recv()
-        for kind in (0, 1):
-            add_into(kept.at[2 + turn, kind], theirs.at[turn, kind], model_width)
+            target[at, :] = target[at, :] + other[at, :]
+
+    def join(kind, place):
+        to_chip[kind][place].wait_recv()
+        add_into(mine(place, kind), theirs.at[place, kind], model_width)
+
+    def direct(kind, chunk):
+        (to_x if chunk in by_x else to_y)[kind][chunk].start()
+
+    def relay(kind, chunk):
+        corners[kind][chunk].wait_recv()
+        place, then = (1, to_y) if chunk in by_x else (2, to_x)
+        span = spans[chunk]
+        add_into(mine(place, kind).at[span], relayed.at[kind, span], chunk_rows)
+        then[kind][chunk].start()
+
+    def close(kind, chunk):
+        span = spans[chunk]
+        for source, part in enumerate((to_x, to_y)):
+            part[kind][chunk].wait_recv()
+            add_into(mine(3, kind).at[span], final.at[source, kind, span], chunk_rows)
+        if chunk < groups - 1:
+            across[chunk][kind].start()
+
+    def slot_of(turn, kind):
+        place = turn // 2
+        return (1 - turn % 2) * place + (turn % 2) * (4 + 2 * place + kind)
+
+    def send_to_chip(turn, kind):
+        for place in range(4):
+
+            @pl.when(turn == 2 * place)
+            def _():
+                to_chip[kind][place].start()
+
+    @pl.loop(0, 8)
+    def _(turn):
+        load = pltpu.make_async_copy(
+            mixture_ref.at[bits_away(7 - turn)], pair.at[1], load_sem.at[2]
+        )
+        load.start()
+        load.wait()
+        kept[slot_of(turn, 1)] = plain_product(branch_across[...], pair[1]).astype(jnp.bfloat16)
+        send_to_chip(turn, 1)
+
+        @pl.when(turn == 2)
+        def _():
+            join(1, 0)
+            for chunk in chunks:
+                corners[1][chunk].start()
+
+        for place in (1, 2):
+
+            @pl.when(turn == 2 * place + 2)
+            def _():
+                join(1, place)
+
+    for chunk in chunks:
+        direct(1, chunk)
 
     @pl.loop(0, 8)
     def _(turn):
         source = bits_away(7 - turn)
-        slot = (turn % 2) * (2 + turn // 2) + (1 - turn % 2) * ((turn // 2) % 2)
         loads = (
             pltpu.make_async_copy(weights_ref.at[source], held, load_sem.at[0]),
             pltpu.make_async_copy(queries_ref.at[source], pair.at[0], load_sem.at[1]),
@@ -1598,15 +1780,15 @@
         )
         for each in loads:
             each.start()
-        for index in (2, 3):
-
-            @pl.when(turn == 2 * index)
+        for place in range(4):
+
+            @pl.when(turn == 2 * place)
             def _():
-                to_chip[index - 2].wait_send()
+                to_chip[1][place].wait_send()
 
         for each in loads:
             each.wait()
-        grad_query_block, grad_output_block, grad_bias = backward_block(
+        grad_query_block, grad_bias = backward_block(
             prompts,
             answers,
             heads,
@@ -1615,82 +1797,73 @@
             share_ref,
             normed_ref,
             branch_ref,
-            held[0],
-            held[1],
+            held[:, 0].reshape(-1, block),
+            held[:, 1].reshape(-1, block),
             pair[0],
             pair[1],
             log_ref.at[source],
             prompt_kv_ref,
             answer_kv_ref,
             normed_across,
-            branch_across,
             key_sums,
             own_sums,
             grad_normed,
         )
-        kept[slot, 0] = grad_query_block
-        kept[slot, 1] = grad_output_block
+        kept[slot_of(turn, 0)] = grad_query_block
         vectors[10:11, lanes(source)] = grad_bias
-        for index in range(4):
-
-            @pl.when(turn == 2 * index)
-            def _():
-                to_chip[index].start()
+        send_to_chip(turn, 0)
+
+        @pl.when(turn == 1)
+        def _():
+            for chunk in chunks:
+                relay(1, chunk)
 
         @pl.when(turn == 2)
         def _():
-            join(0)
+            join(0, 0)
             for chunk in chunks:
-                corner_x[chunk].start()
-                corner_y[chunk].start()
+                corners[0][chunk].start()
 
         @pl.when(turn == 4)
         def _():
-            join(1)
-            for chunk in chunks[:2]:
-                y_second[chunk].start()
+            join(0, 1)
+            join(1, 3)
+
+        @pl.when(turn == 5)
+        def _():
+            for chunk in chunks:
+                close(1, chunk)
 
         @pl.when(turn == 6)
         def _():
-            join(2)
-            for chunk in chunks[:2]:
-                x_first[chunk].start()
+            join(0, 2)
+            for chunk in (by_x[0], by_y[0]):
+                direct(0, chunk)
+            for chunk in (by_x[0], by_y[0]):
+                relay(0, chunk)
+
+        @pl.when(turn == 7)
+        def _():
+            direct(0, by_x[1])
+            relay(0, by_x[1])
 
     kv_part[:, :, :width] = (key_sums[:, :, :width] * scale).astype(jnp.bfloat16)
     kv_part[:, :, width:] = key_sums[:, :, width:].astype(jnp.bfloat16)
-    for each in kv_copies:
-        each.start()
-    for chunk in chunks:
-        span = spans[chunk]
-        corner_y[chunk].wait_recv()
-        add_into(kept.at[4, 1, span], relayed.at[1, span], chunk_rows)
-        x_second[chunk].start()
-        corner_x[chunk].wait_recv()
-        add_into(kept.at[3, 0, span], relayed.at[0, span], chunk_rows)
-        y_first[chunk].start()
-        if chunk + 2 < groups:
-            x_first[chunk + 2].start()
-            y_second[chunk + 2].start()
-    join(3)
-
-    def close(chunk):
-        span = spans[chunk]
-        for kind, parts in ((0, (x_first, y_first)), (1, (x_second, y_second))):
-            for part in parts:
-                part[chunk].wait_recv()
-            for turn in (0, 1):
-                add_into(kept.at[5, kind, span], final.at[turn, kind, span], chunk_rows)
-            if chunk < groups - 1:
-                across[chunk][kind].start()
-
-    for each in kv_copies:
-        each.wait_recv()
+    kv_sums.start()
+    join(0, 3)
+    kv_sums.pass_on()
+    for part in (to_x, to_y):
+        part[0][by_x[0]].wait_send()
+    direct(0, by_y[1])
+    relay(0, by_y[1])
+    close(0, by_x[0])
+
     own_prompt = prompts * prompt_rows
+    total = kv_sums.total()
     for prompt in range(prompts):
-        total = kv_part[prompt, prompt_place(here), :].astype(jnp.float32)
-        for index in range(len(peers)):
-            total = total + kv_come[index, prompt].astype(jnp.float32)
-        kv_rows[prompt * prompt_rows : (prompt + 1) * prompt_rows, :] = total.astype(jnp.bfloat16)
+        kv_rows[prompt * prompt_rows : (prompt + 1) * prompt_rows, :] = total[prompt].astype(
+            jnp.bfloat16
+        )
     kv_rows[own_prompt:, :width] = (own_sums[:, :width] * scale).astype(jnp.bfloat16)
     kv_rows[own_prompt:, width:] = own_sums[:, width:].astype(jnp.bfloat16)
     keyval_part[...] = (
@@ -1698,21 +1871,21 @@
         .astype(jnp.bfloat16)
         .reshape(keyval_part.shape)
     )
-    for each in keyval_copies:
-        each.start()
-    close(0)
+    keyval_sums.start()
+    close(0, by_y[0])
+    keyval_sums.pass_on()
     load_hidden.wait()
     vectors[11:12, :width] = jnp.sum(
         kv_rows[:, width:].astype(jnp.float32), axis=0, keepdims=True
     )
-    piece = 64
-    vectors[8:10, :] = jnp.zeros((2, model_width), jnp.float32)
+    piece = 16
+    grad_normed[...] += transposed_product(kv_rows[...], keyval_ref[...])
 
     @pl.loop(0, states_ref.shape[0] // piece)
     def _(turn):
         at = chunk_of(turn, piece)
         scaled, inverse = norm_stats(states_ref[at, :].astype(jnp.float32))
-        grad_out = grad_normed[at, :] + transposed_product(kv_rows[at, :], keyval_ref[...])
+        grad_out = grad_normed[at, :]
         weighted = grad_out * gain_ref[...]
         grad_in = inverse * (
             weighted
@@ -1725,14 +1898,7 @@
 
     for each in vector_copies:
         each.start()
-    close(1)
-    for each in keyval_copies:
-        each.wait_recv()
-    for other in range(groups):
-        total = keyval_part[other, here].astype(jnp.float32)
-        for index in range(len(peers)):
-            total = total + keyval_come[index, other].astype(jnp.float32)
-        keyval_sum[other] = total.astype(jnp.bfloat16)
+    keyval_sum[...] = keyval_sums.total().astype(jnp.bfloat16)
     for each in keyval_across:
         each.start()
     for each in vector_copies:
@@ -1743,7 +1909,7 @@
     vectors[:, lanes(here)] = total
     for each in vector_across:
         each.start()
-    close(2)
+    close(0, by_x[1])
     for each in vector_across:
         each.wait_recv()
     total = vectors[:, lanes(here)]
@@ -1753,8 +1919,7 @@
     for each in vector_out:
         each.start()
     vectors_ref[:, lanes(here)] = vector_sum[...]
-    for chunk in chunks[3:]:
-        close(chunk)
+    close(0, by_y[1])
     for each in keyval_across:
         each.wait_recv()
     total = keyval_sum[group].astype(jnp.float32)
@@ -1769,16 +1934,37 @@
         @pl.loop(0, chunk_rows // step)
         def _(turn):
             at = chunk_of(turn, step)
-            total = kept[5, kind, pl.ds(own + turn * step, step), :].astype(jnp.float32)
+            total = kept[10 + kind, pl.ds(own + turn * step, step), :].astype(jnp.float32)
             for other in range(groups - 1):
                 total = total + come[other, kind, at, :].astype(jnp.float32)
             out_ref[at, :] = total
 
     for each in vector_out:
         each.wait_recv()
-    for each in to_chip[2:] + corner_x + corner_y + x_first + y_second + x_second + y_first:
+    device = group * 8 + here
+    share = model_width // (8 * groups)
+    parts = width // share
+    columns = vectors_ref[:, chunk_of(device // parts, width)]
+    picked = columns
+    for part in range(1, parts):
+        moved = jnp.concatenate([columns[:, part * share :], columns[:, : part * share]], axis=1)
+        picked = jnp.where(device % parts == part, moved, picked)
+    own_vectors_ref[...] = picked
+    up_share = own_up_ref.shape[1]
+    in_row = model_width // up_share
+    up_columns = vectors_ref[:, chunk_of(device % in_row, up_share)]
+    up_own = jnp.zeros((1, up_share), jnp.float32)
+    for row in range(known_up_ref.shape[0]):
+        up_own = jnp.where(device // in_row == row, up_columns[row : row + 1, :], up_own)
+    own_up_ref[...] = up_own
+    for each in to_chip[0] + corners[0] + corners[1] + to_x[1] + to_y[1]:
         each.wait_send()
-    for each in kv_copies + keyval_copies + vector_copies + vector_out:
+    for chunk in chunks[1:]:
+        to_x[0][chunk].wait_send()
+        to_y[0][chunk].wait_send()
+    kv_sums.finish()
+    keyval_sums.finish()
+    for each in vector_copies + vector_out:
         each.wait_send()
     for each in sum(across, []) + keyval_across + vector_across:
         each.wait_send()
@@ -1799,7 +1985,10 @@
     states,
     gain,
     keyval_full,
-    known,
+    known_up,
+    known_sums,
+    known_columns,
+    known_squares,
     groups,
     prompts,
     answers,
@@ -1807,7 +1996,7 @@
     call_number,
 ):
     token_rows, model_width = normed.shape
-    block = weights.shape[3]
+    block = weights.shape[4]
     heads = block // HEAD_WIDTH
     keyval_width = keyval_full.shape[1]
     weight_rows = model_width // groups
@@ -1825,10 +2014,12 @@
             jax.ShapeDtypeStruct((weight_rows, block), wide),
             jax.ShapeDtypeStruct((keyval_rows, keyval_width), wide),
             jax.ShapeDtypeStruct((VECTOR_ROWS, model_width), wide),
+            jax.ShapeDtypeStruct((VECTOR_ROWS, HEAD_WIDTH), wide),
+            jax.ShapeDtypeStruct((1, known_up.size // (8 * groups)), wide),
             jax.ShapeDtypeStruct((token_rows, model_width), kind),
         ),
-        in_specs=[scalars] * 2 + [anywhere] * 4 + [inside] * 9,
-        out_specs=(inside,) * 5,
+        in_specs=[scalars] * 2 + [anywhere] * 4 + [inside] * 12,
+        out_specs=(inside,) * 7,
         scratch_shapes=[
             pltpu.VMEM((model_width, token_rows), kind),
             pltpu.VMEM((model_width, token_rows), kind),
@@ -1836,26 +2027,30 @@
             pltpu.VMEM(answer_kv.shape, wide),
             pltpu.VMEM((token_rows, model_width), wide),
             pltpu.VMEM((token_rows, model_width), wide),
-            pltpu.VMEM((2, model_width, block), kind),
+            pltpu.VMEM(weights.shape[1:], kind),
             pltpu.VMEM((2, token_rows, block), kind),
-            pltpu.VMEM((6, 2, model_width, block), kind),
+            pltpu.VMEM((12, model_width, block), kind),
             pltpu.VMEM((4, 2, model_width, block), kind),
             pltpu.VMEM((2, model_width, block), kind),
             pltpu.VMEM((2, 2, model_width, block), kind),
             pltpu.VMEM((others, 2, weight_rows, block), kind),
             pltpu.VMEM(prompt_kv.shape, kind),
-            pltpu.VMEM((7, prompts, prompt_rows, keyval_width), kind),
+            pltpu.VMEM((4, prompts, prompt_rows, keyval_width), kind),
+            pltpu.VMEM((4, prompts, prompt_rows, keyval_width), kind),
+            pltpu.VMEM((3, prompts, prompt_rows, keyval_width), kind),
             pltpu.VMEM((token_rows, keyval_width), kind),
             pltpu.VMEM((groups, 8, keyval_rows, keyval_width), kind),
-            pltpu.VMEM((7, groups, keyval_rows, keyval_width), kind),
+            pltpu.VMEM((4, groups, keyval_rows, keyval_width), kind),
+            pltpu.VMEM((4, groups, keyval_rows, keyval_width), kind),
+            pltpu.VMEM((3, groups, keyval_rows, keyval_width), kind),
             pltpu.VMEM((groups, keyval_rows, keyval_width), kind),
             pltpu.VMEM((others, keyval_rows, keyval_width), kind),
             pltpu.VMEM((VECTOR_ROWS, model_width), wide),
             pltpu.VMEM((7, VECTOR_ROWS, block), wide),
             pltpu.VMEM((VECTOR_ROWS, block), wide),
             pltpu.VMEM((others, VECTOR_ROWS, block), wide),
-            dma((4 + 6 * groups,)),
-            dma((4 + 6 * groups,)),
+            dma((8 + 6 * groups,)),
+            dma((8 + 6 * groups,)),
             dma((4 * others,)),
             dma((4 * others,)),
             dma((4, 7)),
@@ -1889,7 +2084,10 @@
         states,
         gain.reshape(1, -1),
         keyval_full,
-        known,
+        known_up,
+        known_sums,
+        known_columns,
+        known_squares,
     )
 
 
@@ -1952,23 +2150,24 @@
     up_cols = lax.all_gather(up_weight, "grp", axis=0, tiled=True)
     down_cols = lax.all_gather(down_weight, "grp", axis=0, tiled=True)
 
-    query_own = lax.all_gather(query_weight, "grp", axis=0, tiled=True)
-    output_own = lax.all_gather(output_weight, "grp", axis=0, tiled=True)
+    projections = lax.all_gather(jnp.stack([query_weight, output_weight]), "grp", axis=0)
     count_parts = jnp.stack([own_count // 128, own_count % 128]).astype(jnp.bfloat16)
-    smalls = jnp.concatenate(
-        [
-            first_gain,
-            first_shift,
-            query_bias,
-            output_bias,
-            second_gain,
-            second_shift,
-            down_bias,
-            up_bias,
-            count_parts,
-        ]
-    )
-    smalls = jnp.pad(smalls, (0, SMALL_ROWS * block - smalls.shape[0])).reshape(SMALL_ROWS, block)
+    smalls, small_at = jnp.zeros((SMALL_ROWS * block,), jnp.bfloat16), 0
+    for each in (
+        first_gain,
+        first_shift,
+        query_bias,
+        output_bias,
+        second_gain,
+        second_shift,
+        down_bias,
+        up_bias,
+        count_parts,
+    ):
+        behind = SMALL_ROWS * block - small_at - each.shape[0]
+        smalls = smalls + jnp.pad(each, (small_at, behind))
+        small_at += each.shape[0]
+    smalls = smalls.reshape(SMALL_ROWS, block)
     pack = jnp.concatenate([keyval_weight.reshape(-1, block), smalls], axis=0)
     packed = spread(pack, groups, 0, kernels)
     keyval_pack = pack.shape[0] - SMALL_ROWS
@@ -2009,8 +2208,7 @@
     if kernels:
         weights, queries, mixture, log_total, hidden, normed_two = gather_attention(
             owning,
-            query_own,
-            output_own,
+            projections,
             normed_one,
             query_offset,
             prompt_kv,
@@ -2025,7 +2223,8 @@
             8,
         )
     else:
-        weights = lax.all_gather(jnp.stack([query_own, output_own]), "tok", axis=0)
+        weights = lax.all_gather(projections, "tok", axis=0)
+        weights = jnp.swapaxes(weights, 1, 2).reshape(token_devices, 2, model_width, block)
         queries, mixture, log_total, hidden, normed_two = attention_forward(
             place,
             owning,
@@ -2043,32 +2242,49 @@
             answer_count,
         )
 
+    teacher = own_rows(prompt_teacher, answer_teacher)
+    every_token = token_rows * groups * token_devices
+    factors = (every_token / valid_count * valid_rows)[:, None]
     if kernels:
         group_two, activated, slope = gather_and_up(normed_two, up_cols, up_here, 2)
-        (feed_term,) = product_and_reduce(activated, down_cols, None, 3)
+        result_rows, grad_branch_two, grad_result, own_squares, grad_down_offset = (
+            product_and_reduce(
+                activated,
+                down_cols,
+                None,
+                hidden,
+                teacher,
+                3,
+                down_offset.reshape(1, -1),
+                valid_rows[:, None],
+                factors,
+            )
+        )
+        _, grad_pre_active, grad_down_cols, grad_up_offset = gather_and_grad(
+            grad_branch_two, down_cols, activated, slope, 4
+        )
+        grad_hidden, grad_up_cols, grad_branch_one, second_sums = product_and_reduce(
+            grad_pre_active,
+            up_cols,
+            group_two,
+            hidden,
+            grad_result,
+            5,
+            gain_two.reshape(1, -1),
+        )
+        grad_up_offset = grad_up_offset.reshape(-1)
     else:
         group_two = lax.all_gather(normed_two, "tok", axis=0, tiled=True)
         pre_active = plain_product(group_two, up_cols) + up_here
         activated = jax.nn.gelu(pre_active, approximate=True).astype(jnp.bfloat16)
         feed_term = for_sending(transposed_product(activated, down_cols))
         feed_term = lax.psum_scatter(feed_term, "tok", scatter_dimension=0, tiled=True)
-        feed_term = feed_term.astype(jnp.float32)
-    result_rows = hidden + feed_term + down_offset
-
-    teacher = own_rows(prompt_teacher, answer_teacher).astype(jnp.float32)
-    differ = result_rows - teacher
-    own_squares = jnp.sum(valid_rows[:, None] * differ * differ)
-    every_token = token_rows * groups * token_devices
-    grad_result = every_token / valid_count * valid_rows[:, None] * differ
-    grad_branch_two = grad_result.astype(jnp.bfloat16)
-
-    if kernels:
-        _, grad_pre_active, grad_down_cols, grad_up_offset = gather_and_grad(
-            grad_branch_two, down_cols, activated, slope, 4
-        )
-        grad_normed_two, grad_up_cols = product_and_reduce(grad_pre_active, up_cols, group_two, 5)
-        grad_up_offset = grad_up_offset.reshape(-1)
-    else:
+        result_rows = hidden + feed_term.astype(jnp.float32) + down_offset
+        differ = result_rows - teacher.astype(jnp.float32)
+        own_squares = jnp.sum(valid_rows[:, None] * differ * differ)
+        grad_result = factors * differ
+        grad_branch_two = grad_result.astype(jnp.bfloat16)
+        grad_down_offset = column_sums(grad_branch_two)
         group_grad_two = lax.all_gather(grad_branch_two, "tok", axis=0, tiled=True)
         grad_activated = plain_product(group_grad_two, down_cols)
         _, gelu_back = jax.vjp(
@@ -2082,38 +2298,31 @@
         grad_down_cols = for_sending(weight_product(group_grad_two, activated))
         grad_up_cols = for_sending(weight_product(group_two, grad_pre_active))
         grad_up_offset = column_sums(grad_pre_active)
+        scaled_two, inverse_two = norm_stats(hidden)
+        grad_norm_two, grad_gain_two, grad_shift_two = norm_backward(
+            grad_normed_two, gain_two, scaled_two, inverse_two
+        )
+        grad_hidden = grad_result + grad_norm_two
+        grad_branch_one = grad_hidden.astype(jnp.bfloat16)
+        grad_output_offset = column_sums(grad_branch_one)
     grad_down_weight = lax.psum_scatter(grad_down_cols, "grp", scatter_dimension=0, tiled=True)
-    grad_down_offset = column_sums(grad_branch_two)
-    scaled_two, inverse_two = norm_stats(hidden)
-    grad_norm_two, grad_gain_two, grad_shift_two = norm_backward(
-        grad_normed_two, gain_two, scaled_two, inverse_two
-    )
-    grad_hidden = grad_result + grad_norm_two
-    grad_branch_one = grad_hidden.astype(jnp.bfloat16)
-    grad_down_weight, grad_up_cols, grad_branch_one = lax.optimization_barrier(
-        (grad_down_weight, grad_up_cols, grad_branch_one)
-    )
+    grad_down_weight, grad_up_cols = lax.optimization_barrier((grad_down_weight, grad_up_cols))
     grad_up_weight = lax.psum_scatter(grad_up_cols, "grp", scatter_dimension=0, tiled=True)
-    grad_output_offset = column_sums(grad_branch_one)
 
     share = (owning[:, None] == jnp.arange(prompt_count)[None, :]).astype(jnp.float32).reshape(-1)
     grad_up_place = lax.dynamic_update_slice_in_dim(
         jnp.zeros((hidden_units,), jnp.float32), grad_up_offset, ff_start, 0
     )
     if kernels:
-        known = jnp.concatenate(
-            [
-                grad_up_place,
-                grad_output_offset,
-                grad_gain_two,
-                grad_shift_two,
-                grad_down_offset,
-                jnp.zeros((3 * model_width + HEAD_WIDTH,), jnp.float32),
-                own_squares.reshape(1),
-            ]
-        )
-        known = jnp.pad(known, (0, VECTOR_ROWS * model_width - known.shape[0]))
-        grad_query_own, grad_output_own, grad_keyval_own, vectors, grad_inputs = backward_reduce(
+        (
+            grad_query_own,
+            grad_output_own,
+            grad_keyval_own,
+            vectors,
+            mine,
+            grad_up_own,
+            grad_inputs,
+        ) = backward_reduce(
             owning,
             share,
             weights,
@@ -2128,7 +2337,10 @@
             states,
             gain_one,
             keyval_full,
-            known.reshape(VECTOR_ROWS, model_width),
+            grad_up_place.reshape(-1, model_width),
+            second_sums,
+            grad_down_offset,
+            own_squares,
             groups,
             prompt_count,
             answer_count,
@@ -2136,17 +2348,9 @@
             6,
         )
         value_total = vectors[11, :HEAD_WIDTH]
-        squared_sum = vectors[11, HEAD_WIDTH]
-        device = group_index * token_devices + token_index
-        mine = lax.dynamic_slice_in_dim(
-            vectors.reshape(VECTOR_ROWS, -1, share_size), device, 1, axis=1
-        )[:, 0]
-        own_vectors = [mine[row] for row in (8, 9, 10, 4, 5, 6, 7)]
-        grad_up_own = lax.dynamic_slice_in_dim(
-            vectors[: hidden_units // model_width].reshape(-1),
-            device * up_bias.shape[0],
-            up_bias.shape[0],
-        )
+        squared_sum = vectors[12, 0]
+        own_vectors = [mine[row, :share_size] for row in (8, 9, 10, 4, 5, 6, 7)]
+        grad_up_own = grad_up_own.reshape(-1)
     else:
         grad_rows = keyval_start + keyval_pack
         grad_weights, grad_normed_one, grad_prompt_kv, grad_answer_kv, grad_query_offset = (

time: 640 us -> 603 us (0.942)
  other arithmetic: 30.8 us -> 17.5 us
  Pallas kernels: 539 us -> 526 us
  local copies, waits for them, and re-layouts: 33 us -> 26.5 us
    pallas_call x1, Pallas kernels: 144 us -> 129 us  [backward_reduce(): pl.pallas_call(functools.partial(backward_reduce_kernel, prompts, answers...]
    pallas_call x2, Pallas kernels: 130 us -> 143 us  [product_and_reduce(): pl.pallas_call(functools.partial(product_reduce_kernel, with_grad), out_s...]
    reduce_sum x4 -> x0, other arithmetic: 10 us -> none  [the longest x1 5.07 us: body(): own_squares = jnp.sum(valid_rows[:, None] * differ * differ)]
    pallas_call x1, Pallas kernels: 29 us -> 21.6 us  [spread(): pl.pallas_call(functools.partial(spread_kernel, groups), out_shape=jax.Sh...]
  transfers between devices with their start and end apart: 6 -> 5, of which waited for: 1 -> 2; matrix products, arithmetic and copies ran while one was open for 8% -> 6% of each run, Pallas kernels for 64% -> 65%
where the time goes in v6:
time: 603 us; the launch traced here: 597 us
  Pallas kernels  526 us (87%)
  local copies, waits for them, and re-layouts  26.5 us (4%)
  between operations  19 us (3%)
  other arithmetic  17.5 us (3%)
  waiting for transfers between devices  6.99 us (1%)
    pallas_call x2, Pallas kernels, product_and_reduce(): pl.pallas_call(functools.partial(product_reduce_kernel, with_grad), out_s...  143 us
    pallas_call x1, Pallas kernels, backward_reduce(): pl.pallas_call(functools.partial(backward_reduce_kernel, prompts, answers...  129 us
    pallas_call x1, Pallas kernels, gather_attention(): pl.pallas_call(functools.partial(gather_attention_kernel, prompts, answer...  88.7 us
    pallas_call x1, Pallas kernels, gather_and_grad(): pl.pallas_call(grad_kernel, out_shape=(jax.ShapeDtypeStruct((8, token_row...  69.8 us
    pallas_call x1, Pallas kernels, gather_and_up(): pl.pallas_call(up_kernel, out_shape=(jax.ShapeDtypeStruct((8, token_rows,...  61.7 us
    pallas_call x1, Pallas kernels, spread(): pl.pallas_call(functools.partial(spread_kernel, groups), out_shape=jax.Sh...  21.6 us
    pallas_call x1, Pallas kernels, tok_gather_small(): pl.pallas_call(small_gather_kernel, out_shape=jax.ShapeDtypeStruct((promp...  12.5 us
  transfers between devices with their start and end apart: 5, of which 2 were waited for; matrix products, arithmetic and copies ran while one was open for 6% of the time, Pallas kernels for 65%

profile of v6, /device:TPU:0, one launch (start us, length us, event | category | flops | bytes accessed | tf_op | source)
XLA Modules:
  0.0 596.8 jit_solution(17336274882549212777)
XLA Ops:
  7.4 1.9 pad_maximum_fusion.2
  9.3 0.7 all-gather.5.cloned.1.call-update
  14.2 21.6 %spread.1 = bf16[8,4,80,256]{3,2,1,0:T(8,128)(2,1)} custom-call(bf16[80,256]{1,0:T(8,128)(2,1)} %pad_maximum_fusion.3.own_ref), custom_call_target="tpu_custom_call" | custom-call | tf_op jit(solution)/shard_map/spread/pallas_call | solution.py:138
  35.8 1.9 slice_convert_fusion
  37.7 1.4 reshape.180
  39.5 0.8 copy-done.7
  44.2 12.5 %tok_gather_small.1.prompt_kv_ref = bf16[2,1024,256]{2,1,0:T(8,128)(2,1)} custom-call(bf16[2,128,256]{2,1,0:T(8,128)(2,1)} %bitcast.68), custom_call_target="tpu_custom_call" | custom-call | tf_op jit(solution)/shard_map/tok_gather_small/pallas_call | solution.py:772
  59.4 0.9 slice_bitcast_fusion.3
  62.3 1.5 slice_reduce_fusion
  65.2 0.7 broadcast_multiply_fusion.refs_4_
  65.8 1.2 pad_maximum_fusion.states_ref
  67.1 1.3 pad_maximum_fusion.1.refs_1_
  68.4 88.7 %gather_attention.1 = (bf16[8,4,2,512,256]{4,3,2,1,0:T(8,128)(2,1)}, bf16[8,384,256]{2,1,0:T(8,128)(2,1)}, bf16[8,384,256]{2,1,0:T(8,128)(2,1)}, f32[8,2,384]{2,...) custom-call(s32[1]{0:T(128)} %dynamic_slice.6.owner_ref, bf16[4,2,512,256]{3,2,1,0:T(8,128)(2,1)} %bitcast.78, ...), custom_call_target="tpu_custom_call" | custom-call | flops 12884901888 | bytes 250000000 | tf_op jit(solution)/shard_map/gather_attention/pallas_call | solution.py:1157
  157.1 61.7 %gather_and_up.1 = (bf16[8,384,2048]{2,1,0:T(8,128)(2,1)}, bf16[8,384,1024]{2,1,0:T(8,128)(2,1)}, bf16[8,384,1024]{2,1,0:T(8,128)(2,1)}) custom-call(bf16[384,2048]{1,0:T(8,128)(2,1)} %get-tuple-element.49.own_ref, bf16[2048,1024]{1,0:T(8,128)(2,1)} %all-gather.5.cloned.1.call-done.up_hbm.weight_hbm, f32[1,1024]{1,0:T(1,128)} %bitcast.75), custom_call_target="tpu_custom_call" | custom-call | flops 12884901888 | bytes 150000000 | tf_op jit(solution)/shard_map/gather_and_up/pallas_call | solution.py:332
  218.8 3.8 all-gather.7.cloned.1.call-done.weight_hbm.down_hbm
  222.6 70.0 %product_and_reduce.2 = (bf16[384,2048]{1,0:T(8,128)(2,1)}, bf16[384,2048]{1,0:T(8,128)(2,1)}, f32[384,2048]{1,0:T(8,128)}, f32[1,2048]{1,0:T(1,128)}, f32[1,2048]{1,0:T(1,128)}) custom-call(bf16[8,384,1024]{2,1,0:T(8,128)(2,1)} %get-tuple-element.50.narrow_ref.active_ref, bf16[2048,1024]{1,0:T(8,128)(2,1)} %all-gather.7.cloned.1.call-done.weight_hbm.down_hbm, ...), custom_call_target="tpu_custom_call" | custom-call | flops 12884901888 | bytes 150000000 | tf_op jit(solution)/shard_map/product_and_reduce/pallas_call | solution.py:731
  292.6 69.8 %gather_and_grad.1 = (bf16[8,384,2048]{2,1,0:T(8,128)(2,1)}, bf16[8,384,1024]{2,1,0:T(8,128)(2,1)}, bf16[2048,1024]{1,0:T(8,128)(2,1)}, f32[1,1024]{1,0:T(1,128)}) custom-call(bf16[384,2048]{1,0:T(8,128)(2,1)} %get-tuple-element.56.own_ref, bf16[2048,1024]{1,0:T(8,128)(2,1)} %all-gather.7.cloned.1.call-done.weight_hbm.down_hbm, ...), custom_call_target="tpu_custom_call" | custom-call | flops 25769803776 | bytes 150000000 | tf_op jit(solution)/shard_map/gather_and_grad/pallas_call | solution.py:446
  362.4 72.9 %product_and_reduce.3 = (f32[384,2048]{1,0:T(8,128)}, bf16[2048,1024]{1,0:T(8,128)(2,1)}, bf16[384,2048]{1,0:T(8,128)(2,1)}, f32[8,2048]{1,0:T(8,128)}) custom-call(bf16[8,384,1024]{2,1,0:T(8,128)(2,1)} %get-tuple-element.58.narrow_ref, bf16[2048,1024]{1,0:T(8,128)(2,1)} %all-gather.5.cloned.1.call-done.up_hbm.weight_hbm, ...), custom_call_target="tpu_custom_call" | custom-call | flops 25769803776 | bytes 150000000 | tf_op jit(solution)/shard_map/product_and_reduce/pallas_call | solution.py:731
  435.3 1.8 reduce-scatter.3.cloned.1.call-done
  437.8 1.2 compare_convert_fusion.share_ref
  439.9 128.9 %backward_reduce.1 = (f32[512,256]{1,0:T(8,128)}, f32[512,256]{1,0:T(8,128)}, f32[64,256]{1,0:T(8,128)}, f32[16,2048]{1,0:T(8,128)}, f32[16,128]{1,0:T(8,128)}, ...) custom-call(s32[1]{0:T(128)} %dynamic_slice.6.owner_ref, f32[2]{0:T(128)} %compare_convert_fusion.share_ref, ...), custom_call_target="tpu_custom_call" | custom-call | flops 20132659200 | bytes 250000000 | tf_op jit(solution)/shard_map/backward_reduce/pallas_call | solution.py:2010
  568.8 1.2 slice.110
  570.0 2.4 slice.100
  572.4 2.3 slice.98
  575.3 1.2 slice_bitcast_fusion.8
  576.5 1.4 slice_bitcast_fusion.4
  577.9 1.9 slice_bitcast_fusion.1
  579.8 1.9 slice_bitcast_fusion.2
  581.7 1.6 convert_element_type.66
  583.2 2.8 convert_element_type.65
  586.0 0.8 copy.62
  587.5 0.8 copy.64
  (104 shorter events, 14.7 us)
Async XLA Ops:
  7.2 3.6 copy-start.14
  7.2 4.2 copy-start.17
  7.2 6.2 %copy-start.25 = (bf16[64]{0:T(256)(128)(2,1)S(1)}, bf16[64]{0:T(256)(128)(2,1)}, u32[]{:S(2)}) copy-start(bf16[64]{0:T(256)(128)(2,1)} %param.28) | copy-start | bytes 388
  7.2 6.2 %copy-start.24 = (bf16[64]{0:T(256)(128)(2,1)S(1)}, bf16[64]{0:T(256)(128)(2,1)}, u32[]{:S(2)}) copy-start(bf16[64]{0:T(256)(128)(2,1)} %param.29) | copy-start | bytes 388
  7.2 6.2 %copy-start.23 = (bf16[64]{0:T(256)(128)(2,1)S(1)}, bf16[64]{0:T(256)(128)(2,1)}, u32[]{:S(2)}) copy-start(bf16[64]{0:T(256)(128)(2,1)} %param.31) | copy-start | bytes 388
  7.2 6.2 %copy-start.22 = (bf16[64]{0:T(256)(128)(2,1)S(1)}, bf16[64]{0:T(256)(128)(2,1)}, u32[]{:S(2)}) copy-start(bf16[64]{0:T(256)(128)(2,1)} %param.35) | copy-start | bytes 388
  7.3 6.2 %copy-start.21 = (bf16[64]{0:T(256)(128)(2,1)S(1)}, bf16[64]{0:T(256)(128)(2,1)}, u32[]{:S(2)}) copy-start(bf16[64]{0:T(256)(128)(2,1)} %param.36) | copy-start | bytes 388
  7.3 6.2 %copy-start.20 = (bf16[64]{0:T(256)(128)(2,1)S(1)}, bf16[64]{0:T(256)(128)(2,1)}, u32[]{:S(2)}) copy-start(bf16[64]{0:T(256)(128)(2,1)} %param.37) | copy-start | bytes 388
  7.3 6.2 %copy-start.18 = (bf16[256]{0:T(256)(128)(2,1)S(1)}, bf16[256]{0:T(256)(128)(2,1)}, u32[]{:S(2)}) copy-start(bf16[256]{0:T(256)(128)(2,1)} %param.39) | copy-start | bytes 1540
  7.3 6.2 %copy-start.19 = (bf16[64]{0:T(256)(128)(2,1)S(1)}, bf16[64]{0:T(256)(128)(2,1)}, u32[]{:S(2)}) copy-start(bf16[64]{0:T(256)(128)(2,1)} %param.41) | copy-start | bytes 388
  7.3 6.3 %copy-start.13 = (bf16[64,256]{1,0:T(8,128)(2,1)S(1)}, bf16[64,256]{1,0:T(8,128)(2,1)}, u32[]{:S(2)}) copy-start(bf16[64,256]{1,0:T(8,128)(2,1)} %param.32) | copy-start | bytes 98308
  7.3 61.1 %all-gather.9.cloned.1.call-start = ((), (), s32[]{:S(2)}) async-start(), calls=%async_computation.6 | async-start | bytes 2621440 | tf_op jit(solution)/shard_map/all_gather | solution.py:2153
  9.3 147.8 %all-gather.5.cloned.1.call-start = ((), (), s32[]{:S(2)}) async-start(), calls=%async_computation.2 | async-start | bytes 5242880 | tf_op jit(solution)/shard_map/all_gather | solution.py:2150
  10.0 212.6 %all-gather.7.cloned.1.call-start = ((), (), s32[]{:S(2)}) async-start(), calls=%async_computation.3 | async-start | bytes 5242880 | tf_op jit(solution)/shard_map/all_gather | solution.py:2151
  10.8 426.4 %reduce-scatter.3.cloned.1.call-start = ((), (), s32[]{:S(2)}) async-start(), calls=%async_computation.4 | async-start | bytes 5242880 | tf_op jit(solution)/shard_map/reduce_scatter | solution.py:2308
  35.8 4.7 copy-start.2
  37.7 3.0 copy-start
  37.7 3.0 copy-start.1
  39.5 1.5 copy-start.26
  40.7 1.6 copy-start.6
  42.2 23.6 %copy-start.3 = (bf16[384,2048]{1,0:T(8,128)(2,1)}, bf16[384,2048]{1,0:T(8,128)(2,1)S(1)}, u32[]{:S(2)}) copy-start(bf16[384,2048]{1,0:T(8,128)(2,1)S(1)} %fusion.5.normed_ref) | copy-start | bytes 4718596
  42.3 18.9 %copy-start.27 = (s32[8]{0:T(128)S(1)}, s32[8]{0:T(128)}, u32[]{:S(2)}) copy-start(s32[8]{0:T(128)} %param.23) | copy-start | bytes 100
  60.4 7.9 %copy-start.8 = (f32[384,1]{1,0:T(8,128)}, f32[384,1]{1,0:T(8,128)S(1)}, u32[]{:S(2)}) copy-start(f32[384,1]{1,0:T(8,128)S(1)} %copy.53.refs_3_) | copy-start | bytes 4612
  65.1 2.0 copy-start.4
  65.1 2.0 copy-start.11
  362.4 220.9 %reduce-scatter.5.cloned.1.call-start = ((), (), s32[]{:S(2)}) async-start(), calls=%async_computation.5 | async-start | bytes 5242880 | tf_op jit(solution)/shard_map/reduce_scatter | solution.py:2310
  435.3 3.6 copy-start.15
  570.0 11.7 %copy-start.5 = (bf16[512,1024]{1,0:T(8,128)(2,1)S(1)}, bf16[512,1024]{1,0:T(8,128)(2,1)}, u32[]{:S(2)}) copy-start(bf16[512,1024]{1,0:T(8,128)(2,1)} %reduce-scatter.3.cloned.1.call-done) | copy-start | bytes 3145732
  581.7 4.4 copy-start.10
  581.7 5.2 copy-start.12
  581.7 5.8 copy-start.9
  583.2 5.0 copy-start.16
  (1 other events, 0.8 us)
Sparse Core Ops, SparseCore 0:
  10.3 49.6 all-gather.8
  61.6 80.0 all-gather.4
  143.3 79.2 all-gather.6
  362.5 74.5 reduce-scatter.2
  439.4 94.0 reduce-scatter.4

commit v7 on v6

--- a/solution.py
+++ b/solution.py
@@ -493,7 +493,7 @@
         *refs, wide, across, sums, wide_sem = refs
     else:
         hidden_hbm, teacher_hbm, offset_ref, valid_ref, factor_ref, *refs = refs
-        out_ref, branch_ref, grad_result_ref, squares_ref, columns_ref, *refs = refs
+        prompt_ref, answer_ref, branch_ref, grad_result_ref, squares_ref, columns_ref, *refs = refs
     (
         weight,
         narrow,
@@ -626,11 +626,23 @@
         store = pltpu.make_async_copy(weight, grad_ref, weight_sem)
         store.start()
 
-    for each in (x_first, y_second, x_second, y_first):
-        each.wait_recv()
-
     for each in row_loads:
         each.wait()
+    if not with_grad:
+        for start, part, come in ((0, x_first, 0), (half, y_second, 1)):
+            part.wait_recv()
+
+            @pl.loop(0, half // step)
+            def _(turn):
+                at = pl.ds(pl.multiple_of(start + turn * step, step), step)
+                base = hidden_rows[at, :] + offset_ref[...] + mine[3, at, :].astype(jnp.float32)
+                hidden_rows[at, :] = base + final[come, at, :].astype(jnp.float32)
+
+        y_first.wait_recv()
+        x_second.wait_recv()
+    else:
+        for each in (x_first, y_second, x_second, y_first):
+            each.wait_recv()
 
     def total_of(at):
         total = mine[3, at, :].astype(jnp.float32) + final[0, at, :].astype(jnp.float32)
@@ -661,19 +673,28 @@
     else:
         squares_ref[...] = jnp.zeros_like(squares_ref)
         columns_ref[...] = jnp.zeros_like(columns_ref)
-
-        @pl.loop(0, rows // step)
-        def _(turn):
-            at = chunk_of(turn, step)
-            result = hidden_rows[at, :] + total_of(at) + offset_ref[...]
-            differ = result - other_rows[at, :].astype(jnp.float32)
-            grad_result = factor_ref[at, :] * differ
-            branch = grad_result.astype(jnp.bfloat16)
-            out_ref[at, :] = result.astype(jnp.bfloat16)
-            grad_result_ref[at, :] = grad_result
-            branch_ref[at, :] = branch
-            squares_ref[...] += jnp.sum(valid_ref[at, :] * differ * differ, axis=0, keepdims=True)
-            columns_ref[...] += jnp.sum(branch.astype(jnp.float32), axis=0, keepdims=True)
+        own_prompt = prompt_ref.shape[0]
+        for start, stop, come, out_ref, before in (
+            (0, half, 1, prompt_ref, 0),
+            (half, own_prompt, 0, prompt_ref, 0),
+            (own_prompt, rows, 0, answer_ref, own_prompt),
+        ):
+
+            @pl.loop(0, (stop - start) // step)
+            def _(turn):
+                at = pl.ds(pl.multiple_of(start + turn * step, step), step)
+                out = pl.ds(pl.multiple_of(start - before + turn * step, step), step)
+                result = hidden_rows[at, :] + final[come, at, :].astype(jnp.float32)
+                differ = result - other_rows[at, :].astype(jnp.float32)
+                grad_result = factor_ref[at, :] * differ
+                branch = grad_result.astype(jnp.bfloat16)
+                out_ref[out, :] = result.astype(jnp.bfloat16)
+                grad_result_ref[at, :] = grad_result
+                branch_ref[at, :] = branch
+                squared = valid_ref[at, :] * differ * differ
+                column = branch.astype(jnp.float32)
+                squares_ref[...] += squared[:8, :] + squared[8:, :]
+                columns_ref[...] += column[:8, :] + column[8:, :]
 
     if with_grad:
         store.wait()
@@ -681,7 +702,7 @@
         each.wait_send()
 
 
-def product_and_reduce(narrow, weight, wide, rows, second, call_number, *small):
+def product_and_reduce(narrow, weight, wide, rows, second, call_number, own_prompt, *small):
     _, token_rows, width = narrow.shape
     model_width = weight.shape[0]
     with_grad = wide is not None
@@ -690,7 +711,7 @@
     dma = pltpu.SemaphoreType.DMA
     block = (token_rows, model_width)
     kind, long = jnp.bfloat16, jnp.float32
-    line = jax.ShapeDtypeStruct((1, model_width), long)
+    line = jax.ShapeDtypeStruct((8, model_width), long)
     narrow_rows, long_rows = jax.ShapeDtypeStruct(block, kind), jax.ShapeDtypeStruct(block, long)
     scratch = [
         pltpu.VMEM(weight.shape, kind),
@@ -725,8 +746,15 @@
         ]
         operands.append(wide)
     else:
-        out_shape = (narrow_rows, narrow_rows, long_rows, line, line)
-        out_specs = (inside,) * 5
+        out_shape = (
+            jax.ShapeDtypeStruct((own_prompt, model_width), kind),
+            jax.ShapeDtypeStruct((token_rows - own_prompt, model_width), kind),
+            narrow_rows,
+            long_rows,
+            line,
+            line,
+        )
+        out_specs = (inside,) * 6
     operands += [rows, second]
     return pl.pallas_call(
         functools.partial(product_reduce_kernel, with_grad),
@@ -1539,7 +1567,8 @@
     vectors_ref,
     own_vectors_ref,
     own_up_ref,
-    grad_input_ref,
+    grad_prompt_ref,
+    grad_answer_ref,
     normed_across,
     branch_across,
     key_sums,
@@ -1548,6 +1577,7 @@
     grad_hidden,
     held,
     pair,
+    early,
     kept,
     theirs,
     relayed,
@@ -1575,6 +1605,7 @@
     peer_send,
     peer_recv,
     load_sem,
+    early_sem,
     hidden_sem,
 ):
     width = HEAD_WIDTH
@@ -1691,8 +1722,24 @@
         for turn in range(groups - 1)
     ]
 
+    def fetch(turn):
+        source, slot = bits_away(7 - turn), turn % 2
+        return (
+            pltpu.make_async_copy(weights_ref.at[source], held.at[slot], load_sem.at[slot, 0]),
+            pltpu.make_async_copy(queries_ref.at[source], pair.at[slot, 0], load_sem.at[slot, 1]),
+            pltpu.make_async_copy(mixture_ref.at[source], pair.at[slot, 1], load_sem.at[slot, 2]),
+        )
+
+    def fetch_early(turn):
+        return pltpu.make_async_copy(
+            mixture_ref.at[bits_away(7 - turn)], early.at[turn % 2], early_sem.at[turn % 2]
+        )
+
+    fetch_early(0).start()
     load_hidden = pltpu.make_async_copy(hidden_hbm, grad_hidden, hidden_sem)
     load_hidden.start()
+    for each in fetch(0):
+        each.start()
     greet_all(peers, other_groups)
     normed_across[...] = jnp.transpose(normed_ref[...])
     branch_across[...] = jnp.transpose(branch_ref[...])
@@ -1702,8 +1749,9 @@
     vectors[...] = jnp.zeros_like(vectors)
     vectors[: known_up_ref.shape[0], :] = known_up_ref[...]
     vectors[4:7, :] = known_sums_ref[0:3, :]
-    vectors[7:8, :] = known_columns_ref[...]
-    squares = jnp.sum(known_squares_ref[...], axis=1, keepdims=True)
+    vectors[7:8, :] = jnp.sum(known_columns_ref[...], axis=0, keepdims=True)
+    squares = jnp.sum(known_squares_ref[...], axis=0, keepdims=True)
+    squares = jnp.sum(squares, axis=1, keepdims=True)
     vectors[12:13, :] = jnp.broadcast_to(squares, (1, model_width))
 
     def add_into(target, other, rows):
@@ -1747,12 +1795,14 @@
 
     @pl.loop(0, 8)
     def _(turn):
-        load = pltpu.make_async_copy(
-            mixture_ref.at[bits_away(7 - turn)], pair.at[1], load_sem.at[2]
-        )
-        load.start()
-        load.wait()
-        kept[slot_of(turn, 1)] = plain_product(branch_across[...], pair[1]).astype(jnp.bfloat16)
+        @pl.when(turn < 7)
+        def _():
+            fetch_early(turn + 1).start()
+
+        fetch_early(turn).wait()
+        kept[slot_of(turn, 1)] = plain_product(
+            branch_across[...], early[turn % 2]
+        ).astype(jnp.bfloat16)
         send_to_chip(turn, 1)
 
         @pl.when(turn == 2)
@@ -1772,21 +1822,20 @@
 
     @pl.loop(0, 8)
     def _(turn):
-        source = bits_away(7 - turn)
-        loads = (
-            pltpu.make_async_copy(weights_ref.at[source], held, load_sem.at[0]),
-            pltpu.make_async_copy(queries_ref.at[source], pair.at[0], load_sem.at[1]),
-            pltpu.make_async_copy(mixture_ref.at[source], pair.at[1], load_sem.at[2]),
-        )
-        for each in loads:
-            each.start()
+        source, now = bits_away(7 - turn), turn % 2
+
+        @pl.when(turn < 7)
+        def _():
+            for each in fetch(turn + 1):
+                each.start()
+
         for place in range(4):
 
             @pl.when(turn == 2 * place)
             def _():
                 to_chip[1][place].wait_send()
 
-        for each in loads:
+        for each in fetch(turn):
             each.wait()
         grad_query_block, grad_bias = backward_block(
             prompts,
@@ -1797,10 +1846,10 @@
             share_ref,
             normed_ref,
             branch_ref,
-            held[:, 0].reshape(-1, block),
-            held[:, 1].reshape(-1, block),
-            pair[0],
-            pair[1],
+            held[now, :, 0].reshape(-1, block),
+            held[now, :, 1].reshape(-1, block),
+            pair[now, 0],
+            pair[now, 1],
             log_ref.at[source],
             prompt_kv_ref,
             answer_kv_ref,
@@ -1874,6 +1923,7 @@
     keyval_sums.start()
     close(0, by_y[0])
     keyval_sums.pass_on()
+    close(0, by_x[1])
     load_hidden.wait()
     vectors[11:12, :width] = jnp.sum(
         kv_rows[:, width:].astype(jnp.float32), axis=0, keepdims=True
@@ -1881,20 +1931,25 @@
     piece = 16
     grad_normed[...] += transposed_product(kv_rows[...], keyval_ref[...])
 
-    @pl.loop(0, states_ref.shape[0] // piece)
-    def _(turn):
-        at = chunk_of(turn, piece)
-        scaled, inverse = norm_stats(states_ref[at, :].astype(jnp.float32))
-        grad_out = grad_normed[at, :]
-        weighted = grad_out * gain_ref[...]
-        grad_in = inverse * (
-            weighted
-            - jnp.mean(weighted, axis=-1, keepdims=True)
-            - scaled * jnp.mean(weighted * scaled, axis=-1, keepdims=True)
-        )
-        grad_input_ref[at, :] = (grad_hidden[at, :] + grad_in).astype(jnp.bfloat16)
-        vectors[8:9, :] += jnp.sum(grad_out * scaled, axis=0, keepdims=True)
-        vectors[9:10, :] += jnp.sum(grad_out, axis=0, keepdims=True)
+    start = 0
+    for out_ref in (grad_prompt_ref, grad_answer_ref):
+
+        @pl.loop(0, out_ref.shape[0] // piece)
+        def _(turn):
+            at = pl.ds(pl.multiple_of(start + turn * piece, piece), piece)
+            scaled, inverse = norm_stats(states_ref[at, :].astype(jnp.float32))
+            grad_out = grad_normed[at, :]
+            weighted = grad_out * gain_ref[...]
+            grad_in = inverse * (
+                weighted
+                - jnp.mean(weighted, axis=-1, keepdims=True)
+                - scaled * jnp.mean(weighted * scaled, axis=-1, keepdims=True)
+            )
+            out_ref[chunk_of(turn, piece), :] = (grad_hidden[at, :] + grad_in).astype(jnp.bfloat16)
+            vectors[8:9, :] += jnp.sum(grad_out * scaled, axis=0, keepdims=True)
+            vectors[9:10, :] += jnp.sum(grad_out, axis=0, keepdims=True)
+
+        start += out_ref.shape[0]
 
     for each in vector_copies:
         each.start()
@@ -1909,7 +1964,6 @@
     vectors[:, lanes(here)] = total
     for each in vector_across:
         each.start()
-    close(0, by_x[1])
     for each in vector_across:
         each.wait_recv()
     total = vectors[:, lanes(here)]
@@ -2016,10 +2070,11 @@
             jax.ShapeDtypeStruct((VECTOR_ROWS, model_width), wide),
             jax.ShapeDtypeStruct((VECTOR_ROWS, HEAD_WIDTH), wide),
             jax.ShapeDtypeStruct((1, known_up.size // (8 * groups)), wide),
-            jax.ShapeDtypeStruct((token_rows, model_width), kind),
+            jax.ShapeDtypeStruct((prompts * prompt_rows, model_width), kind),
+            jax.ShapeDtypeStruct((token_rows - prompts * prompt_rows, model_width), kind),
         ),
         in_specs=[scalars] * 2 + [anywhere] * 4 + [inside] * 12,
-        out_specs=(inside,) * 7,
+        out_specs=(inside,) * 8,
         scratch_shapes=[
             pltpu.VMEM((model_width, token_rows), kind),
             pltpu.VMEM((model_width, token_rows), kind),
@@ -2027,7 +2082,8 @@
             pltpu.VMEM(answer_kv.shape, wide),
             pltpu.VMEM((token_rows, model_width), wide),
             pltpu.VMEM((token_rows, model_width), wide),
-            pltpu.VMEM(weights.shape[1:], kind),
+            pltpu.VMEM((2,) + weights.shape[1:], kind),
+            pltpu.VMEM((2, 2, token_rows, block), kind),
             pltpu.VMEM((2, token_rows, block), kind),
             pltpu.VMEM((12, model_width, block), kind),
             pltpu.VMEM((4, 2, model_width, block), kind),
@@ -2055,7 +2111,8 @@
             dma((4 * others,)),
             dma((4, 7)),
             dma((4, 7)),
-            dma((3,)),
+            dma((2, 3)),
+            dma((2,)),
             dma,
         ],
         compiler_params=pltpu.CompilerParams(
@@ -2089,6 +2146,59 @@
         known_columns,
         known_squares,
     )
+
+
+def finish_kernel(share_size, model_width, *refs):
+    half = len(refs) - 17
+    (
+        vectors_ref,
+        own_vectors_ref,
+        own_up_ref,
+        count_ref,
+        prompt_ref,
+        answer_ref,
+        query_ref,
+        output_ref,
+        keyval_ref,
+        up_ref,
+        down_ref,
+    ) = refs[:half]
+    prompt_out, answer_out, query_out, output_out, keyval_out, up_out, down_out, *outs = refs[half:]
+    prompt_out[...] = prompt_ref[...]
+    answer_out[...] = answer_ref[...]
+    query_out[...] = query_ref[...]
+    output_out[...] = output_ref[...]
+    keyval_out[...] = keyval_ref[...]
+    up_out[...] = up_ref[...].astype(jnp.float32)
+    down_out[...] = down_ref[...].astype(jnp.float32)
+    *vector_outs, up_bias_out, value_out, loss_out = outs
+    for row, out_ref in zip((8, 9, 10, 4, 5, 6, 7), vector_outs):
+        out_ref[...] = own_vectors_ref[row : row + 1, :share_size]
+    up_bias_out[...] = own_up_ref[...]
+    value_out[...] = vectors_ref[11:12, :HEAD_WIDTH]
+    loss_out[...] = vectors_ref[12:13, :1] / (count_ref[...] * model_width)
+
+
+def finish(share_size, vectors, own_vectors, own_up, valid_count, *arrays):
+    wide = jnp.float32
+    model_width = vectors.shape[1]
+    kinds = [array.dtype for array in arrays[:5]] + [wide, wide]
+    shapes = [jax.ShapeDtypeStruct(array.shape, kind) for array, kind in zip(arrays, kinds)]
+    shapes += [jax.ShapeDtypeStruct((1, share_size), wide)] * 7
+    shapes += [
+        jax.ShapeDtypeStruct(own_up.shape, wide),
+        jax.ShapeDtypeStruct((1, HEAD_WIDTH), wide),
+        jax.ShapeDtypeStruct((1, 1), wide),
+    ]
+    inside = pl.BlockSpec(memory_space=pltpu.VMEM)
+    return pl.pallas_call(
+        functools.partial(finish_kernel, share_size, model_width),
+        out_shape=tuple(shapes),
+        in_specs=[inside] * (4 + len(arrays)),
+        out_specs=(inside,) * len(shapes),
+        compiler_params=pltpu.CompilerParams(vmem_limit_bytes=VMEM_BYTES),
+        name="finish",
+    )(vectors, own_vectors, own_up, valid_count.reshape(1, 1), *arrays)
 
 
 def by_group(values):
@@ -2247,7 +2357,7 @@
     factors = (every_token / valid_count * valid_rows)[:, None]
     if kernels:
         group_two, activated, slope = gather_and_up(normed_two, up_cols, up_here, 2)
-        result_rows, grad_branch_two, grad_result, own_squares, grad_down_offset = (
+        prompt_out, answer_out, grad_branch_two, grad_result, own_squares, grad_down_offset = (
             product_and_reduce(
                 activated,
                 down_cols,
@@ -2255,6 +2365,7 @@
                 hidden,
                 teacher,
                 3,
+                own_prompt,
                 down_offset.reshape(1, -1),
                 valid_rows[:, None],
                 factors,
@@ -2270,6 +2381,7 @@
             hidden,
             grad_result,
             5,
+            own_prompt,
             gain_two.reshape(1, -1),
         )
         grad_up_offset = grad_up_offset.reshape(-1)
@@ -2280,6 +2392,7 @@
         feed_term = for_sending(transposed_product(activated, down_cols))
         feed_term = lax.psum_scatter(feed_term, "tok", scatter_dimension=0, tiled=True)
         result_rows = hidden + feed_term.astype(jnp.float32) + down_offset
+        prompt_out, answer_out = result_rows[:own_prompt], result_rows[own_prompt:]
         differ = result_rows - teacher.astype(jnp.float32)
         own_squares = jnp.sum(valid_rows[:, None] * differ * differ)
         grad_result = factors * differ
@@ -2321,7 +2434,8 @@
             vectors,
             mine,
             grad_up_own,
-            grad_inputs,
+            prompt_grad,
+            answer_grad,
         ) = backward_reduce(
             owning,
             share,
@@ -2347,10 +2461,35 @@
             prompt_rows,
             6,
         )
-        value_total = vectors[11, :HEAD_WIDTH]
-        squared_sum = vectors[12, 0]
-        own_vectors = [mine[row, :share_size] for row in (8, 9, 10, 4, 5, 6, 7)]
-        grad_up_own = grad_up_own.reshape(-1)
+        (
+            prompt_grad,
+            answer_grad,
+            grad_query_own,
+            grad_output_own,
+            grad_keyval_own,
+            grad_up_weight,
+            grad_down_weight,
+            *own_vectors,
+            grad_up_own,
+            value_total,
+            loss_value,
+        ) = finish(
+            share_size,
+            vectors,
+            mine,
+            grad_up_own,
+            valid_count,
+            prompt_grad,
+            answer_grad,
+            grad_query_own,
+            grad_output_own,
+            grad_keyval_own,
+            grad_up_weight,
+            grad_down_weight,
+        )
+        own_vectors = [each.reshape(-1) for each in own_vectors]
+        grad_up_own, value_total = grad_up_own.reshape(-1), value_total.reshape(-1)
+        loss_value = loss_value.reshape(())
     else:
         grad_rows = keyval_start + keyval_pack
         grad_weights, grad_normed_one, grad_prompt_kv, grad_answer_kv, grad_query_offset = (
@@ -2429,18 +2568,17 @@
         grad_query_own = grad_weights[:weight_rows]
         grad_output_own = grad_weights[weight_rows:keyval_start]
         grad_keyval_own = grad_weights[keyval_start:].reshape(keyval_rows, keyval_width)
-        grad_inputs = grad_inputs.astype(jnp.bfloat16)
-    loss_value = squared_sum / (valid_count * model_width)
-
-    def split_rows(values):
-        values = values.astype(jnp.bfloat16)
+        prompt_grad, answer_grad = grad_inputs[:own_prompt], grad_inputs[own_prompt:]
+        loss_value = squared_sum / (valid_count * model_width)
+
+    def row_outputs(prompt_part, answer_part):
         return (
-            values[:own_prompt].reshape(prompt_states.shape),
-            values[own_prompt:].reshape(answer_states.shape),
-        )
-
-    prompt_out, answer_out = split_rows(result_rows)
-    prompt_grad, answer_grad = split_rows(grad_inputs)
+            prompt_part.astype(jnp.bfloat16).reshape(prompt_states.shape),
+            answer_part.astype(jnp.bfloat16).reshape(answer_states.shape),
+        )
+
+    prompt_out, answer_out = row_outputs(prompt_out, answer_out)
+    prompt_grad, answer_grad = row_outputs(prompt_grad, answer_grad)
     pieces = own_vectors
     return (
         prompt_out,

time: 603 us -> 591 us (0.980)
  local copies, waits for them, and re-layouts: 26.5 us -> 13.3 us
  Pallas kernels: 526 us -> 534 us
  transfers between devices with their start and end apart: 5 -> 5, of which waited for: 2 -> 2; matrix products, arithmetic and copies ran while one was open for 6% -> 4% of each run, Pallas kernels for 65% -> 67%
where the time goes in v7:
time: 591 us; the launch traced here: 586 us
  Pallas kernels  534 us (90%)
  between operations  17.2 us (3%)
  local copies, waits for them, and re-layouts  13.3 us (2%)
  other arithmetic  13.1 us (2%)
  waiting for transfers between devices  7 us (1%)
    pallas_call x2, Pallas kernels, product_and_reduce(): pl.pallas_call(functools.partial(product_reduce_kernel, with_grad), out_s...  142 us
    pallas_call x1, Pallas kernels, backward_reduce(): pl.pallas_call(functools.partial(backward_reduce_kernel, prompts, answers...  132 us
    pallas_call x1, Pallas kernels, gather_attention(): pl.pallas_call(functools.partial(gather_attention_kernel, prompts, answer...  88.7 us
    pallas_call x1, Pallas kernels, gather_and_grad(): pl.pallas_call(grad_kernel, out_shape=(jax.ShapeDtypeStruct((8, token_row...  69.8 us
    pallas_call x1, Pallas kernels, gather_and_up(): pl.pallas_call(up_kernel, out_shape=(jax.ShapeDtypeStruct((8, token_rows,...  61.7 us
    pallas_call x1, Pallas kernels, spread(): pl.pallas_call(functools.partial(spread_kernel, groups), out_shape=jax.Sh...  21.5 us
    pallas_call x1, Pallas kernels, tok_gather_small(): pl.pallas_call(small_gather_kernel, out_shape=jax.ShapeDtypeStruct((promp...  12.5 us
  transfers between devices with their start and end apart: 5, of which 2 were waited for; matrix products, arithmetic and copies ran while one was open for 4% of the time, Pallas kernels for 67%

profile of v7, /device:TPU:0, one launch (start us, length us, event | category | flops | bytes accessed | tf_op | source)
XLA Modules:
  0.0 585.8 jit_solution(979627761015704136)
XLA Ops:
  7.4 1.9 pad_maximum_fusion.2
  9.3 0.7 all-gather.5.cloned.1.call-update
  10.1 0.7 all-gather.7.cloned.1.call-update
  14.2 21.5 %spread.1 = bf16[8,4,80,256]{3,2,1,0:T(8,128)(2,1)} custom-call(bf16[80,256]{1,0:T(8,128)(2,1)} %pad_maximum_fusion.3.own_ref), custom_call_target="tpu_custom_call" | custom-call | tf_op jit(solution)/shard_map/spread/pallas_call | solution.py:138
  35.8 1.9 slice_convert_fusion
  37.7 1.4 reshape.220
  39.5 0.8 copy-done.7
  42.9 0.7 slice.62
  44.2 12.5 %tok_gather_small.1.prompt_kv_ref = bf16[2,1024,256]{2,1,0:T(8,128)(2,1)} custom-call(bf16[2,128,256]{2,1,0:T(8,128)(2,1)} %bitcast.58), custom_call_target="tpu_custom_call" | custom-call | tf_op jit(solution)/shard_map/tok_gather_small/pallas_call | solution.py:800
  56.7 0.7 reshape_reshape.17.bias_ref
  57.4 0.7 reshape_reshape.18.offset_ref
  58.0 0.7 reshape_reshape.19.gain_ref.refs_3_
  58.7 0.7 reshape_reshape.20.shift_ref
  59.4 0.9 slice_bitcast_fusion.1
  60.5 0.7 reshape_reshape.21.refs_2_
  62.3 1.5 slice_reduce_fusion
  65.2 0.7 broadcast_multiply_fusion.refs_4_
  65.9 1.2 pad_maximum_fusion.states_ref
  67.1 1.3 pad_maximum_fusion.1.refs_1_
  68.4 88.7 %gather_attention.1 = (bf16[8,4,2,512,256]{4,3,2,1,0:T(8,128)(2,1)}, bf16[8,384,256]{2,1,0:T(8,128)(2,1)}, bf16[8,384,256]{2,1,0:T(8,128)(2,1)}, f32[8,2,384]{2,...) custom-call(s32[1]{0:T(128)} %dynamic_slice.6.owner_ref, bf16[4,2,512,256]{3,2,1,0:T(8,128)(2,1)} %bitcast.68, ...), custom_call_target="tpu_custom_call" | custom-call | flops 12884901888 | bytes 250000000 | tf_op jit(solution)/shard_map/gather_attention/pallas_call | solution.py:1185
  157.1 61.7 %gather_and_up.1 = (bf16[8,384,2048]{2,1,0:T(8,128)(2,1)}, bf16[8,384,1024]{2,1,0:T(8,128)(2,1)}, bf16[8,384,1024]{2,1,0:T(8,128)(2,1)}) custom-call(bf16[384,2048]{1,0:T(8,128)(2,1)} %get-tuple-element.68.own_ref, bf16[2048,1024]{1,0:T(8,128)(2,1)} %all-gather.5.cloned.1.call-done.up_hbm.weight_hbm, f32[1,1024]{1,0:T(1,128)} %bitcast.66), custom_call_target="tpu_custom_call" | custom-call | flops 12884901888 | bytes 150000000 | tf_op jit(solution)/shard_map/gather_and_up/pallas_call | solution.py:332
  218.8 3.8 all-gather.7.cloned.1.call-done.weight_hbm.down_hbm
  222.6 69.2 %product_and_reduce.2 = (bf16[256,2048]{1,0:T(8,128)(2,1)}, bf16[128,2048]{1,0:T(8,128)(2,1)}, bf16[384,2048]{1,0:T(8,128)(2,1)}, f32[384,2048]{1,0:T(8,128)}, f32[8,2048]{1,0:T(8,128)}, /*index=5*/f32[8,2048]{1,0:T(8,128)}) custom-call(bf16[8,384,1024]{2,1,0:T(8,128)(2,1)} %get-tuple-element.69.narrow_ref.active_ref, ...), custom_call_target="tpu_custom_call" | custom-call | flops 12884901888 | bytes 150000000 | tf_op jit(solution)/shard_map/product_and_reduce/pallas_call | solution.py:759
  291.8 69.8 %gather_and_grad.1 = (bf16[8,384,2048]{2,1,0:T(8,128)(2,1)}, bf16[8,384,1024]{2,1,0:T(8,128)(2,1)}, bf16[2048,1024]{1,0:T(8,128)(2,1)}, f32[1,1024]{1,0:T(1,128)}) custom-call(bf16[384,2048]{1,0:T(8,128)(2,1)} %get-tuple-element.76.own_ref, bf16[2048,1024]{1,0:T(8,128)(2,1)} %all-gather.7.cloned.1.call-done.weight_hbm.down_hbm, ...), custom_call_target="tpu_custom_call" | custom-call | flops 25769803776 | bytes 150000000 | tf_op jit(solution)/shard_map/gather_and_grad/pallas_call | solution.py:446
  361.7 72.9 %product_and_reduce.3 = (f32[384,2048]{1,0:T(8,128)}, bf16[2048,1024]{1,0:T(8,128)(2,1)}, bf16[384,2048]{1,0:T(8,128)(2,1)}, f32[8,2048]{1,0:T(8,128)}) custom-call(bf16[8,384,1024]{2,1,0:T(8,128)(2,1)} %get-tuple-element.78.narrow_ref, bf16[2048,1024]{1,0:T(8,128)(2,1)} %all-gather.5.cloned.1.call-done.up_hbm.weight_hbm, ...), custom_call_target="tpu_custom_call" | custom-call | flops 25769803776 | bytes 150000000 | tf_op jit(solution)/shard_map/product_and_reduce/pallas_call | solution.py:759
  434.6 1.8 reduce-scatter.3.cloned.1.call-done.refs_10_
  436.4 0.7 broadcast_in_dim_reshape.4.gain_ref
  437.1 1.2 compare_convert_fusion.share_ref
  439.2 132.5 %backward_reduce.1 = (f32[512,256]{1,0:T(8,128)}, f32[512,256]{1,0:T(8,128)}, f32[64,256]{1,0:T(8,128)}, f32[16,2048]{1,0:T(8,128)}, f32[16,128]{1,0:T(8,128)}, ...) custom-call(s32[1]{0:T(128)} %dynamic_slice.6.owner_ref, f32[2]{0:T(128)} %compare_convert_fusion.share_ref, ...), custom_call_target="tpu_custom_call" | custom-call | flops 20132659200 | bytes 250000000 | tf_op jit(solution)/shard_map/backward_reduce/pallas_call | solution.py:2064
  571.7 5.5 finish.1
  577.2 1.0 copy.60
  578.2 0.8 copy.61
  (88 shorter events, 8.1 us)
Async XLA Ops:
  7.2 3.6 copy-start.12
  7.2 4.2 copy-start.14
  7.2 6.2 %copy-start.22 = (bf16[64]{0:T(256)(128)(2,1)S(1)}, bf16[64]{0:T(256)(128)(2,1)}, u32[]{:S(2)}) copy-start(bf16[64]{0:T(256)(128)(2,1)} %param.28) | copy-start | bytes 388
  7.2 6.2 %copy-start.21 = (bf16[64]{0:T(256)(128)(2,1)S(1)}, bf16[64]{0:T(256)(128)(2,1)}, u32[]{:S(2)}) copy-start(bf16[64]{0:T(256)(128)(2,1)} %param.29) | copy-start | bytes 388
  7.2 6.2 %copy-start.20 = (bf16[64]{0:T(256)(128)(2,1)S(1)}, bf16[64]{0:T(256)(128)(2,1)}, u32[]{:S(2)}) copy-start(bf16[64]{0:T(256)(128)(2,1)} %param.31) | copy-start | bytes 388
  7.2 6.2 %copy-start.19 = (bf16[64]{0:T(256)(128)(2,1)S(1)}, bf16[64]{0:T(256)(128)(2,1)}, u32[]{:S(2)}) copy-start(bf16[64]{0:T(256)(128)(2,1)} %param.35) | copy-start | bytes 388
  7.3 6.2 %copy-start.18 = (bf16[64]{0:T(256)(128)(2,1)S(1)}, bf16[64]{0:T(256)(128)(2,1)}, u32[]{:S(2)}) copy-start(bf16[64]{0:T(256)(128)(2,1)} %param.36) | copy-start | bytes 388
  7.3 6.2 %copy-start.17 = (bf16[64]{0:T(256)(128)(2,1)S(1)}, bf16[64]{0:T(256)(128)(2,1)}, u32[]{:S(2)}) copy-start(bf16[64]{0:T(256)(128)(2,1)} %param.37) | copy-start | bytes 388
  7.3 6.2 %copy-start.15 = (bf16[256]{0:T(256)(128)(2,1)S(1)}, bf16[256]{0:T(256)(128)(2,1)}, u32[]{:S(2)}) copy-start(bf16[256]{0:T(256)(128)(2,1)} %param.39) | copy-start | bytes 1540
  7.3 6.2 %copy-start.16 = (bf16[64]{0:T(256)(128)(2,1)S(1)}, bf16[64]{0:T(256)(128)(2,1)}, u32[]{:S(2)}) copy-start(bf16[64]{0:T(256)(128)(2,1)} %param.41) | copy-start | bytes 388
  7.3 6.3 %copy-start.11 = (bf16[64,256]{1,0:T(8,128)(2,1)S(1)}, bf16[64,256]{1,0:T(8,128)(2,1)}, u32[]{:S(2)}) copy-start(bf16[64,256]{1,0:T(8,128)(2,1)} %param.32) | copy-start | bytes 98308
  7.3 61.1 %all-gather.9.cloned.1.call-start = ((), (), s32[]{:S(2)}) async-start(), calls=%async_computation.6 | async-start | bytes 2621440 | tf_op jit(solution)/shard_map/all_gather | solution.py:2263
  9.3 147.9 %all-gather.5.cloned.1.call-start = ((), (), s32[]{:S(2)}) async-start(), calls=%async_computation.2 | async-start | bytes 5242880 | tf_op jit(solution)/shard_map/all_gather | solution.py:2260
  10.0 212.6 %all-gather.7.cloned.1.call-start = ((), (), s32[]{:S(2)}) async-start(), calls=%async_computation.3 | async-start | bytes 5242880 | tf_op jit(solution)/shard_map/all_gather | solution.py:2261
  10.8 425.7 %reduce-scatter.3.cloned.1.call-start = ((), (), s32[]{:S(2)}) async-start(), calls=%async_computation.4 | async-start | bytes 5242880 | tf_op jit(solution)/shard_map/reduce_scatter | solution.py:2421
  35.8 4.7 copy-start.2
  37.7 3.0 copy-start
  37.7 3.0 copy-start.1
  39.4 0.8 copy-start.7
  39.5 1.5 copy-start.23
  40.7 1.6 copy-start.5
  42.2 23.6 %copy-start.3 = (bf16[384,2048]{1,0:T(8,128)(2,1)}, bf16[384,2048]{1,0:T(8,128)(2,1)S(1)}, u32[]{:S(2)}) copy-start(bf16[384,2048]{1,0:T(8,128)(2,1)S(1)} %fusion.5.normed_ref) | copy-start | bytes 4718596
  42.2 18.9 %copy-start.24 = (s32[8]{0:T(128)S(1)}, s32[8]{0:T(128)}, u32[]{:S(2)}) copy-start(s32[8]{0:T(128)} %param.23) | copy-start | bytes 100
  60.4 7.9 %copy-start.8 = (f32[384,1]{1,0:T(8,128)}, f32[384,1]{1,0:T(8,128)S(1)}, u32[]{:S(2)}) copy-start(f32[384,1]{1,0:T(8,128)S(1)} %copy.53.refs_3_) | copy-start | bytes 4612
  65.1 2.0 copy-start.4
  65.2 2.0 copy-start.10
  361.7 210.0 %reduce-scatter.5.cloned.1.call-start = ((), (), s32[]{:S(2)}) async-start(), calls=%async_computation.5 | async-start | bytes 5242880 | tf_op jit(solution)/shard_map/reduce_scatter | solution.py:2423
  434.6 3.6 copy-start.13
  571.6 5.5 copy-start.6
  571.7 6.5 %copy-start.9 = (bf16[128,2048]{1,0:T(8,128)(2,1)S(1)}, bf16[128,2048]{1,0:T(8,128)(2,1)}, u32[]{:S(2)}) copy-start(bf16[128,2048]{1,0:T(8,128)(2,1)} %get-tuple-element.72) | copy-start | bytes 1572868
Sparse Core Ops, SparseCore 0:
  10.3 49.6 all-gather.8
  61.6 80.0 all-gather.4
  143.3 79.2 all-gather.6
  361.8 74.5 reduce-scatter.2
  438.7 103.8 reduce-scatter.4

commit v8 on v7

--- a/solution.py
+++ b/solution.py
@@ -1598,6 +1598,7 @@
     vector_come,
     vector_sum,
     vector_over,
+    row_sums,
     send_sem,
     recv_sem,
     over_send,
@@ -1622,13 +1623,13 @@
     def copy(source, target, device):
         return remote(next(counter), source, target, device, send_sem, recv_sem)
 
-    def over(index, source, target, turn):
+    def over(index, source, target, other):
         return pltpu.make_async_remote_copy(
             src_ref=source,
             dst_ref=target,
             send_sem=over_send.at[index],
             recv_sem=over_recv.at[index],
-            device_id={"grp": other_groups[turn]},
+            device_id={"grp": other},
             device_id_type=MESH,
         )
 
@@ -1645,9 +1646,10 @@
             for index in range(len(peers))
         ]
 
+    beside, beyond = group + 1 - 2 * (group % 2), (group + 2) % groups
     spans = [
-        pl.ds(pl.multiple_of(((group + 1 + chunk) % groups) * chunk_rows, chunk_rows), chunk_rows)
-        for chunk in range(groups)
+        pl.ds(pl.multiple_of(owner * chunk_rows, chunk_rows), chunk_rows)
+        for owner in ((beside + 2) % groups, beside, beyond, group)
     ]
     chunks = range(groups)
     by_x, by_y = chunks[: groups // 2], chunks[groups // 2 :]
@@ -1680,8 +1682,11 @@
     to_x = pieces_to(2, lambda kind: final.at[0, kind], on_x)
     to_y = pieces_to(1, lambda kind: final.at[1, kind], on_y)
     across = [
-        [over(2 * turn + kind, mine(3, kind).at[spans[turn]], come.at[turn, kind], turn) for kind in kinds]
-        for turn in range(groups - 1)
+        [
+            over(2 * turn + kind, mine(3, kind).at[spans[turn]], come.at[turn, kind], other)
+            for kind in kinds
+        ]
+        for turn, other in enumerate((beside, beside, beyond))
     ]
 
     def lanes(device):
@@ -1714,11 +1719,16 @@
     )
     first_over = 2 * (groups - 1)
     keyval_across = [
-        over(first_over + turn, keyval_sum.at[other_groups[turn]], keyval_over.at[turn], turn)
+        over(first_over + turn, keyval_sum.at[other_groups[turn]], keyval_over.at[turn], other_groups[turn])
         for turn in range(groups - 1)
     ]
     vector_across = [
-        over(first_over + groups - 1 + turn, vectors.at[:, lanes(here)], vector_over.at[turn], turn)
+        over(
+            first_over + groups - 1 + turn,
+            vectors.at[:, lanes(here)],
+            vector_over.at[turn],
+            other_groups[turn],
+        )
         for turn in range(groups - 1)
     ]
 
@@ -1747,6 +1757,7 @@
     own_sums[...] = jnp.zeros_like(own_sums)
     grad_normed[...] = jnp.zeros_like(grad_normed)
     vectors[...] = jnp.zeros_like(vectors)
+    row_sums[...] = jnp.zeros_like(row_sums)
     vectors[: known_up_ref.shape[0], :] = known_up_ref[...]
     vectors[4:7, :] = known_sums_ref[0:3, :]
     vectors[7:8, :] = jnp.sum(known_columns_ref[...], axis=0, keepdims=True)
@@ -1779,8 +1790,13 @@
         for source, part in enumerate((to_x, to_y)):
             part[kind][chunk].wait_recv()
             add_into(mine(3, kind).at[span], final.at[source, kind, span], chunk_rows)
-        if chunk < groups - 1:
+        if chunk < 2:
             across[chunk][kind].start()
+
+    def hand_on(kind):
+        across[0][kind].wait_recv()
+        add_into(mine(3, kind).at[spans[2]], come.at[0, kind], chunk_rows)
+        across[2][kind].start()
 
     def slot_of(turn, kind):
         place = turn // 2
@@ -1905,7 +1921,6 @@
         part[0][by_x[0]].wait_send()
     direct(0, by_y[1])
     relay(0, by_y[1])
-    close(0, by_x[0])
 
     own_prompt = prompts * prompt_rows
     total = kv_sums.total()
@@ -1921,9 +1936,7 @@
         .reshape(keyval_part.shape)
     )
     keyval_sums.start()
-    close(0, by_y[0])
-    keyval_sums.pass_on()
-    close(0, by_x[1])
+    close(0, by_x[0])
     load_hidden.wait()
     vectors[11:12, :width] = jnp.sum(
         kv_rows[:, width:].astype(jnp.float32), axis=0, keepdims=True
@@ -1946,16 +1959,20 @@
                 - scaled * jnp.mean(weighted * scaled, axis=-1, keepdims=True)
             )
             out_ref[chunk_of(turn, piece), :] = (grad_hidden[at, :] + grad_in).astype(jnp.bfloat16)
-            vectors[8:9, :] += jnp.sum(grad_out * scaled, axis=0, keepdims=True)
-            vectors[9:10, :] += jnp.sum(grad_out, axis=0, keepdims=True)
+            by_gain = grad_out * scaled
+            row_sums[:8, :] += by_gain[:8, :] + by_gain[8:, :]
+            row_sums[8:, :] += grad_out[:8, :] + grad_out[8:, :]
 
         start += out_ref.shape[0]
 
+    vectors[8:9, :] = jnp.sum(row_sums[:8, :], axis=0, keepdims=True)
+    vectors[9:10, :] = jnp.sum(row_sums[8:, :], axis=0, keepdims=True)
     for each in vector_copies:
         each.start()
-    keyval_sum[...] = keyval_sums.total().astype(jnp.bfloat16)
-    for each in keyval_across:
-        each.start()
+    close(0, by_y[0])
+    hand_on(1)
+    keyval_sums.pass_on()
+    close(0, by_x[1])
     for each in vector_copies:
         each.wait_recv()
     total = vectors[:, lanes(here)]
@@ -1964,6 +1981,10 @@
     vectors[:, lanes(here)] = total
     for each in vector_across:
         each.start()
+    keyval_sum[...] = keyval_sums.total().astype(jnp.bfloat16)
+    for each in keyval_across:
+        each.start()
+    hand_on(0)
     for each in vector_across:
         each.wait_recv()
     total = vectors[:, lanes(here)]
@@ -1981,7 +2002,7 @@
         total = total + keyval_over[turn].astype(jnp.float32)
     grad_keyval_ref[...] = total
     for kind, out_ref in ((0, grad_query_ref), (1, grad_output_ref)):
-        for turn in range(groups - 1):
+        for turn in (1, 2):
             across[turn][kind].wait_recv()
         own = pl.multiple_of(group * chunk_rows, chunk_rows)
 
@@ -1989,7 +2010,7 @@
         def _(turn):
             at = chunk_of(turn, step)
             total = kept[10 + kind, pl.ds(own + turn * step, step), :].astype(jnp.float32)
-            for other in range(groups - 1):
+            for other in (1, 2):
                 total = total + come[other, kind, at, :].astype(jnp.float32)
             out_ref[at, :] = total
 
@@ -2105,6 +2126,7 @@
             pltpu.VMEM((7, VECTOR_ROWS, block), wide),
             pltpu.VMEM((VECTOR_ROWS, block), wide),
             pltpu.VMEM((others, VECTOR_ROWS, block), wide),
+            pltpu.VMEM((16, model_width), wide),
             dma((8 + 6 * groups,)),
             dma((8 + 6 * groups,)),
             dma((4 * others,)),
@@ -2355,7 +2377,11 @@
     teacher = own_rows(prompt_teacher, answer_teacher)
     every_token = token_rows * groups * token_devices
     factors = (every_token / valid_count * valid_rows)[:, None]
+    share = (owning[:, None] == jnp.arange(prompt_count)[None, :]).astype(jnp.float32).reshape(-1)
     if kernels:
+        down_row, gain_row, share = lax.optimization_barrier(
+            (down_offset.reshape(1, -1), gain_one.reshape(1, -1), share)
+        )
         group_two, activated, slope = gather_and_up(normed_two, up_cols, up_here, 2)
         prompt_out, answer_out, grad_branch_two, grad_result, own_squares, grad_down_offset = (
             product_and_reduce(
@@ -2366,7 +2392,7 @@
                 teacher,
                 3,
                 own_prompt,
-                down_offset.reshape(1, -1),
+                down_row,
                 valid_rows[:, None],
                 factors,
             )
@@ -2422,7 +2448,6 @@
     grad_down_weight, grad_up_cols = lax.optimization_barrier((grad_down_weight, grad_up_cols))
     grad_up_weight = lax.psum_scatter(grad_up_cols, "grp", scatter_dimension=0, tiled=True)
 
-    share = (owning[:, None] == jnp.arange(prompt_count)[None, :]).astype(jnp.float32).reshape(-1)
     grad_up_place = lax.dynamic_update_slice_in_dim(
         jnp.zeros((hidden_units,), jnp.float32), grad_up_offset, ff_start, 0
     )
@@ -2449,7 +2474,7 @@
             prompt_kv,
             answer_kv,
             states,
-            gain_one,
+            gain_row,
             keyval_full,
             grad_up_place.reshape(-1, model_width),
             second_sums,
@@ -2653,7 +2678,7 @@
         rows,
         P(),
     )
-    kernels = mesh.shape["tok"] == 8
+    kernels = mesh.shape["tok"] == 8 and mesh.shape["grp"] == 4
     return jax.shard_map(
         functools.partial(body, kernels),
         mesh=mesh,

time: 591 us -> 581 us (0.983)
  Pallas kernels: 534 us -> 526 us
    pallas_call x1, Pallas kernels: 132 us -> 124 us  [backward_reduce(): pl.pallas_call(functools.partial(backward_reduce_kernel, prompts, answers...]
  transfers between devices with their start and end apart: 5 -> 5, of which waited for: 2 -> 2; matrix products, arithmetic and copies ran while one was open for 4% -> 4% of each run, Pallas kernels for 67% -> 66%
where the time goes in v8:
time: 581 us; the launch traced here: 576 us
  Pallas kernels  526 us (91%)
  between operations  17.2 us (3%)
  local copies, waits for them, and re-layouts  13.3 us (2%)
  other arithmetic  13.1 us (2%)
  waiting for transfers between devices  5.97 us (1%)
    pallas_call x2, Pallas kernels, product_and_reduce(): pl.pallas_call(functools.partial(product_reduce_kernel, with_grad), out_s...  142 us
    pallas_call x1, Pallas kernels, backward_reduce(): pl.pallas_call(functools.partial(backward_reduce_kernel, prompts, answers...  124 us
    pallas_call x1, Pallas kernels, gather_attention(): pl.pallas_call(functools.partial(gather_attention_kernel, prompts, answer...  88.5 us
    pallas_call x1, Pallas kernels, gather_and_grad(): pl.pallas_call(grad_kernel, out_shape=(jax.ShapeDtypeStruct((8, token_row...  69.8 us
    pallas_call x1, Pallas kernels, gather_and_up(): pl.pallas_call(up_kernel, out_shape=(jax.ShapeDtypeStruct((8, token_rows,...  61.7 us
    pallas_call x1, Pallas kernels, spread(): pl.pallas_call(functools.partial(spread_kernel, groups), out_shape=jax.Sh...  21.5 us
    pallas_call x1, Pallas kernels, tok_gather_small(): pl.pallas_call(small_gather_kernel, out_shape=jax.ShapeDtypeStruct((promp...  12.5 us
  transfers between devices with their start and end apart: 5, of which 2 were waited for; matrix products, arithmetic and copies ran while one was open for 4% of the time, Pallas kernels for 66%

profile of v8, /device:TPU:0, one launch (start us, length us, event | category | flops | bytes accessed | tf_op | source)
XLA Modules:
  0.0 576.2 jit_solution(7270012200456135536)
XLA Ops:
  7.4 1.9 pad_maximum_fusion.2
  9.3 0.7 all-gather.5.cloned.1.call-update
  10.1 0.7 all-gather.7.cloned.1.call-update
  14.2 21.5 %spread.1 = bf16[8,4,80,256]{3,2,1,0:T(8,128)(2,1)} custom-call(bf16[80,256]{1,0:T(8,128)(2,1)} %pad_maximum_fusion.3.own_ref), custom_call_target="tpu_custom_call" | custom-call | tf_op jit(solution)/shard_map/spread/pallas_call | solution.py:138
  35.8 1.9 slice_convert_fusion
  37.7 1.4 reshape.220
  39.5 0.8 copy-done.7
  42.9 0.7 slice.62
  44.2 0.7 broadcast_in_dim_reshape.4.gain_ref
  44.9 12.5 %tok_gather_small.1.prompt_kv_ref = bf16[2,1024,256]{2,1,0:T(8,128)(2,1)} custom-call(bf16[2,128,256]{2,1,0:T(8,128)(2,1)} %bitcast.58), custom_call_target="tpu_custom_call" | custom-call | tf_op jit(solution)/shard_map/tok_gather_small/pallas_call | solution.py:800
  57.3 0.7 reshape_reshape.17.bias_ref
  58.0 0.7 reshape_reshape.18.offset_ref
  58.7 0.7 reshape_reshape.19.gain_ref.refs_3_
  59.4 0.7 reshape_reshape.20.shift_ref
  60.1 0.9 slice_bitcast_fusion.1
  61.1 0.7 reshape_reshape.21.refs_2_
  62.4 1.2 compare_convert_fusion.share_ref
  64.2 1.5 slice_reduce_fusion
  67.0 0.7 broadcast_multiply_fusion.refs_4_
  67.7 1.2 pad_maximum_fusion.states_ref
  68.9 1.3 pad_maximum_fusion.1.refs_1_
  70.2 88.5 %gather_attention.1 = (bf16[8,4,2,512,256]{4,3,2,1,0:T(8,128)(2,1)}, bf16[8,384,256]{2,1,0:T(8,128)(2,1)}, bf16[8,384,256]{2,1,0:T(8,128)(2,1)}, f32[8,2,384]{2,...) custom-call(s32[1]{0:T(128)} %dynamic_slice.6.owner_ref, bf16[4,2,512,256]{3,2,1,0:T(8,128)(2,1)} %bitcast.68, ...), custom_call_target="tpu_custom_call" | custom-call | flops 12884901888 | bytes 250000000 | tf_op jit(solution)/shard_map/gather_attention/pallas_call | solution.py:1185
  158.7 61.7 %gather_and_up.1 = (bf16[8,384,2048]{2,1,0:T(8,128)(2,1)}, bf16[8,384,1024]{2,1,0:T(8,128)(2,1)}, bf16[8,384,1024]{2,1,0:T(8,128)(2,1)}) custom-call(bf16[384,2048]{1,0:T(8,128)(2,1)} %get-tuple-element.71.own_ref, bf16[2048,1024]{1,0:T(8,128)(2,1)} %all-gather.5.cloned.1.call-done.up_hbm.weight_hbm, f32[1,1024]{1,0:T(1,128)} %bitcast.66), custom_call_target="tpu_custom_call" | custom-call | flops 12884901888 | bytes 150000000 | tf_op jit(solution)/shard_map/gather_and_up/pallas_call | solution.py:332
  220.4 2.2 all-gather.7.cloned.1.call-done.weight_hbm.down_hbm
  222.6 69.2 %product_and_reduce.2 = (bf16[256,2048]{1,0:T(8,128)(2,1)}, bf16[128,2048]{1,0:T(8,128)(2,1)}, bf16[384,2048]{1,0:T(8,128)(2,1)}, f32[384,2048]{1,0:T(8,128)}, f32[8,2048]{1,0:T(8,128)}, /*index=5*/f32[8,2048]{1,0:T(8,128)}) custom-call(bf16[8,384,1024]{2,1,0:T(8,128)(2,1)} %get-tuple-element.72.narrow_ref.active_ref, ...), custom_call_target="tpu_custom_call" | custom-call | flops 12884901888 | bytes 150000000 | tf_op jit(solution)/shard_map/product_and_reduce/pallas_call | solution.py:759
  291.8 69.8 %gather_and_grad.1 = (bf16[8,384,2048]{2,1,0:T(8,128)(2,1)}, bf16[8,384,1024]{2,1,0:T(8,128)(2,1)}, bf16[2048,1024]{1,0:T(8,128)(2,1)}, f32[1,1024]{1,0:T(1,128)}) custom-call(bf16[384,2048]{1,0:T(8,128)(2,1)} %get-tuple-element.81.own_ref, bf16[2048,1024]{1,0:T(8,128)(2,1)} %all-gather.7.cloned.1.call-done.weight_hbm.down_hbm, ...), custom_call_target="tpu_custom_call" | custom-call | flops 25769803776 | bytes 150000000 | tf_op jit(solution)/shard_map/gather_and_grad/pallas_call | solution.py:446
  361.7 72.9 %product_and_reduce.3 = (f32[384,2048]{1,0:T(8,128)}, bf16[2048,1024]{1,0:T(8,128)(2,1)}, bf16[384,2048]{1,0:T(8,128)(2,1)}, f32[8,2048]{1,0:T(8,128)}) custom-call(bf16[8,384,1024]{2,1,0:T(8,128)(2,1)} %get-tuple-element.83.narrow_ref, bf16[2048,1024]{1,0:T(8,128)(2,1)} %all-gather.5.cloned.1.call-done.up_hbm.weight_hbm, ...), custom_call_target="tpu_custom_call" | custom-call | flops 25769803776 | bytes 150000000 | tf_op jit(solution)/shard_map/product_and_reduce/pallas_call | solution.py:759
  434.6 2.3 reduce-scatter.3.cloned.1.call-done.refs_10_
  437.9 124.1 %backward_reduce.1 = (f32[512,256]{1,0:T(8,128)}, f32[512,256]{1,0:T(8,128)}, f32[64,256]{1,0:T(8,128)}, f32[16,2048]{1,0:T(8,128)}, f32[16,128]{1,0:T(8,128)}, ...) custom-call(s32[1]{0:T(128)} %dynamic_slice.6.owner_ref, f32[2]{0:T(128)} %compare_convert_fusion.share_ref, ...), custom_call_target="tpu_custom_call" | custom-call | flops 20132659200 | bytes 250000000 | tf_op jit(solution)/shard_map/backward_reduce/pallas_call | solution.py:2085
  562.1 5.5 finish.1
  567.6 1.0 copy.60
  568.6 0.8 copy.61
  (88 shorter events, 8.1 us)
Async XLA Ops:
  7.2 3.6 copy-start.12
  7.2 4.2 copy-start.14
  7.2 6.2 %copy-start.22 = (bf16[64]{0:T(256)(128)(2,1)S(1)}, bf16[64]{0:T(256)(128)(2,1)}, u32[]{:S(2)}) copy-start(bf16[64]{0:T(256)(128)(2,1)} %param.28) | copy-start | bytes 388
  7.2 6.2 %copy-start.21 = (bf16[64]{0:T(256)(128)(2,1)S(1)}, bf16[64]{0:T(256)(128)(2,1)}, u32[]{:S(2)}) copy-start(bf16[64]{0:T(256)(128)(2,1)} %param.29) | copy-start | bytes 388
  7.2 6.2 %copy-start.20 = (bf16[64]{0:T(256)(128)(2,1)S(1)}, bf16[64]{0:T(256)(128)(2,1)}, u32[]{:S(2)}) copy-start(bf16[64]{0:T(256)(128)(2,1)} %param.31) | copy-start | bytes 388
  7.2 6.2 %copy-start.19 = (bf16[64]{0:T(256)(128)(2,1)S(1)}, bf16[64]{0:T(256)(128)(2,1)}, u32[]{:S(2)}) copy-start(bf16[64]{0:T(256)(128)(2,1)} %param.35) | copy-start | bytes 388
  7.3 6.2 %copy-start.18 = (bf16[64]{0:T(256)(128)(2,1)S(1)}, bf16[64]{0:T(256)(128)(2,1)}, u32[]{:S(2)}) copy-start(bf16[64]{0:T(256)(128)(2,1)} %param.36) | copy-start | bytes 388
  7.3 6.2 %copy-start.17 = (bf16[64]{0:T(256)(128)(2,1)S(1)}, bf16[64]{0:T(256)(128)(2,1)}, u32[]{:S(2)}) copy-start(bf16[64]{0:T(256)(128)(2,1)} %param.37) | copy-start | bytes 388
  7.3 6.2 %copy-start.15 = (bf16[256]{0:T(256)(128)(2,1)S(1)}, bf16[256]{0:T(256)(128)(2,1)}, u32[]{:S(2)}) copy-start(bf16[256]{0:T(256)(128)(2,1)} %param.39) | copy-start | bytes 1540
  7.3 6.2 %copy-start.16 = (bf16[64]{0:T(256)(128)(2,1)S(1)}, bf16[64]{0:T(256)(128)(2,1)}, u32[]{:S(2)}) copy-start(bf16[64]{0:T(256)(128)(2,1)} %param.41) | copy-start | bytes 388
  7.3 6.3 %copy-start.11 = (bf16[64,256]{1,0:T(8,128)(2,1)S(1)}, bf16[64,256]{1,0:T(8,128)(2,1)}, u32[]{:S(2)}) copy-start(bf16[64,256]{1,0:T(8,128)(2,1)} %param.32) | copy-start | bytes 98308
  7.3 62.9 %all-gather.9.cloned.1.call-start = ((), (), s32[]{:S(2)}) async-start(), calls=%async_computation.6 | async-start | bytes 2621440 | tf_op jit(solution)/shard_map/all_gather | solution.py:2285
  9.3 149.5 %all-gather.5.cloned.1.call-start = ((), (), s32[]{:S(2)}) async-start(), calls=%async_computation.2 | async-start | bytes 5242880 | tf_op jit(solution)/shard_map/all_gather | solution.py:2282
  10.0 212.6 %all-gather.7.cloned.1.call-start = ((), (), s32[]{:S(2)}) async-start(), calls=%async_computation.3 | async-start | bytes 5242880 | tf_op jit(solution)/shard_map/all_gather | solution.py:2283
  10.8 426.2 %reduce-scatter.3.cloned.1.call-start = ((), (), s32[]{:S(2)}) async-start(), calls=%async_computation.4 | async-start | bytes 5242880 | tf_op jit(solution)/shard_map/reduce_scatter | solution.py:2447
  35.8 4.7 copy-start.2
  37.7 3.0 copy-start
  37.7 3.0 copy-start.1
  39.4 0.8 copy-start.7
  39.5 1.5 copy-start.23
  40.7 1.6 copy-start.5
  42.2 25.5 %copy-start.3 = (bf16[384,2048]{1,0:T(8,128)(2,1)}, bf16[384,2048]{1,0:T(8,128)(2,1)S(1)}, u32[]{:S(2)}) copy-start(bf16[384,2048]{1,0:T(8,128)(2,1)S(1)} %fusion.5.normed_ref) | copy-start | bytes 4718596
  42.2 19.6 %copy-start.24 = (s32[8]{0:T(128)S(1)}, s32[8]{0:T(128)}, u32[]{:S(2)}) copy-start(s32[8]{0:T(128)} %param.23) | copy-start | bytes 100
  61.1 9.1 %copy-start.8 = (f32[384,1]{1,0:T(8,128)}, f32[384,1]{1,0:T(8,128)S(1)}, u32[]{:S(2)}) copy-start(f32[384,1]{1,0:T(8,128)S(1)} %copy.53.refs_3_) | copy-start | bytes 4612
  67.0 2.0 copy-start.4
  67.0 2.0 copy-start.10
  361.7 200.4 %reduce-scatter.5.cloned.1.call-start = ((), (), s32[]{:S(2)}) async-start(), calls=%async_computation.5 | async-start | bytes 5242880 | tf_op jit(solution)/shard_map/reduce_scatter | solution.py:2449
  434.6 2.4 copy-start.13
  562.1 5.5 copy-start.6
  562.1 6.5 %copy-start.9 = (bf16[128,2048]{1,0:T(8,128)(2,1)S(1)}, bf16[128,2048]{1,0:T(8,128)(2,1)}, u32[]{:S(2)}) copy-start(bf16[128,2048]{1,0:T(8,128)(2,1)} %get-tuple-element.76) | copy-start | bytes 1572868
Sparse Core Ops, SparseCore 0:
  10.3 49.6 all-gather.8
  61.6 80.0 all-gather.4
  143.3 79.2 all-gather.6
  361.8 75.1 reduce-scatter.2
  439.2 89.8 reduce-scatter.4

commit v9 on v8

--- a/solution.py
+++ b/solution.py
@@ -1902,15 +1902,15 @@
         @pl.when(turn == 6)
         def _():
             join(0, 2)
-            for chunk in (by_x[0], by_y[0]):
+            for chunk in by_x:
                 direct(0, chunk)
-            for chunk in (by_x[0], by_y[0]):
+            for chunk in by_x:
                 relay(0, chunk)
 
         @pl.when(turn == 7)
         def _():
-            direct(0, by_x[1])
-            relay(0, by_x[1])
+            direct(0, by_y[0])
+            relay(0, by_y[0])
 
     kv_part[:, :, :width] = (key_sums[:, :, :width] * scale).astype(jnp.bfloat16)
     kv_part[:, :, width:] = key_sums[:, :, width:].astype(jnp.bfloat16)
@@ -1969,10 +1969,10 @@
     vectors[9:10, :] = jnp.sum(row_sums[8:, :], axis=0, keepdims=True)
     for each in vector_copies:
         each.start()
-    close(0, by_y[0])
+    close(0, by_x[1])
     hand_on(1)
     keyval_sums.pass_on()
-    close(0, by_x[1])
+    close(0, by_y[0])
     for each in vector_copies:
         each.wait_recv()
     total = vectors[:, lanes(here)]

time: 581 us -> 583 us (level)
  no operation moved by 1% of the time
where the time goes in v9:
time: 583 us; the launch traced here: 578 us
  Pallas kernels  527 us (90%)
  between operations  17.2 us (3%)
  local copies, waits for them, and re-layouts  13.3 us (2%)
  other arithmetic  13.1 us (2%)
  waiting for transfers between devices  5.97 us (1%)
    pallas_call x2, Pallas kernels, product_and_reduce(): pl.pallas_call(functools.partial(product_reduce_kernel, with_grad), out_s...  142 us
    pallas_call x1, Pallas kernels, backward_reduce(): pl.pallas_call(functools.partial(backward_reduce_kernel, prompts, answers...  125 us
    pallas_call x1, Pallas kernels, gather_attention(): pl.pallas_call(functools.partial(gather_attention_kernel, prompts, answer...  88.5 us
    pallas_call x1, Pallas kernels, gather_and_grad(): pl.pallas_call(grad_kernel, out_shape=(jax.ShapeDtypeStruct((8, token_row...  69.8 us
    pallas_call x1, Pallas kernels, gather_and_up(): pl.pallas_call(up_kernel, out_shape=(jax.ShapeDtypeStruct((8, token_rows,...  61.7 us
    pallas_call x1, Pallas kernels, spread(): pl.pallas_call(functools.partial(spread_kernel, groups), out_shape=jax.Sh...  21.5 us
    pallas_call x1, Pallas kernels, tok_gather_small(): pl.pallas_call(small_gather_kernel, out_shape=jax.ShapeDtypeStruct((promp...  12.5 us
  transfers between devices with their start and end apart: 5, of which 2 were waited for; matrix products, arithmetic and copies ran while one was open for 4% of the time, Pallas kernels for 66%

profile of v9, /device:TPU:0, one launch (start us, length us, event | category | flops | bytes accessed | tf_op | source)
XLA Modules:
  0.0 577.5 jit_solution(3588931559913129974)
XLA Ops:
  7.4 1.9 pad_maximum_fusion.2
  9.3 0.7 all-gather.5.cloned.1.call-update
  10.1 0.7 all-gather.7.cloned.1.call-update
  14.2 21.5 %spread.1 = bf16[8,4,80,256]{3,2,1,0:T(8,128)(2,1)} custom-call(bf16[80,256]{1,0:T(8,128)(2,1)} %pad_maximum_fusion.3.own_ref), custom_call_target="tpu_custom_call" | custom-call | tf_op jit(solution)/shard_map/spread/pallas_call | solution.py:138
  35.8 1.9 slice_convert_fusion
  37.7 1.4 reshape.220
  39.5 0.8 copy-done.7
  42.9 0.7 slice.62
  44.2 0.7 broadcast_in_dim_reshape.4.gain_ref
  44.9 12.5 %tok_gather_small.1.prompt_kv_ref = bf16[2,1024,256]{2,1,0:T(8,128)(2,1)} custom-call(bf16[2,128,256]{2,1,0:T(8,128)(2,1)} %bitcast.58), custom_call_target="tpu_custom_call" | custom-call | tf_op jit(solution)/shard_map/tok_gather_small/pallas_call | solution.py:800
  57.3 0.7 reshape_reshape.17.bias_ref
  58.0 0.7 reshape_reshape.18.offset_ref
  58.7 0.7 reshape_reshape.19.gain_ref.refs_3_
  59.4 0.7 reshape_reshape.20.shift_ref
  60.1 0.9 slice_bitcast_fusion.1
  61.1 0.7 reshape_reshape.21.refs_2_
  62.4 1.2 compare_convert_fusion.share_ref
  64.2 1.5 slice_reduce_fusion
  67.0 0.7 broadcast_multiply_fusion.refs_4_
  67.7 1.2 pad_maximum_fusion.states_ref
  68.9 1.3 pad_maximum_fusion.1.refs_1_
  70.2 88.5 %gather_attention.1 = (bf16[8,4,2,512,256]{4,3,2,1,0:T(8,128)(2,1)}, bf16[8,384,256]{2,1,0:T(8,128)(2,1)}, bf16[8,384,256]{2,1,0:T(8,128)(2,1)}, f32[8,2,384]{2,...) custom-call(s32[1]{0:T(128)} %dynamic_slice.6.owner_ref, bf16[4,2,512,256]{3,2,1,0:T(8,128)(2,1)} %bitcast.68, ...), custom_call_target="tpu_custom_call" | custom-call | flops 12884901888 | bytes 250000000 | tf_op jit(solution)/shard_map/gather_attention/pallas_call | solution.py:1185
  158.7 61.7 %gather_and_up.1 = (bf16[8,384,2048]{2,1,0:T(8,128)(2,1)}, bf16[8,384,1024]{2,1,0:T(8,128)(2,1)}, bf16[8,384,1024]{2,1,0:T(8,128)(2,1)}) custom-call(bf16[384,2048]{1,0:T(8,128)(2,1)} %get-tuple-element.71.own_ref, bf16[2048,1024]{1,0:T(8,128)(2,1)} %all-gather.5.cloned.1.call-done.up_hbm.weight_hbm, f32[1,1024]{1,0:T(1,128)} %bitcast.66), custom_call_target="tpu_custom_call" | custom-call | flops 12884901888 | bytes 150000000 | tf_op jit(solution)/shard_map/gather_and_up/pallas_call | solution.py:332
  220.4 2.2 all-gather.7.cloned.1.call-done.weight_hbm.down_hbm
  222.6 69.2 %product_and_reduce.2 = (bf16[256,2048]{1,0:T(8,128)(2,1)}, bf16[128,2048]{1,0:T(8,128)(2,1)}, bf16[384,2048]{1,0:T(8,128)(2,1)}, f32[384,2048]{1,0:T(8,128)}, f32[8,2048]{1,0:T(8,128)}, /*index=5*/f32[8,2048]{1,0:T(8,128)}) custom-call(bf16[8,384,1024]{2,1,0:T(8,128)(2,1)} %get-tuple-element.72.narrow_ref.active_ref, ...), custom_call_target="tpu_custom_call" | custom-call | flops 12884901888 | bytes 150000000 | tf_op jit(solution)/shard_map/product_and_reduce/pallas_call | solution.py:759
  291.8 69.8 %gather_and_grad.1 = (bf16[8,384,2048]{2,1,0:T(8,128)(2,1)}, bf16[8,384,1024]{2,1,0:T(8,128)(2,1)}, bf16[2048,1024]{1,0:T(8,128)(2,1)}, f32[1,1024]{1,0:T(1,128)}) custom-call(bf16[384,2048]{1,0:T(8,128)(2,1)} %get-tuple-element.81.own_ref, bf16[2048,1024]{1,0:T(8,128)(2,1)} %all-gather.7.cloned.1.call-done.weight_hbm.down_hbm, ...), custom_call_target="tpu_custom_call" | custom-call | flops 25769803776 | bytes 150000000 | tf_op jit(solution)/shard_map/gather_and_grad/pallas_call | solution.py:446
  361.7 72.9 %product_and_reduce.3 = (f32[384,2048]{1,0:T(8,128)}, bf16[2048,1024]{1,0:T(8,128)(2,1)}, bf16[384,2048]{1,0:T(8,128)(2,1)}, f32[8,2048]{1,0:T(8,128)}) custom-call(bf16[8,384,1024]{2,1,0:T(8,128)(2,1)} %get-tuple-element.83.narrow_ref, bf16[2048,1024]{1,0:T(8,128)(2,1)} %all-gather.5.cloned.1.call-done.up_hbm.weight_hbm, ...), custom_call_target="tpu_custom_call" | custom-call | flops 25769803776 | bytes 150000000 | tf_op jit(solution)/shard_map/product_and_reduce/pallas_call | solution.py:759
  434.6 2.3 reduce-scatter.3.cloned.1.call-done.refs_10_
  437.9 125.5 %backward_reduce.1 = (f32[512,256]{1,0:T(8,128)}, f32[512,256]{1,0:T(8,128)}, f32[64,256]{1,0:T(8,128)}, f32[16,2048]{1,0:T(8,128)}, f32[16,128]{1,0:T(8,128)}, ...) custom-call(s32[1]{0:T(128)} %dynamic_slice.6.owner_ref, f32[2]{0:T(128)} %compare_convert_fusion.share_ref, ...), custom_call_target="tpu_custom_call" | custom-call | flops 20132659200 | bytes 250000000 | tf_op jit(solution)/shard_map/backward_reduce/pallas_call | solution.py:2085
  563.5 5.5 finish.1
  569.0 1.0 copy.60
  570.0 0.8 copy.61
  (88 shorter events, 8.1 us)
Async XLA Ops:
  7.2 3.6 copy-start.12
  7.2 4.2 copy-start.14
  7.2 6.2 %copy-start.22 = (bf16[64]{0:T(256)(128)(2,1)S(1)}, bf16[64]{0:T(256)(128)(2,1)}, u32[]{:S(2)}) copy-start(bf16[64]{0:T(256)(128)(2,1)} %param.28) | copy-start | bytes 388
  7.2 6.2 %copy-start.21 = (bf16[64]{0:T(256)(128)(2,1)S(1)}, bf16[64]{0:T(256)(128)(2,1)}, u32[]{:S(2)}) copy-start(bf16[64]{0:T(256)(128)(2,1)} %param.29) | copy-start | bytes 388
  7.2 6.2 %copy-start.20 = (bf16[64]{0:T(256)(128)(2,1)S(1)}, bf16[64]{0:T(256)(128)(2,1)}, u32[]{:S(2)}) copy-start(bf16[64]{0:T(256)(128)(2,1)} %param.31) | copy-start | bytes 388
  7.2 6.2 %copy-start.19 = (bf16[64]{0:T(256)(128)(2,1)S(1)}, bf16[64]{0:T(256)(128)(2,1)}, u32[]{:S(2)}) copy-start(bf16[64]{0:T(256)(128)(2,1)} %param.35) | copy-start | bytes 388
  7.3 6.2 %copy-start.18 = (bf16[64]{0:T(256)(128)(2,1)S(1)}, bf16[64]{0:T(256)(128)(2,1)}, u32[]{:S(2)}) copy-start(bf16[64]{0:T(256)(128)(2,1)} %param.36) | copy-start | bytes 388
  7.3 6.2 %copy-start.17 = (bf16[64]{0:T(256)(128)(2,1)S(1)}, bf16[64]{0:T(256)(128)(2,1)}, u32[]{:S(2)}) copy-start(bf16[64]{0:T(256)(128)(2,1)} %param.37) | copy-start | bytes 388
  7.3 6.2 %copy-start.15 = (bf16[256]{0:T(256)(128)(2,1)S(1)}, bf16[256]{0:T(256)(128)(2,1)}, u32[]{:S(2)}) copy-start(bf16[256]{0:T(256)(128)(2,1)} %param.39) | copy-start | bytes 1540
  7.3 6.2 %copy-start.16 = (bf16[64]{0:T(256)(128)(2,1)S(1)}, bf16[64]{0:T(256)(128)(2,1)}, u32[]{:S(2)}) copy-start(bf16[64]{0:T(256)(128)(2,1)} %param.41) | copy-start | bytes 388
  7.3 6.3 %copy-start.11 = (bf16[64,256]{1,0:T(8,128)(2,1)S(1)}, bf16[64,256]{1,0:T(8,128)(2,1)}, u32[]{:S(2)}) copy-start(bf16[64,256]{1,0:T(8,128)(2,1)} %param.32) | copy-start | bytes 98308
  7.3 62.9 %all-gather.9.cloned.1.call-start = ((), (), s32[]{:S(2)}) async-start(), calls=%async_computation.6 | async-start | bytes 2621440 | tf_op jit(solution)/shard_map/all_gather | solution.py:2285
  9.3 149.5 %all-gather.5.cloned.1.call-start = ((), (), s32[]{:S(2)}) async-start(), calls=%async_computation.2 | async-start | bytes 5242880 | tf_op jit(solution)/shard_map/all_gather | solution.py:2282
  10.0 212.6 %all-gather.7.cloned.1.call-start = ((), (), s32[]{:S(2)}) async-start(), calls=%async_computation.3 | async-start | bytes 5242880 | tf_op jit(solution)/shard_map/all_gather | solution.py:2283
  10.8 426.2 %reduce-scatter.3.cloned.1.call-start = ((), (), s32[]{:S(2)}) async-start(), calls=%async_computation.4 | async-start | bytes 5242880 | tf_op jit(solution)/shard_map/reduce_scatter | solution.py:2447
  35.8 4.7 copy-start.2
  37.7 3.0 copy-start
  37.7 3.0 copy-start.1
  39.4 0.8 copy-start.7
  39.5 1.5 copy-start.23
  40.7 1.6 copy-start.5
  42.2 25.5 %copy-start.3 = (bf16[384,2048]{1,0:T(8,128)(2,1)}, bf16[384,2048]{1,0:T(8,128)(2,1)S(1)}, u32[]{:S(2)}) copy-start(bf16[384,2048]{1,0:T(8,128)(2,1)S(1)} %fusion.5.normed_ref) | copy-start | bytes 4718596
  42.2 19.6 %copy-start.24 = (s32[8]{0:T(128)S(1)}, s32[8]{0:T(128)}, u32[]{:S(2)}) copy-start(s32[8]{0:T(128)} %param.23) | copy-start | bytes 100
  61.1 9.1 %copy-start.8 = (f32[384,1]{1,0:T(8,128)}, f32[384,1]{1,0:T(8,128)S(1)}, u32[]{:S(2)}) copy-start(f32[384,1]{1,0:T(8,128)S(1)} %copy.53.refs_3_) | copy-start | bytes 4612
  67.0 2.0 copy-start.4
  67.0 2.0 copy-start.10
  361.7 201.8 %reduce-scatter.5.cloned.1.call-start = ((), (), s32[]{:S(2)}) async-start(), calls=%async_computation.5 | async-start | bytes 5242880 | tf_op jit(solution)/shard_map/reduce_scatter | solution.py:2449
  434.6 2.4 copy-start.13
  563.4 5.5 copy-start.6
  563.5 6.5 %copy-start.9 = (bf16[128,2048]{1,0:T(8,128)(2,1)S(1)}, bf16[128,2048]{1,0:T(8,128)(2,1)}, u32[]{:S(2)}) copy-start(bf16[128,2048]{1,0:T(8,128)(2,1)} %get-tuple-element.76) | copy-start | bytes 1572868
Sparse Core Ops, SparseCore 0:
  10.3 49.6 all-gather.8
  61.6 80.0 all-gather.4
  143.3 79.2 all-gather.6
  361.8 75.1 reduce-scatter.2
  439.2 89.8 reduce-scatter.4
